TPU v7x, 32 devices: a whole 2x2x4 slice. The times are simulated.
32 devices in a mesh: tensor: 2 (over core), dp: 4 (over z), ctx: 4 (over y, x).
Axes of the slice: x: 2, y: 2, z: 4, core: 2. Of those that a mesh axis runs over, the one named last changes fastest.
Arguments:
- tokens: bfloat16 [4, 1024, 2560], P('dp', 'ctx'), may hold values from -6 to 6
- segments: int32 [4, 1024], P('dp'), may hold values from 0 to 2, as said below
- gain_attn: bfloat16 [2560], replicated, may hold values from 0.5 to 1.5
- w_qa: bfloat16 [2560, 768], replicated, may hold values from -0.125 to 0.125
- gain_q: bfloat16 [768], replicated, may hold values from 0.5 to 1.5
- w_kva: bfloat16 [2560, 288], replicated, may hold values from -0.125 to 0.125
- gain_kv: bfloat16 [256], replicated, may hold values from 0.5 to 1.5
- w_qb: bfloat16 [768, 3840], P(None, 'tensor'), may hold values from -0.3125 to 0.3125
- w_kvb: bfloat16 [256, 5120], P(None, 'tensor'), may hold values from -0.375 to 0.375
- w_o: bfloat16 [2560, 2560], P(('dp', 'ctx'), 'tensor'), may hold values from -3 to 3
- gain_mlp: bfloat16 [2560], replicated, may hold values from 0.5 to 1.5
- w_gate: bfloat16 [2560, 6400], P(('dp', 'ctx'), 'tensor'), may hold values from -0.125 to 0.125
- w_up: bfloat16 [2560, 6400], P(('dp', 'ctx'), 'tensor'), may hold values from -0.125 to 0.125
- w_down: bfloat16 [2560, 6400], P(('dp', 'ctx'), 'tensor'), may hold values from -0.625 to 0.625
- cotangent: bfloat16 [4, 1024, 2560], P('dp', 'ctx'), may hold values from -6 to 6
Outputs:
- layer_out: bfloat16 [4, 1024, 2560], P('dp', 'ctx')
- grad_tokens: bfloat16 [4, 1024, 2560], P('dp', 'ctx')
- grad_gain_attn: float32 [2560], replicated
- grad_w_qa: float32 [2560, 768], P(('dp', 'ctx'))
- grad_gain_q: float32 [768], replicated
- grad_w_kva: float32 [2560, 288], P(('dp', 'ctx'))
- grad_gain_kv: float32 [256], replicated
- grad_w_qb: float32 [768, 3840], P(None, 'tensor')
- grad_w_kvb: float32 [256, 5120], P(None, 'tensor')
- grad_w_o: float32 [2560, 2560], P(('dp', 'ctx'), 'tensor')
- grad_gain_mlp: float32 [2560], replicated
- grad_w_gate: float32 [2560, 6400], P(('dp', 'ctx'), 'tensor')
- grad_w_up: float32 [2560, 6400], P(('dp', 'ctx'), 'tensor')
- grad_w_down: float32 [2560, 6400], P(('dp', 'ctx'), 'tensor')
Inputs may be any that keep to these rules, and one draw needn't show every extreme that they name: `segments`: in each sequence the segment numbers start at 0, never fall, rise by at most one from a token to the next, and the last token has number 2.
All inputs are finite; a program needn't handle non-finite values.
Results may differ from a plain program's by a relative error of at most 0.02.
Values may be sent and summed in bfloat16 or wider, within the bound.
No kernel may reach another device: no remote copies, remote signals or barrier semaphores. Data moves between devices by JAX's collectives and lax.ppermute only.
A program may use at most 640 MiB of HBM per device.

v0:
```python
import math

import jax
import jax.numpy as jnp
from jax import lax
from jax.sharding import PartitionSpec as P

NOPE = 64
ROPE = 32
VDIM = 64
KVRANK = 256


eps_norm = 1e-05
res_scale = 1.4 / math.sqrt(62.0)
rope_base = 10000.0
masked_score = -1e30
precise = lax.Precision.HIGHEST


def rms_scale(values):
    return values * lax.rsqrt(jnp.mean(values * values, axis=-1, keepdims=True) + eps_norm)


def rms_back(values, grad):
    return jax.vjp(rms_scale, values)[1](grad)[0]


def rotary_tables(positions):
    freqs = rope_base ** (-jnp.arange(0, ROPE, 2).astype(jnp.float32) / ROPE)
    angles = positions.astype(jnp.float32)[:, None] * freqs[None, :]
    angles = jnp.concatenate([angles, angles], axis=1)
    return (jnp.cos(angles), jnp.sin(angles))


def rotate(values, cosine, sine):
    half = values.shape[-1] // 2
    turned = jnp.concatenate([-values[..., half:], values[..., :half]], axis=-1)
    return values * cosine + turned * sine


def rotate_back(grad, cosine, sine):
    half = grad.shape[-1] // 2
    scaled = grad * sine
    turned = jnp.concatenate([scaled[..., half:], -scaled[..., :half]], axis=-1)
    return grad * cosine + turned


def body(
    tokens,
    segments,
    gain_attn,
    w_qa,
    gain_q,
    w_kva,
    gain_kv,
    w_qb,
    w_kvb,
    w_o,
    gain_mlp,
    w_gate,
    w_up,
    w_down,
    cotangent,
):
    rows = tokens.shape[1]
    segment_all = segments[0]
    length = segment_all.shape[0]
    first_row = lax.axis_index("ctx") * rows
    local_index = first_row + jnp.arange(rows, dtype=jnp.int32)
    segment_own = lax.dynamic_slice_in_dim(segment_all, first_row, rows)
    doc_start = jnp.sum((segment_all[None, :] < segment_own[:, None]).astype(jnp.int32), axis=1)
    cosine, sine = rotary_tables(local_index - doc_start)
    allowed = (segment_own[:, None] == segment_all[None, :]) & (
        jnp.arange(length, dtype=jnp.int32)[None, :] <= local_index[:, None]
    )
    gain_in = gain_attn.astype(jnp.float32)
    gain_query = gain_q.astype(jnp.float32)
    gain_latent = gain_kv.astype(jnp.float32)
    gain_middle = gain_mlp.astype(jnp.float32)
    w_kvb_wide = w_kvb.astype(jnp.float32)
    hidden_in = tokens[0].astype(jnp.float32)
    scaled_in = rms_scale(hidden_in)
    normed_in = (scaled_in * gain_in).astype(jnp.bfloat16)
    q_latent = jnp.dot(normed_in, w_qa, preferred_element_type=jnp.float32)
    q_scaled = rms_scale(q_latent)
    q_normed = (q_scaled * gain_query).astype(jnp.bfloat16)
    kv_latent = jnp.dot(normed_in, w_kva, preferred_element_type=jnp.float32)
    c_round = rms_scale(kv_latent[:, :KVRANK]).astype(jnp.bfloat16)
    c_round_wide = c_round.astype(jnp.float32)
    key_rope = rotate(kv_latent[:, KVRANK:], cosine, sine).astype(jnp.bfloat16)
    heads_local = w_qb.shape[1] // (NOPE + ROPE)
    q_raw = jnp.dot(q_normed, w_qb, preferred_element_type=jnp.float32).reshape(
        rows, heads_local, NOPE + ROPE
    )
    q_rot = jnp.concatenate(
        [q_raw[..., :NOPE], rotate(q_raw[..., NOPE:], cosine[:, None, :], sine[:, None, :])],
        axis=-1,
    ).astype(jnp.bfloat16)
    payload = (c_round, key_rope)
    shared, rope_all = (
        lax.all_gather(payload[0], "ctx", axis=0, tiled=True),
        lax.all_gather(payload[1], "ctx", axis=0, tiled=True),
    )
    c_normed_all = (shared.astype(jnp.float32) * gain_latent).astype(jnp.bfloat16)
    kv_all = jnp.dot(c_normed_all, w_kvb, preferred_element_type=jnp.float32).astype(jnp.bfloat16)
    kv_heads = kv_all.reshape(length, heads_local, NOPE + VDIM)
    keys = jnp.concatenate(
        [kv_heads[..., :NOPE], jnp.broadcast_to(rope_all[:, None, :], (length, heads_local, ROPE))],
        axis=-1,
    )
    value_heads = kv_heads[..., NOPE:]
    group = math.gcd(heads_local, 4)
    count_groups = heads_local // group
    score_scale = 1.0 / math.sqrt(NOPE + ROPE)

    def by_group(array):
        return array.reshape(array.shape[0], count_groups, group, array.shape[2]).transpose(
            1, 0, 2, 3
        )

    def ungroup(array):
        return array.transpose(1, 0, 2, 3).reshape(array.shape[1], heads_local, array.shape[3])

    q_groups = by_group(q_rot)
    k_groups = by_group(keys)
    v_groups = by_group(value_heads)

    def scores_of(q_block, k_block):
        raw = (
            jnp.einsum("qhd,khd->hqk", q_block, k_block, preferred_element_type=jnp.float32)
            * score_scale
        )
        return jnp.where(allowed[None], raw, masked_score)

    def attend(parts):
        q_block, k_block, v_block = parts
        scores = scores_of(q_block, k_block)
        highest = jnp.max(scores, axis=-1, keepdims=True)
        weights = jnp.exp(scores - highest)
        total = jnp.sum(weights, axis=-1, keepdims=True)
        weights_low = (weights / total).astype(jnp.bfloat16)
        mixed = jnp.einsum("hqk,khd->qhd", weights_low, v_block, preferred_element_type=jnp.float32)
        return (mixed, (highest + jnp.log(total))[..., 0])

    group_mixed, group_log_total = lax.map(attend, (q_groups, k_groups, v_groups))
    heads_out = ungroup(group_mixed).reshape(rows, heads_local * VDIM).astype(jnp.bfloat16)
    attn_part = jnp.einsum(
        "tc,nc->tn",
        heads_out,
        lax.all_gather(w_o, ("dp", "ctx"), axis=0, tiled=True),
        preferred_element_type=jnp.float32,
    )
    attn_full = lax.psum(attn_part, "tensor")
    resid = hidden_in + res_scale * attn_full
    resid_scaled = rms_scale(resid)
    normed_mid = (resid_scaled * gain_middle).astype(jnp.bfloat16)
    ff_local = w_gate.shape[1]
    pieces = (
        lax.all_gather(w_gate, ("dp", "ctx"), axis=0, tiled=True),
        lax.all_gather(w_up, ("dp", "ctx"), axis=0, tiled=True),
    )
    columns = normed_mid
    gate = jnp.dot(columns, pieces[0], preferred_element_type=jnp.float32)
    up_proj = jnp.dot(columns, pieces[1], preferred_element_type=jnp.float32)
    sigma = jax.nn.sigmoid(gate)
    silu_gate = gate * sigma
    hidden_mid = (silu_gate * up_proj).astype(jnp.bfloat16)
    mlp_part = jnp.einsum(
        "tf,nf->tn",
        hidden_mid,
        lax.all_gather(w_down, ("dp", "ctx"), axis=0, tiled=True),
        preferred_element_type=jnp.float32,
    )
    mlp_full = lax.psum(mlp_part.astype(jnp.bfloat16), "tensor").astype(jnp.float32)
    layer_out = (resid + res_scale * mlp_full).astype(jnp.bfloat16)[None]
    grad_out = cotangent[0].astype(jnp.float32)
    grad_mlp = (res_scale * grad_out).astype(jnp.bfloat16)
    columns = grad_mlp
    grad_hidden = jnp.dot(
        columns,
        lax.all_gather(w_down, ("dp", "ctx"), axis=0, tiled=True),
        preferred_element_type=jnp.float32,
    )
    grad_gate = (grad_hidden * up_proj * sigma * (1.0 + gate * (1.0 - sigma))).astype(jnp.bfloat16)
    grad_up = (grad_hidden * silu_gate).astype(jnp.bfloat16)
    pieces = (
        lax.all_gather(w_gate, ("dp", "ctx"), axis=0, tiled=True),
        lax.all_gather(w_up, ("dp", "ctx"), axis=0, tiled=True),
    )
    block = jnp.einsum("tf,nf->tn", grad_gate, pieces[0], preferred_element_type=jnp.float32)
    block = block + jnp.einsum("tf,nf->tn", grad_up, pieces[1], preferred_element_type=jnp.float32)
    grad_normed_mid = lax.psum(block, "tensor")
    grad_gain_mlp = jnp.sum(grad_normed_mid * resid_scaled, axis=0)
    grad_resid = grad_out + rms_back(resid, grad_normed_mid * gain_middle)
    grad_attn = (res_scale * grad_resid).astype(jnp.bfloat16)
    columns = grad_attn
    grad_heads = jnp.dot(
        columns,
        lax.all_gather(w_o, ("dp", "ctx"), axis=0, tiled=True),
        preferred_element_type=jnp.float32,
    ).astype(jnp.bfloat16)
    grad_groups = by_group(grad_heads.reshape(rows, heads_local, VDIM))

    def attend_back(parts):
        q_block, k_block, v_block, grad_block, log_total = parts
        scores = scores_of(q_block, k_block)
        probs = jnp.exp(scores - log_total[..., None])
        grad_probs = jnp.einsum(
            "qhd,khd->hqk", grad_block, v_block, preferred_element_type=jnp.float32
        )
        inner = jnp.sum(probs * grad_probs, axis=-1, keepdims=True)
        grad_scores = (probs * (grad_probs - inner)).astype(jnp.bfloat16)
        grad_query = (
            jnp.einsum("hqk,khd->qhd", grad_scores, k_block, preferred_element_type=jnp.float32)
            * score_scale
        )
        grad_key = (
            jnp.einsum("hqk,qhd->khd", grad_scores, q_block, preferred_element_type=jnp.float32)
            * score_scale
        )
        grad_value = jnp.einsum(
            "hqk,qhd->khd",
            probs.astype(jnp.bfloat16),
            grad_block,
            preferred_element_type=jnp.float32,
        )
        return (grad_query, grad_key, grad_value)

    grad_q_groups, grad_k_groups, grad_v_groups = lax.map(
        attend_back, (q_groups, k_groups, v_groups, grad_groups, group_log_total)
    )
    grad_q_rot = ungroup(grad_q_groups)
    grad_keys = ungroup(grad_k_groups)
    grad_values = ungroup(grad_v_groups)
    grad_kv_all = jnp.concatenate([grad_keys[..., :NOPE], grad_values], axis=-1).reshape(
        length, heads_local * (NOPE + VDIM)
    )
    grad_rope_all = jnp.sum(grad_keys[..., NOPE:], axis=1)
    grad_w_kvb = jnp.einsum(
        "tr,tc->rc",
        c_normed_all.astype(jnp.float32),
        grad_kv_all,
        precision=precise,
        preferred_element_type=jnp.float32,
    )
    grad_c_all = jnp.einsum(
        "tc,rc->tr", grad_kv_all, w_kvb_wide, precision=precise, preferred_element_type=jnp.float32
    )
    grad_c_part, grad_rope_part = (
        lax.psum_scatter(
            grad_c_all.astype(jnp.bfloat16), "ctx", scatter_dimension=0, tiled=True
        ).astype(jnp.float32),
        lax.psum_scatter(
            grad_rope_all.astype(jnp.bfloat16), "ctx", scatter_dimension=0, tiled=True
        ).astype(jnp.float32),
    )
    grad_q_raw = jnp.concatenate(
        [
            grad_q_rot[..., :NOPE],
            rotate_back(grad_q_rot[..., NOPE:], cosine[:, None, :], sine[:, None, :]),
        ],
        axis=-1,
    )
    grad_q_raw = grad_q_raw.reshape(rows, heads_local * (NOPE + ROPE)).astype(jnp.bfloat16)
    grad_w_qb = jnp.einsum("tr,tc->rc", q_normed, grad_q_raw, preferred_element_type=jnp.float32)
    grad_q_part = jnp.einsum("tc,rc->tr", grad_q_raw, w_qb, preferred_element_type=jnp.float32)
    grad_q_normed, grad_c_normed, grad_key_rope = (
        lax.psum(grad_q_part.astype(jnp.bfloat16), "tensor").astype(jnp.float32),
        lax.psum(grad_c_part.astype(jnp.bfloat16), "tensor").astype(jnp.float32),
        lax.psum(grad_rope_part.astype(jnp.bfloat16), "tensor").astype(jnp.float32),
    )
    grad_gain_q = jnp.sum(grad_q_normed * q_scaled, axis=0)
    grad_gain_kv = jnp.sum(grad_c_normed * c_round_wide, axis=0)
    grad_q_latent = rms_back(q_latent, grad_q_normed * gain_query).astype(jnp.bfloat16)
    grad_c_latent = rms_back(kv_latent[:, :KVRANK], grad_c_normed * gain_latent)
    grad_kv_latent = jnp.concatenate(
        [grad_c_latent, rotate_back(grad_key_rope, cosine, sine)], axis=1
    ).astype(jnp.bfloat16)
    grad_normed_in = jnp.einsum(
        "tr,dr->td", grad_q_latent, w_qa, preferred_element_type=jnp.float32
    )
    grad_normed_in = grad_normed_in + jnp.einsum(
        "tr,dr->td", grad_kv_latent, w_kva, preferred_element_type=jnp.float32
    )
    grad_gain_attn = jnp.sum(grad_normed_in * scaled_in, axis=0)
    grad_tokens = (grad_resid + rms_back(hidden_in, grad_normed_in * gain_in)).astype(jnp.bfloat16)[
        None
    ]
    out_width = heads_local * VDIM
    query_width = grad_q_latent.shape[1]
    grad_rows = lax.psum_scatter(
        jnp.concatenate(
            [
                jnp.einsum("tn,tc->nc", grad_attn, heads_out, preferred_element_type=jnp.float32),
                jnp.einsum("tn,tf->nf", normed_mid, grad_gate, preferred_element_type=jnp.float32),
                jnp.einsum("tn,tf->nf", normed_mid, grad_up, preferred_element_type=jnp.float32),
                jnp.einsum("tn,tf->nf", grad_mlp, hidden_mid, preferred_element_type=jnp.float32),
                jnp.einsum(
                    "tn,tr->nr", normed_in, grad_q_latent, preferred_element_type=jnp.float32
                ),
                jnp.einsum(
                    "tn,tr->nr", normed_in, grad_kv_latent, preferred_element_type=jnp.float32
                ),
            ],
            axis=1,
        ),
        ("dp", "ctx"),
        scatter_dimension=0,
        tiled=True,
    )
    offset = out_width
    grad_w_o = grad_rows[:, :offset]
    grad_w_gate = grad_rows[:, offset : offset + ff_local]
    offset = offset + ff_local
    grad_w_up = grad_rows[:, offset : offset + ff_local]
    offset = offset + ff_local
    grad_w_down = grad_rows[:, offset : offset + ff_local]
    offset = offset + ff_local
    grad_w_qa = grad_rows[:, offset : offset + query_width]
    offset = offset + query_width
    grad_w_kva = grad_rows[:, offset:]
    summed = lax.psum(
        (grad_gain_attn, grad_gain_q, grad_gain_kv, grad_w_qb, grad_w_kvb, grad_gain_mlp),
        ("dp", "ctx"),
    )
    return (
        layer_out,
        grad_tokens,
        summed[0],
        grad_w_qa,
        summed[1],
        grad_w_kva,
        summed[2],
        summed[3],
        summed[4],
        grad_w_o,
        summed[5],
        grad_w_gate,
        grad_w_up,
        grad_w_down,
    )


def solution(mesh):
    placed = (
        P("dp", "ctx", None),
        P("dp", None),
        P(),
        P(),
        P(),
        P(),
        P(),
        P(None, "tensor"),
        P(None, "tensor"),
        P(("dp", "ctx"), "tensor"),
        P(),
        P(("dp", "ctx"), "tensor"),
        P(("dp", "ctx"), "tensor"),
        P(("dp", "ctx"), "tensor"),
        P("dp", "ctx", None),
    )
    return jax.shard_map(
        body,
        mesh=mesh,
        in_specs=placed,
        out_specs=(
            P("dp", "ctx", None),
            P("dp", "ctx", None),
            P(),
            P(("dp", "ctx"), None),
            P(),
            P(("dp", "ctx"), None),
            P(),
            P(None, "tensor"),
            P(None, "tensor"),
            P(("dp", "ctx"), "tensor"),
            P(),
            P(("dp", "ctx"), "tensor"),
            P(("dp", "ctx"), "tensor"),
            P(("dp", "ctx"), "tensor"),
        ),
        check_vma=False,
    )
```

profile of v0, /device:TPU:12, one launch (start us, length us, event | category | flops | bytes accessed | tf_op | source)
XLA Modules:
  0.0 4406.4 jit_solution(13513251819271523449)
XLA Ops:
  15.1 16.4 all_gather.22
  33.4 4.0 convolution_convert_fusion
  42.3 8.0 copy.57
  51.2 8.1 all_gather.23
  68.7 36.6 while.28
  69.1 2.6 fusion.174
  72.9 3.3 fusion.176
  80.2 3.3 fusion.176
  87.5 3.3 fusion.176
  94.7 3.3 fusion.176
  102.0 3.3 fusion.176
  105.3 4.2 all-gather.5.cloned.1.call-done
  109.5 6.5 fusion.117
  118.4 19.2 all-reduce.10.cloned.1.call-done
  143.0 184.7 %all-gather.9.cloned.1.call-done = bf16[2560,3200]{1,0:T(8,128)(2,1)} async-done(((bf16[160,3200]{1,0:T(8,128)(2,1)}), bf16[2560,3200]{1,0:T(8,128)(2,1)}) %all-gather.9.cloned.1.call-update) | async-done | bytes 16384016 | tf_op jit(solution)/shard_map/all_gather | solution.py:161
  327.7 12.3 fusion.119
  340.1 176.7 %all-gather.7.cloned.1.call-done = bf16[2560,3200]{1,0:T(8,128)(2,1)} async-done(((bf16[160,3200]{1,0:T(8,128)(2,1)}), bf16[2560,3200]{1,0:T(8,128)(2,1)}) %all-gather.7.cloned.1.call-update) | async-done | bytes 16384016 | tf_op jit(solution)/shard_map/all_gather | solution.py:160
  516.8 12.3 fusion.118
  529.1 176.7 %all-gather.11.cloned.1.call-done = bf16[2560,3200]{1,0:T(8,128)(2,1)} async-done(((bf16[160,3200]{1,0:T(8,128)(2,1)}), bf16[2560,3200]{1,0:T(8,128)(2,1)}) %all-gather.11.cloned.1.call-update) | async-done | bytes 16384016 | tf_op jit(solution)/shard_map/all_gather | solution.py:172
  705.9 15.4 multiply_convert_fusion.1
  721.3 12.4 fusion.120
  733.7 12.9 convolution_add_fusion.1
  746.7 11.8 convolution_convert_fusion.1
  758.5 10.7 all-reduce.12.cloned.1.call-done
  769.3 3.9 multiply_reduce_fusion.1
  777.0 5.6 convolution_convert_fusion.2
  784.8 75.1 %while.29 = (s32[]{:T(128)}, f32[5,256,4,96]{1,3,2,0:T(8,128)}, f32[5,1024,4,96]{1,3,2,0:T(8,128)}, f32[5,1024,4,64]{1,3,2,0:T(8,128)}, bf16[5,1024,4,96]{1,3,2,...) while((s32[]{:T(128)}, f32[5,256,4,96]{1,3,2,0:T(8,128)}, ...), condition=%wide.region_15.16_spmd.clone, body=%wide.region_13.15_spmd.clone.sunk | while | flops 889420800 | bytes 38313096 | solution.py:230
  787.1 2.8 multiply_reduce_fusion.7
  791.3 3.2 fusion.188
  794.5 2.7 fusion.187
  802.1 2.8 multiply_reduce_fusion.7
  806.2 3.2 fusion.188
  809.4 2.7 fusion.187
  817.0 2.8 multiply_reduce_fusion.7
  821.1 3.2 fusion.188
  824.3 2.7 fusion.187
  831.9 2.8 multiply_reduce_fusion.7
  836.1 3.2 fusion.188
  839.3 2.7 fusion.187
  846.9 2.8 multiply_reduce_fusion.7
  851.0 3.2 fusion.188
  854.2 2.7 fusion.187
  864.4 7.9 convolution_dynamic-update-slice_fusion.3
  872.3 3.0 slice.117
  875.3 10.3 pad_maximum_fusion
  885.6 10.1 convolution_convert_fusion.3
  896.0 17.7 convolution_dynamic-update-slice_fusion.2
  913.8 13.2 convolution_dynamic-update-slice_fusion.1
  931.6 9.8 fusion.85
  947.1 17.4 convolution_dynamic-update-slice_fusion
  966.1 4.0 psum.89
  970.3 20.2 all-reduce.18.cloned.1.call-done
  994.4 6.0 convolution_dynamic-update-slice_fusion.4
  1000.4 3.1 convolution_dynamic-update-slice_fusion.5
  1003.6 5.2 fusion.102
  1010.7 4.0 fusion.115
  1014.7 2.8 fusion.61
  1017.5 70.4 %all-reduce.1 = (f32[2560]{0:T(1024)}, f32[768]{0:T(1024)}, f32[256]{0:T(256)}, f32[2560]{0:T(1024)}) all-reduce(f32[2560]{0:T(1024)S(1)} %get-tuple-element.165, f32[768]{0:T(1024)S(1)} %get-tuple-element.167, f32[256]{0:T(256)S(1)} %get-tuple-element.169, ...), channel_id=1, replica_groups=mesh['tensor'=2,'dp'=4,'ctx'=4] {'dp','ctx'}, use_global_device_ids=true, to_apply=%region_26.27 | all-reduce | flops 6144 | bytes 49152 | tf_op jit(solution)/shard_map/psum | solution.py:323
  1087.9 3.7 fusion.67
  1091.6 3.8 fusion.68
  1095.3 3088.1 %all-reduce.16.cloned.1.call-done = (f32[2560,11936]{1,0:T(8,128)}, f32[256,2560]{1,0:T(8,128)}) async-done(((f32[2560,11936]{1,0:T(8,128)}, f32[256,2560]{1,0:T(8,128)}), (f32[2560,11936]{1,0:T(8,128)}, f32[256,2560]{1,0:T(8,128)})) %all-reduce.16.cloned.1.call-update) | async-done | bytes 124846096
  4189.3 7.2 fusion.110
  4196.5 195.9 %all-reduce.14.cloned.1.call-done = f32[768,1920]{1,0:T(8,128)} async-done(((f32[768,1920]{1,0:T(8,128)}), f32[768,1920]{1,0:T(8,128)}) %all-reduce.14.cloned.1.call-update) | async-done | bytes 5898256 | tf_op jit(solution)/shard_map/psum | solution.py:323
  4392.3 5.8 copy.110
  (240 shorter events, 116.4 us)
Async XLA Ops:
  7.2 30.3 copy-start
  7.2 102.3 %all-gather.5.cloned.1.call-start = ((), (), s32[]{:S(2)}) async-start(), calls=%async_computation.2 | async-start | bytes 6963200 | tf_op jit(solution)/shard_map/all_gather | solution.py:151
  7.9 129.7 %all-reduce.10.cloned.1.call-start = ((), (), s32[]{:S(2)}) async-start(), calls=%async_computation.3 | async-start | bytes 5242880 | tf_op jit(solution)/shard_map/psum | solution.py:154
  8.7 24.7 copy-start.39
  10.4 4.7 copy-start.48
  10.4 21.1 copy-start.41
  11.1 26.4 copy-start.29
  11.8 19.7 copy-start.26
  11.8 19.7 copy-start.1
  11.8 19.7 copy-start.20
  14.4 36.3 copy-start.18
  15.0 17.8 copy-start.44
  31.5 1.9 copy-start.15
  31.5 1.9 copy-start.17
  32.9 4.6 copy-start.10
  33.4 4.0 copy-start.37
  42.3 8.0 copy-start.28
  50.6 13.3 copy-start.12
  50.8 11.0 copy-start.31
  50.8 11.0 copy-start.33
  116.0 2.4 copy-start.50
  116.0 211.7 %all-gather.9.cloned.1.call-start = ((), (), s32[]{:S(2)}) async-start(), calls=%async_computation.5 | async-start | bytes 17408000 | tf_op jit(solution)/shard_map/all_gather | solution.py:161
  116.8 400.0 %all-gather.7.cloned.1.call-start = ((), (), s32[]{:S(2)}) async-start(), calls=%async_computation.4 | async-start | bytes 17408000 | tf_op jit(solution)/shard_map/all_gather | solution.py:160
  117.3 588.5 %all-gather.11.cloned.1.call-start = ((), (), s32[]{:S(2)}) async-start(), calls=%async_computation.6 | async-start | bytes 17408000 | tf_op jit(solution)/shard_map/all_gather | solution.py:172
  117.9 651.3 %all-reduce.12.cloned.1.call-start = ((), (), s32[]{:S(2)}) async-start(), calls=%async_computation.7 | async-start | bytes 5242880 | tf_op jit(solution)/shard_map/psum | solution.py:193
  140.2 1.5 copy-start.5
  746.6 200.1 %reduce-scatter.3.cloned.1.call-start = ((), (), s32[]{:S(2)}) async-start(), calls=%async_computation.8 | async-start | bytes 655360 | tf_op jit(solution)/shard_map/reduce_scatter | solution.py:251
  769.3 3.9 copy-start.6
  769.3 4.1 copy-start.14
  775.6 1.5 copy-start.7
  784.8 75.1 %copy-start.34 = (f32[256,32]{0,1:T(8,128)S(1)}, f32[256,32]{0,1:T(8,128)}, u32[]{:S(2)}) copy-start(f32[256,32]{0,1:T(8,128)} %copy-done.33) | copy-start | bytes 98308
  859.8 4.6 copy-start.8
  862.0 10.3 slice-start
  864.4 7.9 slice-start.1
  895.8 70.3 %reduce-scatter.5.cloned.1.call-start = ((), (), s32[]{:S(2)}) async-start(), calls=%async_computation.9 | async-start | bytes 81920 | tf_op jit(solution)/shard_map/reduce_scatter | solution.py:254
  896.0 17.8 copy-start.13
  896.0 17.7 copy-start.24
  927.0 4.5 copy-start.16
  927.0 4.5 copy-start.40
  931.6 9.8 copy-start.32
  941.3 49.1 %all-reduce.18.cloned.1.call-start = ((), (), s32[]{:S(2)}) async-start(), calls=%async_computation.12 | async-start | bytes 3670016 | tf_op jit(solution)/shard_map/psum | solution.py:175
  944.0 0.9 copy-start.21
  946.8 23.3 copy-start.36
  946.8 43.7 copy-start.19
  946.8 43.7 copy-start.45
  946.8 44.9 %copy-start.47 = (f32[256]{0:T(256)S(1)}, f32[256]{0:T(256)}, u32[]{:S(2)}) copy-start(f32[256]{0:T(256)} %copy-done.46) | copy-start | bytes 3076
  946.8 46.0 %copy-start.30 = (f32[768]{0:T(1024)S(1)}, f32[768]{0:T(1024)}, u32[]{:S(2)}) copy-start(f32[768]{0:T(1024)} %copy-done.29) | copy-start | bytes 9220
  946.8 46.0 %copy-start.38 = (f32[256]{0:T(256)S(1)}, f32[256]{0:T(256)}, u32[]{:S(2)}) copy-start(f32[256]{0:T(256)} %copy-done.37) | copy-start | bytes 3076
  946.8 47.5 %copy-start.52 = (f32[256]{0:T(256)S(1)}, f32[256]{0:T(256)}, u32[]{:S(2)}) copy-start(f32[256]{0:T(256)} %copy-done.51) | copy-start | bytes 3076
  946.9 47.5 %copy-start.27 = (f32[2560]{0:T(1024)S(1)}, f32[2560]{0:T(1024)}, u32[]{:S(2)}) copy-start(f32[2560]{0:T(1024)} %copy-done.26) | copy-start | bytes 30724
  946.9 47.5 %copy-start.42 = (f32[256]{0:T(256)S(1)}, f32[256]{0:T(256)}, u32[]{:S(2)}) copy-start(f32[256]{0:T(256)} %copy-done.41) | copy-start | bytes 3076
  946.9 3236.6 %all-reduce.16.cloned.1.call-start = ((), (), s32[]{:S(2)}) async-start(), calls=%async_computation.11 | async-start | bytes 251658240
  990.5 3.9 copy-start.2
  990.5 3.9 copy-start.11
  1003.5 3388.8 %all-reduce.14.cloned.1.call-start = ((), (), s32[]{:S(2)}) async-start(), calls=%async_computation.10 | async-start | bytes 11796480 | tf_op jit(solution)/shard_map/psum | solution.py:323
  1008.7 0.7 copy-start.53
  1008.7 1.9 copy-start.22
  1010.6 4.0 copy-start.3
  1010.7 4.0 copy-start.25
  1014.7 2.8 copy-start.43
  1014.7 73.1 %copy-start.49 = (f32[256]{0:T(256)S(1)}, f32[256]{0:T(256)}, u32[]{:S(2)}) copy-start(f32[256]{0:T(256)} %copy-done.48) | copy-start | bytes 3076
  1087.8 3.7 copy-start.4
  1087.9 3.7 copy-start.9
  4392.3 5.8 copy-start.23
  (3 other events, 1.7 us)
Sparse Core Ops, SparseCore 0:
  10.7 98.7 all-gather.4
  116.2 21.4 all-reduce.9
  140.7 186.9 all-gather.8
  330.6 186.1 all-gather.6
  519.7 186.1 all-gather.10
  746.8 22.4 all-reduce.11
  895.9 25.6 reduce-scatter.2
  941.5 24.5 reduce-scatter.4
  969.2 21.2 all-reduce.17
  1003.6 3179.7 all-reduce.15
  4190.3 201.9 all-reduce.13
where the time goes:
time: 4420 us; the launch traced here: 4410 us
  waiting for transfers between devices  3880 us (88%)
  matrix products  293 us (7%)
  blocking collectives  98.9 us (2%)
  other arithmetic  68.6 us (2%)
  local copies, waits for them, and re-layouts  47.5 us (1%)
    unnamed x12, waiting for transfers between devices  3090 us
    psum x1, waiting for transfers between devices, body(): lax.psum((grad_gain_attn, grad_gain_q, grad_gain_kv, grad_w_qb, grad_w_kv...  196 us
    all_gather x1, waiting for transfers between devices, body(): lax.all_gather(w_up, ('dp', 'ctx'), axis=0, tiled=True)  185 us
    all_gather x1, waiting for transfers between devices, body(): lax.all_gather(w_gate, ('dp', 'ctx'), axis=0, tiled=True)  177 us
    all_gather x1, waiting for transfers between devices, body(): lax.all_gather(w_down, ('dp', 'ctx'), axis=0, tiled=True)  177 us
  transfers between devices with their start and end apart: 11, of which 10 were waited for; matrix products, arithmetic and copies ran while one was open for 5% of the time, Pallas kernels for 0%

commit v1 on v0

v1 whole, which is shorter than its diff:
```python
import functools
import math

import jax
import jax.numpy as jnp
import numpy as np
from jax import lax
from jax.experimental import pallas as pl
from jax.experimental.pallas import tpu as pltpu
from jax.sharding import PartitionSpec as P

NOPE = 64
ROPE = 32
VDIM = 64
KVRANK = 256
LANES = 128
QUERY_BLOCK = 256

eps_norm = 1e-05
res_scale = 1.4 / math.sqrt(62.0)
rope_base = 10000.0
masked_score = -1e30
score_scale = 1.0 / math.sqrt(NOPE + ROPE)
exponent = score_scale * math.log2(math.e)

f32 = jnp.float32
bf16 = jnp.bfloat16


def rms_scale(values):
    return values * lax.rsqrt(jnp.mean(values * values, axis=-1, keepdims=True) + eps_norm)


def rms_back(values, grad):
    return jax.vjp(rms_scale, values)[1](grad)[0]


def rotate(values, cosine, sine):
    half = values.shape[-1] // 2
    turned = jnp.concatenate([-values[..., half:], values[..., :half]], axis=-1)
    return values * cosine + turned * sine


def rotate_back(grad, cosine, sine):
    half = grad.shape[-1] // 2
    scaled = grad * sine
    turned = jnp.concatenate([scaled[..., half:], -scaled[..., :half]], axis=-1)
    return grad * cosine + turned


def dot(left, right, contract):
    return lax.dot_general(left, right, (contract, ((), ())), preferred_element_type=f32)


NN = ((1,), (0,))
NT = ((1,), (1,))
TN = ((0,), (0,))


def exchange(value, axis, step, size):
    return lax.ppermute(value, axis, [(i, i ^ step) for i in range(size)])


def pick(stacked, index):
    return lax.dynamic_index_in_dim(stacked, index, axis=0, keepdims=False)


def spread_queries(heads):
    out = np.zeros((heads, NOPE + ROPE, heads, 2, LANES), np.float32)
    half = ROPE // 2
    for h in range(heads):
        for j in range(NOPE + ROPE):
            out[h, j, h, 0, j] = 1.0
        for j in range(half):
            out[h, NOPE + half + j, h, 1, NOPE + j] = -1.0
            out[h, NOPE + j, h, 1, NOPE + half + j] = 1.0
    return out.reshape(heads * (NOPE + ROPE), heads * 2 * LANES)


def spread_keys(heads):
    out = np.zeros((heads, NOPE + VDIM, heads, 2, LANES), np.float32)
    for h in range(heads):
        for j in range(NOPE):
            out[h, j, h, 0, j] = 1.0
        for j in range(VDIM):
            out[h, NOPE + j, h, 1, j] = 1.0
    return out.reshape(heads * (NOPE + VDIM), heads * 2 * LANES)


def spread_rope(heads):
    out = np.zeros((ROPE, heads, 2, LANES), np.float32)
    for j in range(ROPE):
        out[j, :, 0, NOPE + j] = 1.0
    return out.reshape(ROPE, heads * 2 * LANES)


def spread_values(heads):
    out = np.zeros((heads, VDIM, heads, LANES), np.float32)
    for h in range(heads):
        for j in range(VDIM):
            out[h, j, h, j] = 1.0
    return out.reshape(heads * VDIM, heads * LANES)


def split_low(value):
    first = value.astype(bf16).astype(f32)
    second = (value - first).astype(bf16).astype(f32)
    third = (value - first - second).astype(bf16).astype(f32)
    return first, second, third


def forward_kernel(
    qn_ref, kvn_ref, wq_ref, wkv_ref, cos_ref, sin_ref, qtab_ref, ktab_ref, o_ref, q_ref, k_ref, v_ref
):
    length = qn_ref.shape[0]
    block = min(QUERY_BLOCK, length)
    raw = jnp.dot(qn_ref[...], wq_ref[...], preferred_element_type=f32)
    query = raw[:, :LANES] * cos_ref[...] + raw[:, LANES:] * sin_ref[...] + qtab_ref[...]
    q_ref[...] = query.astype(bf16)
    both = jnp.dot(kvn_ref[...], wkv_ref[...], preferred_element_type=f32)
    k_ref[...] = (both[:, :LANES] + ktab_ref[...]).astype(bf16)
    lane = lax.broadcasted_iota(jnp.int32, (length, LANES), 1)
    ones = (lane >= VDIM) & (lane < VDIM + 3)
    v_ref[...] = jnp.where(ones, 1.0, both[:, LANES:]).astype(bf16)
    lane = lax.broadcasted_iota(jnp.int32, (block, LANES), 1)
    after = lax.broadcasted_iota(jnp.int32, (block, block), 1) > lax.broadcasted_iota(
        jnp.int32, (block, block), 0
    )
    for i in range(length // block):
        here = pl.ds(i * block, block)
        query = q_ref[here, :]
        own = dot(query, k_ref[here, :], NT)
        own = jnp.where(after, masked_score, own)
        highest = jnp.max(own, axis=1, keepdims=True)
        if i:
            before = pl.ds(0, i * block)
            past = dot(query, k_ref[before, :], NT)
            highest = jnp.maximum(highest, jnp.max(past, axis=1, keepdims=True))
        weights = jnp.exp2((own - highest) * exponent).astype(bf16)
        mixed = dot(weights, v_ref[here, :], NN)
        if i:
            weights = jnp.exp2((past - highest) * exponent).astype(bf16)
            mixed = mixed + dot(weights, v_ref[before, :], NN)
        total = mixed[:, VDIM : VDIM + 1]
        o_ref[here, :] = jnp.where(lane < VDIM, mixed / total, 0.0).astype(bf16)
        first, second, third = split_low(-(highest + jnp.log2(total) / exponent))
        at = NOPE + ROPE
        kept = jnp.where(
            lane == at,
            first,
            jnp.where(
                lane == at + 1, second, jnp.where(lane == at + 2, third, query.astype(f32))
            ),
        )
        q_ref[here, :] = kept.astype(bf16)


def backward_kernel(
    q_ref, k_ref, v_ref, o_ref, g_ref, cos_ref, sin_ref, dq_ref, dkv_ref, grad_ref, dk_acc, dv_acc
):
    length = q_ref.shape[0]
    block = min(QUERY_BLOCK, length)
    grad = g_ref[...].astype(f32)
    inner = jnp.sum(grad * o_ref[...].astype(f32), axis=1, keepdims=True)
    first, second, third = split_low(-inner)
    lane = lax.broadcasted_iota(jnp.int32, (length, LANES), 1)
    grad = jnp.where(
        lane == VDIM,
        first,
        jnp.where(lane == VDIM + 1, second, jnp.where(lane == VDIM + 2, third, grad)),
    )
    grad_ref[...] = grad.astype(bf16)
    after = lax.broadcasted_iota(jnp.int32, (block, block), 0) > lax.broadcasted_iota(
        jnp.int32, (block, block), 1
    )
    for i in reversed(range(length // block)):
        here = pl.ds(i * block, block)
        query, grad = q_ref[here, :], grad_ref[here, :]

        def part(span, masked):
            keys = k_ref[span, :]
            scores = dot(keys, query, NT)
            if masked:
                scores = jnp.where(after, masked_score, scores)
            probs = jnp.exp2(scores * exponent)
            inward = dot(v_ref[span, :], grad, NT)
            low = (probs * inward).astype(bf16)
            dv = dot(probs.astype(bf16), grad, NN)
            dk = dot(low, query, NN)
            if i == length // block - 1:
                dv_acc[span, :] = dv
                dk_acc[span, :] = dk
            else:
                dv_acc[span, :] += dv
                dk_acc[span, :] += dk
            return dot(low, keys, TN)

        dq = part(here, True)
        if i:
            dq = dq + part(pl.ds(0, i * block), False)
        dq = dq * score_scale
        dq_ref[here, :LANES] = (dq * cos_ref[here, :]).astype(bf16)
        dq_ref[here, LANES:] = (dq * sin_ref[here, :]).astype(bf16)
    dkv_ref[:, :LANES] = jnp.where(lane < NOPE + ROPE, dk_acc[...] * score_scale, 0.0).astype(bf16)
    dkv_ref[:, LANES:] = jnp.where(lane < VDIM, dv_acc[...], 0.0).astype(bf16)


def kernel_params():
    return pltpu.CompilerParams(
        dimension_semantics=("arbitrary",), vmem_limit_bytes=48 * 1024 * 1024
    )


def attend(qn, kvn, wq, wkv, cosine, sine, qtab, ktab):
    length = qn.shape[0]
    heads = wq.shape[1] // (2 * LANES)
    whole = lambda a: pl.BlockSpec(a.shape, lambda h: (0, 0))
    column = lambda rows, width: pl.BlockSpec((rows, width), lambda h: (0, h))
    out = jax.ShapeDtypeStruct((length, heads * LANES), bf16)
    scores = heads * length * length
    return pl.pallas_call(
        forward_kernel,
        grid=(heads,),
        in_specs=[
            whole(qn),
            whole(kvn),
            column(wq.shape[0], 2 * LANES),
            column(wkv.shape[0], 2 * LANES),
            whole(cosine),
            whole(sine),
            whole(qtab),
            whole(ktab),
        ],
        out_specs=[column(length, LANES)] * 4,
        out_shape=[out] * 4,
        compiler_params=kernel_params(),
        cost_estimate=pl.CostEstimate(
            flops=4 * scores * LANES, bytes_accessed=16 * length * heads * LANES, transcendentals=scores
        ),
    )(qn, kvn, wq, wkv, cosine, sine, qtab, ktab)


def attend_back(q, k, v, o, g, cosine, sine):
    length = q.shape[0]
    heads = q.shape[1] // LANES
    whole = lambda a: pl.BlockSpec(a.shape, lambda h: (0, 0))
    column = lambda width: pl.BlockSpec((length, width), lambda h: (0, h))
    out = jax.ShapeDtypeStruct((length, heads * 2 * LANES), bf16)
    scores = heads * length * length
    return pl.pallas_call(
        backward_kernel,
        grid=(heads,),
        in_specs=[column(LANES)] * 5 + [whole(cosine), whole(sine)],
        out_specs=[column(2 * LANES)] * 2,
        out_shape=[out] * 2,
        scratch_shapes=[
            pltpu.VMEM((length, LANES), bf16),
            pltpu.VMEM((length, LANES), f32),
            pltpu.VMEM((length, LANES), f32),
        ],
        compiler_params=kernel_params(),
        cost_estimate=pl.CostEstimate(
            flops=10 * scores * LANES, bytes_accessed=24 * length * heads * LANES, transcendentals=scores
        ),
    )(q, k, v, o, g, cosine, sine)


def body(
    sizes,
    tokens,
    segments,
    gain_attn,
    w_qa,
    gain_q,
    w_kva,
    gain_kv,
    w_qb,
    w_kvb,
    w_o,
    gain_mlp,
    w_gate,
    w_up,
    w_down,
    cotangent,
):
    nt, nz, nc = sizes
    t, z, c = lax.axis_index("tensor"), lax.axis_index("dp"), lax.axis_index("ctx")
    rows, width = tokens.shape[1:]
    half = rows // nt
    block = w_o.shape[0]
    length = nc * rows
    heads = w_qb.shape[1] // (NOPE + ROPE) // nc
    ff = w_gate.shape[1] // nz
    qrank = w_qa.shape[1]

    def turn(value):
        lead = value.shape[:-1]
        return jnp.swapaxes(value.reshape(lead + (nz, nc, block)), -3, -2).reshape(lead + (width,))

    def turn_back(value):
        lead = value.shape[:-1]
        return jnp.swapaxes(value.reshape(lead + (nc, nz, block)), -3, -2).reshape(lead + (width,))

    def swap(value):
        return exchange(value, "tensor", 1, nt)

    def both_halves(value):
        other = swap(value)
        first = jnp.where(t == 0, value, other)
        second = jnp.where(t == 0, other, value)
        return first, second

    def gather_ctx(value):
        pieces = [value] + [exchange(value, "ctx", k, nc) for k in range(1, nc)]
        first, second = both_halves(jnp.stack(pieces))
        return jnp.concatenate(
            [part for j in range(nc) for part in (pick(first, c ^ j), pick(second, c ^ j))], axis=0
        )

    def scatter_ctx(value):
        parts = value.reshape(nc, nt, half, value.shape[1])
        keep = jnp.where(t == 0, parts[:, 0], parts[:, 1])
        give = jnp.where(t == 0, parts[:, 1], parts[:, 0]).astype(bf16)
        parts = (keep + swap(give).astype(f32)).astype(bf16)
        total = pick(parts, c).astype(f32)
        for k in range(1, nc):
            total = total + exchange(pick(parts, c ^ k), "ctx", k, nc).astype(f32)
        return total

    def gather_dp(value):
        pieces = []
        for k in range(nz):
            piece = exchange(value, "dp", k, nz) if k else value
            pieces += [piece, swap(piece)]
        return jnp.concatenate(pieces, axis=0)

    def scatter_dp(value):
        parts = value.reshape(nz, nt, half, value.shape[1])
        total = None
        for k in range(nz):
            piece = parts[k, 0] + swap(parts[k, 1].astype(bf16)).astype(f32)
            if k:
                piece = exchange(piece.astype(bf16), "dp", k, nz).astype(f32)
            total = piece if total is None else total + piece
        return total

    def spread_dp(value):
        parts = jnp.swapaxes(value.reshape(block, nz, -1), 0, 1)
        pieces = [pick(parts, z)]
        for k in range(1, nz):
            pieces.append(exchange(pick(parts, z ^ k), "dp", k, nz))
        pieces = jnp.stack(pieces)
        return jnp.concatenate([pick(pieces, z ^ j)[None] for j in range(nz)], axis=0)

    def spread_dp_back(parts):
        pieces = [pick(parts, z)]
        for k in range(1, nz):
            pieces.append(exchange(pick(parts, z ^ k), "dp", k, nz))
        pieces = jnp.stack(pieces)
        return jnp.concatenate([pick(pieces, z ^ j) for j in range(nz)], axis=1)

    def gather_weight(value):
        parts = spread_dp(value).reshape(nz * block, ff)
        return lax.all_gather(parts, "ctx", axis=0, tiled=True)

    def scatter_weight(value):
        parts = lax.psum_scatter(value.astype(bf16), "ctx", scatter_dimension=0, tiled=True)
        return spread_dp_back(parts.reshape(nz, block, ff)).astype(f32)

    full_down = gather_weight(w_down)
    full_gate = gather_weight(w_gate)
    full_up = gather_weight(w_up)

    out_parts = jnp.swapaxes(w_o.reshape(block, nc, heads * VDIM), 0, 1)
    pieces = [pick(out_parts, c)]
    for k in range(1, nc):
        pieces.append(exchange(pick(out_parts, c ^ k), "ctx", k, nc))
    pieces = jnp.stack(pieces)
    own_out = jnp.concatenate([pick(pieces, c ^ j)[None] for j in range(nc)], axis=0)
    pieces = [own_out] + [exchange(own_out, "dp", k, nz) for k in range(1, nz)]
    pieces = jnp.stack(pieces)
    full_out = jnp.concatenate([pick(pieces, z ^ j)[:, None] for j in range(nz)], axis=1)
    spread_v = jnp.asarray(spread_values(heads), bf16)
    full_out = dot(full_out.reshape(width, heads * VDIM), spread_v, NN).astype(bf16)

    spread_q = jnp.asarray(spread_queries(heads), bf16)
    spread_k = jnp.asarray(spread_keys(heads), bf16)
    own_qb = lax.dynamic_slice_in_dim(w_qb, c * heads * (NOPE + ROPE), heads * (NOPE + ROPE), axis=1)
    own_kvb = lax.dynamic_slice_in_dim(w_kvb, c * heads * (NOPE + VDIM), heads * (NOPE + VDIM), axis=1)
    wide_qb = dot(own_qb, spread_q, NN).astype(bf16)
    wide_kvb = jnp.concatenate(
        [dot(own_kvb, spread_k, NN).astype(bf16), jnp.asarray(spread_rope(heads), bf16)], axis=0
    )

    segment_all = segments[0]
    doc_start = jnp.sum((segment_all[None, :] < segment_all[:, None]).astype(jnp.int32), axis=1)
    positions = (jnp.arange(length, dtype=jnp.int32) - doc_start).astype(f32)
    freqs = rope_base ** (-jnp.arange(0, ROPE, 2).astype(f32) / ROPE)
    angles = positions[:, None] * freqs[None, :]
    angles = jnp.concatenate([angles, angles], axis=1)
    cosine, sine = jnp.cos(angles), jnp.sin(angles)
    fill = lambda width, value: jnp.full((length, width), value, f32)
    tail = LANES - NOPE - ROPE
    cos_table = jnp.concatenate([fill(NOPE, 1.0), cosine, fill(tail, 0.0)], axis=1)
    sin_table = jnp.concatenate([fill(NOPE, 0.0), sine, fill(tail, 0.0)], axis=1)
    same = (segment_all[:, None] == jnp.arange(3, dtype=jnp.int32)[None, :]).astype(f32)
    query_table = jnp.concatenate(
        [fill(NOPE + ROPE + 3, 0.0), same * masked_score, fill(tail - 6, 0.0)], axis=1
    )
    key_table = jnp.concatenate(
        [fill(NOPE + ROPE, 0.0), fill(3, 1.0), 1.0 - same, fill(tail - 6, 0.0)], axis=1
    )
    first_row = c * rows + t * half
    own_cos = lax.dynamic_slice_in_dim(cosine, first_row, half)
    own_sin = lax.dynamic_slice_in_dim(sine, first_row, half)

    gain_in = gain_attn.astype(f32)
    gain_query = gain_q.astype(f32)
    gain_latent = gain_kv.astype(f32)
    gain_middle = turn(gain_mlp.astype(f32))
    own_tokens = lax.dynamic_slice_in_dim(tokens[0], t * half, half)
    own_cotangent = turn(lax.dynamic_slice_in_dim(cotangent[0], t * half, half))
    hidden_in = own_tokens.astype(f32)
    scaled_in = rms_scale(hidden_in)
    normed_in = (scaled_in * gain_in).astype(bf16)
    q_latent = dot(normed_in, w_qa, NN)
    kv_latent = dot(normed_in, w_kva, NN)
    q_scaled = rms_scale(q_latent)
    q_normed = (q_scaled * gain_query).astype(bf16)
    c_round = rms_scale(kv_latent[:, :KVRANK]).astype(bf16).astype(f32)
    c_normed = (c_round * gain_latent).astype(bf16)
    key_rope = rotate(kv_latent[:, KVRANK:], own_cos, own_sin).astype(bf16)
    latents = gather_ctx(jnp.concatenate([q_normed, c_normed, key_rope], axis=1))
    qn, kvn = latents[:, :qrank], latents[:, qrank:]
    heads_out, q_rot, keys, values = attend(
        qn, kvn, wide_qb, wide_kvb, cos_table, sin_table, query_table, key_table
    )
    attn = scatter_ctx(dot(heads_out, full_out, NT))
    resid = turn(own_tokens).astype(f32) + res_scale * attn
    resid_scaled = rms_scale(resid)
    normed_mid = gather_dp((resid_scaled * gain_middle).astype(bf16))
    gate = dot(normed_mid, full_gate, NN)
    up_proj = dot(normed_mid, full_up, NN)
    sigma = jax.nn.sigmoid(gate)
    silu_gate = gate * sigma
    hidden_mid = (silu_gate * up_proj).astype(bf16)
    mlp = scatter_dp(dot(hidden_mid, full_down, NT))
    layer_out = (resid + res_scale * mlp).astype(bf16)
    layer_out = turn_back(jnp.concatenate(both_halves(layer_out), axis=0))[None]

    grad_out = own_cotangent.astype(f32)
    grad_mlp = gather_dp((res_scale * grad_out).astype(bf16))
    grad_hidden = dot(grad_mlp, full_down, NN)
    grad_gate = (grad_hidden * up_proj * sigma * (1.0 + gate * (1.0 - sigma))).astype(bf16)
    grad_up = (grad_hidden * silu_gate).astype(bf16)
    grad_normed_mid = scatter_dp(dot(grad_gate, full_gate, NT) + dot(grad_up, full_up, NT))
    grad_w_down = scatter_weight(dot(grad_mlp, hidden_mid, TN))
    grad_w_gate = scatter_weight(dot(normed_mid, grad_gate, TN))
    grad_w_up = scatter_weight(dot(normed_mid, grad_up, TN))
    grad_gain_mlp = jnp.sum(grad_normed_mid * resid_scaled, axis=0)
    grad_resid = grad_out + rms_back(resid, grad_normed_mid * gain_middle)

    grad_attn = gather_ctx((res_scale * grad_resid).astype(bf16))
    grad_heads = dot(grad_attn, full_out, NN).astype(bf16)
    grad_out_part = dot(dot(grad_attn, heads_out, TN).astype(bf16), spread_v, NT).astype(bf16)
    grad_out_part = jnp.swapaxes(grad_out_part.reshape(nc, nz, block, heads * VDIM), 0, 1)
    total = pick(grad_out_part, z).astype(f32)
    for k in range(1, nz):
        total = total + exchange(pick(grad_out_part, z ^ k), "dp", k, nz).astype(f32)
    total = total.astype(bf16)
    pieces = [pick(total, c)]
    for k in range(1, nc):
        pieces.append(exchange(pick(total, c ^ k), "ctx", k, nc))
    pieces = jnp.stack(pieces)
    grad_w_o = jnp.concatenate([pick(pieces, c ^ j) for j in range(nc)], axis=1).astype(f32)

    grad_q, grad_kv = attend_back(q_rot, keys, values, heads_out, grad_heads, cos_table, sin_table)
    grad_latents = scatter_ctx(
        jnp.concatenate([dot(grad_q, wide_qb, NT), dot(grad_kv, wide_kvb, NT)], axis=1)
    )
    grad_wide_qb = dot(dot(qn, grad_q, TN).astype(bf16), spread_q, NT)
    grad_wide_qb = jnp.pad(
        grad_wide_qb.astype(bf16), ((0, 0), (0, heads * (VDIM - ROPE)))
    )
    grad_wide_kvb = dot(dot(kvn[:, :KVRANK], grad_kv, TN).astype(bf16), spread_k, NT).astype(bf16)
    grad_ups = jnp.concatenate([grad_wide_qb, grad_wide_kvb], axis=0)
    grad_ups = lax.psum_scatter(grad_ups, "dp", scatter_dimension=0, tiled=True)
    grad_ups = lax.all_gather(grad_ups, ("dp", "ctx"), axis=0, tiled=False)
    grad_ups = grad_ups.reshape(nz, nc, -1, heads * (NOPE + VDIM))
    grad_ups = jnp.swapaxes(grad_ups, 0, 1).reshape(nc, qrank + KVRANK, heads * (NOPE + VDIM))
    grad_w_qb = jnp.swapaxes(grad_ups[:, :qrank, : heads * (NOPE + ROPE)], 0, 1)
    grad_w_qb = grad_w_qb.reshape(qrank, -1).astype(f32)
    grad_w_kvb = jnp.swapaxes(grad_ups[:, qrank:], 0, 1).reshape(KVRANK, -1).astype(f32)

    grad_q_normed = grad_latents[:, :qrank]
    grad_c_normed = grad_latents[:, qrank : qrank + KVRANK]
    grad_key_rope = grad_latents[:, qrank + KVRANK :]
    grad_gain_q = jnp.sum(grad_q_normed * q_scaled, axis=0)
    grad_gain_kv = jnp.sum(grad_c_normed * c_round, axis=0)
    grad_q_latent = rms_back(q_latent, grad_q_normed * gain_query).astype(bf16)
    grad_c_latent = rms_back(kv_latent[:, :KVRANK], grad_c_normed * gain_latent)
    grad_kv_latent = jnp.concatenate(
        [grad_c_latent, rotate_back(grad_key_rope, own_cos, own_sin)], axis=1
    ).astype(bf16)
    grad_normed_in = dot(grad_q_latent, w_qa, NT) + dot(grad_kv_latent, w_kva, NT)
    grad_gain_attn = jnp.sum(grad_normed_in * scaled_in, axis=0)
    grad_tokens = turn_back(grad_resid) + rms_back(hidden_in, grad_normed_in * gain_in)
    grad_tokens = jnp.concatenate(both_halves(grad_tokens.astype(bf16)), axis=0)[None]

    lat_width = qrank + w_kva.shape[1]
    grad_lat = jnp.concatenate(
        [dot(normed_in, grad_q_latent, TN), dot(normed_in, grad_kv_latent, TN)], axis=1
    )
    grad_lat = jnp.stack([grad_lat[:, : lat_width // 2], grad_lat[:, lat_width // 2 :]])
    keep, give = pick(grad_lat, t), pick(grad_lat, 1 - t).astype(bf16)
    parts = (keep + swap(give).astype(f32)).astype(bf16)
    parts = jnp.swapaxes(parts.reshape(nz, nc, block, lat_width // 2), 0, 1)
    total = pick(parts, c).astype(f32)
    for k in range(1, nc):
        total = total + exchange(pick(parts, c ^ k), "ctx", k, nc).astype(f32)
    parts = total.astype(bf16)
    total = pick(parts, z).astype(f32)
    for k in range(1, nz):
        total = total + exchange(pick(parts, z ^ k), "dp", k, nz).astype(f32)
    grad_lat = jnp.concatenate(both_halves(total.astype(bf16)), axis=1).astype(f32)
    grad_w_qa, grad_w_kva = grad_lat[:, :qrank], grad_lat[:, qrank:]

    gains = jnp.concatenate([grad_gain_attn, grad_gain_q, grad_gain_kv, turn_back(grad_gain_mlp)])
    gains = gains.reshape(-1, LANES)
    for axis, size in (("tensor", nt), ("ctx", nc), ("dp", nz)):
        step = 1
        while step < size:
            gains = gains + exchange(gains, axis, step, size)
            step *= 2
    gains = gains.reshape(-1)
    ends = np.cumsum([width, qrank, KVRANK])
    grad_gain_attn, grad_gain_q, grad_gain_kv, grad_gain_mlp = jnp.split(gains, ends)
    return (
        layer_out,
        grad_tokens,
        grad_gain_attn,
        grad_w_qa,
        grad_gain_q,
        grad_w_kva,
        grad_gain_kv,
        grad_w_qb,
        grad_w_kvb,
        grad_w_o,
        grad_gain_mlp,
        grad_w_gate,
        grad_w_up,
        grad_w_down,
    )


def solution(mesh):
    placed = (
        P("dp", "ctx", None),
        P("dp", None),
        P(),
        P(),
        P(),
        P(),
        P(),
        P(None, "tensor"),
        P(None, "tensor"),
        P(("dp", "ctx"), "tensor"),
        P(),
        P(("dp", "ctx"), "tensor"),
        P(("dp", "ctx"), "tensor"),
        P(("dp", "ctx"), "tensor"),
        P("dp", "ctx", None),
    )
    sizes = tuple(mesh.shape[name] for name in ("tensor", "dp", "ctx"))
    return jax.shard_map(
        functools.partial(body, sizes),
        mesh=mesh,
        in_specs=placed,
        out_specs=(
            P("dp", "ctx", None),
            P("dp", "ctx", None),
            P(),
            P(("dp", "ctx"), None),
            P(),
            P(("dp", "ctx"), None),
            P(),
            P(None, "tensor"),
            P(None, "tensor"),
            P(("dp", "ctx"), "tensor"),
            P(),
            P(("dp", "ctx"), "tensor"),
            P(("dp", "ctx"), "tensor"),
            P(("dp", "ctx"), "tensor"),
        ),
        check_vma=False,
    )
```

time: 4420 us -> 1120 us (0.25)
  waiting for transfers between devices: 3880 us -> 479 us
  local copies, waits for them, and re-layouts: 47.5 us -> 225 us
  matrix products: 293 us -> 153 us
  blocking collectives: 98.9 us -> 0 us
  starting transfers between devices: 1.23 us -> 92.1 us
  other arithmetic: 68.6 us -> 113 us
    unnamed x12 -> x8, waiting for transfers between devices: 3090 us -> 0.13 us
    all_gather x4, waiting for transfers between devices: 542 us -> 0.01 us  [the longest x3 0.01 us: gather_weight(): return lax.all_gather(parts, 'ctx', axis=0, tiled=True)]
    ppermute x0 -> x89, waiting for transfers between devices: none -> 479 us  [exchange(): return lax.ppermute(value, axis, [(i, i ^ step) for i in range(size)])]
    psum x4 -> x0, waiting for transfers between devices: 246 us -> none  [the longest x1 196 us: body(): lax.psum((grad_gain_attn, grad_gain_q, grad_gain_kv, grad_w_qb, grad_w_kv...]
    dot_general x59 -> x25, matrix products: 293 us -> 153 us  [dot(): lax.dot_general(left, right, (contract, ((), ())), preferred_element_type...]
    ppermute x0 -> x89, starting transfers between devices: none -> 90.8 us  [exchange(): return lax.ppermute(value, axis, [(i, i ^ step) for i in range(size)])]
    psum x2 -> x0, blocking collectives: 74.3 us -> none  [the longest x1 70.4 us: body(): lax.psum((grad_gain_attn, grad_gain_q, grad_gain_kv, grad_w_qb, grad_w_kv...]
    unnamed x115 -> x263, local copies, waits for them, and re-layouts: 14.3 us -> 88.3 us
  transfers between devices with their start and end apart: 11 -> 97, of which waited for: 10 -> 40; matrix products, arithmetic and copies ran while one was open for 5% -> 33% of each run, Pallas kernels for 0% -> 1%
where the time goes in v1:
time: 1120 us; the launch traced here: 1110 us
  waiting for transfers between devices  479 us (43%)
  local copies, waits for them, and re-layouts  225 us (20%)
  matrix products  153 us (14%)
  other arithmetic  113 us (10%)
  starting transfers between devices  92.1 us (8%)
  Pallas kernels  31 us (3%)
  between operations  16.4 us (1%)
    ppermute x89, waiting for transfers between devices, exchange(): return lax.ppermute(value, axis, [(i, i ^ step) for i in range(size)])  479 us
    dot_general x25, matrix products, dot(): lax.dot_general(left, right, (contract, ((), ())), preferred_element_type...  153 us
    ppermute x89, starting transfers between devices, exchange(): return lax.ppermute(value, axis, [(i, i ^ step) for i in range(size)])  90.8 us
    unnamed x263, local copies, waits for them, and re-layouts  88.3 us
  transfers between devices with their start and end apart: 97, of which 40 were waited for; matrix products, arithmetic and copies ran while one was open for 33% of the time, Pallas kernels for 1%

profile of v1, /device:TPU:12, one launch (start us, length us, event | category | flops | bytes accessed | tf_op | source)
XLA Modules:
  0.0 1109.1 jit_solution(2508110688343060775)
XLA Ops:
  10.2 6.0 constant_dynamic-slice_fusion.12
  24.7 6.2 constant_dynamic-slice_fusion.20
  50.1 9.9 collective-permute-done.29
  65.3 5.5 collective-permute-done.26
  87.6 6.2 constant_dynamic-slice_fusion.28
  118.2 12.3 %collective-permute-done.22 = bf16[160,800]{1,0:T(8,128)(2,1)S(1)} collective-permute-done((bf16[160,800]{1,0:T(8,128)(2,1)}, bf16[160,800]{1,0:T(8,128)(2,1)S(1)}, u32[]{:S(2)}, u32[]{:S(2)}) %collective-permute-start.22) | collective-permute-done | bytes 256032 | tf_op jit(solution)/shard_map/ppermute | solution.py:61
  133.8 14.3 %collective-permute-done.23 = bf16[160,800]{1,0:T(8,128)(2,1)S(1)} collective-permute-done((bf16[160,800]{1,0:T(8,128)(2,1)}, bf16[160,800]{1,0:T(8,128)(2,1)S(1)}, u32[]{:S(2)}, u32[]{:S(2)}) %collective-permute-start.23) | collective-permute-done | bytes 256032 | tf_op jit(solution)/shard_map/ppermute | solution.py:61
  158.0 20.8 %collective-permute-done.7 = bf16[4,160,320]{2,1,0:T(8,128)(2,1)} collective-permute-done((bf16[4,160,320]{2,1,0:T(8,128)(2,1)}, bf16[4,160,320]{2,1,0:T(8,128)(2,1)}, u32[]{:S(2)}, u32[]{:S(2)}) %collective-permute-start.7) | collective-permute-done | bytes 409632 | tf_op jit(solution)/shard_map/ppermute | solution.py:61
  192.9 15.7 %shard_map.290 = (bf16[1024,640]{1,0:T(8,128)(2,1)S(1)}, bf16[1024,640]{1,0:T(8,128)(2,1)}, bf16[1024,640]{1,0:T(8,128)(2,1)}, bf16[1024,640]{1,0:T(8,128)(2,1)}) custom-call(bf16[1024,768]{1,0:T(8,128)(2,1)} %slice.176.qn_ref, bf16[1024,288]{1,0:T(8,128)(2,1)S(1)} %slice.177.kvn_ref, bf16[768,1280]{1,0:T(8,128)(2,1)} %convolution_convert_fusion.7.wq_ref, ...), custom_call_target="tpu_custom_call" | custom-call | flops 2684354560 | bytes 10485760 | tf_op jit(solution)/shard_map/pallas_call | solution.py:221
  208.6 6.7 fusion.99
  235.6 33.9 %collective-permute-done.43 = bf16[128,2560]{1,0:T(8,128)(2,1)} collective-permute-done((bf16[128,2560]{1,0:T(8,128)(2,1)}, bf16[128,2560]{1,0:T(8,128)(2,1)}, u32[]{:S(2)}, u32[]{:S(2)}) %collective-permute-start.43) | collective-permute-done | bytes 655392 | tf_op jit(solution)/shard_map/ppermute | solution.py:61
  269.5 12.1 %collective-permute-done.41 = bf16[128,2560]{1,0:T(8,128)(2,1)} collective-permute-done((bf16[128,2560]{1,0:T(8,128)(2,1)}, bf16[128,2560]{1,0:T(8,128)(2,1)}, u32[]{:S(2)}, u32[]{:S(2)}) %collective-permute-start.41) | collective-permute-done | bytes 655392 | tf_op jit(solution)/shard_map/ppermute | solution.py:61
  286.9 6.2 fusion.7
  299.7 11.2 %collective-permute-done.11 = bf16[128,2560]{1,0:T(8,128)(2,1)S(1)} collective-permute-done((bf16[128,2560]{1,0:T(8,128)(2,1)S(1)}, bf16[128,2560]{1,0:T(8,128)(2,1)S(1)}, u32[]{:S(2)}, u32[]{:S(2)}) %collective-permute-start.11) | collective-permute-done | bytes 655392 | tf_op jit(solution)/shard_map/ppermute | solution.py:61
  311.0 14.3 %collective-permute-done.13 = bf16[128,2560]{1,0:T(8,128)(2,1)S(1)} collective-permute-done((bf16[128,2560]{1,0:T(8,128)(2,1)S(1)}, bf16[128,2560]{1,0:T(8,128)(2,1)S(1)}, u32[]{:S(2)}, u32[]{:S(2)}) %collective-permute-start.13) | collective-permute-done | bytes 655392 | tf_op jit(solution)/shard_map/ppermute | solution.py:61
  335.9 37.7 %collective-permute-done.19 = bf16[128,2560]{1,0:T(8,128)(2,1)S(1)} collective-permute-done((bf16[128,2560]{1,0:T(8,128)(2,1)S(1)}, bf16[128,2560]{1,0:T(8,128)(2,1)S(1)}, u32[]{:S(2)}, u32[]{:S(2)}) %collective-permute-start.19) | collective-permute-done | bytes 655392 | tf_op jit(solution)/shard_map/ppermute | solution.py:61
  373.6 9.1 collective-permute-done.17
  390.2 10.1 fusion.101
  400.3 10.5 fusion.100
  410.8 13.4 %multiply_convert_fusion = (bf16[1024,800]{0,1:T(8,128)(2,1)}, bf16[1024,800]{0,1:T(8,128)(2,1)S(1)}, bf16[1024,800]{0,1:T(8,128)(2,1)}) fusion(f32[1024,800]{0,1:T(8,128)} %fusion.100, f32[1024,800]{0,1:T(8,128)} %fusion.101, bf16[1024,2560]{1,0:T(8,128)(2,1)} %constant_dynamic-update-slice_fusion.8, bf16[2560,800]{1,0:T(8,128)(2,1)} %all-gather.10.cloned.1.call-done), kind=kOutput, calls=%fused_computation.31 | convolution fusion | flops 4206592000 | bytes 20807680 | tf_op jit(solution)/shard_map/dot_general | solution.py:52
  424.2 8.6 fusion.103
  432.8 9.9 convolution_add_fusion
  450.0 10.8 fusion.102
  460.9 6.9 convert.37
  481.2 24.8 %collective-permute-done.47 = bf16[128,2560]{1,0:T(8,128)(2,1)S(1)} collective-permute-done((bf16[128,2560]{1,0:T(8,128)(2,1)S(1)}, bf16[128,2560]{1,0:T(8,128)(2,1)S(1)}, u32[]{:S(2)}, u32[]{:S(2)}) %collective-permute-start.47) | collective-permute-done | bytes 655392 | tf_op jit(solution)/shard_map/ppermute | solution.py:61
  506.1 16.7 %collective-permute-done.51 = bf16[128,2560]{1,0:T(8,128)(2,1)S(1)} collective-permute-done((bf16[128,2560]{1,0:T(8,128)(2,1)S(1)}, bf16[128,2560]{1,0:T(8,128)(2,1)S(1)}, u32[]{:S(2)}, u32[]{:S(2)}) %collective-permute-start.51) | collective-permute-done | bytes 655392 | tf_op jit(solution)/shard_map/ppermute | solution.py:61
  522.8 40.2 %collective-permute-done.49 = bf16[128,2560]{1,0:T(8,128)(2,1)S(1)} collective-permute-done((bf16[128,2560]{1,0:T(8,128)(2,1)S(1)}, bf16[128,2560]{1,0:T(8,128)(2,1)S(1)}, u32[]{:S(2)}, u32[]{:S(2)}) %collective-permute-start.49) | collective-permute-done | bytes 655392 | tf_op jit(solution)/shard_map/ppermute | solution.py:61
  564.8 14.1 %collective-permute-done.36 = bf16[128,2560]{1,0:T(8,128)(2,1)S(1)} collective-permute-done((bf16[128,2560]{1,0:T(8,128)(2,1)S(1)}, bf16[128,2560]{1,0:T(8,128)(2,1)S(1)}, u32[]{:S(2)}, u32[]{:S(2)}) %collective-permute-start.36) | collective-permute-done | bytes 655392 | tf_op jit(solution)/shard_map/ppermute | solution.py:61
  578.9 11.0 collective-permute-done.34
  595.7 15.1 %collective-permute-done.54 = bf16[128,2560]{1,0:T(8,128)(2,1)S(1)} collective-permute-done((bf16[128,2560]{1,0:T(8,128)(2,1)S(1)}, bf16[128,2560]{1,0:T(8,128)(2,1)S(1)}, u32[]{:S(2)}, u32[]{:S(2)}) %collective-permute-start.54) | collective-permute-done | bytes 655392 | tf_op jit(solution)/shard_map/ppermute | solution.py:61
  610.7 11.1 %collective-permute-done.53 = bf16[128,2560]{1,0:T(8,128)(2,1)S(1)} collective-permute-done((bf16[128,2560]{1,0:T(8,128)(2,1)S(1)}, bf16[128,2560]{1,0:T(8,128)(2,1)S(1)}, u32[]{:S(2)}, u32[]{:S(2)}) %collective-permute-start.53) | collective-permute-done | bytes 655392 | tf_op jit(solution)/shard_map/ppermute | solution.py:61
  630.0 5.3 convolution_convert_fusion.10.g_ref
  635.2 15.3 %shard_map.291 = (bf16[1024,1280]{1,0:T(8,128)(2,1)}, bf16[1024,1280]{1,0:T(8,128)(2,1)}) custom-call(bf16[1024,640]{1,0:T(8,128)(2,1)S(1)} %copy-done.7, bf16[1024,640]{1,0:T(8,128)(2,1)S(1)} %copy-done.8, bf16[1024,640]{1,0:T(8,128)(2,1)S(1)} %copy-done.9, bf16[1024,640]{1,0:T(8,128)(2,1)} %copy-done.5, ...), custom_call_target="tpu_custom_call" | custom-call | flops 6710886400 | bytes 15728640 | tf_op jit(solution)/shard_map/pallas_call | solution.py:250
  654.5 6.3 convolution_convert_fusion.11
  663.4 8.4 convolution_convert_fusion
  671.8 7.2 copy.216
  680.4 8.5 convolution_convert_fusion.2
  688.9 7.2 copy.212
  697.5 8.4 convolution_convert_fusion.1
  705.9 7.3 copy.214
  724.6 6.7 reshape.312
  731.4 8.3 fusion.96
  739.7 6.5 copy.239
  746.1 10.3 convolution_convert_fusion.5
  768.0 6.5 copy.240
  782.2 5.0 collective-permute-done.74
  787.2 13.9 %collective-permute-done.76 = bf16[4,160,320]{2,1,0:T(8,128)(2,1)} collective-permute-done((bf16[4,160,320]{2,1,0:T(8,128)(2,1)}, bf16[4,160,320]{2,1,0:T(8,128)(2,1)}, u32[]{:S(2)}, u32[]{:S(2)}) %collective-permute-start.76) | collective-permute-done | bytes 409632 | tf_op jit(solution)/shard_map/ppermute | solution.py:61
  801.2 7.0 collective-permute-done.75
  826.8 6.3 collective-permute-done.57
  833.1 13.7 %collective-permute-done.59 = bf16[128,1056]{1,0:T(8,128)(2,1)} collective-permute-done((bf16[128,1056]{1,0:T(8,128)(2,1)}, bf16[128,1056]{1,0:T(8,128)(2,1)}, u32[]{:S(2)}, u32[]{:S(2)}) %collective-permute-start.59) | collective-permute-done | bytes 270368 | tf_op jit(solution)/shard_map/ppermute | solution.py:61
  863.6 9.1 fusion.6
  882.2 5.9 collective-permute-start.64
  917.9 7.0 collective-permute-done.88
  935.1 8.8 collective-permute-done.67
  945.0 13.2 %collective-permute-done.69 = bf16[4,160,528]{2,1,0:T(8,128)(2,1)} collective-permute-done((bf16[4,160,528]{2,1,0:T(8,128)(2,1)}, bf16[4,160,528]{2,1,0:T(8,128)(2,1)}, u32[]{:S(2)}, u32[]{:S(2)}) %collective-permute-start.69) | collective-permute-done | bytes 675872 | tf_op jit(solution)/shard_map/ppermute | solution.py:61
  959.9 6.7 collective-permute-done.68
  973.8 23.6 %collective-permute-done.84 = bf16[160,800]{1,0:T(8,128)(2,1)S(1)} collective-permute-done((bf16[160,800]{1,0:T(8,128)(2,1)S(1)}, bf16[160,800]{1,0:T(8,128)(2,1)S(1)}, u32[]{:S(2)}, u32[]{:S(2)}) %collective-permute-start.84) | collective-permute-done | bytes 256032 | tf_op jit(solution)/shard_map/ppermute | solution.py:61
  1003.7 34.2 %collective-permute-done.72 = bf16[160,528]{1,0:T(8,128)(2,1)S(1)} collective-permute-done((bf16[160,528]{1,0:T(8,128)(2,1)S(1)}, bf16[160,528]{1,0:T(8,128)(2,1)S(1)}, u32[]{:S(2)}, u32[]{:S(2)}) %collective-permute-start.72) | collective-permute-done | bytes 168992 | tf_op jit(solution)/shard_map/ppermute | solution.py:61
  1037.9 6.2 collective-permute-done.71
  1057.4 9.5 reshape.317
  1066.8 9.7 copy.201
  1078.0 5.5 convert_bitcast_fusion
  1088.8 6.4 copy.202
  1095.2 6.6 copy.209
  (613 shorter events, 350.9 us)
Async XLA Ops:
  7.2 383.0 %all-gather.8.cloned.1.call-start = ((), (), s32[]{:S(2)}) async-start(), calls=%async_computation.5 | async-start | bytes 5734400 | tf_op jit(solution)/shard_map/all_gather | solution.py:364
  17.0 27.1 %collective-permute-start.27 = (bf16[160,800]{1,0:T(8,128)(2,1)}, bf16[160,800]{1,0:T(8,128)(2,1)}, u32[]{:S(2)}, u32[]{:S(2)}) collective-permute-start(bf16[160,800]{1,0:T(8,128)(2,1)} %bitcast.465), channel_id=1, source_target_pairs={{0,4},{4,0},{8,12},{12,8},{1,5},{5,1},{9,13},{13,9},{2,6},{6,2},{1... | collective-permute-start | bytes 768008 | tf_op jit(solution)/shard_map/ppermute | solution.py:61
  18.2 30.4 %collective-permute-start.28 = (bf16[160,800]{1,0:T(8,128)(2,1)}, bf16[160,800]{1,0:T(8,128)(2,1)}, u32[]{:S(2)}, u32[]{:S(2)}) collective-permute-start(bf16[160,800]{1,0:T(8,128)(2,1)} %bitcast.464), channel_id=1, source_target_pairs={{0,8},{4,12},{8,0},{12,4},{1,9},{5,13},{9,1},{13,5},{2,10},{6,14},... | collective-permute-start | bytes 768008 | tf_op jit(solution)/shard_map/ppermute | solution.py:61
  21.5 38.5 %collective-permute-start.29 = (bf16[160,800]{1,0:T(8,128)(2,1)}, bf16[160,800]{1,0:T(8,128)(2,1)}, u32[]{:S(2)}, u32[]{:S(2)}) collective-permute-start(bf16[160,800]{1,0:T(8,128)(2,1)} %bitcast.463), channel_id=1, source_target_pairs={{0,12},{4,8},{8,4},{12,0},{1,13},{5,9},{9,5},{13,1},{2,14},{6,10},... | collective-permute-start | bytes 768008 | tf_op jit(solution)/shard_map/ppermute | solution.py:61
  31.7 30.2 %collective-permute-start.24 = (bf16[160,800]{1,0:T(8,128)(2,1)}, bf16[160,800]{1,0:T(8,128)(2,1)}, u32[]{:S(2)}, u32[]{:S(2)}) collective-permute-start(bf16[160,800]{1,0:T(8,128)(2,1)} %bitcast.469), channel_id=1, source_target_pairs={{0,4},{4,0},{8,12},{12,8},{1,5},{5,1},{9,13},{13,9},{2,6},{6,2},{1... | collective-permute-start | bytes 768008 | tf_op jit(solution)/shard_map/ppermute | solution.py:61
  33.8 31.5 %collective-permute-start.25 = (bf16[160,800]{1,0:T(8,128)(2,1)}, bf16[160,800]{1,0:T(8,128)(2,1)}, u32[]{:S(2)}, u32[]{:S(2)}) collective-permute-start(bf16[160,800]{1,0:T(8,128)(2,1)} %bitcast.468), channel_id=1, source_target_pairs={{0,8},{4,12},{8,0},{12,4},{1,9},{5,13},{9,1},{13,5},{2,10},{6,14},... | collective-permute-start | bytes 768008 | tf_op jit(solution)/shard_map/ppermute | solution.py:61
  48.5 60.9 %collective-permute-start.4 = (bf16[160,320]{1,0:T(8,128)(2,1)}, bf16[160,320]{1,0:T(8,128)(2,1)}, u32[]{:S(2)}, u32[]{:S(2)}) collective-permute-start(bf16[160,320]{1,0:T(8,128)(2,1)} %bitcast.477), channel_id=1, source_target_pairs={{0,1},{1,0},{2,3},{3,2},{4,5},{5,4},{6,7},{7,6},{8,9},{9,8},{10,11... | collective-permute-start | bytes 307208 | tf_op jit(solution)/shard_map/ppermute | solution.py:61
  60.0 51.0 %collective-permute-start.5 = (bf16[160,320]{1,0:T(8,128)(2,1)}, bf16[160,320]{1,0:T(8,128)(2,1)}, u32[]{:S(2)}, u32[]{:S(2)}) collective-permute-start(bf16[160,320]{1,0:T(8,128)(2,1)} %bitcast.476), channel_id=1, source_target_pairs={{0,2},{1,3},{2,0},{3,1},{4,6},{5,7},{6,4},{7,5},{8,10},{9,11},{10,... | collective-permute-start | bytes 307208 | tf_op jit(solution)/shard_map/ppermute | solution.py:61
  61.9 52.1 %collective-permute-start.6 = (bf16[160,320]{1,0:T(8,128)(2,1)}, bf16[160,320]{1,0:T(8,128)(2,1)}, u32[]{:S(2)}, u32[]{:S(2)}) collective-permute-start(bf16[160,320]{1,0:T(8,128)(2,1)} %bitcast.475), channel_id=1, source_target_pairs={{0,3},{1,2},{2,1},{3,0},{4,7},{5,6},{6,5},{7,4},{8,11},{9,10},{10,... | collective-permute-start | bytes 307208 | tf_op jit(solution)/shard_map/ppermute | solution.py:61
  74.5 325.8 %all-gather.6.cloned.1.call-start = ((), (), s32[]{:S(2)}) async-start(), calls=%async_computation.4 | async-start | bytes 5734400 | tf_op jit(solution)/shard_map/all_gather | solution.py:364
  84.3 66.0 %collective-permute-start.1 = (bf16[128,1056]{1,0:T(8,128)(2,1)}, bf16[128,1056]{1,0:T(8,128)(2,1)}, u32[]{:S(2)}, u32[]{:S(2)}) collective-permute-start(bf16[128,1056]{1,0:T(8,128)(2,1)} %get-tuple-element.219), channel_id=1, source_target_pairs={{0,2},{1,3},{2,0},{3,1},{4,6},{5,7},{6,4},{7,5},{8,10},{9,11},{10,... | collective-permute-start | bytes 811016 | tf_op jit(solution)/shard_map/ppermute | solution.py:61
  109.5 42.3 %collective-permute-start = (bf16[128,1056]{1,0:T(8,128)(2,1)}, bf16[128,1056]{1,0:T(8,128)(2,1)S(1)}, u32[]{:S(2)}, u32[]{:S(2)}) collective-permute-start(bf16[128,1056]{1,0:T(8,128)(2,1)} %get-tuple-element.219), channel_id=1, source_target_pairs={{0,1},{1,0},{2,3},{3,2},{4,5},{5,4},{6,7},{7,6},{8,9},{9,8},{10,11... | collective-permute-start | bytes 811016 | tf_op jit(solution)/shard_map/ppermute | solution.py:61
  114.0 34.1 %collective-permute-start.23 = (bf16[160,800]{1,0:T(8,128)(2,1)}, bf16[160,800]{1,0:T(8,128)(2,1)S(1)}, u32[]{:S(2)}, u32[]{:S(2)}) collective-permute-start(bf16[160,800]{1,0:T(8,128)(2,1)} %bitcast.471), channel_id=1, source_target_pairs={{0,12},{4,8},{8,4},{12,0},{1,13},{5,9},{9,5},{13,1},{2,14},{6,10},... | collective-permute-start | bytes 768008 | tf_op jit(solution)/shard_map/ppermute | solution.py:61
  115.6 36.2 %collective-permute-start.2 = (bf16[128,1056]{1,0:T(8,128)(2,1)}, bf16[128,1056]{1,0:T(8,128)(2,1)S(1)}, u32[]{:S(2)}, u32[]{:S(2)}) collective-permute-start(bf16[128,1056]{1,0:T(8,128)(2,1)} %get-tuple-element.219), channel_id=1, source_target_pairs={{0,3},{1,2},{2,1},{3,0},{4,7},{5,6},{6,5},{7,4},{8,11},{9,10},{10,... | collective-permute-start | bytes 811016 | tf_op jit(solution)/shard_map/ppermute | solution.py:61
  130.6 27.4 %collective-permute-start.8 = (bf16[4,160,320]{2,1,0:T(8,128)(2,1)}, bf16[4,160,320]{2,1,0:T(8,128)(2,1)}, u32[]{:S(2)}, u32[]{:S(2)}) collective-permute-start(bf16[4,160,320]{2,1,0:T(8,128)(2,1)} %get-tuple-element.207), channel_id=1, source_target_pairs={{0,8},{4,12},{8,0},{12,4},{1,9},{5,13},{9,1},{13,5},{2,10},{6,14},... | collective-permute-start | bytes 1228808 | tf_op jit(solution)/shard_map/ppermute | solution.py:61
  148.2 30.6 %collective-permute-start.7 = (bf16[4,160,320]{2,1,0:T(8,128)(2,1)}, bf16[4,160,320]{2,1,0:T(8,128)(2,1)}, u32[]{:S(2)}, u32[]{:S(2)}) collective-permute-start(bf16[4,160,320]{2,1,0:T(8,128)(2,1)} %get-tuple-element.207), channel_id=1, source_target_pairs={{0,4},{4,0},{8,12},{12,8},{1,5},{5,1},{9,13},{13,9},{2,6},{6,2},{1... | collective-permute-start | bytes 1228808 | tf_op jit(solution)/shard_map/ppermute | solution.py:61
  150.3 29.5 %collective-permute-start.9 = (bf16[4,160,320]{2,1,0:T(8,128)(2,1)}, bf16[4,160,320]{2,1,0:T(8,128)(2,1)}, u32[]{:S(2)}, u32[]{:S(2)}) collective-permute-start(bf16[4,160,320]{2,1,0:T(8,128)(2,1)} %get-tuple-element.207), channel_id=1, source_target_pairs={{0,12},{4,8},{8,4},{12,0},{1,13},{5,9},{9,5},{13,1},{2,14},{6,10},... | collective-permute-start | bytes 1228808 | tf_op jit(solution)/shard_map/ppermute | solution.py:61
  155.2 31.4 %collective-permute-start.3 = (bf16[4,128,1056]{1,2,0:T(8,128)(2,1)}, bf16[4,128,1056]{1,2,0:T(8,128)(2,1)}, u32[]{:S(2)}, u32[]{:S(2)}) collective-permute-start(bf16[4,128,1056]{1,2,0:T(8,128)(2,1)} %copy.178), channel_id=1, source_target_pairs={{0,16},{16,0},{1,17},{17,1},{2,18},{18,2},{3,19},{19,3},{4,20},{20... | collective-permute-start | bytes 3244040 | tf_op jit(solution)/shard_map/ppermute | solution.py:61
  157.7 253.0 %all-gather.10.cloned.1.call-start = ((), (), s32[]{:S(2)}) async-start(), calls=%async_computation.6 | async-start | bytes 5734400 | tf_op jit(solution)/shard_map/all_gather | solution.py:364
  217.2 69.7 %collective-permute-start.10 = (bf16[4,128,2560]{2,1,0:T(8,128)(2,1)}, bf16[4,128,2560]{2,1,0:T(8,128)(2,1)}, u32[]{:S(2)}, u32[]{:S(2)}) collective-permute-start(bf16[4,128,2560]{2,1,0:T(8,128)(2,1)} %fusion.10), channel_id=1, source_target_pairs={{0,16},{16,0},{1,17},{17,1},{2,18},{18,2},{3,19},{19,3},{4,20},{20... | collective-permute-start | bytes 7864328 | tf_op jit(solution)/shard_map/ppermute | solution.py:61
  223.5 46.0 %collective-permute-start.43 = (bf16[128,2560]{1,0:T(8,128)(2,1)}, bf16[128,2560]{1,0:T(8,128)(2,1)}, u32[]{:S(2)}, u32[]{:S(2)}) collective-permute-start(bf16[128,2560]{1,0:T(8,128)(2,1)} %get-tuple-element.94), channel_id=1, source_target_pairs={{0,12},{4,8},{8,4},{12,0},{1,13},{5,9},{9,5},{13,1},{2,14},{6,10},... | collective-permute-start | bytes 1966088 | tf_op jit(solution)/shard_map/ppermute | solution.py:61
  225.0 56.6 %collective-permute-start.41 = (bf16[128,2560]{1,0:T(8,128)(2,1)}, bf16[128,2560]{1,0:T(8,128)(2,1)}, u32[]{:S(2)}, u32[]{:S(2)}) collective-permute-start(bf16[128,2560]{1,0:T(8,128)(2,1)} %get-tuple-element.94), channel_id=1, source_target_pairs={{0,8},{4,12},{8,0},{12,4},{1,9},{5,13},{9,1},{13,5},{2,10},{6,14},... | collective-permute-start | bytes 1966088 | tf_op jit(solution)/shard_map/ppermute | solution.py:61
  227.3 54.3 %collective-permute-start.39 = (bf16[128,2560]{1,0:T(8,128)(2,1)}, bf16[128,2560]{1,0:T(8,128)(2,1)}, u32[]{:S(2)}, u32[]{:S(2)}) collective-permute-start(bf16[128,2560]{1,0:T(8,128)(2,1)} %get-tuple-element.94), channel_id=1, source_target_pairs={{0,4},{4,0},{8,12},{12,8},{1,5},{5,1},{9,13},{13,9},{2,6},{6,2},{1... | collective-permute-start | bytes 1966088 | tf_op jit(solution)/shard_map/ppermute | solution.py:61
  227.3 54.8 %collective-permute-start.38 = (bf16[128,2560]{1,0:T(8,128)(2,1)}, bf16[128,2560]{1,0:T(8,128)(2,1)}, u32[]{:S(2)}, u32[]{:S(2)}) collective-permute-start(bf16[128,2560]{1,0:T(8,128)(2,1)} %get-tuple-element.94), channel_id=1, source_target_pairs={{0,16},{16,0},{1,17},{17,1},{2,18},{18,2},{3,19},{19,3},{4,20},{20... | collective-permute-start | bytes 1966088 | tf_op jit(solution)/shard_map/ppermute | solution.py:61
  235.4 617.0 %reduce-scatter.11.cloned.1.call-start = ((), (), s32[]{:S(2)}) async-start(), calls=%async_computation.7 | async-start | bytes 1638400 | tf_op jit(solution)/shard_map/reduce_scatter | solution.py:487
  269.5 65.6 %collective-permute-start.44 = (bf16[128,2560]{1,0:T(8,128)(2,1)}, bf16[128,2560]{1,0:T(8,128)(2,1)S(1)}, u32[]{:S(2)}, u32[]{:S(2)}) collective-permute-start(bf16[128,2560]{1,0:T(8,128)(2,1)} %collective-permute-done.43), channel_id=1, source_target_pairs={{0,16},{16,0},{1,17},{17,1},{2,18},{18,2},{3,19},{19,3},{4,20},{20... | collective-permute-start | bytes 1966088 | tf_op jit(solution)/shard_map/ppermute | solution.py:61
  293.8 31.4 %collective-permute-start.13 = (bf16[128,2560]{1,0:T(8,128)(2,1)S(1)}, bf16[128,2560]{1,0:T(8,128)(2,1)S(1)}, u32[]{:S(2)}, u32[]{:S(2)}) collective-permute-start(bf16[128,2560]{1,0:T(8,128)(2,1)S(1)} %get-tuple-element.126), channel_id=1, source_target_pairs={{0,3},{1,2},{2,1},{3,0},{4,7},{5,6},{6,5},{7,4},{8,11},{9,10},{10,... | collective-permute-start | bytes 1966088 | tf_op jit(solution)/shard_map/ppermute | solution.py:61
  296.4 30.1 %collective-permute-start.12 = (bf16[128,2560]{1,0:T(8,128)(2,1)S(1)}, bf16[128,2560]{1,0:T(8,128)(2,1)S(1)}, u32[]{:S(2)}, u32[]{:S(2)}) collective-permute-start(bf16[128,2560]{1,0:T(8,128)(2,1)S(1)} %get-tuple-element.127), channel_id=1, source_target_pairs={{0,2},{1,3},{2,0},{3,1},{4,6},{5,7},{6,4},{7,5},{8,10},{9,11},{10,... | collective-permute-start | bytes 1966088 | tf_op jit(solution)/shard_map/ppermute | solution.py:61
  328.2 45.4 %collective-permute-start.19 = (bf16[128,2560]{1,0:T(8,128)(2,1)S(1)}, bf16[128,2560]{1,0:T(8,128)(2,1)S(1)}, u32[]{:S(2)}, u32[]{:S(2)}) collective-permute-start(bf16[128,2560]{1,0:T(8,128)(2,1)S(1)} %get-tuple-element.96), channel_id=1, source_target_pairs={{0,12},{4,8},{8,4},{12,0},{1,13},{5,9},{9,5},{13,1},{2,14},{6,10},... | collective-permute-start | bytes 1966088 | tf_op jit(solution)/shard_map/ppermute | solution.py:61
  328.8 54.0 %collective-permute-start.17 = (bf16[128,2560]{1,0:T(8,128)(2,1)S(1)}, bf16[128,2560]{1,0:T(8,128)(2,1)S(1)}, u32[]{:S(2)}, u32[]{:S(2)}) collective-permute-start(bf16[128,2560]{1,0:T(8,128)(2,1)S(1)} %get-tuple-element.96), channel_id=1, source_target_pairs={{0,8},{4,12},{8,0},{12,4},{1,9},{5,13},{9,1},{13,5},{2,10},{6,14},... | collective-permute-start | bytes 1966088 | tf_op jit(solution)/shard_map/ppermute | solution.py:61
  333.0 49.8 %collective-permute-start.15 = (bf16[128,2560]{1,0:T(8,128)(2,1)S(1)}, bf16[128,2560]{1,0:T(8,128)(2,1)S(1)}, u32[]{:S(2)}, u32[]{:S(2)}) collective-permute-start(bf16[128,2560]{1,0:T(8,128)(2,1)S(1)} %get-tuple-element.96), channel_id=1, source_target_pairs={{0,4},{4,0},{8,12},{12,8},{1,5},{5,1},{9,13},{13,9},{2,6},{6,2},{1... | collective-permute-start | bytes 1966088 | tf_op jit(solution)/shard_map/ppermute | solution.py:61
  333.0 50.3 %collective-permute-start.14 = (bf16[128,2560]{1,0:T(8,128)(2,1)S(1)}, bf16[128,2560]{1,0:T(8,128)(2,1)S(1)}, u32[]{:S(2)}, u32[]{:S(2)}) collective-permute-start(bf16[128,2560]{1,0:T(8,128)(2,1)S(1)} %get-tuple-element.96), channel_id=1, source_target_pairs={{0,16},{16,0},{1,17},{17,1},{2,18},{18,2},{3,19},{19,3},{4,20},{20... | collective-permute-start | bytes 1966088 | tf_op jit(solution)/shard_map/ppermute | solution.py:61
  449.0 31.2 %collective-permute-start.45 = (bf16[128,2560]{1,0:T(8,128)(2,1)}, bf16[128,2560]{1,0:T(8,128)(2,1)}, u32[]{:S(2)}, u32[]{:S(2)}) collective-permute-start(bf16[128,2560]{1,0:T(8,128)(2,1)} %get-tuple-element.112), channel_id=1, source_target_pairs={{0,16},{16,0},{1,17},{17,1},{2,18},{18,2},{3,19},{19,3},{4,20},{20... | collective-permute-start | bytes 1966088 | tf_op jit(solution)/shard_map/ppermute | solution.py:61
  469.8 95.0 %collective-permute-start.30 = (bf16[128,2560]{1,0:T(8,128)(2,1)S(1)}, bf16[128,2560]{1,0:T(8,128)(2,1)S(1)}, u32[]{:S(2)}, u32[]{:S(2)}) collective-permute-start(bf16[128,2560]{1,0:T(8,128)(2,1)S(1)} %get-tuple-element.116), channel_id=1, source_target_pairs={{0,16},{16,0},{1,17},{17,1},{2,18},{18,2},{3,19},{19,3},{4,20},{20... | collective-permute-start | bytes 1966088 | tf_op jit(solution)/shard_map/ppermute | solution.py:61
  473.6 32.4 %collective-permute-start.47 = (bf16[128,2560]{1,0:T(8,128)(2,1)S(1)}, bf16[128,2560]{1,0:T(8,128)(2,1)S(1)}, u32[]{:S(2)}, u32[]{:S(2)}) collective-permute-start(bf16[128,2560]{1,0:T(8,128)(2,1)S(1)} %get-tuple-element.99), channel_id=1, source_target_pairs={{0,4},{4,0},{8,12},{12,8},{1,5},{5,1},{9,13},{13,9},{2,6},{6,2},{1... | collective-permute-start | bytes 1966088 | tf_op jit(solution)/shard_map/ppermute | solution.py:61
  477.1 45.7 %collective-permute-start.51 = (bf16[128,2560]{1,0:T(8,128)(2,1)S(1)}, bf16[128,2560]{1,0:T(8,128)(2,1)S(1)}, u32[]{:S(2)}, u32[]{:S(2)}) collective-permute-start(bf16[128,2560]{1,0:T(8,128)(2,1)S(1)} %get-tuple-element.100), channel_id=1, source_target_pairs={{0,12},{4,8},{8,4},{12,0},{1,13},{5,9},{9,5},{13,1},{2,14},{6,10},... | collective-permute-start | bytes 1966088 | tf_op jit(solution)/shard_map/ppermute | solution.py:61
  477.6 85.4 %collective-permute-start.49 = (bf16[128,2560]{1,0:T(8,128)(2,1)S(1)}, bf16[128,2560]{1,0:T(8,128)(2,1)S(1)}, u32[]{:S(2)}, u32[]{:S(2)}) collective-permute-start(bf16[128,2560]{1,0:T(8,128)(2,1)S(1)} %get-tuple-element.101), channel_id=1, source_target_pairs={{0,8},{4,12},{8,0},{12,4},{1,9},{5,13},{9,1},{13,5},{2,10},{6,14},... | collective-permute-start | bytes 1966088 | tf_op jit(solution)/shard_map/ppermute | solution.py:61
  480.2 84.6 %collective-permute-start.32 = (bf16[128,2560]{1,0:T(8,128)(2,1)S(1)}, bf16[128,2560]{1,0:T(8,128)(2,1)S(1)}, u32[]{:S(2)}, u32[]{:S(2)}) collective-permute-start(bf16[128,2560]{1,0:T(8,128)(2,1)S(1)} %get-tuple-element.102), channel_id=1, source_target_pairs={{0,4},{4,0},{8,12},{12,8},{1,5},{5,1},{9,13},{13,9},{2,6},{6,2},{1... | collective-permute-start | bytes 1966088 | tf_op jit(solution)/shard_map/ppermute | solution.py:61
  506.0 72.9 %collective-permute-start.36 = (bf16[128,2560]{1,0:T(8,128)(2,1)S(1)}, bf16[128,2560]{1,0:T(8,128)(2,1)S(1)}, u32[]{:S(2)}, u32[]{:S(2)}) collective-permute-start(bf16[128,2560]{1,0:T(8,128)(2,1)S(1)} %get-tuple-element.103), channel_id=1, source_target_pairs={{0,12},{4,8},{8,4},{12,0},{1,13},{5,9},{9,5},{13,1},{2,14},{6,10},... | collective-permute-start | bytes 1966088 | tf_op jit(solution)/shard_map/ppermute | solution.py:61
  522.8 67.2 %collective-permute-start.34 = (bf16[128,2560]{1,0:T(8,128)(2,1)S(1)}, bf16[128,2560]{1,0:T(8,128)(2,1)S(1)}, u32[]{:S(2)}, u32[]{:S(2)}) collective-permute-start(bf16[128,2560]{1,0:T(8,128)(2,1)S(1)} %get-tuple-element.104), channel_id=1, source_target_pairs={{0,8},{4,12},{8,0},{12,4},{1,9},{5,13},{9,1},{13,5},{2,10},{6,14},... | collective-permute-start | bytes 1966088 | tf_op jit(solution)/shard_map/ppermute | solution.py:61
  592.4 29.4 %collective-permute-start.53 = (bf16[128,2560]{1,0:T(8,128)(2,1)S(1)}, bf16[128,2560]{1,0:T(8,128)(2,1)S(1)}, u32[]{:S(2)}, u32[]{:S(2)}) collective-permute-start(bf16[128,2560]{1,0:T(8,128)(2,1)S(1)} %get-tuple-element.90), channel_id=1, source_target_pairs={{0,2},{1,3},{2,0},{3,1},{4,6},{5,7},{6,4},{7,5},{8,10},{9,11},{10,... | collective-permute-start | bytes 1966088 | tf_op jit(solution)/shard_map/ppermute | solution.py:61
  594.1 27.7 %collective-permute-start.52 = (bf16[128,2560]{1,0:T(8,128)(2,1)S(1)}, bf16[128,2560]{1,0:T(8,128)(2,1)S(1)}, u32[]{:S(2)}, u32[]{:S(2)}) collective-permute-start(bf16[128,2560]{1,0:T(8,128)(2,1)S(1)} %get-tuple-element.90), channel_id=1, source_target_pairs={{0,1},{1,0},{2,3},{3,2},{4,5},{5,4},{6,7},{7,6},{8,9},{9,8},{10,11... | collective-permute-start | bytes 1966088 | tf_op jit(solution)/shard_map/ppermute | solution.py:61
  663.3 234.2 %reduce-scatter.17.cloned.1.call-start = ((), (), s32[]{:S(2)}) async-start(), calls=%async_computation.11 | async-start | bytes 5734400 | tf_op jit(solution)/shard_map/reduce_scatter | solution.py:367
  679.0 247.8 %reduce-scatter.13.cloned.1.call-start = ((), (), s32[]{:S(2)}) async-start(), calls=%async_computation.9 | async-start | bytes 5734400 | tf_op jit(solution)/shard_map/reduce_scatter | solution.py:367
  696.1 232.9 %reduce-scatter.15.cloned.1.call-start = ((), (), s32[]{:S(2)}) async-start(), calls=%async_computation.10 | async-start | bytes 5734400 | tf_op jit(solution)/shard_map/reduce_scatter | solution.py:367
  713.2 344.2 %all-gather.12.cloned.1.call-start = ((), (), s32[]{:S(2)}) async-start(), calls=%async_computation.8 | async-start | bytes 5570560 | tf_op jit(solution)/shard_map/all_gather | solution.py:488
  716.5 63.3 %collective-permute-start.37 = (bf16[128,2560]{1,0:T(8,128)(2,1)}, bf16[128,2560]{1,0:T(8,128)(2,1)}, u32[]{:S(2)}, u32[]{:S(2)}) collective-permute-start(bf16[128,2560]{1,0:T(8,128)(2,1)} %get-tuple-element.139), channel_id=1, source_target_pairs={{0,16},{16,0},{1,17},{17,1},{2,18},{18,2},{3,19},{19,3},{4,20},{20... | collective-permute-start | bytes 1966088 | tf_op jit(solution)/shard_map/ppermute | solution.py:61
  765.7 35.5 %collective-permute-start.76 = (bf16[4,160,320]{2,1,0:T(8,128)(2,1)}, bf16[4,160,320]{2,1,0:T(8,128)(2,1)}, u32[]{:S(2)}, u32[]{:S(2)}) collective-permute-start(bf16[4,160,320]{2,1,0:T(8,128)(2,1)} %get-tuple-element.131), channel_id=1, source_target_pairs={{0,12},{4,8},{8,4},{12,0},{1,13},{5,9},{9,5},{13,1},{2,14},{6,10},... | collective-permute-start | bytes 1228808 | tf_op jit(solution)/shard_map/ppermute | solution.py:61
  765.7 42.5 %collective-permute-start.75 = (bf16[4,160,320]{2,1,0:T(8,128)(2,1)S(1)}, bf16[4,160,320]{2,1,0:T(8,128)(2,1)}, u32[]{:S(2)}, u32[]{:S(2)}) collective-permute-start(bf16[4,160,320]{2,1,0:T(8,128)(2,1)S(1)} %get-tuple-element.132), channel_id=1, source_target_pairs={{0,8},{4,12},{8,0},{12,4},{1,9},{5,13},{9,1},{13,5},{2,10},{6,14},... | collective-permute-start | bytes 1228808 | tf_op jit(solution)/shard_map/ppermute | solution.py:61
  779.8 34.2 %collective-permute-start.56 = (bf16[4,128,1056]{1,2,0:T(8,128)(2,1)}, bf16[4,128,1056]{1,2,0:T(8,128)(2,1)}, u32[]{:S(2)}, u32[]{:S(2)}) collective-permute-start(bf16[4,128,1056]{1,2,0:T(8,128)(2,1)} %copy.195), channel_id=1, source_target_pairs={{0,16},{16,0},{1,17},{17,1},{2,18},{18,2},{3,19},{19,3},{4,20},{20... | collective-permute-start | bytes 3244040 | tf_op jit(solution)/shard_map/ppermute | solution.py:61
  900.3 31.5 %collective-permute-start.87 = (bf16[160,800]{1,0:T(8,128)(2,1)}, bf16[160,800]{1,0:T(8,128)(2,1)}, u32[]{:S(2)}, u32[]{:S(2)}) collective-permute-start(bf16[160,800]{1,0:T(8,128)(2,1)} %get-tuple-element.151), channel_id=1, source_target_pairs={{0,8},{4,12},{8,0},{12,4},{1,9},{5,13},{9,1},{13,5},{2,10},{6,14},... | collective-permute-start | bytes 768008 | tf_op jit(solution)/shard_map/ppermute | solution.py:61
  904.1 27.8 %collective-permute-start.86 = (bf16[160,800]{1,0:T(8,128)(2,1)}, bf16[160,800]{1,0:T(8,128)(2,1)}, u32[]{:S(2)}, u32[]{:S(2)}) collective-permute-start(bf16[160,800]{1,0:T(8,128)(2,1)} %get-tuple-element.152), channel_id=1, source_target_pairs={{0,4},{4,0},{8,12},{12,8},{1,5},{5,1},{9,13},{13,9},{2,6},{6,2},{1... | collective-permute-start | bytes 768008 | tf_op jit(solution)/shard_map/ppermute | solution.py:61
  915.4 28.5 %collective-permute-start.67 = (bf16[4,160,528]{2,1,0:T(8,128)(2,1)}, bf16[4,160,528]{2,1,0:T(8,128)(2,1)}, u32[]{:S(2)}, u32[]{:S(2)}) collective-permute-start(bf16[4,160,528]{2,1,0:T(8,128)(2,1)} %get-tuple-element.122), channel_id=1, source_target_pairs={{0,1},{1,0},{2,3},{3,2},{4,5},{5,4},{6,7},{7,6},{8,9},{9,8},{10,11... | collective-permute-start | bytes 2027528 | tf_op jit(solution)/shard_map/ppermute | solution.py:61
  916.2 41.9 %collective-permute-start.69 = (bf16[4,160,528]{2,1,0:T(8,128)(2,1)}, bf16[4,160,528]{2,1,0:T(8,128)(2,1)}, u32[]{:S(2)}, u32[]{:S(2)}) collective-permute-start(bf16[4,160,528]{2,1,0:T(8,128)(2,1)} %get-tuple-element.123), channel_id=1, source_target_pairs={{0,3},{1,2},{2,1},{3,0},{4,7},{5,6},{6,5},{7,4},{8,11},{9,10},{10,... | collective-permute-start | bytes 2027528 | tf_op jit(solution)/shard_map/ppermute | solution.py:61
  924.9 41.7 %collective-permute-start.68 = (bf16[4,160,528]{2,1,0:T(8,128)(2,1)}, bf16[4,160,528]{2,1,0:T(8,128)(2,1)}, u32[]{:S(2)}, u32[]{:S(2)}) collective-permute-start(bf16[4,160,528]{2,1,0:T(8,128)(2,1)} %get-tuple-element.124), channel_id=1, source_target_pairs={{0,2},{1,3},{2,0},{3,1},{4,6},{5,7},{6,4},{7,5},{8,10},{9,11},{10,... | collective-permute-start | bytes 2027528 | tf_op jit(solution)/shard_map/ppermute | solution.py:61
  931.8 113.0 %collective-permute-start.82 = (bf16[160,800]{1,0:T(8,128)(2,1)}, bf16[160,800]{1,0:T(8,128)(2,1)S(1)}, u32[]{:S(2)}, u32[]{:S(2)}) collective-permute-start(bf16[160,800]{1,0:T(8,128)(2,1)} %get-tuple-element.166), channel_id=1, source_target_pairs={{0,12},{4,8},{8,4},{12,0},{1,13},{5,9},{9,5},{13,1},{2,14},{6,10},... | collective-permute-start | bytes 768008 | tf_op jit(solution)/shard_map/ppermute | solution.py:61
  931.8 41.0 %collective-permute-start.85 = (bf16[160,800]{1,0:T(8,128)(2,1)S(1)}, bf16[160,800]{1,0:T(8,128)(2,1)S(1)}, u32[]{:S(2)}, u32[]{:S(2)}) collective-permute-start(bf16[160,800]{1,0:T(8,128)(2,1)S(1)} %get-tuple-element.158), channel_id=1, source_target_pairs={{0,12},{4,8},{8,4},{12,0},{1,13},{5,9},{9,5},{13,1},{2,14},{6,10},... | collective-permute-start | bytes 768008 | tf_op jit(solution)/shard_map/ppermute | solution.py:61
  943.9 53.5 %collective-permute-start.84 = (bf16[160,800]{1,0:T(8,128)(2,1)S(1)}, bf16[160,800]{1,0:T(8,128)(2,1)S(1)}, u32[]{:S(2)}, u32[]{:S(2)}) collective-permute-start(bf16[160,800]{1,0:T(8,128)(2,1)S(1)} %get-tuple-element.159), channel_id=1, source_target_pairs={{0,8},{4,12},{8,0},{12,4},{1,9},{5,13},{9,1},{13,5},{2,10},{6,14},... | collective-permute-start | bytes 768008 | tf_op jit(solution)/shard_map/ppermute | solution.py:61
  958.1 39.3 %collective-permute-start.83 = (bf16[160,800]{1,0:T(8,128)(2,1)S(1)}, bf16[160,800]{1,0:T(8,128)(2,1)S(1)}, u32[]{:S(2)}, u32[]{:S(2)}) collective-permute-start(bf16[160,800]{1,0:T(8,128)(2,1)S(1)} %get-tuple-element.160), channel_id=1, source_target_pairs={{0,4},{4,0},{8,12},{12,8},{1,5},{5,1},{9,13},{13,9},{2,6},{6,2},{1... | collective-permute-start | bytes 768008 | tf_op jit(solution)/shard_map/ppermute | solution.py:61
  969.0 33.4 %collective-permute-start.70 = (bf16[160,528]{1,0:T(8,128)(2,1)S(1)}, bf16[160,528]{1,0:T(8,128)(2,1)S(1)}, u32[]{:S(2)}, u32[]{:S(2)}) collective-permute-start(bf16[160,528]{1,0:T(8,128)(2,1)S(1)} %get-tuple-element.193), channel_id=1, source_target_pairs={{0,4},{4,0},{8,12},{12,8},{1,5},{5,1},{9,13},{13,9},{2,6},{6,2},{1... | collective-permute-start | bytes 506888 | tf_op jit(solution)/shard_map/ppermute | solution.py:61
  972.8 72.0 %collective-permute-start.81 = (bf16[160,800]{1,0:T(8,128)(2,1)S(1)}, bf16[160,800]{1,0:T(8,128)(2,1)S(1)}, u32[]{:S(2)}, u32[]{:S(2)}) collective-permute-start(bf16[160,800]{1,0:T(8,128)(2,1)S(1)} %copy-done.64), channel_id=1, source_target_pairs={{0,8},{4,12},{8,0},{12,4},{1,9},{5,13},{9,1},{13,5},{2,10},{6,14},... | collective-permute-start | bytes 768008 | tf_op jit(solution)/shard_map/ppermute | solution.py:61
  997.4 40.4 %collective-permute-start.72 = (bf16[160,528]{1,0:T(8,128)(2,1)S(1)}, bf16[160,528]{1,0:T(8,128)(2,1)S(1)}, u32[]{:S(2)}, u32[]{:S(2)}) collective-permute-start(bf16[160,528]{1,0:T(8,128)(2,1)S(1)} %get-tuple-element.194), channel_id=1, source_target_pairs={{0,12},{4,8},{8,4},{12,0},{1,13},{5,9},{9,5},{13,1},{2,14},{6,10},... | collective-permute-start | bytes 506888 | tf_op jit(solution)/shard_map/ppermute | solution.py:61
  997.4 46.6 %collective-permute-start.71 = (bf16[160,528]{1,0:T(8,128)(2,1)S(1)}, bf16[160,528]{1,0:T(8,128)(2,1)S(1)}, u32[]{:S(2)}, u32[]{:S(2)}) collective-permute-start(bf16[160,528]{1,0:T(8,128)(2,1)S(1)} %get-tuple-element.195), channel_id=1, source_target_pairs={{0,8},{4,12},{8,0},{12,4},{1,9},{5,13},{9,1},{13,5},{2,10},{6,14},... | collective-permute-start | bytes 506888 | tf_op jit(solution)/shard_map/ppermute | solution.py:61
  1002.4 42.5 %collective-permute-start.80 = (bf16[160,800]{1,0:T(8,128)(2,1)S(1)}, bf16[160,800]{1,0:T(8,128)(2,1)S(1)}, u32[]{:S(2)}, u32[]{:S(2)}) collective-permute-start(bf16[160,800]{1,0:T(8,128)(2,1)S(1)} %copy-done.63), channel_id=1, source_target_pairs={{0,4},{4,0},{8,12},{12,8},{1,5},{5,1},{9,13},{13,9},{2,6},{6,2},{1... | collective-permute-start | bytes 768008 | tf_op jit(solution)/shard_map/ppermute | solution.py:61
  (140 other events, 1463.7 us)
Sparse Core Ops, SparseCore 0:
  74.6 73.6 all-gather.7
  157.9 56.7 all-gather.5
  235.5 56.7 all-gather.9
  663.5 31.1 reduce-scatter.10
  697.5 56.5 reduce-scatter.16
  757.1 55.9 reduce-scatter.12
  816.2 68.3 reduce-scatter.14
  887.3 163.7 all-gather.11

commit v2 on v1

v2 whole, which is shorter than its diff:
```python
import functools
import math

import jax
import jax.numpy as jnp
import numpy as np
from jax import lax
from jax.experimental import pallas as pl
from jax.experimental.pallas import tpu as pltpu
from jax.sharding import PartitionSpec as P

NOPE = 64
ROPE = 32
VDIM = 64
KVRANK = 256
LANES = 128
QUERY_BLOCK = 256

eps_norm = 1e-05
res_scale = 1.4 / math.sqrt(62.0)
rope_base = 10000.0
masked_score = -1e30
score_scale = 1.0 / math.sqrt(NOPE + ROPE)
exponent = score_scale * math.log2(math.e)

f32 = jnp.float32
bf16 = jnp.bfloat16


def rms_scale(values):
    return values * lax.rsqrt(jnp.mean(values * values, axis=-1, keepdims=True) + eps_norm)


def dot(left, right, contract):
    return lax.dot_general(left, right, (contract, ((), ())), preferred_element_type=f32)


NN = ((1,), (0,))
NT = ((1,), (1,))
TN = ((0,), (0,))


def exchange(value, axis, step, size):
    return lax.ppermute(value, axis, [(i, i ^ step) for i in range(size)])


def after(value, *done):
    return lax.optimization_barrier((value,) + done)[0]


def pick(stacked, index):
    return lax.dynamic_index_in_dim(stacked, index, axis=0, keepdims=False)


def spread_queries(heads):
    out = np.zeros((heads, NOPE + ROPE, heads, 2, LANES), np.float32)
    half = ROPE // 2
    for h in range(heads):
        for j in range(NOPE + ROPE):
            out[h, j, h, 0, j] = 1.0
        for j in range(half):
            out[h, NOPE + half + j, h, 1, NOPE + j] = -1.0
            out[h, NOPE + j, h, 1, NOPE + half + j] = 1.0
    return out.reshape(heads * (NOPE + ROPE), heads * 2 * LANES)


def spread_keys(heads):
    out = np.zeros((heads, NOPE + VDIM, heads, 2, LANES), np.float32)
    for h in range(heads):
        for j in range(NOPE):
            out[h, j, h, 0, j] = 1.0
        for j in range(VDIM):
            out[h, NOPE + j, h, 1, j] = 1.0
    return out.reshape(heads * (NOPE + VDIM), heads * 2 * LANES)


def spread_rope(heads):
    out = np.zeros((ROPE, heads, 2, LANES), np.float32)
    for j in range(ROPE):
        out[j, :, 0, NOPE + j] = 1.0
    return out.reshape(ROPE, heads * 2 * LANES)


def spread_values(heads):
    out = np.zeros((heads, VDIM, heads, LANES), np.float32)
    for h in range(heads):
        for j in range(VDIM):
            out[h, j, h, j] = 1.0
    return out.reshape(heads * VDIM, heads * LANES)


def split_low(value):
    first = value.astype(bf16).astype(f32)
    second = (value - first).astype(bf16).astype(f32)
    third = (value - first - second).astype(bf16).astype(f32)
    return first, second, third


def rms_back(values, grad):
    inverse = lax.rsqrt(jnp.mean(values * values, axis=-1, keepdims=True) + eps_norm)
    scaled = values * inverse
    return (grad - scaled * jnp.mean(grad * scaled, axis=-1, keepdims=True)) * inverse


def turn_matrix():
    half = ROPE // 2
    out = np.zeros((ROPE, ROPE), np.float32)
    for j in range(half):
        out[half + j, j] = -1.0
        out[j, half + j] = 1.0
    return out


def total_of(refs):
    total = refs[0][...].astype(f32)
    for ref in refs[1:]:
        total = total + ref[...].astype(f32)
    return total


def move_blocks(source, target, outer, inner, block, cast=None):
    for i in range(outer):
        for j in range(inner):
            value = source[:, (i * inner + j) * block : (i * inner + j + 1) * block]
            target[:, (j * outer + i) * block : (j * outer + i + 1) * block] = (
                value if cast is None else cast(value)
            )


SCALARS = pl.BlockSpec(memory_space=pltpu.SMEM)
LOCAL = pl.BlockSpec(memory_space=pltpu.VMEM)


def params(megabytes=48):
    return pltpu.CompilerParams(vmem_limit_bytes=megabytes * 1024 * 1024)


def grid_params(megabytes=48):
    return pltpu.CompilerParams(
        dimension_semantics=("arbitrary",), vmem_limit_bytes=megabytes * 1024 * 1024
    )


def cost(flops=0, moved=0, special=0):
    return pl.CostEstimate(
        flops=flops // 10, bytes_accessed=moved // 10, transcendentals=special // 10
    )


def plain(kernel, ids, operands, outs, scratch=(), flops=0, megabytes=48):
    moved = sum(a.size * a.dtype.itemsize for a in operands)
    moved += sum(math.prod(s) * jnp.dtype(d).itemsize for s, d in outs)
    return pl.pallas_call(
        kernel,
        in_specs=[SCALARS] + [LOCAL] * len(operands),
        out_specs=[LOCAL] * len(outs),
        out_shape=[jax.ShapeDtypeStruct(s, d) for s, d in outs],
        scratch_shapes=list(scratch),
        compiler_params=params(megabytes),
        cost_estimate=cost(flops, moved),
    )(ids, *operands)


def enter_kernel(
    sizes, block, ids, tok, cot, gain_in, gain_query, gain_latent, w_qa, w_kva, cosine, sine, turned,
    normed_ref, lat_ref, q_ref, kv_ref, x_ref, cot_ref, gm_ref, *rest
):
    nt, nz, nc = sizes
    pieces, (inner, plain_ref) = rest[:nc], rest[nc:]
    half = normed_ref.shape[0]
    qrank = w_qa.shape[1]
    here = pl.ds(pl.multiple_of(ids[0] * half, half), half)
    own = tok[here, :]
    hidden = own.astype(f32)
    normed = (rms_scale(hidden) * gain_in[...]).astype(bf16)
    normed_ref[...] = normed
    q_latent = dot(normed, w_qa[...], NN)
    kv_latent = dot(normed, w_kva[...], NT)
    q_ref[...] = q_latent
    kv_ref[...] = kv_latent
    lat_ref[:, :qrank] = (rms_scale(q_latent) * gain_query[...]).astype(bf16)
    c_round = rms_scale(kv_latent[:, :KVRANK]).astype(bf16).astype(f32)
    lat_ref[:, qrank : qrank + KVRANK] = (c_round * gain_latent[...]).astype(bf16)
    rope = kv_latent[:, KVRANK:]
    other = jnp.dot(rope, turned[...], precision=lax.Precision.HIGHEST, preferred_element_type=f32)
    end = qrank + KVRANK + ROPE
    lat_ref[:, qrank + KVRANK : end] = (rope * cosine[...] + other * sine[...]).astype(bf16)
    lat_ref[:, end:] = jnp.zeros((half, lat_ref.shape[1] - end), bf16)
    move_blocks(normed_ref, inner, nz, nc, block)
    span = nz * block
    for k in range(nc):
        start = pl.multiple_of((ids[2] ^ k) * span, span)
        pieces[k][...] = inner[:, pl.ds(start, span)]
    plain_ref[...] = own
    move_blocks(plain_ref, x_ref, nz, nc, block)
    plain_ref[...] = cot[here, :]
    move_blocks(plain_ref, cot_ref, nz, nc, block)
    gm_ref[...] = (res_scale * cot_ref[...].astype(f32)).astype(bf16)


def forward_kernel(
    nt, ids, own_ref, oth_ref, wq_ref, wkv_ref, cos_ref, sin_ref, qtab_ref, ktab_ref,
    oown_ref, ooth_ref, q_ref, k_ref, v_ref, qn_ref, kvn_ref
):
    t, c = ids[0], ids[2]
    nc, half = own_ref.shape[0], own_ref.shape[1]
    length, qrank = qn_ref.shape
    block = nt * half

    @pl.when(pl.program_id(0) == 0)
    def _():
        for j in range(nc):
            for i in range(nt):
                rows = pl.ds((j * nt + i) * half, half)
                value = jnp.where(t == i, own_ref[c ^ j], oth_ref[c ^ j])
                qn_ref[rows, :] = value[:, :qrank]
                kvn_ref[rows, :] = value[:, qrank:]

    raw = jnp.dot(qn_ref[...], wq_ref[...], preferred_element_type=f32)
    query = raw[:, :LANES] * cos_ref[...] + raw[:, LANES:] * sin_ref[...] + qtab_ref[...]
    q_ref[...] = query.astype(bf16)
    both = jnp.dot(kvn_ref[...], wkv_ref[...], preferred_element_type=f32)
    k_ref[...] = (both[:, :LANES] + ktab_ref[...]).astype(bf16)
    lane = lax.broadcasted_iota(jnp.int32, (length, LANES), 1)
    ones = (lane >= VDIM) & (lane < VDIM + 3)
    v_ref[...] = jnp.where(ones, 1.0, both[:, LANES:]).astype(bf16)
    lane = lax.broadcasted_iota(jnp.int32, (block, LANES), 1)
    after = lax.broadcasted_iota(jnp.int32, (block, block), 1) > lax.broadcasted_iota(
        jnp.int32, (block, block), 0
    )
    for i in range(nc):
        here = pl.ds(i * block, block)
        query = q_ref[here, :]
        own = dot(query, k_ref[here, :], NT)
        own = jnp.where(after, masked_score, own)
        highest = jnp.max(own, axis=1, keepdims=True)
        if i:
            before = pl.ds(0, i * block)
            past = dot(query, k_ref[before, :], NT)
            highest = jnp.maximum(highest, jnp.max(past, axis=1, keepdims=True))
        weights = jnp.exp2((own - highest) * exponent).astype(bf16)
        mixed = dot(weights, v_ref[here, :], NN)
        if i:
            weights = jnp.exp2((past - highest) * exponent).astype(bf16)
            mixed = mixed + dot(weights, v_ref[before, :], NN)
        total = mixed[:, VDIM : VDIM + 1]
        out = jnp.where(lane < VDIM, mixed / total, 0.0).astype(bf16)
        for j in range(nt):
            part = out[j * half : (j + 1) * half]

            @pl.when(t == j)
            def _():
                oown_ref[c ^ i] = part

            @pl.when(t != j)
            def _():
                ooth_ref[c ^ i] = part

        first, second, third = split_low(-(highest + jnp.log2(total) / exponent))
        at = NOPE + ROPE
        kept = jnp.where(
            lane == at,
            first,
            jnp.where(lane == at + 1, second, jnp.where(lane == at + 2, third, query.astype(f32))),
        )
        q_ref[here, :] = kept.astype(bf16)


def backward_kernel(
    nt, ids, q_ref, k_ref, v_ref, oown_ref, ooth_ref, gown_ref, goth_ref, cos_ref, sin_ref,
    dq_ref, dkv_ref, grad_ref, dk_acc, dv_acc
):
    t, c = ids[0], ids[2]
    nc, half = gown_ref.shape[0], gown_ref.shape[1]
    length = q_ref.shape[0]
    block = nt * half
    lane = lax.broadcasted_iota(jnp.int32, (half, LANES), 1)
    for j in range(nc):
        for i in range(nt):
            grad = jnp.where(t == i, gown_ref[c ^ j], goth_ref[c ^ j]).astype(f32)
            out = jnp.where(t == i, oown_ref[c ^ j], ooth_ref[c ^ j]).astype(f32)
            first, second, third = split_low(-jnp.sum(grad * out, axis=1, keepdims=True))
            grad = jnp.where(
                lane == VDIM,
                first,
                jnp.where(lane == VDIM + 1, second, jnp.where(lane == VDIM + 2, third, grad)),
            )
            grad_ref[pl.ds((j * nt + i) * half, half), :] = grad.astype(bf16)
    after = lax.broadcasted_iota(jnp.int32, (block, block), 0) > lax.broadcasted_iota(
        jnp.int32, (block, block), 1
    )
    for i in reversed(range(nc)):
        here = pl.ds(i * block, block)
        query, grad = q_ref[here, :], grad_ref[here, :]

        def part(span, masked):
            keys = k_ref[span, :]
            scores = dot(keys, query, NT)
            if masked:
                scores = jnp.where(after, masked_score, scores)
            probs = jnp.exp2(scores * exponent)
            inward = dot(v_ref[span, :], grad, NT)
            low = (probs * inward).astype(bf16)
            dv = dot(probs.astype(bf16), grad, NN)
            dk = dot(low, query, NN)
            if i == nc - 1:
                dv_acc[span, :] = dv
                dk_acc[span, :] = dk
            else:
                dv_acc[span, :] += dv
                dk_acc[span, :] += dk
            return dot(low, keys, TN)

        dq = part(here, True)
        if i:
            dq = dq + part(pl.ds(0, i * block), False)
        dq = dq * score_scale
        dq_ref[here, :LANES] = (dq * cos_ref[here, :]).astype(bf16)
        dq_ref[here, LANES:] = (dq * sin_ref[here, :]).astype(bf16)
    lane = lax.broadcasted_iota(jnp.int32, (length, LANES), 1)
    dkv_ref[:, :LANES] = jnp.where(lane < NOPE + ROPE, dk_acc[...] * score_scale, 0.0).astype(bf16)
    dkv_ref[:, LANES:] = jnp.where(lane < VDIM, dv_acc[...], 0.0).astype(bf16)


def attend(nt, ids, own, oth, wq, wkv, cosine, sine, qtab, ktab):
    nc, half, _ = own.shape
    length = nc * nt * half
    qrank, kvrank = wq.shape[0], wkv.shape[0]
    heads = wq.shape[1] // (2 * LANES)
    whole = lambda a: pl.BlockSpec(a.shape, lambda h, ids: (0,) * a.ndim)
    column = lambda rows, width: pl.BlockSpec((rows, width), lambda h, ids: (0, h))
    split = pl.BlockSpec((nc, half, LANES), lambda h, ids: (0, 0, h))
    out = jax.ShapeDtypeStruct((length, heads * LANES), bf16)
    out_split = jax.ShapeDtypeStruct((nc, half, heads * LANES), bf16)
    kept = [jax.ShapeDtypeStruct((length, qrank), bf16), jax.ShapeDtypeStruct((length, kvrank), bf16)]
    return pl.pallas_call(
        functools.partial(forward_kernel, nt),
        grid_spec=pltpu.PrefetchScalarGridSpec(
            num_scalar_prefetch=1,
            grid=(heads,),
            in_specs=[
                whole(own),
                whole(oth),
                column(qrank, 2 * LANES),
                column(kvrank, 2 * LANES),
                whole(cosine),
                whole(sine),
                whole(qtab),
                whole(ktab),
            ],
            out_specs=[split] * 2 + [column(length, LANES)] * 3 + [whole(a) for a in kept],
        ),
        out_shape=[out_split] * 2 + [out] * 3 + kept,
        compiler_params=grid_params(),
        cost_estimate=cost(
            4 * heads * length * (length * LANES + qrank * 2 * LANES),
            16 * length * heads * LANES,
            heads * length * length // 2,
        ),
    )(ids, own, oth, wq, wkv, cosine, sine, qtab, ktab)


def attend_back(nt, ids, q, k, v, oown, ooth, gown, goth, cosine, sine):
    nc, half, _ = oown.shape
    length = q.shape[0]
    heads = q.shape[1] // LANES
    whole = lambda a: pl.BlockSpec(a.shape, lambda h, ids: (0, 0))
    column = lambda width: pl.BlockSpec((length, width), lambda h, ids: (0, h))
    split = pl.BlockSpec((nc, half, LANES), lambda h, ids: (0, 0, h))
    out = jax.ShapeDtypeStruct((length, heads * 2 * LANES), bf16)
    return pl.pallas_call(
        functools.partial(backward_kernel, nt),
        grid_spec=pltpu.PrefetchScalarGridSpec(
            num_scalar_prefetch=1,
            grid=(heads,),
            in_specs=[column(LANES)] * 3 + [split] * 4 + [whole(cosine), whole(sine)],
            out_specs=[column(2 * LANES)] * 2,
            scratch_shapes=[
                pltpu.VMEM((length, LANES), bf16),
                pltpu.VMEM((length, LANES), f32),
                pltpu.VMEM((length, LANES), f32),
            ],
        ),
        out_shape=[out] * 2,
        compiler_params=grid_params(),
        cost_estimate=cost(
            8 * heads * length * length * LANES,
            24 * length * heads * LANES,
            heads * length * length // 2,
        ),
    )(ids, q, k, v, oown, ooth, gown, goth, cosine, sine)


def split_kernel(axis, pieces, count, ids, *refs):
    width = refs[count].shape[2]
    for k in range(pieces):
        for j in range(pieces):

            @pl.when((ids[axis] ^ k) == j)
            def _():
                for i in range(count):
                    refs[count + k][i] = refs[i][:, j * width : (j + 1) * width]


def join_kernel(axis, pieces, ids, *refs):
    targets = refs[pieces:]
    width = refs[0].shape[2]
    for k in range(pieces):
        for j in range(pieces):

            @pl.when((ids[axis] ^ k) == j)
            def _():
                for i, target in enumerate(targets):
                    target[:, j * width : (j + 1) * width] = refs[k][i].astype(target.dtype)


def stack_kernel(axis, pieces, ids, *refs):
    for k in range(pieces):
        for i in range(refs[k].shape[0]):
            refs[pieces][i, ids[axis] ^ k] = refs[k][i]


def rows_kernel(ids, own, oth, target):
    half = own.shape[0]
    target[pl.ds(pl.multiple_of(ids[0] * half, half), half), :] = own[...]
    target[pl.ds(pl.multiple_of((1 - ids[0]) * half, half), half), :] = oth[...]


def spread_kernel(heads, pieces, ids, *refs):
    target = refs[pieces]
    target[...] = jnp.zeros_like(target)
    for k in range(pieces):
        for j in range(refs[k].shape[0]):
            for h in range(heads):
                target[j, ids[1] ^ k, :, h * LANES : h * LANES + VDIM] = refs[k][
                    j, :, h * VDIM : (h + 1) * VDIM
                ]


def out_kernel(own, oth, weight, keep, give):
    half = own.shape[1]
    both = jnp.concatenate([own[0], oth[0]], axis=0)
    result = dot(both, weight[...], NT)
    keep[0] = result[:half]
    give[0] = result[half:].astype(bf16)


def project_out(own, oth, weight):
    nc, half, deep = own.shape
    width = weight.shape[0]
    piece = lambda w: pl.BlockSpec((1, half, w), lambda k: (k, 0, 0))
    return pl.pallas_call(
        out_kernel,
        grid=(nc,),
        in_specs=[piece(deep)] * 2 + [pl.BlockSpec(weight.shape, lambda k: (0, 0))],
        out_specs=[piece(width)] * 2,
        out_shape=[
            jax.ShapeDtypeStruct((nc, half, width), f32),
            jax.ShapeDtypeStruct((nc, half, width), bf16),
        ],
        compiler_params=grid_params(),
        cost_estimate=cost(4 * nc * half * deep * width, 2 * weight.size + 16 * nc * half * width),
    )(own, oth, weight)


def heads_kernel(own, oth, weight, gown, goth):
    half = own.shape[1]
    both = jnp.concatenate([own[0], oth[0]], axis=0)
    result = dot(both, weight[...], NN).astype(bf16)
    gown[0] = result[:half]
    goth[0] = result[half:]


def project_heads(own, oth, weight):
    nc, half, width = own.shape
    deep = weight.shape[1]
    piece = lambda w: pl.BlockSpec((1, half, w), lambda k: (k, 0, 0))
    return pl.pallas_call(
        heads_kernel,
        grid=(nc,),
        in_specs=[piece(width)] * 2 + [pl.BlockSpec(weight.shape, lambda k: (0, 0))],
        out_specs=[piece(deep)] * 2,
        out_shape=[jax.ShapeDtypeStruct((nc, half, deep), bf16)] * 2,
        compiler_params=grid_params(),
        cost_estimate=cost(4 * nc * half * deep * width, 2 * weight.size + 8 * nc * half * width),
    )(own, oth, weight)


def middle_kernel(pieces, ids, *refs):
    tokens, gain, resid_ref, normed_ref = refs[pieces:]
    resid = tokens[...].astype(f32) + res_scale * total_of(refs[:pieces])
    resid_ref[...] = resid
    normed_ref[...] = (rms_scale(resid) * gain[...]).astype(bf16)


def leave_kernel(sizes, block, pieces, ids, *refs):
    resid, target, inner = refs[pieces:]
    nt, nz, nc = sizes
    inner[...] = resid[...] + res_scale * total_of(refs[:pieces])
    move_blocks(inner, target, nc, nz, block, lambda value: value.astype(bf16))


def mlp_kernel(
    own_steps, nm_own, nm_oth, gm_own, gm_oth, pair_hbm, down_hbm,
    hid_ref, gg_ref, gu_ref, gn_own, gn_oth, ml_own, ml_oth, w_gate, w_up, w_down, sems
):
    step = pl.program_id(0)
    blocks = sems.shape[1]
    deep = w_down.shape[0] // blocks
    copies = [
        [
            pltpu.make_async_copy(
                source.at[pl.ds((j * count + at) * deep, deep), :],
                target.at[pl.ds(j * deep, deep), :],
                sems.at[i, j],
            )
            for j in range(blocks)
        ]
        for i, (source, count, at, target) in enumerate(
            ((pair_hbm, 2, 0, w_gate), (pair_hbm, 2, 1, w_up), (down_hbm, 1, 0, w_down))
        )
    ]

    def ready(i):
        @pl.when(step == 0)
        def _():
            for copy in copies[i]:
                copy.wait()

    @pl.when(step == 0)
    def _():
        for group in copies:
            for copy in group:
                copy.start()

    mine = step < own_steps
    normed = jnp.where(mine, nm_own[...], nm_oth[...])
    ready(0)
    gate = dot(normed, w_gate[...], NN)
    ready(1)
    up_proj = dot(normed, w_up[...], NN)
    ready(2)
    grad_hidden = dot(jnp.where(mine, gm_own[...], gm_oth[...]), w_down[...], NN)
    sigma = jax.nn.sigmoid(gate)
    silu_gate = gate * sigma
    hidden = (silu_gate * up_proj).astype(bf16)
    grad_gate = (grad_hidden * up_proj * sigma * (1.0 + gate * (1.0 - sigma))).astype(bf16)
    grad_up = (grad_hidden * silu_gate).astype(bf16)
    hid_ref[...] = hidden
    gg_ref[...] = grad_gate
    gu_ref[...] = grad_up
    grad_normed = (dot(grad_gate, w_gate[...], NT) + dot(grad_up, w_up[...], NT)).astype(bf16)
    mlp = dot(hidden, w_down[...], NT).astype(bf16)

    @pl.when(mine)
    def _():
        gn_own[...] = grad_normed
        ml_own[...] = mlp

    @pl.when(jnp.logical_not(mine))
    def _():
        gn_oth[...] = grad_normed
        ml_oth[...] = mlp


def feed_forward(blocks, nm_own, nm_oth, gm_own, gm_oth, pair, down):
    rows, width = nm_own.shape
    ff = down.shape[1]
    block = min(rows, 256)
    steps = rows // block
    own = pl.BlockSpec((block, width), lambda i: (jnp.minimum(i, steps - 1), 0))
    oth = pl.BlockSpec((block, width), lambda i: (jnp.maximum(i - steps, 0), 0))
    inner = pl.BlockSpec((block, ff), lambda i: (i, 0))
    anywhere = pl.BlockSpec(memory_space=pl.ANY)
    held = jax.ShapeDtypeStruct((2 * rows, ff), bf16)
    part = jax.ShapeDtypeStruct((rows, width), bf16)
    return pl.pallas_call(
        functools.partial(mlp_kernel, steps),
        grid=(2 * steps,),
        in_specs=[own, oth, own, oth] + [anywhere] * 2,
        out_specs=[inner] * 3 + [own, oth, own, oth],
        out_shape=[held] * 3 + [part] * 4,
        scratch_shapes=[pltpu.VMEM((width, ff), bf16)] * 3
        + [pltpu.SemaphoreType.DMA((3, blocks))],
        compiler_params=grid_params(56),
        cost_estimate=cost(
            24 * rows * width * ff, 6 * width * ff + 16 * rows * width, 2 * rows * ff
        ),
    )(nm_own, nm_oth, gm_own, gm_oth, pair, down)


def product_kernel(count, targets, *refs):
    left = refs[:count]
    per = count // 2
    for i in range(targets):
        right = refs[count + i * per : count + (i + 1) * per]
        total = None
        for j in range(count):
            rows = left[j].shape[0]
            value = right[j // 2][(j % 2) * rows : (j % 2 + 1) * rows, :]
            term = dot(left[j][...], value, TN)
            total = term if total is None else total + term
        span = total.shape[0]
        refs[-1][i * span : (i + 1) * span, :] = total.astype(bf16)


def products(lefts, rights, parts):
    rows, width = lefts[0].shape
    ff = rights[0][0].shape[1]
    span = width // parts
    count = len(rights)
    flat = [a for group in rights for a in group]
    return pl.pallas_call(
        functools.partial(product_kernel, len(lefts), count),
        grid=(parts,),
        in_specs=[pl.BlockSpec((rows, span), lambda i: (0, i))] * len(lefts)
        + [pl.BlockSpec(a.shape, lambda i: (0, 0)) for a in flat],
        out_specs=pl.BlockSpec((count * span, ff), lambda i: (i, 0)),
        out_shape=jax.ShapeDtypeStruct((parts * count * span, ff), bf16),
        compiler_params=grid_params(),
        cost_estimate=cost(
            2 * count * len(lefts) * rows * width * ff,
            2 * len(lefts) * rows * width + 2 * count * width * ff,
        ),
    )(*lefts, *flat)


def back_middle_kernel(pieces, ids, *refs):
    resid_ref, cot, gain, grad_ref, attn_ref, gain_ref = refs[pieces:]
    grad_normed = total_of(refs[:pieces])
    resid = resid_ref[...]
    gain_ref[...] = jnp.sum(grad_normed * rms_scale(resid), axis=0, keepdims=True)
    grad = cot[...].astype(f32) + rms_back(resid, grad_normed * gain[...])
    grad_ref[...] = grad
    attn_ref[...] = (res_scale * grad).astype(bf16)


def grad_out_kernel(heads, ids, own, oth, oown, ooth, target):
    nz, _, block, _ = target.shape
    flat = lambda ref: ref[...].reshape(-1, ref.shape[2])
    total = dot(flat(own), flat(oown), TN) + dot(flat(oth), flat(ooth), TN)
    total = total.astype(bf16)
    for i in range(nz):
        for h in range(heads):
            target[ids[1] ^ i, 0, :, h * VDIM : (h + 1) * VDIM] = total[
                i * block : (i + 1) * block, h * LANES : h * LANES + VDIM
            ]


def grad_out_weight(sizes, block, ids, own, oth, oown, ooth):
    nt, nz, nc = sizes
    _, half, width = own.shape
    deep = oown.shape[2]
    heads = deep // LANES
    left = pl.BlockSpec((nc, half, nz * block), lambda j, ids: (0, 0, j))
    right = pl.BlockSpec((nc, half, deep), lambda j, ids: (0, 0, 0))
    return pl.pallas_call(
        functools.partial(grad_out_kernel, heads),
        grid_spec=pltpu.PrefetchScalarGridSpec(
            num_scalar_prefetch=1,
            grid=(nc,),
            in_specs=[left, left, right, right],
            out_specs=pl.BlockSpec((nz, 1, block, heads * VDIM), lambda j, ids: (0, j, 0, 0)),
        ),
        out_shape=jax.ShapeDtypeStruct((nz, nc, block, heads * VDIM), bf16),
        compiler_params=grid_params(),
        cost_estimate=cost(4 * nc * half * width * deep, 4 * nc * half * (width + deep)),
    )(ids, own, oth, oown, ooth)


def grad_latent_kernel(ids, gq, gkv, wq, wkv, keep, give, inner):
    half = keep.shape[1]
    qrank = wq.shape[0]
    inner[:, :qrank] = dot(gq[...], wq[...], NT)
    inner[:, qrank:] = dot(gkv[...], wkv[...], NT)
    keep[0] = inner[pl.ds(pl.multiple_of(ids[0] * half, half), half), :]
    give[0] = inner[pl.ds(pl.multiple_of((1 - ids[0]) * half, half), half), :].astype(bf16)


def grad_latent(sizes, ids, gq, gkv, wq, wkv):
    nt, _, nc = sizes
    length, deep = gq.shape
    block = length // nc
    half = block // nt
    width = wq.shape[0] + wkv.shape[0]
    rows = pl.BlockSpec((block, deep), lambda k, ids: (ids[2] ^ k, 0))
    whole = lambda a: pl.BlockSpec(a.shape, lambda k, ids: (0, 0))
    piece = pl.BlockSpec((1, half, width), lambda k, ids: (k, 0, 0))
    return pl.pallas_call(
        grad_latent_kernel,
        grid_spec=pltpu.PrefetchScalarGridSpec(
            num_scalar_prefetch=1,
            grid=(nc,),
            in_specs=[rows, rows, whole(wq), whole(wkv)],
            out_specs=[piece, piece],
            scratch_shapes=[pltpu.VMEM((block, width), f32)],
        ),
        out_shape=[
            jax.ShapeDtypeStruct((nc, half, width), f32),
            jax.ShapeDtypeStruct((nc, half, width), bf16),
        ],
        compiler_params=grid_params(),
        cost_estimate=cost(2 * length * deep * width, 4 * length * deep + 4 * width * deep),
    )(ids, gq, gkv, wq, wkv)


def grad_ups_kernel(qn, kvn, gq, gkv, target):
    qrank = qn.shape[1]
    both = dot(qn[...], gq[...], TN)
    straight, turned = both[:, :LANES], both[:, LANES:]
    lane = lax.broadcasted_iota(jnp.int32, straight.shape, 1)
    half = ROPE // 2
    low = (lane >= NOPE) & (lane < NOPE + half)
    high = (lane >= NOPE + half) & (lane < NOPE + ROPE)
    straight = straight + jnp.where(low, pltpu.roll(turned, LANES - half, 1), 0.0)
    straight = straight - jnp.where(high, pltpu.roll(turned, half, 1), 0.0)
    target[:qrank, :] = straight.astype(bf16)
    both = dot(kvn[:, :KVRANK], gkv[...], TN)
    lane = lax.broadcasted_iota(jnp.int32, (KVRANK, LANES), 1)
    values = pltpu.roll(both[:, LANES:], NOPE, 1)
    target[qrank:, :] = jnp.where(lane < NOPE, both[:, :LANES], values).astype(bf16)


def grad_ups(qn, kvn, gq, gkv):
    length, qrank = qn.shape
    heads = gq.shape[1] // (2 * LANES)
    whole = lambda a: pl.BlockSpec(a.shape, lambda h: (0, 0))
    column = pl.BlockSpec((length, 2 * LANES), lambda h: (0, h))
    return pl.pallas_call(
        grad_ups_kernel,
        grid=(heads,),
        in_specs=[whole(qn), whole(kvn), column, column],
        out_specs=pl.BlockSpec((qrank + KVRANK, LANES), lambda h: (0, h)),
        out_shape=jax.ShapeDtypeStruct((qrank + KVRANK, heads * LANES), bf16),
        compiler_params=grid_params(),
        cost_estimate=cost(
            4 * length * (qrank + KVRANK) * heads * LANES, 2 * length * (qrank + heads * 4 * LANES)
        ),
    )(qn, kvn, gq, gkv)


def finish_ups_kernel(heads, pieces, ids, source, q_ref, kv_ref):
    qrank = q_ref.shape[0]
    wide = NOPE + ROPE
    for j in range(pieces):
        value = source[ids[2] ^ j]
        for h in range(heads):
            start = (j * heads + h) * wide
            q_ref[:, start : start + wide] = value[:qrank, h * LANES : h * LANES + wide].astype(f32)
        start = j * heads * LANES
        kv_ref[:, start : start + heads * LANES] = value[qrank:, :].astype(f32)


def grad_enter_kernel(pieces, ids, *refs):
    q_ref, kv_ref, gain_query, gain_latent, cosine, sine, turned, lat_ref, gain_q, gain_kv = refs[
        pieces:
    ]
    qrank = q_ref.shape[1]
    total = total_of(refs[:pieces])
    q_latent, c_latent = q_ref[...], kv_ref[:, :KVRANK]
    grad_q, grad_c, grad_rope = total[:, :qrank], total[:, qrank : qrank + KVRANK], total[:, qrank + KVRANK : qrank + KVRANK + ROPE]
    gain_q[...] = jnp.sum(grad_q * rms_scale(q_latent), axis=0, keepdims=True)
    c_round = rms_scale(c_latent).astype(bf16).astype(f32)
    gain_kv[...] = jnp.sum(grad_c * c_round, axis=0, keepdims=True)
    lat_ref[:, :qrank] = rms_back(q_latent, grad_q * gain_query[...]).astype(bf16)
    lat_ref[:, qrank : qrank + KVRANK] = rms_back(c_latent, grad_c * gain_latent[...]).astype(bf16)
    other = jnp.dot(
        grad_rope * sine[...], turned[...], precision=lax.Precision.HIGHEST, preferred_element_type=f32
    )
    end = qrank + KVRANK + ROPE
    lat_ref[:, qrank + KVRANK : end] = (grad_rope * cosine[...] - other).astype(bf16)
    lat_ref[:, end:] = jnp.zeros((lat_ref.shape[0], lat_ref.shape[1] - end), bf16)


def grad_tokens_kernel(
    sizes, block, ids, lat, w_qa, w_kva, tok, gain_in, grad_ref, target, gain_ref, inner
):
    nt, nz, nc = sizes
    half = lat.shape[0]
    qrank = w_qa.shape[1]
    grad = dot(lat[:, :qrank], w_qa[...], NT) + dot(
        lat[:, qrank : qrank + KVRANK + ROPE], w_kva[...], NN
    )
    here = pl.ds(pl.multiple_of(ids[0] * half, half), half)
    hidden = tok[here, :].astype(f32)
    gain_ref[...] = jnp.sum(grad * rms_scale(hidden), axis=0, keepdims=True)
    move_blocks(grad_ref, inner, nc, nz, block)
    target[...] = (inner[...] + rms_back(hidden, grad * gain_in[...])).astype(bf16)


def grad_down_kernel(share, ids, own, oth, gown, goth, target):
    nz, block, wide = target.shape
    flat = lambda ref: ref[...].reshape(-1, ref.shape[2])
    columns = pl.ds(pl.multiple_of(ids[0] * share, share), wide)
    right = lambda ref: ref[:, :, columns].reshape(-1, wide)
    total = (dot(flat(own), right(gown), TN) + dot(flat(oth), right(goth), TN)).astype(bf16)
    for i in range(nz):
        target[ids[1] ^ i] = total[i * block : (i + 1) * block, :]


def finish_down_kernel(share, ids, own, oth, q_ref, kv_ref):
    first = jnp.where(ids[0] == 0, own[...], oth[...]).astype(f32)
    second = jnp.where(ids[0] == 0, oth[...], own[...]).astype(f32)
    rest = q_ref.shape[1] - share
    q_ref[:, :share] = first[:, :share]
    q_ref[:, share:] = second[:, :rest]
    kv_ref[...] = second[:, rest : rest + kv_ref.shape[1]]


def body(
    sizes,
    tokens,
    segments,
    gain_attn,
    w_qa,
    gain_q,
    w_kva,
    gain_kv,
    w_qb,
    w_kvb,
    w_o,
    gain_mlp,
    w_gate,
    w_up,
    w_down,
    cotangent,
):
    nt, nz, nc = sizes
    t, z, c = lax.axis_index("tensor"), lax.axis_index("dp"), lax.axis_index("ctx")
    ids = jnp.stack([t, z, c]).astype(jnp.int32)
    rows, width = tokens.shape[1:]
    half = rows // nt
    block = w_o.shape[0]
    length = nc * rows
    heads = w_qb.shape[1] // (NOPE + ROPE) // nc
    ff = w_gate.shape[1] // nz
    qrank, kvrank = w_qa.shape[1], w_kva.shape[1]
    w_kva = w_kva.T
    lat_width = -(-(qrank + kvrank) // LANES) * LANES
    line = nz == 4

    def turn_gain(value):
        return jnp.swapaxes(value.reshape(nz, nc, block), 0, 1).reshape(1, width)

    def swap(value):
        return exchange(value, "tensor", 1, nt)

    def along_ctx(value):
        if nc != 4:
            return [value] + [exchange(value, "ctx", k, nc) for k in range(1, nc)]
        cut = value.shape[0] // 2
        first, second = exchange(value, "ctx", 1, nc), exchange(value, "ctx", 2, nc)
        upper = exchange(second[:cut], "ctx", 1, nc)
        lower = exchange(first[cut:], "ctx", 2, nc)
        return [value, first, second, jnp.concatenate([upper, lower])]

    def back_ctx(parts):
        if nc != 4:
            return across(parts, "ctx", nc)
        cut = parts[0].shape[0] // 2
        upper = exchange(parts[3][:cut], "ctx", 1, nc).astype(f32)
        lower = exchange(parts[3][cut:], "ctx", 2, nc).astype(f32)
        first, second = parts[1].astype(f32), parts[2].astype(f32)
        first = jnp.concatenate([first[:cut], first[cut:] + lower]).astype(bf16)
        second = jnp.concatenate([second[:cut] + upper, second[cut:]]).astype(bf16)
        return [parts[0], exchange(first, "ctx", 1, nc), exchange(second, "ctx", 2, nc)]

    def gather_dp(value):
        if not line:
            return [value] + [exchange(value, "dp", k, nz) for k in range(1, nz)]
        first, second = exchange(value, "dp", 1, nz), exchange(value, "dp", 2, nz)
        near = lax.ppermute(value, "dp", [(1, 2), (2, 1)])
        far = lax.ppermute(second, "dp", [(1, 0), (2, 3)])
        return [value, first, second, jnp.where((z == 0) | (z == 3), far, near)]

    def scatter_dp(parts):
        if not line:
            return [parts[0]] + [exchange(parts[k], "dp", k, nz) for k in range(1, nz)]
        far = lax.ppermute(parts[3], "dp", [(0, 1), (3, 2)])
        first = exchange(parts[1], "dp", 1, nz)
        near = lax.ppermute(parts[3], "dp", [(1, 2), (2, 1)])
        second = (parts[2].astype(f32) + far.astype(f32)).astype(bf16)
        return [parts[0], first, exchange(second, "dp", 2, nz), near]

    def split_columns(values, axis, at, pieces):
        deep, wide = values[0].shape[0], values[0].shape[1] // pieces
        if pieces > 4:
            parts = jnp.stack(values).reshape(len(values), deep, pieces, wide)
            parts = jnp.moveaxis(parts, 2, 0)
            return [pick(parts, lax.axis_index(axis) ^ k) for k in range(pieces)]
        outs = [((len(values), deep, wide), values[0].dtype)] * pieces
        return plain(functools.partial(split_kernel, at, pieces, len(values)), ids, values, outs)

    def join_columns(parts, axis, at):
        pieces, (count, deep, wide) = len(parts), parts[0].shape
        if pieces > 4:
            stacked = jnp.stack(parts)
            index = lax.axis_index(axis)
            parts = [pick(stacked, index ^ j) for j in range(pieces)]
            return list(jnp.concatenate(parts, axis=2).astype(f32))
        outs = [((deep, pieces * wide), f32)] * count
        return plain(functools.partial(join_kernel, at, pieces), ids, parts, outs)

    def stack_blocks(parts, at):
        count = parts[0].shape[0]
        outs = [((count, len(parts)) + parts[0].shape[1:], parts[0].dtype)]
        return plain(functools.partial(stack_kernel, at, len(parts)), ids, parts, outs)[0]

    def across(parts, axis, size):
        return [parts[0]] + [exchange(parts[k], axis, k, size) for k in range(1, size)]

    def join_rows(own):
        outs = [((rows, width), bf16)]
        return plain(rows_kernel, ids, [own, swap(own)], outs)[0][None]

    def weight_parts(*values):
        return across(split_columns(values, "dp", 1, nz), "dp", nz)

    def gather_weights(parts):
        parts = stack_blocks(parts, 1).reshape(-1, ff)
        return lax.all_gather(parts, "ctx", axis=0, tiled=True)

    def scatter_weights(value):
        return lax.psum_scatter(value, "ctx", scatter_dimension=0, tiled=True)

    def weight_rows(value):
        parts = value.reshape(-1, nz, block, ff)
        parts = [lax.dynamic_index_in_dim(parts, z ^ k, axis=1, keepdims=False) for k in range(nz)]
        return join_columns(across(parts, "dp", nz), "dp", 1)

    def reduce_ctx(keep, give):
        parts = (keep + swap(give).astype(f32)).astype(bf16)
        return back_ctx([parts[k] for k in range(nc)])

    segment_all = segments[0]
    doc_start = jnp.sum((segment_all[None, :] < segment_all[:, None]).astype(jnp.int32), axis=1)
    positions = (jnp.arange(length, dtype=jnp.int32) - doc_start).astype(f32)
    freqs = rope_base ** (-jnp.arange(0, ROPE, 2).astype(f32) / ROPE)
    angles = positions[:, None] * freqs[None, :]
    angles = jnp.concatenate([angles, angles], axis=1)
    cosine, sine = jnp.cos(angles), jnp.sin(angles)
    fill = lambda width, value: jnp.full((length, width), value, f32)
    tail = LANES - NOPE - ROPE
    cos_table = jnp.concatenate([fill(NOPE, 1.0), cosine, fill(tail, 0.0)], axis=1)
    sin_table = jnp.concatenate([fill(NOPE, 0.0), sine, fill(tail, 0.0)], axis=1)
    same = (segment_all[:, None] == jnp.arange(3, dtype=jnp.int32)[None, :]).astype(f32)
    query_table = jnp.concatenate(
        [fill(NOPE + ROPE + 3, 0.0), same * masked_score, fill(tail - 6, 0.0)], axis=1
    )
    key_table = jnp.concatenate(
        [fill(NOPE + ROPE, 0.0), fill(3, 1.0), 1.0 - same, fill(tail - 6, 0.0)], axis=1
    )
    first_row = c * rows + t * half
    own_cos = lax.dynamic_slice_in_dim(cosine, first_row, half)
    own_sin = lax.dynamic_slice_in_dim(sine, first_row, half)
    turned = jnp.asarray(turn_matrix(), f32)

    gain_in = gain_attn.astype(f32)[None]
    gain_query = gain_q.astype(f32)[None]
    gain_latent = gain_kv.astype(f32)[None]
    gain_middle = turn_gain(gain_mlp.astype(f32))

    spread_q = jnp.asarray(spread_queries(heads), bf16)
    spread_k = jnp.asarray(spread_keys(heads), bf16)
    own_qb = lax.dynamic_slice_in_dim(w_qb, c * heads * (NOPE + ROPE), heads * (NOPE + ROPE), axis=1)
    own_kvb = lax.dynamic_slice_in_dim(w_kvb, c * heads * (NOPE + VDIM), heads * (NOPE + VDIM), axis=1)
    wide_qb = dot(own_qb, spread_q, NN).astype(bf16)
    wide_kvb = jnp.concatenate(
        [
            dot(own_kvb, spread_k, NN).astype(bf16),
            jnp.asarray(spread_rope(heads), bf16),
            jnp.zeros((lat_width - qrank - kvrank, heads * 2 * LANES), bf16),
        ],
        axis=0,
    )

    half_of = lambda w, d: ((half, w), d)
    out_parts = across(split_columns([w_o], "ctx", 2, nc), "ctx", nc)
    down_parts = weight_parts(w_down)
    outs = plain(
        functools.partial(enter_kernel, sizes, block),
        ids,
        [
            tokens[0],
            cotangent[0],
            gain_in,
            gain_query,
            gain_latent,
            w_qa,
            w_kva,
            own_cos,
            own_sin,
            turned,
        ],
        [
            half_of(width, bf16),
            half_of(lat_width, bf16),
            half_of(qrank, f32),
            half_of(kvrank, f32),
            half_of(width, bf16),
            half_of(width, bf16),
            half_of(width, bf16),
        ]
        + [half_of(nz * block, bf16)] * nc,
        [pltpu.VMEM((half, width), bf16)] * 2,
        flops=2 * half * width * (qrank + kvrank),
    )
    _, latents, q_latent, kv_latent, own_tokens, own_cotangent, grad_mlp = outs[:7]
    normed_parts = outs[7:]
    lat_parts = along_ctx(latents)
    tables = (cos_table, sin_table, query_table, key_table)

    out_parts[0] = after(out_parts[0], latents)
    own_out = stack_blocks(out_parts, 2)[0]
    down_parts[0] = after(down_parts[0], own_out, wide_qb, wide_kvb, *tables)
    down = gather_weights(down_parts)
    out_pieces = gather_dp(after(own_out, down_parts[1], down_parts[2], down_parts[3]))
    lat_parts[0] = after(lat_parts[0], out_pieces[1])
    lat_own = jnp.stack(lat_parts)
    lat_oth = swap(lat_own)
    pair_parts = weight_parts(after(w_gate, out_pieces[2]), w_up)
    o_own, o_oth, q_rot, keys, values, qn, kvn = attend(
        nt, ids, lat_own, lat_oth, after(wide_qb, out_pieces[2]), wide_kvb, *tables
    )
    out_pieces[0] = after(out_pieces[0], o_own)
    full_out = plain(
        functools.partial(spread_kernel, heads, nz),
        ids,
        out_pieces,
        [((nc, nz, block, heads * LANES), bf16)],
    )[0].reshape(width, heads * LANES)
    keep, give = project_out(o_own, o_oth, full_out)
    pair_parts[0] = after(pair_parts[0], keep)
    pair = gather_weights(pair_parts)
    gm = gather_dp(after(grad_mlp, *pair_parts[1:]))
    attn = reduce_ctx(keep, give)
    resid, normed_mid = plain(
        functools.partial(middle_kernel, len(attn)),
        ids,
        attn + [own_tokens, gain_middle],
        [half_of(width, f32), half_of(width, bf16)],
    )
    nm = gather_dp(after(normed_mid, gm[1]))
    groups = [range(0, nz // 2), range(nz // 2, nz)]
    nm_all, gm_all, hidden, grad_gate, grad_up, grad_parts, mlp_parts = [], [], [], [], [], [], []
    for group in groups:
        nm_own = jnp.concatenate([nm[k] for k in group])
        gm_own = jnp.concatenate([gm[k] for k in group])
        if hidden:
            nm_own = after(nm_own, hidden[0])
        nm_oth, gm_oth = swap(nm_own), swap(gm_own)
        nm_all += [nm_own, nm_oth]
        gm_all += [gm_own, gm_oth]
        hid, gg, gu, gn_own, gn_oth, ml_own, ml_oth = feed_forward(
            nc, nm_own, nm_oth, gm_own, gm_oth, pair, down
        )
        hidden.append(hid)
        grad_gate.append(gg)
        grad_up.append(gu)
        for parts, own, oth in ((grad_parts, gn_own, gn_oth), (mlp_parts, ml_own, ml_oth)):
            total = (own.astype(f32) + swap(oth).astype(f32)).astype(bf16)
            parts += [total[i * half : (i + 1) * half] for i in range(len(group))]
    grad_normed = scatter_dp(grad_parts)
    gm_all[0] = after(gm_all[0], grad_normed[1])
    down_product = products(gm_all, [hidden], nc)
    down_product = scatter_weights(down_product)
    nm_all[0] = after(nm_all[0], grad_normed[3])
    pair_product = products(nm_all, [grad_gate, grad_up], nc)
    grad_normed[0] = after(grad_normed[0], pair_product)

    grad_resid, grad_attn, grad_gain_mlp = plain(
        functools.partial(back_middle_kernel, nz),
        ids,
        grad_normed + [resid, own_cotangent, gain_middle],
        [half_of(width, f32), half_of(width, bf16), ((1, width), f32)],
    )
    ga_parts = along_ctx(grad_attn)
    mlp_parts = scatter_dp([after(part, grad_attn) for part in mlp_parts])
    ga_own = jnp.stack(ga_parts)
    ga_oth = swap(ga_own)
    pair_product = scatter_weights(after(pair_product, ga_own))
    g_own, g_oth = project_heads(ga_own, ga_oth, full_out)
    grad_q, grad_kv = attend_back(
        nt, ids, q_rot, keys, values, o_own, o_oth, g_own, g_oth, cos_table, sin_table
    )
    mlp_parts[0] = after(mlp_parts[0], grad_q)
    layer_out = plain(
        functools.partial(leave_kernel, sizes, block, nz),
        ids,
        mlp_parts + [resid],
        [half_of(width, bf16)],
        [pltpu.VMEM((half, width), f32)],
    )[0]
    (grad_w_down,) = weight_rows(after(down_product, *mlp_parts))
    grad_lat = reduce_ctx(*grad_latent(sizes, ids, grad_q, grad_kv, wide_qb, wide_kvb))

    ups = grad_ups(qn, after(kvn, grad_lat[0]), grad_q, grad_kv)
    deep = ups.shape[0] // nz
    ups = ups.reshape(nz, deep, heads * LANES)
    ups = scatter_dp([pick(ups, z ^ k) for k in range(nz)])
    out_product = grad_out_weight(
        sizes, block, ids, ga_own, after(ga_oth, grad_lat[0], ups[0]), o_own, o_oth
    )
    grad_lat[0] = after(grad_lat[0], out_product)
    grad_lat, grad_gain_q, grad_gain_kv = plain(
        functools.partial(grad_enter_kernel, len(grad_lat)),
        ids,
        grad_lat + [q_latent, kv_latent, gain_query, gain_latent, own_cos, own_sin, turned],
        [half_of(lat_width, bf16), ((1, qrank), f32), ((1, KVRANK), f32)],
    )
    gl_parts = along_ctx(grad_lat)
    grad_tokens, grad_gain_attn = plain(
        functools.partial(grad_tokens_kernel, sizes, block),
        ids,
        [grad_lat, w_qa, w_kva, tokens[0], gain_in, grad_resid],
        [half_of(width, bf16), ((1, width), f32)],
        [pltpu.VMEM((half, width), f32)],
        flops=2 * half * width * (qrank + kvrank),
    )
    ups[0] = after(ups[0], grad_lat)
    own = sum(p.astype(f32) for p in ups).astype(bf16)
    ups = gather_dp(own)
    out_parts = scatter_dp([out_product[k] for k in range(nz)])
    gl_parts[0] = after(gl_parts[0], grad_tokens)
    gl_own = jnp.stack(gl_parts)
    gl_oth = swap(gl_own)

    xin_own = jnp.stack(across(normed_parts, "ctx", nc))
    xin_oth = swap(xin_own)
    share = lat_width // nt // LANES * LANES
    wide = lat_width - share
    parts = plain(
        functools.partial(grad_down_kernel, share),
        ids,
        [xin_own, xin_oth, gl_own, gl_oth],
        [((nz, block, wide), bf16)],
        flops=2 * length * nz * block * wide,
    )[0]
    ups[0] = after(ups[0], parts)
    ups = stack_blocks([piece[None] for piece in ups], 1).reshape(nz * deep, heads * LANES)
    ups = along_ctx(ups)
    out_parts[0] = after(out_parts[0], parts)
    own = sum(p.astype(f32) for p in out_parts).astype(bf16)
    out_parts = across([pick(own, c ^ k)[None] for k in range(nc)], "ctx", nc)
    own = scatter_dp([parts[k] for k in range(nz)])
    grad_w_gate, grad_w_up = weight_rows(after(pair_product, own[-1]))
    own = sum(p.astype(f32) for p in own).astype(bf16)
    grad_w_qa, grad_w_kva = plain(
        functools.partial(finish_down_kernel, share),
        ids,
        [own, swap(own)],
        [((block, qrank), f32), ((block, kvrank), f32)],
    )
    (grad_w_o,) = join_columns(out_parts, "ctx", 2)
    grad_w_qb, grad_w_kvb = plain(
        functools.partial(finish_ups_kernel, heads, nc),
        ids,
        [jnp.stack(ups)],
        [((qrank, nc * heads * (NOPE + ROPE)), f32), ((KVRANK, nc * heads * LANES), f32)],
    )
    layer_out = join_rows(layer_out)
    grad_tokens = join_rows(grad_tokens)

    turned_gain = jnp.swapaxes(grad_gain_mlp.reshape(nc, nz, block), 0, 1).reshape(1, width)
    gains = jnp.concatenate([grad_gain_attn, grad_gain_q, grad_gain_kv, turned_gain], axis=1)
    gains = gains.reshape(-1, LANES)
    for axis, size in (("tensor", nt), ("ctx", nc), ("dp", nz)):
        step = 1
        while step < size:
            gains = gains + exchange(gains, axis, step, size)
            step *= 2
    gains = gains.reshape(-1)
    ends = np.cumsum([width, qrank, KVRANK])
    grad_gain_attn, grad_gain_q, grad_gain_kv, grad_gain_mlp = jnp.split(gains, ends)
    return (
        layer_out,
        grad_tokens,
        grad_gain_attn,
        grad_w_qa,
        grad_gain_q,
        grad_w_kva,
        grad_gain_kv,
        grad_w_qb,
        grad_w_kvb,
        grad_w_o,
        grad_gain_mlp,
        grad_w_gate,
        grad_w_up,
        grad_w_down,
    )


def solution(mesh):
    placed = (
        P("dp", "ctx", None),
        P("dp", None),
        P(),
        P(),
        P(),
        P(),
        P(),
        P(None, "tensor"),
        P(None, "tensor"),
        P(("dp", "ctx"), "tensor"),
        P(),
        P(("dp", "ctx"), "tensor"),
        P(("dp", "ctx"), "tensor"),
        P(("dp", "ctx"), "tensor"),
        P("dp", "ctx", None),
    )
    sizes = tuple(mesh.shape[name] for name in ("tensor", "dp", "ctx"))
    return jax.shard_map(
        functools.partial(body, sizes),
        mesh=mesh,
        in_specs=placed,
        out_specs=(
            P("dp", "ctx", None),
            P("dp", "ctx", None),
            P(),
            P(("dp", "ctx"), None),
            P(),
            P(("dp", "ctx"), None),
            P(),
            P(None, "tensor"),
            P(None, "tensor"),
            P(("dp", "ctx"), "tensor"),
            P(),
            P(("dp", "ctx"), "tensor"),
            P(("dp", "ctx"), "tensor"),
            P(("dp", "ctx"), "tensor"),
        ),
        check_vma=False,
    )
```

time: 1120 us -> 764 us (0.68)
  waiting for transfers between devices: 479 us -> 302 us
  Pallas kernels: 31 us -> 203 us
  local copies, waits for them, and re-layouts: 225 us -> 53.7 us
  matrix products: 153 us -> 5.62 us
  other arithmetic: 113 us -> 37.4 us
  starting transfers between devices: 92.1 us -> 135 us
    ppermute x89 -> x85, waiting for transfers between devices: 479 us -> 245 us  [exchange(): return lax.ppermute(value, axis, [(i, i ^ step) for i in range(size)])]
    pallas_call x2 -> x33, Pallas kernels: 31 us -> 203 us  [the longest x22 53.8 us: plain(): pl.pallas_call(kernel, in_specs=[SCALARS] + [LOCAL] * len(operands), out_...]
    dot_general x25 -> x2, matrix products: 153 us -> 5.62 us  [dot(): lax.dot_general(left, right, (contract, ((), ())), preferred_element_type...]
    unnamed x263 -> x238, local copies, waits for them, and re-layouts: 88.3 us -> 32.6 us
    ppermute x0 -> x18, starting transfers between devices: none -> 54.2 us  [the longest x4 18.8 us: gather_dp(): far = lax.ppermute(second, 'dp', [(1, 0), (2, 3)])]
    ppermute x0 -> x18, waiting for transfers between devices: none -> 47 us  [the longest x5 25.4 us: scatter_dp(): far = lax.ppermute(parts[3], 'dp', [(0, 1), (3, 2)])]
    reshape x10 -> x6, local copies, waits for them, and re-layouts: 37.5 us -> 0.38 us  [the longest x3 0.19 us: turn_gain(): return jnp.swapaxes(value.reshape(nz, nc, block), 0, 1).reshape(1, width)]
    convert_element_type x12 -> x0, local copies, waits for them, and re-layouts: 31.4 us -> none  [the longest x1 6.41 us: body(): grad_w_qb = grad_w_qb.reshape(qrank, -1).astype(f32)]
  transfers between devices with their start and end apart: 97 -> 107, of which waited for: 40 -> 44; matrix products, arithmetic and copies ran while one was open for 33% -> 9% of each run, Pallas kernels for 1% -> 25%
where the time goes in v2:
time: 764 us; the launch traced here: 753 us
  waiting for transfers between devices  302 us (40%)
  Pallas kernels  203 us (27%)
  starting transfers between devices  135 us (18%)
  local copies, waits for them, and re-layouts  53.7 us (7%)
  other arithmetic  37.4 us (5%)
  between operations  16.1 us (2%)
    ppermute x85, waiting for transfers between devices, exchange(): return lax.ppermute(value, axis, [(i, i ^ step) for i in range(size)])  245 us
    ppermute x85, starting transfers between devices, exchange(): return lax.ppermute(value, axis, [(i, i ^ step) for i in range(size)])  80.8 us
    pallas_call x22, Pallas kernels, plain(): pl.pallas_call(kernel, in_specs=[SCALARS] + [LOCAL] * len(operands), out_...  53.8 us
    pallas_call x2, Pallas kernels, feed_forward(): pl.pallas_call(functools.partial(mlp_kernel, steps), grid=(2 * steps,), i...  52.3 us
    unnamed x238, local copies, waits for them, and re-layouts  32.6 us
    ppermute x5, waiting for transfers between devices, scatter_dp(): far = lax.ppermute(parts[3], 'dp', [(0, 1), (3, 2)])  25.4 us
    pallas_call x2, Pallas kernels, products(): pl.pallas_call(functools.partial(product_kernel, len(lefts), count), grid...  23.2 us
    pallas_call x1, Pallas kernels, attend(): pl.pallas_call(functools.partial(forward_kernel, nt), grid_spec=pltpu.Pre...  21.4 us
  transfers between devices with their start and end apart: 107, of which 44 were waited for; matrix products, arithmetic and copies ran while one was open for 9% of the time, Pallas kernels for 25%

profile of v2, /device:TPU:12, one launch (start us, length us, event | category | flops | bytes accessed | tf_op | source)
XLA Modules:
  0.0 753.4 jit_solution(7654360821603501685)
XLA Ops:
  24.5 3.9 fusion.18
  28.7 3.9 convolution_convert_fusion.wq_ref.wq
  41.5 5.6 shard_map.290
  54.3 3.7 collective-permute-done.7
  63.2 5.3 collective-permute-done.9
  70.6 3.6 collective-permute-start.12
  76.1 18.6 %collective-permute-done.12.refs_2_ = bf16[4,160,320]{2,1,0:T(8,128)(2,1)S(1)} collective-permute-done((bf16[4,160,320]{2,1,0:T(8,128)(2,1)S(1)}, bf16[4,160,320]{2,1,0:T(8,128)(2,1)S(1)}, u32[]{:S(2)}, u32[]{:S(2)}) %collective-permute-start.12) | collective-permute-done | bytes 409632 | tf_op jit(solution)/shard_map/ppermute | solution.py:44
  94.7 5.4 collective-permute-start.13
  107.7 14.6 %collective-permute-done.13 = bf16[4,160,320]{2,1,0:T(8,128)(2,1)} collective-permute-done((bf16[4,160,320]{2,1,0:T(8,128)(2,1)S(1)}, bf16[4,160,320]{2,1,0:T(8,128)(2,1)}, u32[]{:S(2)}, u32[]{:S(2)}) %collective-permute-start.13) | collective-permute-done | bytes 409632 | tf_op jit(solution)/shard_map/ppermute | solution.py:873
  125.5 21.4 %shard_map.294 = (bf16[4,128,640]{2,1,0:T(8,128)(2,1)S(1)}, bf16[4,128,640]{2,1,0:T(8,128)(2,1)S(1)}, bf16[1024,640]{1,0:T(8,128)(2,1)}, bf16[1024,640]{1,0:T(8,...) custom-call(s32[3]{0:T(128)S(1)} %pad_add_fusion.ids, ...), custom_call_target="tpu_custom_call" | custom-call | flops 671088640 | bytes 1048576 | tf_op jit(solution)/shard_map/pallas_call | solution.py:336
  151.0 7.9 %shard_map.296 = (f32[4,128,2560]{2,1,0:T(8,128)}, bf16[4,128,2560]{2,1,0:T(8,128)(2,1)S(1)}) custom-call(bf16[4,128,640]{2,1,0:T(8,128)(2,1)S(1)} %get-tuple-element.122.own.oown_ref.oown, bf16[4,128,640]{2,1,0:T(8,128)(2,1)S(1)} %get-tuple-element.123.oth.ooth_ref.ooth, bf16[2560,640]{1,0:T(8,128)(2,1)} %bitcast.160), custom_call_target="tpu_custom_call" | custom-call | flops 335544320 | bytes 2424832 | tf_op jit(solution)/shard_map/pallas_call | solution.py:452
  160.5 3.2 shard_map.299
  164.5 3.7 collective-permute-start.23
  168.3 3.4 collective-permute-start.35
  171.7 5.3 add_convert_fusion
  179.7 14.6 %collective-permute-done.18 = bf16[64,2560]{1,0:T(8,128)(2,1)S(1)} collective-permute-done((bf16[64,2560]{1,0:T(8,128)(2,1)S(1)}, bf16[64,2560]{1,0:T(8,128)(2,1)S(1)}, u32[]{:S(2)}, u32[]{:S(2)}) %collective-permute-start.18) | collective-permute-done | bytes 327712 | tf_op jit(solution)/shard_map/ppermute | solution.py:44
  197.0 25.6 %collective-permute-done.17.refs_1_ = bf16[128,2560]{1,0:T(8,128)(2,1)S(1)} collective-permute-done((bf16[128,2560]{1,0:T(8,128)(2,1)S(1)}, bf16[128,2560]{1,0:T(8,128)(2,1)S(1)}, u32[]{:S(2)}, u32[]{:S(2)}) %collective-permute-start.17) | collective-permute-done | bytes 655392 | tf_op jit(solution)/shard_map/ppermute | solution.py:44
  225.4 3.4 collective-permute-start.34
  230.5 20.4 %collective-permute-done.24 = bf16[128,2560]{1,0:T(8,128)(2,1)S(1)} collective-permute-done((bf16[128,2560]{1,0:T(8,128)(2,1)}, bf16[128,2560]{1,0:T(8,128)(2,1)S(1)}, u32[]{:S(2)}, u32[]{:S(2)}) %collective-permute-start.24) | collective-permute-done | bytes 655392 | tf_op jit(solution)/shard_map/ppermute | solution.py:44
  251.1 4.2 collective-permute-start.31
  255.3 3.4 collective-permute-done.29
  258.7 6.1 collective-permute-start.30
  264.8 3.9 collective-permute-done.34
  269.7 10.1 %all-gather.3.cloned.1.call-done.pair_hbm = bf16[5120,800]{1,0:T(8,128)(2,1)} async-done(((bf16[1280,800]{1,0:T(8,128)(2,1)}), bf16[5120,800]{1,0:T(8,128)(2,1)}) %all-gather.3.cloned.1.call-update) | async-done | bytes 8192016 | tf_op jit(solution)/shard_map/all_gather | solution.py:921
  279.8 26.0 %shard_map.301 = (bf16[512,800]{1,0:T(8,128)(2,1)}, bf16[512,800]{1,0:T(8,128)(2,1)}, bf16[512,800]{1,0:T(8,128)(2,1)}, bf16[256,2560]{1,0:T(8,128)(2,1)}, bf16[...) custom-call(bf16[256,2560]{1,0:T(8,128)(2,1)} %copy-done.5, ...), custom_call_target="tpu_custom_call" | custom-call | flops 1258291200 | bytes 2277376 | tf_op jit(solution)/shard_map/pallas_call | solution.py:577
  314.1 26.4 %shard_map.302 = (bf16[512,800]{1,0:T(8,128)(2,1)}, bf16[512,800]{1,0:T(8,128)(2,1)}, bf16[512,800]{1,0:T(8,128)(2,1)}, bf16[256,2560]{1,0:T(8,128)(2,1)}, bf16[...) custom-call(bf16[256,2560]{1,0:T(8,128)(2,1)} %copy-done.90, ...), custom_call_target="tpu_custom_call" | custom-call | flops 1258291200 | bytes 2277376 | tf_op jit(solution)/shard_map/pallas_call | solution.py:577
  342.0 8.5 %shard_map.321 = bf16[2560,800]{1,0:T(8,128)(2,1)} custom-call(bf16[256,2560]{1,0:T(8,128)(2,1)S(1)} %copy-done.8, bf16[256,2560]{1,0:T(8,128)(2,1)} %collective-permute-done.26.gm_oth.refs_1_, bf16[256,2560]{1,0:T(8,128)(2,1)} %pad_maximum_fusion.3.gm_own.refs_2_, bf16[256,2560]{1,0:T(8,128)(2,1)} %collective-permute-done.36.gm_oth.refs_3_, ...), custom_call_target="tpu_custom_call" | custom-call | flops 419430400 | bytes 933888 | tf_op jit(solution)/shard_map/pallas_call | solution.py:613
  352.0 2.9 collective-permute-done.37
  358.3 3.5 collective-permute-start.38
  361.8 13.8 %collective-permute-done.40 = bf16[128,2560]{1,0:T(8,128)(2,1)S(1)} collective-permute-done((bf16[128,2560]{1,0:T(8,128)(2,1)S(1)}, bf16[128,2560]{1,0:T(8,128)(2,1)S(1)}, u32[]{:S(2)}, u32[]{:S(2)}) %collective-permute-start.40) | collective-permute-done | bytes 655392 | tf_op jit(solution)/shard_map/ppermute | solution.py:879
  378.0 14.7 %shard_map.303 = bf16[5120,800]{1,0:T(8,128)(2,1)} custom-call(bf16[256,2560]{1,0:T(8,128)(2,1)S(1)} %copy-done.6, bf16[256,2560]{1,0:T(8,128)(2,1)} %collective-permute-done.25.nm_oth.refs_1_, bf16[256,2560]{1,0:T(8,128)(2,1)} %copy-done.90, bf16[256,2560]{1,0:T(8,128)(2,1)} %copy-done.91, bf16[512,800]{1,0:T(8,128)(2,1)S(1)} %copy-done.44, ...), custom_call_target="tpu_custom_call" | custom-call | flops 838860800 | bytes 1343488 | tf_op jit(solution)/shard_map/pallas_call | solution.py:613
  392.6 12.3 %collective-permute-done.41.refs_2_ = bf16[128,2560]{1,0:T(8,128)(2,1)} collective-permute-done((bf16[128,2560]{1,0:T(8,128)(2,1)}, bf16[128,2560]{1,0:T(8,128)(2,1)}, u32[]{:S(2)}, u32[]{:S(2)}) %collective-permute-start.41) | collective-permute-done | bytes 655392 | tf_op jit(solution)/shard_map/ppermute | solution.py:44
  407.1 3.0 shard_map.304
  412.2 13.0 %collective-permute-done.42 = bf16[128,2560]{1,0:T(8,128)(2,1)S(1)} collective-permute-done((bf16[128,2560]{1,0:T(8,128)(2,1)S(1)}, bf16[128,2560]{1,0:T(8,128)(2,1)S(1)}, u32[]{:S(2)}, u32[]{:S(2)}) %collective-permute-start.42) | collective-permute-done | bytes 655392 | tf_op jit(solution)/shard_map/ppermute | solution.py:44
  428.0 4.6 collective-permute-done.45
  444.8 6.9 shard_map.305
  451.8 15.8 %shard_map.306 = (bf16[1024,1280]{1,0:T(8,128)(2,1)}, bf16[1024,1280]{1,0:T(8,128)(2,1)}) custom-call(s32[3]{0:T(128)S(1)} %pad_add_fusion.ids, bf16[1024,640]{1,0:T(8,128)(2,1)S(1)} %copy-done.38, bf16[1024,640]{1,0:T(8,128)(2,1)} %get-tuple-element.159.k_ref, bf16[1024,640]{1,0:T(8,128)(2,1)} %get-tuple-element.160.v_ref, ...), custom_call_target="tpu_custom_call" | custom-call | flops 536870912 | bytes 1572864 | tf_op jit(solution)/shard_map/pallas_call | solution.py:371
  467.7 7.7 %shard_map.309 = (f32[4,128,1152]{2,1,0:T(8,128)}, bf16[4,128,1152]{2,1,0:T(8,128)(2,1)S(1)}) custom-call(s32[3]{0:T(128)S(1)} %pad_add_fusion.ids, bf16[1024,1280]{1,0:T(8,128)(2,1)} %get-tuple-element.163.gq, bf16[1024,1280]{1,0:T(8,128)(2,1)} %get-tuple-element.170.gkv, bf16[768,1280]{1,0:T(8,128)(2,1)S(1)} %copy-done.11, bf16[384,1280]{1,0:T(8,128)(2,1)S(1)} %copy-done.4), custom_call_target="tpu_custom_call" | custom-call | flops 301989888 | bytes 1114112 | tf_op jit(solution)/shard_map/pallas_call | solution.py:689
  476.5 4.0 collective-permute-start.51
  486.5 7.0 shard_map.310
  498.9 4.5 collective-permute-done.55.refs_1_
  504.8 7.3 shard_map.311
  519.0 4.5 collective-permute-done.50.refs_2_
  531.2 4.3 shard_map.313
  537.9 4.7 collective-permute-done.71
  547.3 9.5 %collective-permute-done.78 = bf16[256,640]{1,0:T(8,128)(2,1)S(1)} collective-permute-done((bf16[256,640]{1,0:T(8,128)(2,1)S(1)}, bf16[256,640]{1,0:T(8,128)(2,1)S(1)}, u32[]{:S(2)}, u32[]{:S(2)}) %collective-permute-start.78) | collective-permute-done | bytes 327712 | tf_op jit(solution)/shard_map/ppermute | solution.py:44
  556.8 3.4 collective-permute-done.80
  560.4 3.1 collective-permute-start.83
  576.6 3.8 collective-permute-start.84
  582.8 3.1 collective-permute-done.85
  590.9 3.5 collective-permute-start.93
  596.4 2.9 shard_map.315
  599.4 5.6 collective-permute-done.82
  611.4 4.3 collective-permute-done.63
  618.4 11.5 %collective-permute-done.74 = bf16[160,640]{1,0:T(8,128)(2,1)} collective-permute-done((bf16[160,640]{1,0:T(8,128)(2,1)S(1)}, bf16[160,640]{1,0:T(8,128)(2,1)}, u32[]{:S(2)}, u32[]{:S(2)}) %collective-permute-start.74) | collective-permute-done | bytes 204832 | tf_op jit(solution)/shard_map/ppermute | solution.py:879
  635.0 3.0 collective-permute-start.76
  652.1 12.2 %collective-permute-done.75 = bf16[160,640]{1,0:T(8,128)(2,1)S(1)} collective-permute-done((bf16[160,640]{1,0:T(8,128)(2,1)S(1)}, bf16[160,640]{1,0:T(8,128)(2,1)S(1)}, u32[]{:S(2)}, u32[]{:S(2)}) %collective-permute-start.75) | collective-permute-done | bytes 204832 | tf_op jit(solution)/shard_map/ppermute | solution.py:44
  665.6 4.8 collective-permute-done.101.refs_2_
  671.4 6.0 collective-permute-done.102.refs_3_
  697.4 5.0 shard_map.318
  702.3 12.0 %collective-permute-done.97.refs_1_ = bf16[2,160,800]{2,1,0:T(8,128)(2,1)S(1)} collective-permute-done((bf16[2,160,800]{2,1,0:T(8,128)(2,1)S(1)}, bf16[2,160,800]{2,1,0:T(8,128)(2,1)S(1)}, u32[]{:S(2)}, u32[]{:S(2)}) %collective-permute-start.97) | collective-permute-done | bytes 512032 | tf_op jit(solution)/shard_map/ppermute | solution.py:44
  714.4 15.6 %collective-permute-done.98.refs_2_ = bf16[2,160,800]{2,1,0:T(8,128)(2,1)S(1)} collective-permute-done((bf16[2,160,800]{2,1,0:T(8,128)(2,1)S(1)}, bf16[2,160,800]{2,1,0:T(8,128)(2,1)S(1)}, u32[]{:S(2)}, u32[]{:S(2)}) %collective-permute-start.98) | collective-permute-done | bytes 512032 | tf_op jit(solution)/shard_map/ppermute | solution.py:44
  730.0 13.1 %collective-permute-done.99.refs_3_ = bf16[2,160,800]{2,1,0:T(8,128)(2,1)S(1)} collective-permute-done((bf16[2,160,800]{2,1,0:T(8,128)(2,1)S(1)}, bf16[2,160,800]{2,1,0:T(8,128)(2,1)S(1)}, u32[]{:S(2)}, u32[]{:S(2)}) %collective-permute-start.99) | collective-permute-done | bytes 512032 | tf_op jit(solution)/shard_map/ppermute | solution.py:44
  743.1 3.3 shard_map.320
  (532 shorter events, 214.8 us)
Async XLA Ops:
  7.2 262.5 %all-gather.5.cloned.1.call-start = ((), (), s32[]{:S(2)}) async-start(), calls=%async_computation.3 | async-start | bytes 5734400 | tf_op jit(solution)/shard_map/all_gather | solution.py:921
  11.4 27.0 %collective-permute-start = (bf16[1,160,320]{2,1,0:T(8,128)(2,1)}, bf16[1,160,320]{2,1,0:T(8,128)(2,1)S(1)}, u32[]{:S(2)}, u32[]{:S(2)}) collective-permute-start(bf16[1,160,320]{2,1,0:T(8,128)(2,1)} %get-tuple-element.113), channel_id=1, source_target_pairs={{0,1},{1,0},{2,3},{3,2},{4,5},{5,4},{6,7},{7,6},{8,9},{9,8},{10,11... | collective-permute-start | bytes 307208 | tf_op jit(solution)/shard_map/ppermute | solution.py:44
  12.9 34.3 %collective-permute-start.1 = (bf16[1,160,320]{2,1,0:T(8,128)(2,1)}, bf16[1,160,320]{2,1,0:T(8,128)(2,1)}, u32[]{:S(2)}, u32[]{:S(2)}) collective-permute-start(bf16[1,160,320]{2,1,0:T(8,128)(2,1)} %get-tuple-element.114), channel_id=1, source_target_pairs={{0,2},{1,3},{2,0},{3,1},{4,6},{5,7},{6,4},{7,5},{8,10},{9,11},{10,... | collective-permute-start | bytes 307208 | tf_op jit(solution)/shard_map/ppermute | solution.py:44
  16.6 31.7 %collective-permute-start.3 = (bf16[1,160,800]{2,1,0:T(8,128)(2,1)}, bf16[1,160,800]{2,1,0:T(8,128)(2,1)}, u32[]{:S(2)}, u32[]{:S(2)}) collective-permute-start(bf16[1,160,800]{2,1,0:T(8,128)(2,1)} %get-tuple-element.116), channel_id=1, source_target_pairs={{0,4},{4,0},{8,12},{12,8},{1,5},{5,1},{9,13},{13,9},{2,6},{6,2},{1... | collective-permute-start | bytes 768008 | tf_op jit(solution)/shard_map/ppermute | solution.py:44
  17.1 31.3 %collective-permute-start.4 = (bf16[1,160,800]{2,1,0:T(8,128)(2,1)}, bf16[1,160,800]{2,1,0:T(8,128)(2,1)}, u32[]{:S(2)}, u32[]{:S(2)}) collective-permute-start(bf16[1,160,800]{2,1,0:T(8,128)(2,1)} %get-tuple-element.117), channel_id=1, source_target_pairs={{0,8},{4,12},{8,0},{12,4},{1,9},{5,13},{9,1},{13,5},{2,10},{6,14},... | collective-permute-start | bytes 768008 | tf_op jit(solution)/shard_map/ppermute | solution.py:44
  19.6 28.7 %collective-permute-start.5 = (bf16[1,160,800]{2,1,0:T(8,128)(2,1)}, bf16[1,160,800]{2,1,0:T(8,128)(2,1)}, u32[]{:S(2)}, u32[]{:S(2)}) collective-permute-start(bf16[1,160,800]{2,1,0:T(8,128)(2,1)} %get-tuple-element.118), channel_id=1, source_target_pairs={{0,12},{4,8},{8,4},{12,0},{1,13},{5,9},{9,5},{13,1},{2,14},{6,10},... | collective-permute-start | bytes 768008 | tf_op jit(solution)/shard_map/ppermute | solution.py:44
  50.8 228.9 %all-gather.3.cloned.1.call-start = ((), (), s32[]{:S(2)}) async-start(), calls=%async_computation.2 | async-start | bytes 11468800 | tf_op jit(solution)/shard_map/all_gather | solution.py:921
  70.6 51.8 %collective-permute-start.11 = (bf16[4,128,1152]{2,1,0:T(8,128)(2,1)}, bf16[4,128,1152]{2,1,0:T(8,128)(2,1)}, u32[]{:S(2)}, u32[]{:S(2)}) collective-permute-start(bf16[4,128,1152]{2,1,0:T(8,128)(2,1)} %pad_maximum_fusion.4.own_ref), channel_id=1, source_target_pairs={{0,16},{16,0},{1,17},{17,1},{2,18},{18,2},{3,19},{19,3},{4,20},{20... | collective-permute-start | bytes 3538952 | tf_op jit(solution)/shard_map/ppermute | solution.py:44
  70.6 24.1 %collective-permute-start.12 = (bf16[4,160,320]{2,1,0:T(8,128)(2,1)S(1)}, bf16[4,160,320]{2,1,0:T(8,128)(2,1)S(1)}, u32[]{:S(2)}, u32[]{:S(2)}) collective-permute-start(bf16[4,160,320]{2,1,0:T(8,128)(2,1)S(1)} %bitcast.172), channel_id=1, source_target_pairs={{0,8},{4,12},{8,0},{12,4},{1,9},{5,13},{9,1},{13,5},{2,10},{6,14},... | collective-permute-start | bytes 1228808 | tf_op jit(solution)/shard_map/ppermute | solution.py:44
  74.2 32.2 %collective-permute-start.14 = (bf16[4,160,320]{2,1,0:T(8,128)(2,1)S(1)}, bf16[4,160,320]{2,1,0:T(8,128)(2,1)S(1)}, u32[]{:S(2)}, u32[]{:S(2)}) collective-permute-start(bf16[4,160,320]{2,1,0:T(8,128)(2,1)S(1)} %bitcast.173), channel_id=1, source_target_pairs={{4,8},{8,4},{5,9},{9,5},{6,10},{10,6},{7,11},{11,7},{20,24},{24,20... | collective-permute-start | bytes 1228808 | tf_op jit(solution)/shard_map/ppermute | solution.py:872
  94.7 27.6 %collective-permute-start.13 = (bf16[4,160,320]{2,1,0:T(8,128)(2,1)S(1)}, bf16[4,160,320]{2,1,0:T(8,128)(2,1)}, u32[]{:S(2)}, u32[]{:S(2)}) collective-permute-start(bf16[4,160,320]{2,1,0:T(8,128)(2,1)S(1)} %collective-permute-done.12.refs_2_), channel_id=1, source_target_pairs={{4,0},{8,12},{5,1},{9,13},{6,2},{10,14},{7,3},{11,15},{20,16},{24,... | collective-permute-start | bytes 1228808 | tf_op jit(solution)/shard_map/ppermute | solution.py:873
  103.8 56.7 %collective-permute-start.20 = (bf16[2,160,800]{2,1,0:T(8,128)(2,1)}, bf16[2,160,800]{2,1,0:T(8,128)(2,1)}, u32[]{:S(2)}, u32[]{:S(2)}) collective-permute-start(bf16[2,160,800]{2,1,0:T(8,128)(2,1)} %get-tuple-element.131), channel_id=1, source_target_pairs={{0,4},{4,0},{8,12},{12,8},{1,5},{5,1},{9,13},{13,9},{2,6},{6,2},{1... | collective-permute-start | bytes 1536008 | tf_op jit(solution)/shard_map/ppermute | solution.py:44
  103.8 56.7 %collective-permute-start.21 = (bf16[2,160,800]{2,1,0:T(8,128)(2,1)}, bf16[2,160,800]{2,1,0:T(8,128)(2,1)}, u32[]{:S(2)}, u32[]{:S(2)}) collective-permute-start(bf16[2,160,800]{2,1,0:T(8,128)(2,1)} %get-tuple-element.132), channel_id=1, source_target_pairs={{0,8},{4,12},{8,0},{12,4},{1,9},{5,13},{9,1},{13,5},{2,10},{6,14},... | collective-permute-start | bytes 1536008 | tf_op jit(solution)/shard_map/ppermute | solution.py:44
  106.4 54.0 %collective-permute-start.22 = (bf16[2,160,800]{2,1,0:T(8,128)(2,1)}, bf16[2,160,800]{2,1,0:T(8,128)(2,1)}, u32[]{:S(2)}, u32[]{:S(2)}) collective-permute-start(bf16[2,160,800]{2,1,0:T(8,128)(2,1)} %get-tuple-element.133), channel_id=1, source_target_pairs={{0,12},{4,8},{8,4},{12,0},{1,13},{5,9},{9,5},{13,1},{2,14},{6,10},... | collective-permute-start | bytes 1536008 | tf_op jit(solution)/shard_map/ppermute | solution.py:44
  163.7 454.7 %reduce-scatter.5.cloned.1.call-start = ((), (), s32[]{:S(2)}) async-start(), calls=%async_computation.5 | async-start | bytes 5734400 | tf_op jit(solution)/shard_map/reduce_scatter | solution.py:924
  164.5 60.2 %collective-permute-start.23 = (bf16[128,2560]{1,0:T(8,128)(2,1)}, bf16[128,2560]{1,0:T(8,128)(2,1)S(1)}, u32[]{:S(2)}, u32[]{:S(2)}) collective-permute-start(bf16[128,2560]{1,0:T(8,128)(2,1)} %get-tuple-element.134), channel_id=1, source_target_pairs={{0,4},{4,0},{8,12},{12,8},{1,5},{5,1},{9,13},{13,9},{2,6},{6,2},{1... | collective-permute-start | bytes 1966088 | tf_op jit(solution)/shard_map/ppermute | solution.py:44
  168.2 57.2 %collective-permute-start.33 = (bf16[128,2560]{1,0:T(8,128)(2,1)}, bf16[128,2560]{1,0:T(8,128)(2,1)S(1)}, u32[]{:S(2)}, u32[]{:S(2)}) collective-permute-start(bf16[128,2560]{1,0:T(8,128)(2,1)} %get-tuple-element.134), channel_id=1, source_target_pairs={{0,8},{4,12},{8,0},{12,4},{1,9},{5,13},{9,1},{13,5},{2,10},{6,14},... | collective-permute-start | bytes 1966088 | tf_op jit(solution)/shard_map/ppermute | solution.py:44
  168.3 82.8 %collective-permute-start.35 = (bf16[128,2560]{1,0:T(8,128)(2,1)}, bf16[128,2560]{1,0:T(8,128)(2,1)S(1)}, u32[]{:S(2)}, u32[]{:S(2)}) collective-permute-start(bf16[128,2560]{1,0:T(8,128)(2,1)} %get-tuple-element.134), channel_id=1, source_target_pairs={{4,8},{8,4},{5,9},{9,5},{6,10},{10,6},{7,11},{11,7},{20,24},{24,20... | collective-permute-start | bytes 1966088 | tf_op jit(solution)/shard_map/ppermute | solution.py:872
  177.1 17.1 %collective-permute-start.18 = (bf16[64,2560]{1,0:T(8,128)(2,1)S(1)}, bf16[64,2560]{1,0:T(8,128)(2,1)S(1)}, u32[]{:S(2)}, u32[]{:S(2)}) collective-permute-start(bf16[64,2560]{1,0:T(8,128)(2,1)S(1)} %get-tuple-element.208), channel_id=1, source_target_pairs={{0,1},{1,0},{2,3},{3,2},{4,5},{5,4},{6,7},{7,6},{8,9},{9,8},{10,11... | collective-permute-start | bytes 983048 | tf_op jit(solution)/shard_map/ppermute | solution.py:44
  177.2 17.1 %collective-permute-start.16 = (bf16[64,2560]{1,0:T(8,128)(2,1)S(1)}, bf16[64,2560]{1,0:T(8,128)(2,1)S(1)}, u32[]{:S(2)}, u32[]{:S(2)}) collective-permute-start(bf16[64,2560]{1,0:T(8,128)(2,1)S(1)} %get-tuple-element.210), channel_id=1, source_target_pairs={{0,2},{1,3},{2,0},{3,1},{4,6},{5,7},{6,4},{7,5},{8,10},{9,11},{10,... | collective-permute-start | bytes 983048 | tf_op jit(solution)/shard_map/ppermute | solution.py:44
  194.6 28.1 %collective-permute-start.17 = (bf16[128,2560]{1,0:T(8,128)(2,1)S(1)}, bf16[128,2560]{1,0:T(8,128)(2,1)S(1)}, u32[]{:S(2)}, u32[]{:S(2)}) collective-permute-start(bf16[128,2560]{1,0:T(8,128)(2,1)S(1)} %pad_maximum_fusion.6), channel_id=1, source_target_pairs={{0,1},{1,0},{2,3},{3,2},{4,5},{5,4},{6,7},{7,6},{8,9},{9,8},{10,11... | collective-permute-start | bytes 1966088 | tf_op jit(solution)/shard_map/ppermute | solution.py:44
  196.5 26.1 %collective-permute-start.19 = (bf16[128,2560]{1,0:T(8,128)(2,1)S(1)}, bf16[128,2560]{1,0:T(8,128)(2,1)S(1)}, u32[]{:S(2)}, u32[]{:S(2)}) collective-permute-start(bf16[128,2560]{1,0:T(8,128)(2,1)S(1)} %pad_maximum_fusion.7), channel_id=1, source_target_pairs={{0,2},{1,3},{2,0},{3,1},{4,6},{5,7},{6,4},{7,5},{8,10},{9,11},{10,... | collective-permute-start | bytes 1966088 | tf_op jit(solution)/shard_map/ppermute | solution.py:44
  224.7 26.2 %collective-permute-start.24 = (bf16[128,2560]{1,0:T(8,128)(2,1)}, bf16[128,2560]{1,0:T(8,128)(2,1)S(1)}, u32[]{:S(2)}, u32[]{:S(2)}) collective-permute-start(bf16[128,2560]{1,0:T(8,128)(2,1)} %get-tuple-element.135), channel_id=1, source_target_pairs={{0,4},{4,0},{8,12},{12,8},{1,5},{5,1},{9,13},{13,9},{2,6},{6,2},{1... | collective-permute-start | bytes 1966088 | tf_op jit(solution)/shard_map/ppermute | solution.py:44
  225.3 44.3 %collective-permute-start.26 = (bf16[256,2560]{1,0:T(8,128)(2,1)S(1)}, bf16[256,2560]{1,0:T(8,128)(2,1)}, u32[]{:S(2)}, u32[]{:S(2)}) collective-permute-start(bf16[256,2560]{1,0:T(8,128)(2,1)S(1)} %constant_dynamic-update-slice_fusion.2.gm_own.refs_0_), channel_id=1, source_target_pairs={{0,16},{16,0},{1,17},{17,1},{2,18},{18,2},{3,19},{19,3},{4,20},{20... | collective-permute-start | bytes 3932168 | tf_op jit(solution)/shard_map/ppermute | solution.py:44
  225.4 43.3 %collective-permute-start.34 = (bf16[128,2560]{1,0:T(8,128)(2,1)S(1)}, bf16[128,2560]{1,0:T(8,128)(2,1)S(1)}, u32[]{:S(2)}, u32[]{:S(2)}) collective-permute-start(bf16[128,2560]{1,0:T(8,128)(2,1)S(1)} %collective-permute-done.33), channel_id=1, source_target_pairs={{4,0},{8,12},{5,1},{9,13},{6,2},{10,14},{7,3},{11,15},{20,16},{24,... | collective-permute-start | bytes 1966088 | tf_op jit(solution)/shard_map/ppermute | solution.py:873
  228.9 29.8 %collective-permute-start.29 = (bf16[128,2560]{1,0:T(8,128)(2,1)}, bf16[128,2560]{1,0:T(8,128)(2,1)}, u32[]{:S(2)}, u32[]{:S(2)}) collective-permute-start(bf16[128,2560]{1,0:T(8,128)(2,1)} %get-tuple-element.135), channel_id=1, source_target_pairs={{0,8},{4,12},{8,0},{12,4},{1,9},{5,13},{9,1},{13,5},{2,10},{6,14},... | collective-permute-start | bytes 1966088 | tf_op jit(solution)/shard_map/ppermute | solution.py:44
  251.0 18.7 %collective-permute-start.25 = (bf16[256,2560]{1,0:T(8,128)(2,1)S(1)}, bf16[256,2560]{1,0:T(8,128)(2,1)}, u32[]{:S(2)}, u32[]{:S(2)}) collective-permute-start(bf16[256,2560]{1,0:T(8,128)(2,1)S(1)} %constant_dynamic-update-slice_fusion.nm_own.refs_0_), channel_id=1, source_target_pairs={{0,16},{16,0},{1,17},{17,1},{2,18},{18,2},{3,19},{19,3},{4,20},{20... | collective-permute-start | bytes 3932168 | tf_op jit(solution)/shard_map/ppermute | solution.py:44
  251.1 56.4 %collective-permute-start.31 = (bf16[128,2560]{1,0:T(8,128)(2,1)}, bf16[128,2560]{1,0:T(8,128)(2,1)}, u32[]{:S(2)}, u32[]{:S(2)}) collective-permute-start(bf16[128,2560]{1,0:T(8,128)(2,1)} %get-tuple-element.135), channel_id=1, source_target_pairs={{4,8},{8,4},{5,9},{9,5},{6,10},{10,6},{7,11},{11,7},{20,24},{24,20... | collective-permute-start | bytes 1966088 | tf_op jit(solution)/shard_map/ppermute | solution.py:872
  258.7 48.8 %collective-permute-start.30 = (bf16[128,2560]{1,0:T(8,128)(2,1)}, bf16[128,2560]{1,0:T(8,128)(2,1)}, u32[]{:S(2)}, u32[]{:S(2)}) collective-permute-start(bf16[128,2560]{1,0:T(8,128)(2,1)} %collective-permute-done.29), channel_id=1, source_target_pairs={{4,0},{8,12},{5,1},{9,13},{6,2},{10,14},{7,3},{11,15},{20,16},{24,... | collective-permute-start | bytes 1966088 | tf_op jit(solution)/shard_map/ppermute | solution.py:873
  311.1 29.4 %collective-permute-start.39 = (bf16[128,2560]{1,0:T(8,128)(2,1)S(1)}, bf16[128,2560]{1,0:T(8,128)(2,1)S(1)}, u32[]{:S(2)}, u32[]{:S(2)}) collective-permute-start(bf16[128,2560]{1,0:T(8,128)(2,1)S(1)} %get-tuple-element.226), channel_id=1, source_target_pairs={{0,4},{4,0},{8,12},{12,8},{1,5},{5,1},{9,13},{13,9},{2,6},{6,2},{1... | collective-permute-start | bytes 1966088 | tf_op jit(solution)/shard_map/ppermute | solution.py:44
  350.5 337.2 %reduce-scatter.3.cloned.1.call-start = ((), (), s32[]{:S(2)}) async-start(), calls=%async_computation.4 | async-start | bytes 11468800 | tf_op jit(solution)/shard_map/reduce_scatter | solution.py:924
  356.7 18.9 %collective-permute-start.40 = (bf16[128,2560]{1,0:T(8,128)(2,1)S(1)}, bf16[128,2560]{1,0:T(8,128)(2,1)S(1)}, u32[]{:S(2)}, u32[]{:S(2)}) collective-permute-start(bf16[128,2560]{1,0:T(8,128)(2,1)S(1)} %slice.257), channel_id=1, source_target_pairs={{0,4},{12,8},{1,5},{13,9},{2,6},{14,10},{3,7},{15,11},{16,20},{28,... | collective-permute-start | bytes 1966088 | tf_op jit(solution)/shard_map/ppermute | solution.py:879
  358.3 18.8 %collective-permute-start.38 = (bf16[128,2560]{1,0:T(8,128)(2,1)S(1)}, bf16[128,2560]{1,0:T(8,128)(2,1)S(1)}, u32[]{:S(2)}, u32[]{:S(2)}) collective-permute-start(bf16[128,2560]{1,0:T(8,128)(2,1)S(1)} %slice.257), channel_id=1, source_target_pairs={{4,8},{8,4},{5,9},{9,5},{6,10},{10,6},{7,11},{11,7},{20,24},{24,20... | collective-permute-start | bytes 1966088 | tf_op jit(solution)/shard_map/ppermute | solution.py:881
  376.6 28.3 %collective-permute-start.41 = (bf16[128,2560]{1,0:T(8,128)(2,1)}, bf16[128,2560]{1,0:T(8,128)(2,1)}, u32[]{:S(2)}, u32[]{:S(2)}) collective-permute-start(bf16[128,2560]{1,0:T(8,128)(2,1)} %add_convert_fusion.7), channel_id=1, source_target_pairs={{0,8},{4,12},{8,0},{12,4},{1,9},{5,13},{9,1},{13,5},{2,10},{6,14},... | collective-permute-start | bytes 1966088 | tf_op jit(solution)/shard_map/ppermute | solution.py:44
  443.3 39.0 %collective-permute-start.49 = (bf16[128,2560]{1,0:T(8,128)(2,1)}, bf16[128,2560]{1,0:T(8,128)(2,1)S(1)}, u32[]{:S(2)}, u32[]{:S(2)}) collective-permute-start(bf16[128,2560]{1,0:T(8,128)(2,1)} %get-tuple-element.169), channel_id=1, source_target_pairs={{0,4},{12,8},{1,5},{13,9},{2,6},{14,10},{3,7},{15,11},{16,20},{28,... | collective-permute-start | bytes 1966088 | tf_op jit(solution)/shard_map/ppermute | solution.py:879
  476.5 40.8 %collective-permute-start.51 = (bf16[128,2560]{1,0:T(8,128)(2,1)}, bf16[128,2560]{1,0:T(8,128)(2,1)}, u32[]{:S(2)}, u32[]{:S(2)}) collective-permute-start(bf16[128,2560]{1,0:T(8,128)(2,1)} %get-tuple-element.169), channel_id=1, source_target_pairs={{4,8},{8,4},{5,9},{9,5},{6,10},{10,6},{7,11},{11,7},{20,24},{24,20... | collective-permute-start | bytes 1966088 | tf_op jit(solution)/shard_map/ppermute | solution.py:881
  480.6 34.3 %collective-permute-start.47 = (bf16[128,2560]{1,0:T(8,128)(2,1)}, bf16[128,2560]{1,0:T(8,128)(2,1)S(1)}, u32[]{:S(2)}, u32[]{:S(2)}) collective-permute-start(bf16[128,2560]{1,0:T(8,128)(2,1)} %get-tuple-element.165), channel_id=1, source_target_pairs={{0,4},{4,0},{8,12},{12,8},{1,5},{5,1},{9,13},{13,9},{2,6},{6,2},{1... | collective-permute-start | bytes 1966088 | tf_op jit(solution)/shard_map/ppermute | solution.py:44
  483.3 40.1 %collective-permute-start.50 = (bf16[128,2560]{1,0:T(8,128)(2,1)}, bf16[128,2560]{1,0:T(8,128)(2,1)}, u32[]{:S(2)}, u32[]{:S(2)}) collective-permute-start(bf16[128,2560]{1,0:T(8,128)(2,1)} %add_convert_fusion.6), channel_id=1, source_target_pairs={{0,8},{4,12},{8,0},{12,4},{1,9},{5,13},{9,1},{13,5},{2,10},{6,14},... | collective-permute-start | bytes 1966088 | tf_op jit(solution)/shard_map/ppermute | solution.py:44
  496.0 17.4 %collective-permute-start.57 = (bf16[128,1152]{1,0:T(8,128)(2,1)S(1)}, bf16[128,1152]{1,0:T(8,128)(2,1)S(1)}, u32[]{:S(2)}, u32[]{:S(2)}) collective-permute-start(bf16[128,1152]{1,0:T(8,128)(2,1)S(1)} %pad_maximum_fusion.10), channel_id=1, source_target_pairs={{0,2},{1,3},{2,0},{3,1},{4,6},{5,7},{6,4},{7,5},{8,10},{9,11},{10,... | collective-permute-start | bytes 884744 | tf_op jit(solution)/shard_map/ppermute | solution.py:44
  503.5 24.2 %collective-permute-start.79 = (bf16[256,640]{1,0:T(8,128)(2,1)}, bf16[256,640]{1,0:T(8,128)(2,1)}, u32[]{:S(2)}, u32[]{:S(2)}) collective-permute-start(bf16[256,640]{1,0:T(8,128)(2,1)} %get-tuple-element.220), channel_id=1, source_target_pairs={{0,4},{12,8},{1,5},{13,9},{2,6},{14,10},{3,7},{15,11},{16,20},{28,... | collective-permute-start | bytes 983048 | tf_op jit(solution)/shard_map/ppermute | solution.py:879
  514.3 21.3 %collective-permute-start.68 = (bf16[128,1152]{1,0:T(8,128)(2,1)S(1)}, bf16[128,1152]{1,0:T(8,128)(2,1)S(1)}, u32[]{:S(2)}, u32[]{:S(2)}) collective-permute-start(bf16[128,1152]{1,0:T(8,128)(2,1)S(1)} %get-tuple-element.191.lat), channel_id=1, source_target_pairs={{0,1},{1,0},{2,3},{3,2},{4,5},{5,4},{6,7},{7,6},{8,9},{9,8},{10,11... | collective-permute-start | bytes 884744 | tf_op jit(solution)/shard_map/ppermute | solution.py:44
  515.7 22.1 %collective-permute-start.69 = (bf16[128,1152]{1,0:T(8,128)(2,1)S(1)}, bf16[128,1152]{1,0:T(8,128)(2,1)S(1)}, u32[]{:S(2)}, u32[]{:S(2)}) collective-permute-start(bf16[128,1152]{1,0:T(8,128)(2,1)S(1)} %get-tuple-element.191.lat), channel_id=1, source_target_pairs={{0,2},{1,3},{2,0},{3,1},{4,6},{5,7},{6,4},{7,5},{8,10},{9,11},{10,... | collective-permute-start | bytes 884744 | tf_op jit(solution)/shard_map/ppermute | solution.py:44
  517.3 47.2 %collective-permute-start.66 = (bf16[128,640]{1,0:T(8,128)(2,1)}, bf16[128,640]{1,0:T(8,128)(2,1)S(1)}, u32[]{:S(2)}, u32[]{:S(2)}) collective-permute-start(bf16[128,640]{1,0:T(8,128)(2,1)} %get-tuple-element.190), channel_id=1, source_target_pairs={{0,3},{1,2},{2,1},{3,0},{4,7},{5,6},{6,5},{7,4},{8,11},{9,10},{10,... | collective-permute-start | bytes 491528 | tf_op jit(solution)/shard_map/ppermute | solution.py:44
  527.6 46.4 %collective-permute-start.52 = (bf16[128,2560]{1,0:T(8,128)(2,1)S(1)}, bf16[128,2560]{1,0:T(8,128)(2,1)S(1)}, u32[]{:S(2)}, u32[]{:S(2)}) collective-permute-start(bf16[128,2560]{1,0:T(8,128)(2,1)S(1)} %shard_map.307.own), channel_id=1, source_target_pairs={{0,16},{16,0},{1,17},{17,1},{2,18},{18,2},{3,19},{19,3},{4,20},{20... | collective-permute-start | bytes 1966088 | tf_op jit(solution)/shard_map/ppermute | solution.py:44
  527.7 19.5 %collective-permute-start.81 = (bf16[256,640]{1,0:T(8,128)(2,1)}, bf16[256,640]{1,0:T(8,128)(2,1)S(1)}, u32[]{:S(2)}, u32[]{:S(2)}) collective-permute-start(bf16[256,640]{1,0:T(8,128)(2,1)} %get-tuple-element.220), channel_id=1, source_target_pairs={{4,8},{8,4},{5,9},{9,5},{6,10},{10,6},{7,11},{11,7},{20,24},{24,20... | collective-permute-start | bytes 983048 | tf_op jit(solution)/shard_map/ppermute | solution.py:881
  543.7 16.6 %collective-permute-start.80 = (bf16[256,640]{1,0:T(8,128)(2,1)S(1)}, bf16[256,640]{1,0:T(8,128)(2,1)S(1)}, u32[]{:S(2)}, u32[]{:S(2)}) collective-permute-start(bf16[256,640]{1,0:T(8,128)(2,1)S(1)} %fusion.2), channel_id=1, source_target_pairs={{0,8},{4,12},{8,0},{12,4},{1,9},{5,13},{9,1},{13,5},{2,10},{6,14},... | collective-permute-start | bytes 983048 | tf_op jit(solution)/shard_map/ppermute | solution.py:44
  556.8 38.3 %collective-permute-start.72 = (bf16[4,128,1152]{2,1,0:T(8,128)(2,1)S(1)}, bf16[4,128,1152]{2,1,0:T(8,128)(2,1)}, u32[]{:S(2)}, u32[]{:S(2)}) collective-permute-start(bf16[4,128,1152]{2,1,0:T(8,128)(2,1)S(1)} %pad_maximum_fusion.5.gown), channel_id=1, source_target_pairs={{0,16},{16,0},{1,17},{17,1},{2,18},{18,2},{3,19},{19,3},{4,20},{20... | collective-permute-start | bytes 3538952 | tf_op jit(solution)/shard_map/ppermute | solution.py:44
  573.7 20.8 %collective-permute-start.67 = (bf16[4,128,640]{2,1,0:T(8,128)(2,1)}, bf16[4,128,640]{2,1,0:T(8,128)(2,1)}, u32[]{:S(2)}, u32[]{:S(2)}) collective-permute-start(bf16[4,128,640]{2,1,0:T(8,128)(2,1)} %pad_maximum_fusion.8.own), channel_id=1, source_target_pairs={{0,16},{16,0},{1,17},{17,1},{2,18},{18,2},{3,19},{19,3},{4,20},{20... | collective-permute-start | bytes 1966088 | tf_op jit(solution)/shard_map/ppermute | solution.py:44
  581.5 26.4 %collective-permute-start.91 = (bf16[4,160,320]{2,1,0:T(8,128)(2,1)}, bf16[4,160,320]{2,1,0:T(8,128)(2,1)}, u32[]{:S(2)}, u32[]{:S(2)}) collective-permute-start(bf16[4,160,320]{2,1,0:T(8,128)(2,1)} %get-tuple-element.217), channel_id=1, source_target_pairs={{0,4},{12,8},{1,5},{13,9},{2,6},{14,10},{3,7},{15,11},{16,20},{28,... | collective-permute-start | bytes 1228808 | tf_op jit(solution)/shard_map/ppermute | solution.py:879
  586.6 18.3 %collective-permute-start.82 = (bf16[256,640]{1,0:T(8,128)(2,1)S(1)}, bf16[256,640]{1,0:T(8,128)(2,1)}, u32[]{:S(2)}, u32[]{:S(2)}) collective-permute-start(bf16[256,640]{1,0:T(8,128)(2,1)S(1)} %add_convert_fusion.9), channel_id=1, source_target_pairs={{0,4},{4,0},{8,12},{12,8},{1,5},{5,1},{9,13},{13,9},{2,6},{6,2},{1... | collective-permute-start | bytes 983048 | tf_op jit(solution)/shard_map/ppermute | solution.py:44
  590.9 25.5 %collective-permute-start.93 = (bf16[4,160,320]{2,1,0:T(8,128)(2,1)}, bf16[4,160,320]{2,1,0:T(8,128)(2,1)}, u32[]{:S(2)}, u32[]{:S(2)}) collective-permute-start(bf16[4,160,320]{2,1,0:T(8,128)(2,1)} %get-tuple-element.217), channel_id=1, source_target_pairs={{4,8},{8,4},{5,9},{9,5},{6,10},{10,6},{7,11},{11,7},{20,24},{24,20... | collective-permute-start | bytes 1228808 | tf_op jit(solution)/shard_map/ppermute | solution.py:881
  594.5 37.8 %collective-permute-start.90 = (bf16[4,160,320]{2,1,0:T(8,128)(2,1)}, bf16[4,160,320]{2,1,0:T(8,128)(2,1)}, u32[]{:S(2)}, u32[]{:S(2)}) collective-permute-start(bf16[4,160,320]{2,1,0:T(8,128)(2,1)} %get-tuple-element.218), channel_id=1, source_target_pairs={{0,4},{4,0},{8,12},{12,8},{1,5},{5,1},{9,13},{13,9},{2,6},{6,2},{1... | collective-permute-start | bytes 1228808 | tf_op jit(solution)/shard_map/ppermute | solution.py:44
  595.1 20.5 %collective-permute-start.63 = (f32[48,128]{1,0:T(8,128)S(1)}, f32[48,128]{1,0:T(8,128)S(1)}, u32[]{:S(2)}, u32[]{:S(2)}) collective-permute-start(f32[48,128]{1,0:T(8,128)S(1)} %add.160), channel_id=1, source_target_pairs={{0,8},{4,12},{8,0},{12,4},{1,9},{5,13},{9,1},{13,5},{2,10},{6,14},... | collective-permute-start | bytes 73736 | tf_op jit(solution)/shard_map/ppermute | solution.py:44
  606.1 31.9 %collective-permute-start.86 = (bf16[1024,640]{1,0:T(8,128)(2,1)S(1)}, bf16[1024,640]{1,0:T(8,128)(2,1)}, u32[]{:S(2)}, u32[]{:S(2)}) collective-permute-start(bf16[1024,640]{1,0:T(8,128)(2,1)S(1)} %bitcast.168), channel_id=1, source_target_pairs={{0,1},{1,0},{2,3},{3,2},{4,5},{5,4},{6,7},{7,6},{8,9},{9,8},{10,11... | collective-permute-start | bytes 3932168 | tf_op jit(solution)/shard_map/ppermute | solution.py:44
  607.9 30.2 %collective-permute-start.87 = (bf16[1024,640]{1,0:T(8,128)(2,1)S(1)}, bf16[1024,640]{1,0:T(8,128)(2,1)}, u32[]{:S(2)}, u32[]{:S(2)}) collective-permute-start(bf16[1024,640]{1,0:T(8,128)(2,1)S(1)} %bitcast.169), channel_id=1, source_target_pairs={{0,2},{1,3},{2,0},{3,1},{4,6},{5,7},{6,4},{7,5},{8,10},{9,11},{10,... | collective-permute-start | bytes 3932168 | tf_op jit(solution)/shard_map/ppermute | solution.py:44
  615.6 19.4 %collective-permute-start.92 = (bf16[4,160,320]{2,1,0:T(8,128)(2,1)}, bf16[4,160,320]{2,1,0:T(8,128)(2,1)}, u32[]{:S(2)}, u32[]{:S(2)}) collective-permute-start(bf16[4,160,320]{2,1,0:T(8,128)(2,1)} %fusion), channel_id=1, source_target_pairs={{0,8},{4,12},{8,0},{12,4},{1,9},{5,13},{9,1},{13,5},{2,10},{6,14},... | collective-permute-start | bytes 1228808 | tf_op jit(solution)/shard_map/ppermute | solution.py:44
  638.1 26.1 %collective-permute-start.75 = (bf16[160,640]{1,0:T(8,128)(2,1)S(1)}, bf16[160,640]{1,0:T(8,128)(2,1)S(1)}, u32[]{:S(2)}, u32[]{:S(2)}) collective-permute-start(bf16[160,640]{1,0:T(8,128)(2,1)S(1)} %fusion.6), channel_id=1, source_target_pairs={{0,8},{4,12},{8,0},{12,4},{1,9},{5,13},{9,1},{13,5},{2,10},{6,14},... | collective-permute-start | bytes 614408 | tf_op jit(solution)/shard_map/ppermute | solution.py:44
  646.3 24.1 %collective-permute-start.101 = (bf16[1,160,800]{2,1,0:T(8,128)(2,1)S(1)}, bf16[1,160,800]{2,1,0:T(8,128)(2,1)S(1)}, u32[]{:S(2)}, u32[]{:S(2)}) collective-permute-start(bf16[1,160,800]{2,1,0:T(8,128)(2,1)S(1)} %get-tuple-element.235), channel_id=1, source_target_pairs={{0,8},{4,12},{8,0},{12,4},{1,9},{5,13},{9,1},{13,5},{2,10},{6,14},... | collective-permute-start | bytes 768008 | tf_op jit(solution)/shard_map/ppermute | solution.py:44
  646.6 30.8 %collective-permute-start.102 = (bf16[1,160,800]{2,1,0:T(8,128)(2,1)S(1)}, bf16[1,160,800]{2,1,0:T(8,128)(2,1)S(1)}, u32[]{:S(2)}, u32[]{:S(2)}) collective-permute-start(bf16[1,160,800]{2,1,0:T(8,128)(2,1)S(1)} %get-tuple-element.234), channel_id=1, source_target_pairs={{0,12},{4,8},{8,4},{12,0},{1,13},{5,9},{9,5},{13,1},{2,14},{6,10},... | collective-permute-start | bytes 768008 | tf_op jit(solution)/shard_map/ppermute | solution.py:44
  648.4 44.7 %collective-permute-start.89 = (bf16[512,640]{1,0:T(8,128)(2,1)}, bf16[512,640]{1,0:T(8,128)(2,1)}, u32[]{:S(2)}, u32[]{:S(2)}) collective-permute-start(bf16[512,640]{1,0:T(8,128)(2,1)} %slice.279), channel_id=1, source_target_pairs={{0,2},{1,3},{2,0},{3,1},{4,6},{5,7},{6,4},{7,5},{8,10},{9,11},{10,... | collective-permute-start | bytes 1966088 | tf_op jit(solution)/shard_map/ppermute | solution.py:44
  650.2 42.9 %collective-permute-start.88 = (bf16[512,640]{1,0:T(8,128)(2,1)}, bf16[512,640]{1,0:T(8,128)(2,1)}, u32[]{:S(2)}, u32[]{:S(2)}) collective-permute-start(bf16[512,640]{1,0:T(8,128)(2,1)} %slice.278), channel_id=1, source_target_pairs={{0,1},{1,0},{2,3},{3,2},{4,5},{5,4},{6,7},{7,6},{8,9},{9,8},{10,11... | collective-permute-start | bytes 1966088 | tf_op jit(solution)/shard_map/ppermute | solution.py:44
  689.5 24.8 %collective-permute-start.97 = (bf16[2,160,800]{2,1,0:T(8,128)(2,1)S(1)}, bf16[2,160,800]{2,1,0:T(8,128)(2,1)S(1)}, u32[]{:S(2)}, u32[]{:S(2)}) collective-permute-start(bf16[2,160,800]{2,1,0:T(8,128)(2,1)S(1)} %get-tuple-element.214), channel_id=1, source_target_pairs={{0,4},{4,0},{8,12},{12,8},{1,5},{5,1},{9,13},{13,9},{2,6},{6,2},{1... | collective-permute-start | bytes 1536008 | tf_op jit(solution)/shard_map/ppermute | solution.py:44
  689.6 40.4 %collective-permute-start.98 = (bf16[2,160,800]{2,1,0:T(8,128)(2,1)S(1)}, bf16[2,160,800]{2,1,0:T(8,128)(2,1)S(1)}, u32[]{:S(2)}, u32[]{:S(2)}) collective-permute-start(bf16[2,160,800]{2,1,0:T(8,128)(2,1)S(1)} %get-tuple-element.213), channel_id=1, source_target_pairs={{0,8},{4,12},{8,0},{12,4},{1,9},{5,13},{9,1},{13,5},{2,10},{6,14},... | collective-permute-start | bytes 1536008 | tf_op jit(solution)/shard_map/ppermute | solution.py:44
  692.0 51.1 %collective-permute-start.99 = (bf16[2,160,800]{2,1,0:T(8,128)(2,1)S(1)}, bf16[2,160,800]{2,1,0:T(8,128)(2,1)S(1)}, u32[]{:S(2)}, u32[]{:S(2)}) collective-permute-start(bf16[2,160,800]{2,1,0:T(8,128)(2,1)S(1)} %get-tuple-element.212), channel_id=1, source_target_pairs={{0,12},{4,8},{8,4},{12,0},{1,13},{5,9},{9,5},{13,1},{2,14},{6,10},... | collective-permute-start | bytes 1536008 | tf_op jit(solution)/shard_map/ppermute | solution.py:44
  (161 other events, 1797.5 us)
Sparse Core Ops, SparseCore 0:
  51.0 59.0 all-gather.4
  163.8 115.9 all-gather.2
  350.6 55.8 reduce-scatter.4
  433.6 108.2 reduce-scatter.2

commit v3 on v2

--- a/solution.py
+++ b/solution.py
@@ -438,20 +438,22 @@
 
 
 def out_kernel(own, oth, weight, keep, give):
-    half = own.shape[1]
-    both = jnp.concatenate([own[0], oth[0]], axis=0)
+    per, half, _ = own.shape
+    both = jnp.concatenate([ref[i] for ref in (own, oth) for i in range(per)], axis=0)
     result = dot(both, weight[...], NT)
-    keep[0] = result[:half]
-    give[0] = result[half:].astype(bf16)
+    for i in range(per):
+        keep[i] = result[i * half : (i + 1) * half]
+        give[i] = result[(per + i) * half : (per + i + 1) * half].astype(bf16)
 
 
 def project_out(own, oth, weight):
     nc, half, deep = own.shape
     width = weight.shape[0]
-    piece = lambda w: pl.BlockSpec((1, half, w), lambda k: (k, 0, 0))
+    per = math.gcd(nc, 2)
+    piece = lambda w: pl.BlockSpec((per, half, w), lambda k: (k, 0, 0))
     return pl.pallas_call(
         out_kernel,
-        grid=(nc,),
+        grid=(nc // per,),
         in_specs=[piece(deep)] * 2 + [pl.BlockSpec(weight.shape, lambda k: (0, 0))],
         out_specs=[piece(width)] * 2,
         out_shape=[
@@ -464,20 +466,22 @@
 
 
 def heads_kernel(own, oth, weight, gown, goth):
-    half = own.shape[1]
-    both = jnp.concatenate([own[0], oth[0]], axis=0)
+    per, half, _ = own.shape
+    both = jnp.concatenate([ref[i] for ref in (own, oth) for i in range(per)], axis=0)
     result = dot(both, weight[...], NN).astype(bf16)
-    gown[0] = result[:half]
-    goth[0] = result[half:]
+    for i in range(per):
+        gown[i] = result[i * half : (i + 1) * half]
+        goth[i] = result[(per + i) * half : (per + i + 1) * half]
 
 
 def project_heads(own, oth, weight):
     nc, half, width = own.shape
     deep = weight.shape[1]
-    piece = lambda w: pl.BlockSpec((1, half, w), lambda k: (k, 0, 0))
+    per = math.gcd(nc, 2)
+    piece = lambda w: pl.BlockSpec((per, half, w), lambda k: (k, 0, 0))
     return pl.pallas_call(
         heads_kernel,
-        grid=(nc,),
+        grid=(nc // per,),
         in_specs=[piece(width)] * 2 + [pl.BlockSpec(weight.shape, lambda k: (0, 0))],
         out_specs=[piece(deep)] * 2,
         out_shape=[jax.ShapeDtypeStruct((nc, half, deep), bf16)] * 2,
@@ -501,7 +505,7 @@
 
 
 def mlp_kernel(
-    own_steps, nm_own, nm_oth, gm_own, gm_oth, pair_hbm, down_hbm,
+    nm_own, nm_oth, gm_own, gm_oth, pair_hbm, down_hbm,
     hid_ref, gg_ref, gu_ref, gn_own, gn_oth, ml_own, ml_oth, w_gate, w_up, w_down, sems
 ):
     step = pl.program_id(0)
@@ -533,60 +537,53 @@
             for copy in group:
                 copy.start()
 
-    mine = step < own_steps
-    normed = jnp.where(mine, nm_own[...], nm_oth[...])
+    block = nm_own.shape[0]
+    normed = jnp.concatenate([nm_own[...], nm_oth[...]], axis=0)
     ready(0)
     gate = dot(normed, w_gate[...], NN)
     ready(1)
     up_proj = dot(normed, w_up[...], NN)
     ready(2)
-    grad_hidden = dot(jnp.where(mine, gm_own[...], gm_oth[...]), w_down[...], NN)
+    grad_hidden = dot(jnp.concatenate([gm_own[...], gm_oth[...]], axis=0), w_down[...], NN)
     sigma = jax.nn.sigmoid(gate)
     silu_gate = gate * sigma
     hidden = (silu_gate * up_proj).astype(bf16)
     grad_gate = (grad_hidden * up_proj * sigma * (1.0 + gate * (1.0 - sigma))).astype(bf16)
     grad_up = (grad_hidden * silu_gate).astype(bf16)
-    hid_ref[...] = hidden
-    gg_ref[...] = grad_gate
-    gu_ref[...] = grad_up
+    for target, value in ((hid_ref, hidden), (gg_ref, grad_gate), (gu_ref, grad_up)):
+        target[0] = value[:block]
+        target[1] = value[block:]
+    mlp = dot(hidden, w_down[...], NT).astype(bf16)
+    ml_own[...] = mlp[:block]
+    ml_oth[...] = mlp[block:]
     grad_normed = (dot(grad_gate, w_gate[...], NT) + dot(grad_up, w_up[...], NT)).astype(bf16)
-    mlp = dot(hidden, w_down[...], NT).astype(bf16)
-
-    @pl.when(mine)
-    def _():
-        gn_own[...] = grad_normed
-        ml_own[...] = mlp
-
-    @pl.when(jnp.logical_not(mine))
-    def _():
-        gn_oth[...] = grad_normed
-        ml_oth[...] = mlp
+    gn_own[...] = grad_normed[:block]
+    gn_oth[...] = grad_normed[block:]
 
 
 def feed_forward(blocks, nm_own, nm_oth, gm_own, gm_oth, pair, down):
     rows, width = nm_own.shape
     ff = down.shape[1]
     block = min(rows, 256)
-    steps = rows // block
-    own = pl.BlockSpec((block, width), lambda i: (jnp.minimum(i, steps - 1), 0))
-    oth = pl.BlockSpec((block, width), lambda i: (jnp.maximum(i - steps, 0), 0))
-    inner = pl.BlockSpec((block, ff), lambda i: (i, 0))
+    part_of = pl.BlockSpec((block, width), lambda i: (i, 0))
+    inner = pl.BlockSpec((2, block, ff), lambda i: (0, i, 0))
     anywhere = pl.BlockSpec(memory_space=pl.ANY)
-    held = jax.ShapeDtypeStruct((2 * rows, ff), bf16)
+    held = jax.ShapeDtypeStruct((2, rows, ff), bf16)
     part = jax.ShapeDtypeStruct((rows, width), bf16)
-    return pl.pallas_call(
-        functools.partial(mlp_kernel, steps),
-        grid=(2 * steps,),
-        in_specs=[own, oth, own, oth] + [anywhere] * 2,
-        out_specs=[inner] * 3 + [own, oth, own, oth],
+    made = pl.pallas_call(
+        mlp_kernel,
+        grid=(rows // block,),
+        in_specs=[part_of] * 4 + [anywhere] * 2,
+        out_specs=[inner] * 3 + [part_of] * 4,
         out_shape=[held] * 3 + [part] * 4,
         scratch_shapes=[pltpu.VMEM((width, ff), bf16)] * 3
         + [pltpu.SemaphoreType.DMA((3, blocks))],
-        compiler_params=grid_params(56),
+        compiler_params=grid_params(60),
         cost_estimate=cost(
             24 * rows * width * ff, 6 * width * ff + 16 * rows * width, 2 * rows * ff
         ),
     )(nm_own, nm_oth, gm_own, gm_oth, pair, down)
+    return [a.reshape(2 * rows, ff) for a in made[:3]] + list(made[3:])
 
 
 def product_kernel(count, targets, *refs):

time: 764 us -> 756 us (0.990)
  starting transfers between devices: 135 us -> 148 us
  waiting for transfers between devices: 302 us -> 289 us
    ppermute x85, waiting for transfers between devices: 245 us -> 230 us  [exchange(): return lax.ppermute(value, axis, [(i, i ^ step) for i in range(size)])]
    ppermute x85, starting transfers between devices: 80.8 us -> 92.1 us  [exchange(): return lax.ppermute(value, axis, [(i, i ^ step) for i in range(size)])]
    unnamed x238 -> x230, local copies, waits for them, and re-layouts: 32.6 us -> 28.9 us
  transfers between devices with their start and end apart: 107 -> 107, of which waited for: 44 -> 45; matrix products, arithmetic and copies ran while one was open for 9% -> 9% of each run, Pallas kernels for 25% -> 25%
where the time goes in v3:
time: 756 us; the launch traced here: 746 us
  waiting for transfers between devices  289 us (38%)
  Pallas kernels  199 us (26%)
  starting transfers between devices  148 us (20%)
  local copies, waits for them, and re-layouts  50.9 us (7%)
  other arithmetic  37.3 us (5%)
  between operations  16 us (2%)
    ppermute x85, waiting for transfers between devices, exchange(): return lax.ppermute(value, axis, [(i, i ^ step) for i in range(size)])  230 us
    ppermute x85, starting transfers between devices, exchange(): return lax.ppermute(value, axis, [(i, i ^ step) for i in range(size)])  92.1 us
    pallas_call x22, Pallas kernels, plain(): pl.pallas_call(kernel, in_specs=[SCALARS] + [LOCAL] * len(operands), out_...  54.2 us
    pallas_call x2, Pallas kernels, feed_forward(): pl.pallas_call(mlp_kernel, grid=(rows // block,), in_specs=[part_of] * 4...  47.8 us
    unnamed x230, local copies, waits for them, and re-layouts  28.9 us
    ppermute x5, waiting for transfers between devices, scatter_dp(): far = lax.ppermute(parts[3], 'dp', [(0, 1), (3, 2)])  27.7 us
    pallas_call x2, Pallas kernels, products(): pl.pallas_call(functools.partial(product_kernel, len(lefts), count), grid...  23.1 us
    pallas_call x1, Pallas kernels, attend(): pl.pallas_call(functools.partial(forward_kernel, nt), grid_spec=pltpu.Pre...  21.4 us
  transfers between devices with their start and end apart: 107, of which 45 were waited for; matrix products, arithmetic and copies ran while one was open for 9% of the time, Pallas kernels for 25%

profile of v3, /device:TPU:12, one launch (start us, length us, event | category | flops | bytes accessed | tf_op | source)
XLA Modules:
  0.0 745.6 jit_solution(4019097554692534746)
XLA Ops:
  24.5 3.9 fusion.18
  28.7 3.9 convolution_convert_fusion.wq_ref.wq
  41.5 5.6 shard_map.290
  54.3 3.7 collective-permute-done.7
  63.2 5.3 collective-permute-done.9
  70.6 3.6 collective-permute-start.12
  76.1 18.6 %collective-permute-done.12.refs_2_ = bf16[4,160,320]{2,1,0:T(8,128)(2,1)S(1)} collective-permute-done((bf16[4,160,320]{2,1,0:T(8,128)(2,1)S(1)}, bf16[4,160,320]{2,1,0:T(8,128)(2,1)S(1)}, u32[]{:S(2)}, u32[]{:S(2)}) %collective-permute-start.12) | collective-permute-done | bytes 409632 | tf_op jit(solution)/shard_map/ppermute | solution.py:44
  94.7 5.5 collective-permute-start.13
  100.2 2.8 shard_map.298
  107.7 14.7 %collective-permute-done.13 = bf16[4,160,320]{2,1,0:T(8,128)(2,1)} collective-permute-done((bf16[4,160,320]{2,1,0:T(8,128)(2,1)S(1)}, bf16[4,160,320]{2,1,0:T(8,128)(2,1)}, u32[]{:S(2)}, u32[]{:S(2)}) %collective-permute-start.13) | collective-permute-done | bytes 409632 | tf_op jit(solution)/shard_map/ppermute | solution.py:870
  125.6 21.4 %shard_map.294 = (bf16[4,128,640]{2,1,0:T(8,128)(2,1)S(1)}, bf16[4,128,640]{2,1,0:T(8,128)(2,1)S(1)}, bf16[1024,640]{1,0:T(8,128)(2,1)}, bf16[1024,640]{1,0:T(8,...) custom-call(s32[3]{0:T(128)S(1)} %pad_add_fusion.ids, ...), custom_call_target="tpu_custom_call" | custom-call | flops 671088640 | bytes 1048576 | tf_op jit(solution)/shard_map/pallas_call | solution.py:336
  151.1 7.9 %shard_map.296 = (f32[4,128,2560]{2,1,0:T(8,128)}, bf16[4,128,2560]{2,1,0:T(8,128)(2,1)S(1)}) custom-call(bf16[4,128,640]{2,1,0:T(8,128)(2,1)S(1)} %get-tuple-element.122.own.oown_ref.oown, bf16[4,128,640]{2,1,0:T(8,128)(2,1)S(1)} %get-tuple-element.123.oth.ooth_ref.ooth, bf16[2560,640]{1,0:T(8,128)(2,1)} %bitcast.166), custom_call_target="tpu_custom_call" | custom-call | flops 335544320 | bytes 2424832 | tf_op jit(solution)/shard_map/pallas_call | solution.py:454
  160.5 3.2 shard_map.299
  164.5 3.7 collective-permute-start.23
  168.3 3.3 collective-permute-start.35
  171.7 5.4 add_convert_fusion
  179.6 14.7 %collective-permute-done.18 = bf16[64,2560]{1,0:T(8,128)(2,1)S(1)} collective-permute-done((bf16[64,2560]{1,0:T(8,128)(2,1)S(1)}, bf16[64,2560]{1,0:T(8,128)(2,1)S(1)}, u32[]{:S(2)}, u32[]{:S(2)}) %collective-permute-start.18) | collective-permute-done | bytes 327712 | tf_op jit(solution)/shard_map/ppermute | solution.py:44
  197.0 25.7 %collective-permute-done.17.refs_1_ = bf16[128,2560]{1,0:T(8,128)(2,1)S(1)} collective-permute-done((bf16[128,2560]{1,0:T(8,128)(2,1)S(1)}, bf16[128,2560]{1,0:T(8,128)(2,1)S(1)}, u32[]{:S(2)}, u32[]{:S(2)}) %collective-permute-start.17) | collective-permute-done | bytes 655392 | tf_op jit(solution)/shard_map/ppermute | solution.py:44
  225.5 3.4 collective-permute-start.34
  230.6 20.4 %collective-permute-done.24 = bf16[128,2560]{1,0:T(8,128)(2,1)S(1)} collective-permute-done((bf16[128,2560]{1,0:T(8,128)(2,1)}, bf16[128,2560]{1,0:T(8,128)(2,1)S(1)}, u32[]{:S(2)}, u32[]{:S(2)}) %collective-permute-start.24) | collective-permute-done | bytes 655392 | tf_op jit(solution)/shard_map/ppermute | solution.py:44
  251.2 4.2 collective-permute-start.31
  255.3 3.4 collective-permute-done.29
  258.7 6.1 collective-permute-start.30
  264.9 3.9 collective-permute-done.34
  269.8 10.1 %all-gather.3.cloned.1.call-done.pair_hbm = bf16[5120,800]{1,0:T(8,128)(2,1)} async-done(((bf16[1280,800]{1,0:T(8,128)(2,1)}), bf16[5120,800]{1,0:T(8,128)(2,1)}) %all-gather.3.cloned.1.call-update) | async-done | bytes 8192016 | tf_op jit(solution)/shard_map/all_gather | solution.py:918
  279.8 23.7 %shard_map.301 = (bf16[2,256,800]{2,1,0:T(8,128)(2,1)}, bf16[2,256,800]{2,1,0:T(8,128)(2,1)}, bf16[2,256,800]{2,1,0:T(8,128)(2,1)}, bf16[256,2560]{1,0:T(8,128)(...) custom-call(bf16[256,2560]{1,0:T(8,128)(2,1)} %copy-done.5, ...), custom_call_target="tpu_custom_call" | custom-call | flops 1258291200 | bytes 2277376 | tf_op jit(solution)/shard_map/pallas_call | solution.py:573
  311.0 24.1 %shard_map.302 = (bf16[2,256,800]{2,1,0:T(8,128)(2,1)}, bf16[2,256,800]{2,1,0:T(8,128)(2,1)}, bf16[2,256,800]{2,1,0:T(8,128)(2,1)}, bf16[256,2560]{1,0:T(8,128)(...) custom-call(bf16[256,2560]{1,0:T(8,128)(2,1)} %copy-done.88, ...), custom_call_target="tpu_custom_call" | custom-call | flops 1258291200 | bytes 2277376 | tf_op jit(solution)/shard_map/pallas_call | solution.py:573
  336.4 8.6 %shard_map.321 = bf16[2560,800]{1,0:T(8,128)(2,1)} custom-call(bf16[256,2560]{1,0:T(8,128)(2,1)S(1)} %copy-done.8, bf16[256,2560]{1,0:T(8,128)(2,1)} %collective-permute-done.26.gm_oth.refs_1_, bf16[256,2560]{1,0:T(8,128)(2,1)} %pad_maximum_fusion.3.gm_own.refs_2_, bf16[256,2560]{1,0:T(8,128)(2,1)} %collective-permute-done.36.gm_oth.refs_3_, ...), custom_call_target="tpu_custom_call" | custom-call | flops 419430400 | bytes 933888 | tf_op jit(solution)/shard_map/pallas_call | solution.py:610
  345.2 3.1 collective-permute-done.37
  351.7 3.8 collective-permute-start.38
  355.5 13.5 %collective-permute-done.40 = bf16[128,2560]{1,0:T(8,128)(2,1)S(1)} collective-permute-done((bf16[128,2560]{1,0:T(8,128)(2,1)S(1)}, bf16[128,2560]{1,0:T(8,128)(2,1)S(1)}, u32[]{:S(2)}, u32[]{:S(2)}) %collective-permute-start.40) | collective-permute-done | bytes 655392 | tf_op jit(solution)/shard_map/ppermute | solution.py:876
  371.7 14.5 %shard_map.303 = bf16[5120,800]{1,0:T(8,128)(2,1)} custom-call(bf16[256,2560]{1,0:T(8,128)(2,1)S(1)} %copy-done.6, bf16[256,2560]{1,0:T(8,128)(2,1)} %collective-permute-done.25.nm_oth.refs_1_, bf16[256,2560]{1,0:T(8,128)(2,1)} %copy-done.88, bf16[256,2560]{1,0:T(8,128)(2,1)} %collective-permute-done.32.nm_oth.refs_3_, bf16[512,800]{1,0:T(8,128)(2,1)S(1)} %bitcast.185, ...), custom_call_target="tpu_custom_call" | custom-call | flops 838860800 | bytes 1343488 | tf_op jit(solution)/shard_map/pallas_call | solution.py:610
  386.2 12.4 %collective-permute-done.41.refs_2_ = bf16[128,2560]{1,0:T(8,128)(2,1)} collective-permute-done((bf16[128,2560]{1,0:T(8,128)(2,1)}, bf16[128,2560]{1,0:T(8,128)(2,1)}, u32[]{:S(2)}, u32[]{:S(2)}) %collective-permute-start.41) | collective-permute-done | bytes 655392 | tf_op jit(solution)/shard_map/ppermute | solution.py:44
  399.7 3.2 shard_map.304
  405.0 13.0 %collective-permute-done.42 = bf16[128,2560]{1,0:T(8,128)(2,1)S(1)} collective-permute-done((bf16[128,2560]{1,0:T(8,128)(2,1)S(1)}, bf16[128,2560]{1,0:T(8,128)(2,1)S(1)}, u32[]{:S(2)}, u32[]{:S(2)}) %collective-permute-start.42) | collective-permute-done | bytes 655392 | tf_op jit(solution)/shard_map/ppermute | solution.py:44
  420.8 4.6 collective-permute-done.45
  437.6 6.8 shard_map.305
  444.4 15.9 %shard_map.306 = (bf16[1024,1280]{1,0:T(8,128)(2,1)}, bf16[1024,1280]{1,0:T(8,128)(2,1)}) custom-call(s32[3]{0:T(128)S(1)} %pad_add_fusion.ids, bf16[1024,640]{1,0:T(8,128)(2,1)S(1)} %copy-done.38, bf16[1024,640]{1,0:T(8,128)(2,1)} %get-tuple-element.159.k_ref, bf16[1024,640]{1,0:T(8,128)(2,1)} %get-tuple-element.160.v_ref, ...), custom_call_target="tpu_custom_call" | custom-call | flops 536870912 | bytes 1572864 | tf_op jit(solution)/shard_map/pallas_call | solution.py:371
  460.3 7.7 %shard_map.309 = (f32[4,128,1152]{2,1,0:T(8,128)}, bf16[4,128,1152]{2,1,0:T(8,128)(2,1)S(1)}) custom-call(s32[3]{0:T(128)S(1)} %pad_add_fusion.ids, bf16[1024,1280]{1,0:T(8,128)(2,1)} %get-tuple-element.163.gq, bf16[1024,1280]{1,0:T(8,128)(2,1)} %get-tuple-element.170.gkv, bf16[768,1280]{1,0:T(8,128)(2,1)S(1)} %copy-done.11, bf16[384,1280]{1,0:T(8,128)(2,1)S(1)} %copy-done.4), custom_call_target="tpu_custom_call" | custom-call | flops 301989888 | bytes 1114112 | tf_op jit(solution)/shard_map/pallas_call | solution.py:686
  469.2 5.0 collective-permute-start.51
  479.8 6.8 shard_map.310
  491.9 4.7 collective-permute-done.55.refs_1_
  497.9 7.3 shard_map.311
  512.1 4.8 collective-permute-done.50.refs_2_
  524.6 4.3 shard_map.313
  531.2 4.0 collective-permute-done.71
  540.0 10.4 %collective-permute-done.78 = bf16[256,640]{1,0:T(8,128)(2,1)S(1)} collective-permute-done((bf16[256,640]{1,0:T(8,128)(2,1)S(1)}, bf16[256,640]{1,0:T(8,128)(2,1)S(1)}, u32[]{:S(2)}, u32[]{:S(2)}) %collective-permute-start.78) | collective-permute-done | bytes 327712 | tf_op jit(solution)/shard_map/ppermute | solution.py:44
  552.8 3.0 collective-permute-start.83
  569.1 4.2 collective-permute-start.84
  583.9 2.8 collective-permute-start.93
  589.4 2.9 shard_map.315
  592.4 5.5 collective-permute-done.82
  604.1 3.7 collective-permute-done.63
  610.6 14.1 %collective-permute-done.74 = bf16[160,640]{1,0:T(8,128)(2,1)} collective-permute-done((bf16[160,640]{1,0:T(8,128)(2,1)S(1)}, bf16[160,640]{1,0:T(8,128)(2,1)}, u32[]{:S(2)}, u32[]{:S(2)}) %collective-permute-start.74) | collective-permute-done | bytes 204832 | tf_op jit(solution)/shard_map/ppermute | solution.py:876
  628.1 3.2 collective-permute-start.76
  646.1 11.7 %collective-permute-start.94 = (bf16[1,160,320]{2,1,0:T(8,128)(2,1)S(1)}, bf16[1,160,320]{2,1,0:T(8,128)(2,1)S(1)}, u32[]{:S(2)}, u32[]{:S(2)}) collective-permute-start(bf16[1,160,320]{2,1,0:T(8,128)(2,1)S(1)} %get-tuple-element.244), channel_id=1, source_target_pairs={{0,1},{1,0},{2,3},{3,2},{4,5},{5,4},{6,7},{7,6},{8,9},{9,8},{10,11... | collective-permute-start | bytes 307208 | tf_op jit(solution)/shard_map/ppermute | solution.py:44
  657.9 4.8 collective-permute-done.101.refs_2_
  664.0 6.0 collective-permute-done.102.refs_3_
  686.7 2.9 pad_maximum_fusion.source
  689.6 5.0 shard_map.318
  694.6 12.1 %collective-permute-done.97.refs_1_ = bf16[2,160,800]{2,1,0:T(8,128)(2,1)S(1)} collective-permute-done((bf16[2,160,800]{2,1,0:T(8,128)(2,1)S(1)}, bf16[2,160,800]{2,1,0:T(8,128)(2,1)S(1)}, u32[]{:S(2)}, u32[]{:S(2)}) %collective-permute-start.97) | collective-permute-done | bytes 512032 | tf_op jit(solution)/shard_map/ppermute | solution.py:44
  706.7 15.7 %collective-permute-done.98.refs_2_ = bf16[2,160,800]{2,1,0:T(8,128)(2,1)S(1)} collective-permute-done((bf16[2,160,800]{2,1,0:T(8,128)(2,1)S(1)}, bf16[2,160,800]{2,1,0:T(8,128)(2,1)S(1)}, u32[]{:S(2)}, u32[]{:S(2)}) %collective-permute-start.98) | collective-permute-done | bytes 512032 | tf_op jit(solution)/shard_map/ppermute | solution.py:44
  722.4 12.9 %collective-permute-done.99.refs_3_ = bf16[2,160,800]{2,1,0:T(8,128)(2,1)S(1)} collective-permute-done((bf16[2,160,800]{2,1,0:T(8,128)(2,1)S(1)}, bf16[2,160,800]{2,1,0:T(8,128)(2,1)S(1)}, u32[]{:S(2)}, u32[]{:S(2)}) %collective-permute-start.99) | collective-permute-done | bytes 512032 | tf_op jit(solution)/shard_map/ppermute | solution.py:44
  735.3 3.3 shard_map.320
  (524 shorter events, 209.1 us)
Async XLA Ops:
  7.2 262.5 %all-gather.5.cloned.1.call-start = ((), (), s32[]{:S(2)}) async-start(), calls=%async_computation.3 | async-start | bytes 5734400 | tf_op jit(solution)/shard_map/all_gather | solution.py:918
  11.3 27.0 %collective-permute-start = (bf16[1,160,320]{2,1,0:T(8,128)(2,1)}, bf16[1,160,320]{2,1,0:T(8,128)(2,1)S(1)}, u32[]{:S(2)}, u32[]{:S(2)}) collective-permute-start(bf16[1,160,320]{2,1,0:T(8,128)(2,1)} %get-tuple-element.113), channel_id=1, source_target_pairs={{0,1},{1,0},{2,3},{3,2},{4,5},{5,4},{6,7},{7,6},{8,9},{9,8},{10,11... | collective-permute-start | bytes 307208 | tf_op jit(solution)/shard_map/ppermute | solution.py:44
  12.8 34.3 %collective-permute-start.1 = (bf16[1,160,320]{2,1,0:T(8,128)(2,1)}, bf16[1,160,320]{2,1,0:T(8,128)(2,1)}, u32[]{:S(2)}, u32[]{:S(2)}) collective-permute-start(bf16[1,160,320]{2,1,0:T(8,128)(2,1)} %get-tuple-element.114), channel_id=1, source_target_pairs={{0,2},{1,3},{2,0},{3,1},{4,6},{5,7},{6,4},{7,5},{8,10},{9,11},{10,... | collective-permute-start | bytes 307208 | tf_op jit(solution)/shard_map/ppermute | solution.py:44
  16.6 31.7 %collective-permute-start.3 = (bf16[1,160,800]{2,1,0:T(8,128)(2,1)}, bf16[1,160,800]{2,1,0:T(8,128)(2,1)}, u32[]{:S(2)}, u32[]{:S(2)}) collective-permute-start(bf16[1,160,800]{2,1,0:T(8,128)(2,1)} %get-tuple-element.116), channel_id=1, source_target_pairs={{0,4},{4,0},{8,12},{12,8},{1,5},{5,1},{9,13},{13,9},{2,6},{6,2},{1... | collective-permute-start | bytes 768008 | tf_op jit(solution)/shard_map/ppermute | solution.py:44
  17.0 31.3 %collective-permute-start.4 = (bf16[1,160,800]{2,1,0:T(8,128)(2,1)}, bf16[1,160,800]{2,1,0:T(8,128)(2,1)}, u32[]{:S(2)}, u32[]{:S(2)}) collective-permute-start(bf16[1,160,800]{2,1,0:T(8,128)(2,1)} %get-tuple-element.117), channel_id=1, source_target_pairs={{0,8},{4,12},{8,0},{12,4},{1,9},{5,13},{9,1},{13,5},{2,10},{6,14},... | collective-permute-start | bytes 768008 | tf_op jit(solution)/shard_map/ppermute | solution.py:44
  19.6 28.7 %collective-permute-start.5 = (bf16[1,160,800]{2,1,0:T(8,128)(2,1)}, bf16[1,160,800]{2,1,0:T(8,128)(2,1)}, u32[]{:S(2)}, u32[]{:S(2)}) collective-permute-start(bf16[1,160,800]{2,1,0:T(8,128)(2,1)} %get-tuple-element.118), channel_id=1, source_target_pairs={{0,12},{4,8},{8,4},{12,0},{1,13},{5,9},{9,5},{13,1},{2,14},{6,10},... | collective-permute-start | bytes 768008 | tf_op jit(solution)/shard_map/ppermute | solution.py:44
  50.8 229.0 %all-gather.3.cloned.1.call-start = ((), (), s32[]{:S(2)}) async-start(), calls=%async_computation.2 | async-start | bytes 11468800 | tf_op jit(solution)/shard_map/all_gather | solution.py:918
  70.6 51.8 %collective-permute-start.11 = (bf16[4,128,1152]{2,1,0:T(8,128)(2,1)}, bf16[4,128,1152]{2,1,0:T(8,128)(2,1)}, u32[]{:S(2)}, u32[]{:S(2)}) collective-permute-start(bf16[4,128,1152]{2,1,0:T(8,128)(2,1)} %pad_maximum_fusion.4.own_ref), channel_id=1, source_target_pairs={{0,16},{16,0},{1,17},{17,1},{2,18},{18,2},{3,19},{19,3},{4,20},{20... | collective-permute-start | bytes 3538952 | tf_op jit(solution)/shard_map/ppermute | solution.py:44
  70.6 24.1 %collective-permute-start.12 = (bf16[4,160,320]{2,1,0:T(8,128)(2,1)S(1)}, bf16[4,160,320]{2,1,0:T(8,128)(2,1)S(1)}, u32[]{:S(2)}, u32[]{:S(2)}) collective-permute-start(bf16[4,160,320]{2,1,0:T(8,128)(2,1)S(1)} %bitcast.178), channel_id=1, source_target_pairs={{0,8},{4,12},{8,0},{12,4},{1,9},{5,13},{9,1},{13,5},{2,10},{6,14},... | collective-permute-start | bytes 1228808 | tf_op jit(solution)/shard_map/ppermute | solution.py:44
  74.2 32.2 %collective-permute-start.14 = (bf16[4,160,320]{2,1,0:T(8,128)(2,1)S(1)}, bf16[4,160,320]{2,1,0:T(8,128)(2,1)S(1)}, u32[]{:S(2)}, u32[]{:S(2)}) collective-permute-start(bf16[4,160,320]{2,1,0:T(8,128)(2,1)S(1)} %bitcast.179), channel_id=1, source_target_pairs={{4,8},{8,4},{5,9},{9,5},{6,10},{10,6},{7,11},{11,7},{20,24},{24,20... | collective-permute-start | bytes 1228808 | tf_op jit(solution)/shard_map/ppermute | solution.py:869
  94.7 27.6 %collective-permute-start.13 = (bf16[4,160,320]{2,1,0:T(8,128)(2,1)S(1)}, bf16[4,160,320]{2,1,0:T(8,128)(2,1)}, u32[]{:S(2)}, u32[]{:S(2)}) collective-permute-start(bf16[4,160,320]{2,1,0:T(8,128)(2,1)S(1)} %collective-permute-done.12.refs_2_), channel_id=1, source_target_pairs={{4,0},{8,12},{5,1},{9,13},{6,2},{10,14},{7,3},{11,15},{20,16},{24,... | collective-permute-start | bytes 1228808 | tf_op jit(solution)/shard_map/ppermute | solution.py:870
  103.8 56.6 %collective-permute-start.20 = (bf16[2,160,800]{2,1,0:T(8,128)(2,1)}, bf16[2,160,800]{2,1,0:T(8,128)(2,1)}, u32[]{:S(2)}, u32[]{:S(2)}) collective-permute-start(bf16[2,160,800]{2,1,0:T(8,128)(2,1)} %get-tuple-element.131), channel_id=1, source_target_pairs={{0,4},{4,0},{8,12},{12,8},{1,5},{5,1},{9,13},{13,9},{2,6},{6,2},{1... | collective-permute-start | bytes 1536008 | tf_op jit(solution)/shard_map/ppermute | solution.py:44
  103.8 56.6 %collective-permute-start.21 = (bf16[2,160,800]{2,1,0:T(8,128)(2,1)}, bf16[2,160,800]{2,1,0:T(8,128)(2,1)}, u32[]{:S(2)}, u32[]{:S(2)}) collective-permute-start(bf16[2,160,800]{2,1,0:T(8,128)(2,1)} %get-tuple-element.132), channel_id=1, source_target_pairs={{0,8},{4,12},{8,0},{12,4},{1,9},{5,13},{9,1},{13,5},{2,10},{6,14},... | collective-permute-start | bytes 1536008 | tf_op jit(solution)/shard_map/ppermute | solution.py:44
  106.4 54.0 %collective-permute-start.22 = (bf16[2,160,800]{2,1,0:T(8,128)(2,1)}, bf16[2,160,800]{2,1,0:T(8,128)(2,1)}, u32[]{:S(2)}, u32[]{:S(2)}) collective-permute-start(bf16[2,160,800]{2,1,0:T(8,128)(2,1)} %get-tuple-element.133), channel_id=1, source_target_pairs={{0,12},{4,8},{8,4},{12,0},{1,13},{5,9},{9,5},{13,1},{2,14},{6,10},... | collective-permute-start | bytes 1536008 | tf_op jit(solution)/shard_map/ppermute | solution.py:44
  163.7 446.9 %reduce-scatter.5.cloned.1.call-start = ((), (), s32[]{:S(2)}) async-start(), calls=%async_computation.5 | async-start | bytes 5734400 | tf_op jit(solution)/shard_map/reduce_scatter | solution.py:921
  164.5 60.2 %collective-permute-start.23 = (bf16[128,2560]{1,0:T(8,128)(2,1)}, bf16[128,2560]{1,0:T(8,128)(2,1)S(1)}, u32[]{:S(2)}, u32[]{:S(2)}) collective-permute-start(bf16[128,2560]{1,0:T(8,128)(2,1)} %get-tuple-element.134), channel_id=1, source_target_pairs={{0,4},{4,0},{8,12},{12,8},{1,5},{5,1},{9,13},{13,9},{2,6},{6,2},{1... | collective-permute-start | bytes 1966088 | tf_op jit(solution)/shard_map/ppermute | solution.py:44
  168.2 57.2 %collective-permute-start.33 = (bf16[128,2560]{1,0:T(8,128)(2,1)}, bf16[128,2560]{1,0:T(8,128)(2,1)S(1)}, u32[]{:S(2)}, u32[]{:S(2)}) collective-permute-start(bf16[128,2560]{1,0:T(8,128)(2,1)} %get-tuple-element.134), channel_id=1, source_target_pairs={{0,8},{4,12},{8,0},{12,4},{1,9},{5,13},{9,1},{13,5},{2,10},{6,14},... | collective-permute-start | bytes 1966088 | tf_op jit(solution)/shard_map/ppermute | solution.py:44
  168.3 82.8 %collective-permute-start.35 = (bf16[128,2560]{1,0:T(8,128)(2,1)}, bf16[128,2560]{1,0:T(8,128)(2,1)S(1)}, u32[]{:S(2)}, u32[]{:S(2)}) collective-permute-start(bf16[128,2560]{1,0:T(8,128)(2,1)} %get-tuple-element.134), channel_id=1, source_target_pairs={{4,8},{8,4},{5,9},{9,5},{6,10},{10,6},{7,11},{11,7},{20,24},{24,20... | collective-permute-start | bytes 1966088 | tf_op jit(solution)/shard_map/ppermute | solution.py:869
  177.1 17.1 %collective-permute-start.18 = (bf16[64,2560]{1,0:T(8,128)(2,1)S(1)}, bf16[64,2560]{1,0:T(8,128)(2,1)S(1)}, u32[]{:S(2)}, u32[]{:S(2)}) collective-permute-start(bf16[64,2560]{1,0:T(8,128)(2,1)S(1)} %get-tuple-element.208), channel_id=1, source_target_pairs={{0,1},{1,0},{2,3},{3,2},{4,5},{5,4},{6,7},{7,6},{8,9},{9,8},{10,11... | collective-permute-start | bytes 983048 | tf_op jit(solution)/shard_map/ppermute | solution.py:44
  177.2 17.1 %collective-permute-start.16 = (bf16[64,2560]{1,0:T(8,128)(2,1)S(1)}, bf16[64,2560]{1,0:T(8,128)(2,1)S(1)}, u32[]{:S(2)}, u32[]{:S(2)}) collective-permute-start(bf16[64,2560]{1,0:T(8,128)(2,1)S(1)} %get-tuple-element.210), channel_id=1, source_target_pairs={{0,2},{1,3},{2,0},{3,1},{4,6},{5,7},{6,4},{7,5},{8,10},{9,11},{10,... | collective-permute-start | bytes 983048 | tf_op jit(solution)/shard_map/ppermute | solution.py:44
  194.6 28.1 %collective-permute-start.17 = (bf16[128,2560]{1,0:T(8,128)(2,1)S(1)}, bf16[128,2560]{1,0:T(8,128)(2,1)S(1)}, u32[]{:S(2)}, u32[]{:S(2)}) collective-permute-start(bf16[128,2560]{1,0:T(8,128)(2,1)S(1)} %pad_maximum_fusion.6), channel_id=1, source_target_pairs={{0,1},{1,0},{2,3},{3,2},{4,5},{5,4},{6,7},{7,6},{8,9},{9,8},{10,11... | collective-permute-start | bytes 1966088 | tf_op jit(solution)/shard_map/ppermute | solution.py:44
  196.5 26.1 %collective-permute-start.19 = (bf16[128,2560]{1,0:T(8,128)(2,1)S(1)}, bf16[128,2560]{1,0:T(8,128)(2,1)S(1)}, u32[]{:S(2)}, u32[]{:S(2)}) collective-permute-start(bf16[128,2560]{1,0:T(8,128)(2,1)S(1)} %pad_maximum_fusion.7), channel_id=1, source_target_pairs={{0,2},{1,3},{2,0},{3,1},{4,6},{5,7},{6,4},{7,5},{8,10},{9,11},{10,... | collective-permute-start | bytes 1966088 | tf_op jit(solution)/shard_map/ppermute | solution.py:44
  224.8 26.2 %collective-permute-start.24 = (bf16[128,2560]{1,0:T(8,128)(2,1)}, bf16[128,2560]{1,0:T(8,128)(2,1)S(1)}, u32[]{:S(2)}, u32[]{:S(2)}) collective-permute-start(bf16[128,2560]{1,0:T(8,128)(2,1)} %get-tuple-element.135), channel_id=1, source_target_pairs={{0,4},{4,0},{8,12},{12,8},{1,5},{5,1},{9,13},{13,9},{2,6},{6,2},{1... | collective-permute-start | bytes 1966088 | tf_op jit(solution)/shard_map/ppermute | solution.py:44
  225.4 44.4 %collective-permute-start.26 = (bf16[256,2560]{1,0:T(8,128)(2,1)S(1)}, bf16[256,2560]{1,0:T(8,128)(2,1)}, u32[]{:S(2)}, u32[]{:S(2)}) collective-permute-start(bf16[256,2560]{1,0:T(8,128)(2,1)S(1)} %constant_dynamic-update-slice_fusion.2.gm_own.refs_0_), channel_id=1, source_target_pairs={{0,16},{16,0},{1,17},{17,1},{2,18},{18,2},{3,19},{19,3},{4,20},{20... | collective-permute-start | bytes 3932168 | tf_op jit(solution)/shard_map/ppermute | solution.py:44
  225.5 43.3 %collective-permute-start.34 = (bf16[128,2560]{1,0:T(8,128)(2,1)S(1)}, bf16[128,2560]{1,0:T(8,128)(2,1)S(1)}, u32[]{:S(2)}, u32[]{:S(2)}) collective-permute-start(bf16[128,2560]{1,0:T(8,128)(2,1)S(1)} %collective-permute-done.33), channel_id=1, source_target_pairs={{4,0},{8,12},{5,1},{9,13},{6,2},{10,14},{7,3},{11,15},{20,16},{24,... | collective-permute-start | bytes 1966088 | tf_op jit(solution)/shard_map/ppermute | solution.py:870
  228.9 29.8 %collective-permute-start.29 = (bf16[128,2560]{1,0:T(8,128)(2,1)}, bf16[128,2560]{1,0:T(8,128)(2,1)}, u32[]{:S(2)}, u32[]{:S(2)}) collective-permute-start(bf16[128,2560]{1,0:T(8,128)(2,1)} %get-tuple-element.135), channel_id=1, source_target_pairs={{0,8},{4,12},{8,0},{12,4},{1,9},{5,13},{9,1},{13,5},{2,10},{6,14},... | collective-permute-start | bytes 1966088 | tf_op jit(solution)/shard_map/ppermute | solution.py:44
  251.1 18.7 %collective-permute-start.25 = (bf16[256,2560]{1,0:T(8,128)(2,1)S(1)}, bf16[256,2560]{1,0:T(8,128)(2,1)}, u32[]{:S(2)}, u32[]{:S(2)}) collective-permute-start(bf16[256,2560]{1,0:T(8,128)(2,1)S(1)} %constant_dynamic-update-slice_fusion.nm_own.refs_0_), channel_id=1, source_target_pairs={{0,16},{16,0},{1,17},{17,1},{2,18},{18,2},{3,19},{19,3},{4,20},{20... | collective-permute-start | bytes 3932168 | tf_op jit(solution)/shard_map/ppermute | solution.py:44
  251.2 54.2 %collective-permute-start.31 = (bf16[128,2560]{1,0:T(8,128)(2,1)}, bf16[128,2560]{1,0:T(8,128)(2,1)}, u32[]{:S(2)}, u32[]{:S(2)}) collective-permute-start(bf16[128,2560]{1,0:T(8,128)(2,1)} %get-tuple-element.135), channel_id=1, source_target_pairs={{4,8},{8,4},{5,9},{9,5},{6,10},{10,6},{7,11},{11,7},{20,24},{24,20... | collective-permute-start | bytes 1966088 | tf_op jit(solution)/shard_map/ppermute | solution.py:869
  258.7 46.6 %collective-permute-start.30 = (bf16[128,2560]{1,0:T(8,128)(2,1)}, bf16[128,2560]{1,0:T(8,128)(2,1)}, u32[]{:S(2)}, u32[]{:S(2)}) collective-permute-start(bf16[128,2560]{1,0:T(8,128)(2,1)} %collective-permute-done.29), channel_id=1, source_target_pairs={{4,0},{8,12},{5,1},{9,13},{6,2},{10,14},{7,3},{11,15},{20,16},{24,... | collective-permute-start | bytes 1966088 | tf_op jit(solution)/shard_map/ppermute | solution.py:870
  309.8 25.3 %collective-permute-start.39 = (bf16[128,2560]{1,0:T(8,128)(2,1)}, bf16[128,2560]{1,0:T(8,128)(2,1)}, u32[]{:S(2)}, u32[]{:S(2)}) collective-permute-start(bf16[128,2560]{1,0:T(8,128)(2,1)} %get-tuple-element.226), channel_id=1, source_target_pairs={{0,4},{4,0},{8,12},{12,8},{1,5},{5,1},{9,13},{13,9},{2,6},{6,2},{1... | collective-permute-start | bytes 1966088 | tf_op jit(solution)/shard_map/ppermute | solution.py:44
  344.9 335.1 %reduce-scatter.3.cloned.1.call-start = ((), (), s32[]{:S(2)}) async-start(), calls=%async_computation.4 | async-start | bytes 11468800 | tf_op jit(solution)/shard_map/reduce_scatter | solution.py:921
  350.1 18.9 %collective-permute-start.40 = (bf16[128,2560]{1,0:T(8,128)(2,1)S(1)}, bf16[128,2560]{1,0:T(8,128)(2,1)S(1)}, u32[]{:S(2)}, u32[]{:S(2)}) collective-permute-start(bf16[128,2560]{1,0:T(8,128)(2,1)S(1)} %slice.257), channel_id=1, source_target_pairs={{0,4},{12,8},{1,5},{13,9},{2,6},{14,10},{3,7},{15,11},{16,20},{28,... | collective-permute-start | bytes 1966088 | tf_op jit(solution)/shard_map/ppermute | solution.py:876
  351.7 19.1 %collective-permute-start.38 = (bf16[128,2560]{1,0:T(8,128)(2,1)S(1)}, bf16[128,2560]{1,0:T(8,128)(2,1)S(1)}, u32[]{:S(2)}, u32[]{:S(2)}) collective-permute-start(bf16[128,2560]{1,0:T(8,128)(2,1)S(1)} %slice.257), channel_id=1, source_target_pairs={{4,8},{8,4},{5,9},{9,5},{6,10},{10,6},{7,11},{11,7},{20,24},{24,20... | collective-permute-start | bytes 1966088 | tf_op jit(solution)/shard_map/ppermute | solution.py:878
  370.1 28.6 %collective-permute-start.41 = (bf16[128,2560]{1,0:T(8,128)(2,1)}, bf16[128,2560]{1,0:T(8,128)(2,1)}, u32[]{:S(2)}, u32[]{:S(2)}) collective-permute-start(bf16[128,2560]{1,0:T(8,128)(2,1)} %add_convert_fusion.7), channel_id=1, source_target_pairs={{0,8},{4,12},{8,0},{12,4},{1,9},{5,13},{9,1},{13,5},{2,10},{6,14},... | collective-permute-start | bytes 1966088 | tf_op jit(solution)/shard_map/ppermute | solution.py:44
  436.0 39.7 %collective-permute-start.49 = (bf16[128,2560]{1,0:T(8,128)(2,1)}, bf16[128,2560]{1,0:T(8,128)(2,1)S(1)}, u32[]{:S(2)}, u32[]{:S(2)}) collective-permute-start(bf16[128,2560]{1,0:T(8,128)(2,1)} %get-tuple-element.169), channel_id=1, source_target_pairs={{0,4},{12,8},{1,5},{13,9},{2,6},{14,10},{3,7},{15,11},{16,20},{28,... | collective-permute-start | bytes 1966088 | tf_op jit(solution)/shard_map/ppermute | solution.py:876
  469.2 41.6 %collective-permute-start.51 = (bf16[128,2560]{1,0:T(8,128)(2,1)}, bf16[128,2560]{1,0:T(8,128)(2,1)}, u32[]{:S(2)}, u32[]{:S(2)}) collective-permute-start(bf16[128,2560]{1,0:T(8,128)(2,1)} %get-tuple-element.169), channel_id=1, source_target_pairs={{4,8},{8,4},{5,9},{9,5},{6,10},{10,6},{7,11},{11,7},{20,24},{24,20... | collective-permute-start | bytes 1966088 | tf_op jit(solution)/shard_map/ppermute | solution.py:878
  474.1 34.2 %collective-permute-start.47 = (bf16[128,2560]{1,0:T(8,128)(2,1)}, bf16[128,2560]{1,0:T(8,128)(2,1)S(1)}, u32[]{:S(2)}, u32[]{:S(2)}) collective-permute-start(bf16[128,2560]{1,0:T(8,128)(2,1)} %get-tuple-element.165), channel_id=1, source_target_pairs={{0,4},{4,0},{8,12},{12,8},{1,5},{5,1},{9,13},{13,9},{2,6},{6,2},{1... | collective-permute-start | bytes 1966088 | tf_op jit(solution)/shard_map/ppermute | solution.py:44
  476.8 40.1 %collective-permute-start.50 = (bf16[128,2560]{1,0:T(8,128)(2,1)}, bf16[128,2560]{1,0:T(8,128)(2,1)}, u32[]{:S(2)}, u32[]{:S(2)}) collective-permute-start(bf16[128,2560]{1,0:T(8,128)(2,1)} %add_convert_fusion.6), channel_id=1, source_target_pairs={{0,8},{4,12},{8,0},{12,4},{1,9},{5,13},{9,1},{13,5},{2,10},{6,14},... | collective-permute-start | bytes 1966088 | tf_op jit(solution)/shard_map/ppermute | solution.py:44
  489.4 17.1 %collective-permute-start.57 = (bf16[128,1152]{1,0:T(8,128)(2,1)S(1)}, bf16[128,1152]{1,0:T(8,128)(2,1)S(1)}, u32[]{:S(2)}, u32[]{:S(2)}) collective-permute-start(bf16[128,1152]{1,0:T(8,128)(2,1)S(1)} %pad_maximum_fusion.10), channel_id=1, source_target_pairs={{0,2},{1,3},{2,0},{3,1},{4,6},{5,7},{6,4},{7,5},{8,10},{9,11},{10,... | collective-permute-start | bytes 884744 | tf_op jit(solution)/shard_map/ppermute | solution.py:44
  496.6 24.6 %collective-permute-start.79 = (bf16[256,640]{1,0:T(8,128)(2,1)}, bf16[256,640]{1,0:T(8,128)(2,1)}, u32[]{:S(2)}, u32[]{:S(2)}) collective-permute-start(bf16[256,640]{1,0:T(8,128)(2,1)} %get-tuple-element.220), channel_id=1, source_target_pairs={{0,4},{12,8},{1,5},{13,9},{2,6},{14,10},{3,7},{15,11},{16,20},{28,... | collective-permute-start | bytes 983048 | tf_op jit(solution)/shard_map/ppermute | solution.py:876
  507.4 21.6 %collective-permute-start.68 = (bf16[128,1152]{1,0:T(8,128)(2,1)S(1)}, bf16[128,1152]{1,0:T(8,128)(2,1)S(1)}, u32[]{:S(2)}, u32[]{:S(2)}) collective-permute-start(bf16[128,1152]{1,0:T(8,128)(2,1)S(1)} %get-tuple-element.191.lat), channel_id=1, source_target_pairs={{0,1},{1,0},{2,3},{3,2},{4,5},{5,4},{6,7},{7,6},{8,9},{9,8},{10,11... | collective-permute-start | bytes 884744 | tf_op jit(solution)/shard_map/ppermute | solution.py:44
  509.2 21.5 %collective-permute-start.69 = (bf16[128,1152]{1,0:T(8,128)(2,1)S(1)}, bf16[128,1152]{1,0:T(8,128)(2,1)S(1)}, u32[]{:S(2)}, u32[]{:S(2)}) collective-permute-start(bf16[128,1152]{1,0:T(8,128)(2,1)S(1)} %get-tuple-element.191.lat), channel_id=1, source_target_pairs={{0,2},{1,3},{2,0},{3,1},{4,6},{5,7},{6,4},{7,5},{8,10},{9,11},{10,... | collective-permute-start | bytes 884744 | tf_op jit(solution)/shard_map/ppermute | solution.py:44
  510.7 46.3 %collective-permute-start.66 = (bf16[128,640]{1,0:T(8,128)(2,1)}, bf16[128,640]{1,0:T(8,128)(2,1)S(1)}, u32[]{:S(2)}, u32[]{:S(2)}) collective-permute-start(bf16[128,640]{1,0:T(8,128)(2,1)} %get-tuple-element.190), channel_id=1, source_target_pairs={{0,3},{1,2},{2,1},{3,0},{4,7},{5,6},{6,5},{7,4},{8,11},{9,10},{10,... | collective-permute-start | bytes 491528 | tf_op jit(solution)/shard_map/ppermute | solution.py:44
  521.1 45.4 %collective-permute-start.52 = (bf16[128,2560]{1,0:T(8,128)(2,1)S(1)}, bf16[128,2560]{1,0:T(8,128)(2,1)S(1)}, u32[]{:S(2)}, u32[]{:S(2)}) collective-permute-start(bf16[128,2560]{1,0:T(8,128)(2,1)S(1)} %shard_map.307.own), channel_id=1, source_target_pairs={{0,16},{16,0},{1,17},{17,1},{2,18},{18,2},{3,19},{19,3},{4,20},{20... | collective-permute-start | bytes 1966088 | tf_op jit(solution)/shard_map/ppermute | solution.py:44
  521.2 18.7 %collective-permute-start.81 = (bf16[256,640]{1,0:T(8,128)(2,1)}, bf16[256,640]{1,0:T(8,128)(2,1)S(1)}, u32[]{:S(2)}, u32[]{:S(2)}) collective-permute-start(bf16[256,640]{1,0:T(8,128)(2,1)} %get-tuple-element.220), channel_id=1, source_target_pairs={{4,8},{8,4},{5,9},{9,5},{6,10},{10,6},{7,11},{11,7},{20,24},{24,20... | collective-permute-start | bytes 983048 | tf_op jit(solution)/shard_map/ppermute | solution.py:878
  550.4 37.2 %collective-permute-start.72 = (bf16[4,128,1152]{2,1,0:T(8,128)(2,1)S(1)}, bf16[4,128,1152]{2,1,0:T(8,128)(2,1)}, u32[]{:S(2)}, u32[]{:S(2)}) collective-permute-start(bf16[4,128,1152]{2,1,0:T(8,128)(2,1)S(1)} %pad_maximum_fusion.5.gown), channel_id=1, source_target_pairs={{0,16},{16,0},{1,17},{17,1},{2,18},{18,2},{3,19},{19,3},{4,20},{20... | collective-permute-start | bytes 3538952 | tf_op jit(solution)/shard_map/ppermute | solution.py:44
  552.8 16.3 %collective-permute-start.83 = (bf16[256,640]{1,0:T(8,128)(2,1)S(1)}, bf16[256,640]{1,0:T(8,128)(2,1)}, u32[]{:S(2)}, u32[]{:S(2)}) collective-permute-start(bf16[256,640]{1,0:T(8,128)(2,1)S(1)} %add_convert_fusion.9), channel_id=1, source_target_pairs={{0,8},{4,12},{8,0},{12,4},{1,9},{5,13},{9,1},{13,5},{2,10},{6,14},... | collective-permute-start | bytes 983048 | tf_op jit(solution)/shard_map/ppermute | solution.py:44
  566.1 20.7 %collective-permute-start.67 = (bf16[4,128,640]{2,1,0:T(8,128)(2,1)}, bf16[4,128,640]{2,1,0:T(8,128)(2,1)}, u32[]{:S(2)}, u32[]{:S(2)}) collective-permute-start(bf16[4,128,640]{2,1,0:T(8,128)(2,1)} %pad_maximum_fusion.8.own), channel_id=1, source_target_pairs={{0,16},{16,0},{1,17},{17,1},{2,18},{18,2},{3,19},{19,3},{4,20},{20... | collective-permute-start | bytes 1966088 | tf_op jit(solution)/shard_map/ppermute | solution.py:44
  574.5 26.0 %collective-permute-start.91 = (bf16[4,160,320]{2,1,0:T(8,128)(2,1)}, bf16[4,160,320]{2,1,0:T(8,128)(2,1)}, u32[]{:S(2)}, u32[]{:S(2)}) collective-permute-start(bf16[4,160,320]{2,1,0:T(8,128)(2,1)} %get-tuple-element.217), channel_id=1, source_target_pairs={{0,4},{12,8},{1,5},{13,9},{2,6},{14,10},{3,7},{15,11},{16,20},{28,... | collective-permute-start | bytes 1228808 | tf_op jit(solution)/shard_map/ppermute | solution.py:876
  579.0 18.9 %collective-permute-start.82 = (bf16[256,640]{1,0:T(8,128)(2,1)S(1)}, bf16[256,640]{1,0:T(8,128)(2,1)}, u32[]{:S(2)}, u32[]{:S(2)}) collective-permute-start(bf16[256,640]{1,0:T(8,128)(2,1)S(1)} %add_convert_fusion.9), channel_id=1, source_target_pairs={{0,4},{4,0},{8,12},{12,8},{1,5},{5,1},{9,13},{13,9},{2,6},{6,2},{1... | collective-permute-start | bytes 983048 | tf_op jit(solution)/shard_map/ppermute | solution.py:44
  583.9 24.6 %collective-permute-start.93 = (bf16[4,160,320]{2,1,0:T(8,128)(2,1)}, bf16[4,160,320]{2,1,0:T(8,128)(2,1)}, u32[]{:S(2)}, u32[]{:S(2)}) collective-permute-start(bf16[4,160,320]{2,1,0:T(8,128)(2,1)} %get-tuple-element.217), channel_id=1, source_target_pairs={{4,8},{8,4},{5,9},{9,5},{6,10},{10,6},{7,11},{11,7},{20,24},{24,20... | collective-permute-start | bytes 1228808 | tf_op jit(solution)/shard_map/ppermute | solution.py:878
  586.8 40.3 %collective-permute-start.90 = (bf16[4,160,320]{2,1,0:T(8,128)(2,1)}, bf16[4,160,320]{2,1,0:T(8,128)(2,1)}, u32[]{:S(2)}, u32[]{:S(2)}) collective-permute-start(bf16[4,160,320]{2,1,0:T(8,128)(2,1)} %get-tuple-element.218), channel_id=1, source_target_pairs={{0,4},{4,0},{8,12},{12,8},{1,5},{5,1},{9,13},{13,9},{2,6},{6,2},{1... | collective-permute-start | bytes 1228808 | tf_op jit(solution)/shard_map/ppermute | solution.py:44
  587.5 20.3 %collective-permute-start.63 = (f32[48,128]{1,0:T(8,128)S(1)}, f32[48,128]{1,0:T(8,128)S(1)}, u32[]{:S(2)}, u32[]{:S(2)}) collective-permute-start(f32[48,128]{1,0:T(8,128)S(1)} %add.160), channel_id=1, source_target_pairs={{0,8},{4,12},{8,0},{12,4},{1,9},{5,13},{9,1},{13,5},{2,10},{6,14},... | collective-permute-start | bytes 73736 | tf_op jit(solution)/shard_map/ppermute | solution.py:44
  599.1 32.2 %collective-permute-start.86 = (bf16[1024,640]{1,0:T(8,128)(2,1)S(1)}, bf16[1024,640]{1,0:T(8,128)(2,1)}, u32[]{:S(2)}, u32[]{:S(2)}) collective-permute-start(bf16[1024,640]{1,0:T(8,128)(2,1)S(1)} %bitcast.174), channel_id=1, source_target_pairs={{0,1},{1,0},{2,3},{3,2},{4,5},{5,4},{6,7},{7,6},{8,9},{9,8},{10,11... | collective-permute-start | bytes 3932168 | tf_op jit(solution)/shard_map/ppermute | solution.py:44
  600.5 31.6 %collective-permute-start.87 = (bf16[1024,640]{1,0:T(8,128)(2,1)S(1)}, bf16[1024,640]{1,0:T(8,128)(2,1)}, u32[]{:S(2)}, u32[]{:S(2)}) collective-permute-start(bf16[1024,640]{1,0:T(8,128)(2,1)S(1)} %bitcast.175), channel_id=1, source_target_pairs={{0,2},{1,3},{2,0},{3,1},{4,6},{5,7},{6,4},{7,5},{8,10},{9,11},{10,... | collective-permute-start | bytes 3932168 | tf_op jit(solution)/shard_map/ppermute | solution.py:44
  607.8 20.2 %collective-permute-start.92 = (bf16[4,160,320]{2,1,0:T(8,128)(2,1)}, bf16[4,160,320]{2,1,0:T(8,128)(2,1)}, u32[]{:S(2)}, u32[]{:S(2)}) collective-permute-start(bf16[4,160,320]{2,1,0:T(8,128)(2,1)} %fusion), channel_id=1, source_target_pairs={{0,8},{4,12},{8,0},{12,4},{1,9},{5,13},{9,1},{13,5},{2,10},{6,14},... | collective-permute-start | bytes 1228808 | tf_op jit(solution)/shard_map/ppermute | solution.py:44
  639.3 23.4 %collective-permute-start.101 = (bf16[1,160,800]{2,1,0:T(8,128)(2,1)S(1)}, bf16[1,160,800]{2,1,0:T(8,128)(2,1)S(1)}, u32[]{:S(2)}, u32[]{:S(2)}) collective-permute-start(bf16[1,160,800]{2,1,0:T(8,128)(2,1)S(1)} %get-tuple-element.235), channel_id=1, source_target_pairs={{0,8},{4,12},{8,0},{12,4},{1,9},{5,13},{9,1},{13,5},{2,10},{6,14},... | collective-permute-start | bytes 768008 | tf_op jit(solution)/shard_map/ppermute | solution.py:44
  640.6 29.4 %collective-permute-start.102 = (bf16[1,160,800]{2,1,0:T(8,128)(2,1)S(1)}, bf16[1,160,800]{2,1,0:T(8,128)(2,1)S(1)}, u32[]{:S(2)}, u32[]{:S(2)}) collective-permute-start(bf16[1,160,800]{2,1,0:T(8,128)(2,1)S(1)} %get-tuple-element.234), channel_id=1, source_target_pairs={{0,12},{4,8},{8,4},{12,0},{1,13},{5,9},{9,5},{13,1},{2,14},{6,10},... | collective-permute-start | bytes 768008 | tf_op jit(solution)/shard_map/ppermute | solution.py:44
  641.5 43.8 %collective-permute-start.89 = (bf16[512,640]{1,0:T(8,128)(2,1)}, bf16[512,640]{1,0:T(8,128)(2,1)}, u32[]{:S(2)}, u32[]{:S(2)}) collective-permute-start(bf16[512,640]{1,0:T(8,128)(2,1)} %slice.279), channel_id=1, source_target_pairs={{0,2},{1,3},{2,0},{3,1},{4,6},{5,7},{6,4},{7,5},{8,10},{9,11},{10,... | collective-permute-start | bytes 1966088 | tf_op jit(solution)/shard_map/ppermute | solution.py:44
  643.7 41.7 %collective-permute-start.88 = (bf16[512,640]{1,0:T(8,128)(2,1)}, bf16[512,640]{1,0:T(8,128)(2,1)}, u32[]{:S(2)}, u32[]{:S(2)}) collective-permute-start(bf16[512,640]{1,0:T(8,128)(2,1)} %slice.278), channel_id=1, source_target_pairs={{0,1},{1,0},{2,3},{3,2},{4,5},{5,4},{6,7},{7,6},{8,9},{9,8},{10,11... | collective-permute-start | bytes 1966088 | tf_op jit(solution)/shard_map/ppermute | solution.py:44
  646.1 26.0 %collective-permute-start.94 = (bf16[1,160,320]{2,1,0:T(8,128)(2,1)S(1)}, bf16[1,160,320]{2,1,0:T(8,128)(2,1)S(1)}, u32[]{:S(2)}, u32[]{:S(2)}) collective-permute-start(bf16[1,160,320]{2,1,0:T(8,128)(2,1)S(1)} %get-tuple-element.244), channel_id=1, source_target_pairs={{0,1},{1,0},{2,3},{3,2},{4,5},{5,4},{6,7},{7,6},{8,9},{9,8},{10,11... | collective-permute-start | bytes 307208 | tf_op jit(solution)/shard_map/ppermute | solution.py:44
  681.8 24.9 %collective-permute-start.97 = (bf16[2,160,800]{2,1,0:T(8,128)(2,1)S(1)}, bf16[2,160,800]{2,1,0:T(8,128)(2,1)S(1)}, u32[]{:S(2)}, u32[]{:S(2)}) collective-permute-start(bf16[2,160,800]{2,1,0:T(8,128)(2,1)S(1)} %get-tuple-element.214), channel_id=1, source_target_pairs={{0,4},{4,0},{8,12},{12,8},{1,5},{5,1},{9,13},{13,9},{2,6},{6,2},{1... | collective-permute-start | bytes 1536008 | tf_op jit(solution)/shard_map/ppermute | solution.py:44
  681.8 40.6 %collective-permute-start.98 = (bf16[2,160,800]{2,1,0:T(8,128)(2,1)S(1)}, bf16[2,160,800]{2,1,0:T(8,128)(2,1)S(1)}, u32[]{:S(2)}, u32[]{:S(2)}) collective-permute-start(bf16[2,160,800]{2,1,0:T(8,128)(2,1)S(1)} %get-tuple-element.213), channel_id=1, source_target_pairs={{0,8},{4,12},{8,0},{12,4},{1,9},{5,13},{9,1},{13,5},{2,10},{6,14},... | collective-permute-start | bytes 1536008 | tf_op jit(solution)/shard_map/ppermute | solution.py:44
  684.5 50.8 %collective-permute-start.99 = (bf16[2,160,800]{2,1,0:T(8,128)(2,1)S(1)}, bf16[2,160,800]{2,1,0:T(8,128)(2,1)S(1)}, u32[]{:S(2)}, u32[]{:S(2)}) collective-permute-start(bf16[2,160,800]{2,1,0:T(8,128)(2,1)S(1)} %get-tuple-element.212), channel_id=1, source_target_pairs={{0,12},{4,8},{8,4},{12,0},{1,13},{5,9},{9,5},{13,1},{2,14},{6,10},... | collective-permute-start | bytes 1536008 | tf_op jit(solution)/shard_map/ppermute | solution.py:44
  (157 other events, 1771.7 us)
Sparse Core Ops, SparseCore 0:
  50.9 59.0 all-gather.4
  163.8 116.0 all-gather.2
  345.1 55.9 reduce-scatter.4
  426.4 108.0 reduce-scatter.2

commit v4 on v3

--- a/solution.py
+++ b/solution.py
@@ -109,6 +109,23 @@
         out[half + j, j] = -1.0
         out[j, half + j] = 1.0
     return out
+
+
+def frequencies(lanes, start):
+    half = ROPE // 2
+    out = np.zeros((1, lanes), np.float32)
+    freqs = rope_base ** (-np.arange(0, ROPE, 2).astype(np.float32) / ROPE)
+    out[0, start : start + half] = freqs
+    out[0, start + half : start + ROPE] = freqs
+    return out
+
+
+def documents(segments, index):
+    first = jnp.sum((segments < 1).astype(jnp.int32))
+    second = jnp.sum((segments < 2).astype(jnp.int32))
+    number = (index >= first).astype(jnp.int32) + (index >= second).astype(jnp.int32)
+    start = jnp.where(index >= second, second, jnp.where(index >= first, first, 0))
+    return number, start
 
 
 def total_of(refs):
@@ -162,13 +179,19 @@
 
 
 def enter_kernel(
-    sizes, block, ids, tok, cot, gain_in, gain_query, gain_latent, w_qa, w_kva, cosine, sine, turned,
-    normed_ref, lat_ref, q_ref, kv_ref, x_ref, cot_ref, gm_ref, *rest
+    sizes, block, ids, tok, cot, segments, freqs, gain_in, gain_query, gain_latent, w_qa, w_kva, turned,
+    cos_ref, sin_ref, normed_ref, lat_ref, q_ref, kv_ref, x_ref, cot_ref, gm_ref, *rest
 ):
     nt, nz, nc = sizes
     pieces, (inner, plain_ref) = rest[:nc], rest[nc:]
     half = normed_ref.shape[0]
     qrank = w_qa.shape[1]
+    index = (ids[2] * nt + ids[0]) * half + lax.broadcasted_iota(jnp.int32, (half, ROPE), 0)
+    _, start = documents(segments[...], index)
+    angles = (index - start).astype(f32) * freqs[...]
+    cosine, sine = jnp.cos(angles), jnp.sin(angles)
+    cos_ref[...] = cosine
+    sin_ref[...] = sine
     here = pl.ds(pl.multiple_of(ids[0] * half, half), half)
     own = tok[here, :]
     hidden = own.astype(f32)
@@ -184,7 +207,7 @@
     rope = kv_latent[:, KVRANK:]
     other = jnp.dot(rope, turned[...], precision=lax.Precision.HIGHEST, preferred_element_type=f32)
     end = qrank + KVRANK + ROPE
-    lat_ref[:, qrank + KVRANK : end] = (rope * cosine[...] + other * sine[...]).astype(bf16)
+    lat_ref[:, qrank + KVRANK : end] = (rope * cosine + other * sine).astype(bf16)
     lat_ref[:, end:] = jnp.zeros((half, lat_ref.shape[1] - end), bf16)
     move_blocks(normed_ref, inner, nz, nc, block)
     span = nz * block
@@ -199,8 +222,8 @@
 
 
 def forward_kernel(
-    nt, ids, own_ref, oth_ref, wq_ref, wkv_ref, cos_ref, sin_ref, qtab_ref, ktab_ref,
-    oown_ref, ooth_ref, q_ref, k_ref, v_ref, qn_ref, kvn_ref
+    nt, ids, own_ref, oth_ref, wq_ref, wkv_ref, segments, freqs,
+    oown_ref, ooth_ref, q_ref, k_ref, v_ref, qn_ref, kvn_ref, cos_ref, sin_ref, qtab_ref, ktab_ref
 ):
     t, c = ids[0], ids[2]
     nc, half = own_ref.shape[0], own_ref.shape[1]
@@ -215,6 +238,17 @@
                 value = jnp.where(t == i, own_ref[c ^ j], oth_ref[c ^ j])
                 qn_ref[rows, :] = value[:, :qrank]
                 kvn_ref[rows, :] = value[:, qrank:]
+        index = lax.broadcasted_iota(jnp.int32, (length, LANES), 0)
+        lane = lax.broadcasted_iota(jnp.int32, (length, LANES), 1)
+        number, start = documents(segments[...], index)
+        angles = (index - start).astype(f32) * freqs[...]
+        cos_ref[...] = jnp.where(lane < NOPE + ROPE, jnp.cos(angles), 0.0)
+        sin_ref[...] = jnp.sin(angles)
+        at = lane - (NOPE + ROPE + 3)
+        same = at == number
+        qtab_ref[...] = jnp.where(same, masked_score, 0.0)
+        ones = (at >= -3) & (at < 3) & jnp.logical_not(same)
+        ktab_ref[...] = jnp.where(ones, 1.0, 0.0)
 
     raw = jnp.dot(qn_ref[...], wq_ref[...], preferred_element_type=f32)
     query = raw[:, :LANES] * cos_ref[...] + raw[:, LANES:] * sin_ref[...] + qtab_ref[...]
@@ -322,7 +356,7 @@
     dkv_ref[:, LANES:] = jnp.where(lane < VDIM, dv_acc[...], 0.0).astype(bf16)
 
 
-def attend(nt, ids, own, oth, wq, wkv, cosine, sine, qtab, ktab):
+def attend(nt, ids, own, oth, wq, wkv, segments):
     nc, half, _ = own.shape
     length = nc * nt * half
     qrank, kvrank = wq.shape[0], wkv.shape[0]
@@ -332,7 +366,13 @@
     split = pl.BlockSpec((nc, half, LANES), lambda h, ids: (0, 0, h))
     out = jax.ShapeDtypeStruct((length, heads * LANES), bf16)
     out_split = jax.ShapeDtypeStruct((nc, half, heads * LANES), bf16)
-    kept = [jax.ShapeDtypeStruct((length, qrank), bf16), jax.ShapeDtypeStruct((length, kvrank), bf16)]
+    kept = [
+        jax.ShapeDtypeStruct((length, qrank), bf16),
+        jax.ShapeDtypeStruct((length, kvrank), bf16),
+        jax.ShapeDtypeStruct((length, LANES), f32),
+        jax.ShapeDtypeStruct((length, LANES), f32),
+    ]
+    freqs = jnp.asarray(frequencies(LANES, NOPE))
     return pl.pallas_call(
         functools.partial(forward_kernel, nt),
         grid_spec=pltpu.PrefetchScalarGridSpec(
@@ -343,12 +383,11 @@
                 whole(oth),
                 column(qrank, 2 * LANES),
                 column(kvrank, 2 * LANES),
-                whole(cosine),
-                whole(sine),
-                whole(qtab),
-                whole(ktab),
+                whole(segments),
+                whole(freqs),
             ],
             out_specs=[split] * 2 + [column(length, LANES)] * 3 + [whole(a) for a in kept],
+            scratch_shapes=[pltpu.VMEM((length, LANES), f32)] * 2,
         ),
         out_shape=[out_split] * 2 + [out] * 3 + kept,
         compiler_params=grid_params(),
@@ -357,7 +396,7 @@
             16 * length * heads * LANES,
             heads * length * length // 2,
         ),
-    )(ids, own, oth, wq, wkv, cosine, sine, qtab, ktab)
+    )(ids, own, oth, wq, wkv, segments, freqs)
 
 
 def attend_back(nt, ids, q, k, v, oown, ooth, gown, goth, cosine, sine):
@@ -929,27 +968,6 @@
         parts = (keep + swap(give).astype(f32)).astype(bf16)
         return back_ctx([parts[k] for k in range(nc)])
 
-    segment_all = segments[0]
-    doc_start = jnp.sum((segment_all[None, :] < segment_all[:, None]).astype(jnp.int32), axis=1)
-    positions = (jnp.arange(length, dtype=jnp.int32) - doc_start).astype(f32)
-    freqs = rope_base ** (-jnp.arange(0, ROPE, 2).astype(f32) / ROPE)
-    angles = positions[:, None] * freqs[None, :]
-    angles = jnp.concatenate([angles, angles], axis=1)
-    cosine, sine = jnp.cos(angles), jnp.sin(angles)
-    fill = lambda width, value: jnp.full((length, width), value, f32)
-    tail = LANES - NOPE - ROPE
-    cos_table = jnp.concatenate([fill(NOPE, 1.0), cosine, fill(tail, 0.0)], axis=1)
-    sin_table = jnp.concatenate([fill(NOPE, 0.0), sine, fill(tail, 0.0)], axis=1)
-    same = (segment_all[:, None] == jnp.arange(3, dtype=jnp.int32)[None, :]).astype(f32)
-    query_table = jnp.concatenate(
-        [fill(NOPE + ROPE + 3, 0.0), same * masked_score, fill(tail - 6, 0.0)], axis=1
-    )
-    key_table = jnp.concatenate(
-        [fill(NOPE + ROPE, 0.0), fill(3, 1.0), 1.0 - same, fill(tail - 6, 0.0)], axis=1
-    )
-    first_row = c * rows + t * half
-    own_cos = lax.dynamic_slice_in_dim(cosine, first_row, half)
-    own_sin = lax.dynamic_slice_in_dim(sine, first_row, half)
     turned = jnp.asarray(turn_matrix(), f32)
 
     gain_in = gain_attn.astype(f32)[None]
@@ -980,16 +998,18 @@
         [
             tokens[0],
             cotangent[0],
+            segments,
+            jnp.asarray(frequencies(ROPE, 0)),
             gain_in,
             gain_query,
             gain_latent,
             w_qa,
             w_kva,
-            own_cos,
-            own_sin,
             turned,
         ],
         [
+            half_of(ROPE, f32),
+            half_of(ROPE, f32),
             half_of(width, bf16),
             half_of(lat_width, bf16),
             half_of(qrank, f32),
@@ -1002,22 +1022,21 @@
         [pltpu.VMEM((half, width), bf16)] * 2,
         flops=2 * half * width * (qrank + kvrank),
     )
-    _, latents, q_latent, kv_latent, own_tokens, own_cotangent, grad_mlp = outs[:7]
-    normed_parts = outs[7:]
+    own_cos, own_sin, _, latents, q_latent, kv_latent, own_tokens, own_cotangent, grad_mlp = outs[:9]
+    normed_parts = outs[9:]
     lat_parts = along_ctx(latents)
-    tables = (cos_table, sin_table, query_table, key_table)
 
     out_parts[0] = after(out_parts[0], latents)
     own_out = stack_blocks(out_parts, 2)[0]
-    down_parts[0] = after(down_parts[0], own_out, wide_qb, wide_kvb, *tables)
+    down_parts[0] = after(down_parts[0], own_out, wide_qb, wide_kvb)
     down = gather_weights(down_parts)
     out_pieces = gather_dp(after(own_out, down_parts[1], down_parts[2], down_parts[3]))
     lat_parts[0] = after(lat_parts[0], out_pieces[1])
     lat_own = jnp.stack(lat_parts)
     lat_oth = swap(lat_own)
     pair_parts = weight_parts(after(w_gate, out_pieces[2]), w_up)
-    o_own, o_oth, q_rot, keys, values, qn, kvn = attend(
-        nt, ids, lat_own, lat_oth, after(wide_qb, out_pieces[2]), wide_kvb, *tables
+    o_own, o_oth, q_rot, keys, values, qn, kvn, cos_table, sin_table = attend(
+        nt, ids, lat_own, lat_oth, after(wide_qb, out_pieces[2]), wide_kvb, segments
     )
     out_pieces[0] = after(out_pieces[0], o_own)
     full_out = plain(

time: 756 us -> 751 us (level)
  waiting for transfers between devices: 289 us -> 299 us
    ppermute x85, waiting for transfers between devices: 230 us -> 241 us  [exchange(): return lax.ppermute(value, axis, [(i, i ^ step) for i in range(size)])]
    unnamed x230 -> x228, local copies, waits for them, and re-layouts: 28.9 us -> 27.2 us
  transfers between devices with their start and end apart: 107 -> 107, of which waited for: 45 -> 49; matrix products, arithmetic and copies ran while one was open for 9% -> 8% of each run, Pallas kernels for 25% -> 25%
where the time goes in v4:
time: 751 us; the launch traced here: 742 us
  waiting for transfers between devices  299 us (40%)
  Pallas kernels  201 us (27%)
  starting transfers between devices  143 us (19%)
  local copies, waits for them, and re-layouts  43.5 us (6%)
  other arithmetic  33.6 us (4%)
  between operations  16 us (2%)
    ppermute x85, waiting for transfers between devices, exchange(): return lax.ppermute(value, axis, [(i, i ^ step) for i in range(size)])  241 us
    ppermute x85, starting transfers between devices, exchange(): return lax.ppermute(value, axis, [(i, i ^ step) for i in range(size)])  84.9 us
    pallas_call x22, Pallas kernels, plain(): pl.pallas_call(kernel, in_specs=[SCALARS] + [LOCAL] * len(operands), out_...  54 us
    pallas_call x2, Pallas kernels, feed_forward(): pl.pallas_call(mlp_kernel, grid=(rows // block,), in_specs=[part_of] * 4...  47.8 us
    ppermute x5, waiting for transfers between devices, scatter_dp(): far = lax.ppermute(parts[3], 'dp', [(0, 1), (3, 2)])  27.7 us
    unnamed x228, local copies, waits for them, and re-layouts  27.2 us
    pallas_call x1, Pallas kernels, attend(): pl.pallas_call(functools.partial(forward_kernel, nt), grid_spec=pltpu.Pre...  23.7 us
    pallas_call x2, Pallas kernels, products(): pl.pallas_call(functools.partial(product_kernel, len(lefts), count), grid...  23.1 us
  transfers between devices with their start and end apart: 107, of which 49 were waited for; matrix products, arithmetic and copies ran while one was open for 8% of the time, Pallas kernels for 25%

profile of v4, /device:TPU:12, one launch (start us, length us, event | category | flops | bytes accessed | tf_op | source)
XLA Modules:
  0.0 742.3 jit_solution(4312484150240864859)
XLA Ops:
  25.2 3.8 convolution_convert_fusion.wq_ref.wq
  29.2 5.6 shard_map.308
  36.8 4.2 collective-permute-done.4.refs_2_
  41.0 4.7 collective-permute-done.5.refs_3_
  50.1 5.3 collective-permute-done.7
  57.7 5.7 collective-permute-done.10
  66.4 4.0 collective-permute-start.14
  70.4 18.1 %collective-permute-done.12.refs_2_ = bf16[4,160,320]{2,1,0:T(8,128)(2,1)S(1)} collective-permute-done((bf16[4,160,320]{2,1,0:T(8,128)(2,1)S(1)}, bf16[4,160,320]{2,1,0:T(8,128)(2,1)S(1)}, u32[]{:S(2)}, u32[]{:S(2)}) %collective-permute-start.12) | collective-permute-done | bytes 409632 | tf_op jit(solution)/shard_map/ppermute | solution.py:44
  88.5 6.5 collective-permute-start.13
  95.0 2.8 shard_map.316
  102.9 13.5 %collective-permute-done.13 = bf16[4,160,320]{2,1,0:T(8,128)(2,1)} collective-permute-done((bf16[4,160,320]{2,1,0:T(8,128)(2,1)S(1)}, bf16[4,160,320]{2,1,0:T(8,128)(2,1)}, u32[]{:S(2)}, u32[]{:S(2)}) %collective-permute-start.13) | collective-permute-done | bytes 409632 | tf_op jit(solution)/shard_map/ppermute | solution.py:909
  118.8 23.7 %shard_map.312 = (bf16[4,128,640]{2,1,0:T(8,128)(2,1)S(1)}, bf16[4,128,640]{2,1,0:T(8,128)(2,1)S(1)}, bf16[1024,640]{1,0:T(8,128)(2,1)}, bf16[1024,640]{1,0:T(8,...) custom-call(s32[3]{0:T(128)S(1)} %pad_add_fusion.ids, ...), custom_call_target="tpu_custom_call" | custom-call | flops 671088640 | bytes 1048576 | tf_op jit(solution)/shard_map/pallas_call | solution.py:376
  148.2 7.9 %shard_map.314 = (f32[4,128,2560]{2,1,0:T(8,128)}, bf16[4,128,2560]{2,1,0:T(8,128)(2,1)S(1)}) custom-call(bf16[4,128,640]{2,1,0:T(8,128)(2,1)S(1)} %get-tuple-element.126.own.oown_ref.oown, bf16[4,128,640]{2,1,0:T(8,128)(2,1)S(1)} %get-tuple-element.127.oth.ooth_ref.ooth, bf16[2560,640]{1,0:T(8,128)(2,1)} %bitcast.165), custom_call_target="tpu_custom_call" | custom-call | flops 335544320 | bytes 2424832 | tf_op jit(solution)/shard_map/pallas_call | solution.py:493
  157.6 3.2 shard_map.317
  166.2 2.9 collective-permute-start.35
  169.1 5.2 add_convert_fusion
  176.8 14.8 %collective-permute-done.18 = bf16[64,2560]{1,0:T(8,128)(2,1)S(1)} collective-permute-done((bf16[64,2560]{1,0:T(8,128)(2,1)S(1)}, bf16[64,2560]{1,0:T(8,128)(2,1)S(1)}, u32[]{:S(2)}, u32[]{:S(2)}) %collective-permute-start.18) | collective-permute-done | bytes 327712 | tf_op jit(solution)/shard_map/ppermute | solution.py:44
  194.4 24.8 %collective-permute-done.17.refs_1_ = bf16[128,2560]{1,0:T(8,128)(2,1)S(1)} collective-permute-done((bf16[128,2560]{1,0:T(8,128)(2,1)S(1)}, bf16[128,2560]{1,0:T(8,128)(2,1)S(1)}, u32[]{:S(2)}, u32[]{:S(2)}) %collective-permute-start.17) | collective-permute-done | bytes 655392 | tf_op jit(solution)/shard_map/ppermute | solution.py:44
  222.0 3.4 collective-permute-start.34
  227.1 20.5 %collective-permute-done.24 = bf16[128,2560]{1,0:T(8,128)(2,1)S(1)} collective-permute-done((bf16[128,2560]{1,0:T(8,128)(2,1)}, bf16[128,2560]{1,0:T(8,128)(2,1)S(1)}, u32[]{:S(2)}, u32[]{:S(2)}) %collective-permute-start.24) | collective-permute-done | bytes 655392 | tf_op jit(solution)/shard_map/ppermute | solution.py:44
  247.8 4.0 collective-permute-start.31
  251.8 3.5 collective-permute-done.29
  255.3 6.1 collective-permute-start.30
  261.4 3.9 collective-permute-done.34
  266.3 10.0 %all-gather.3.cloned.1.call-done.pair_hbm = bf16[5120,800]{1,0:T(8,128)(2,1)} async-done(((bf16[1280,800]{1,0:T(8,128)(2,1)}), bf16[5120,800]{1,0:T(8,128)(2,1)}) %all-gather.3.cloned.1.call-update) | async-done | bytes 8192016 | tf_op jit(solution)/shard_map/all_gather | solution.py:957
  276.3 23.8 %shard_map.319 = (bf16[2,256,800]{2,1,0:T(8,128)(2,1)}, bf16[2,256,800]{2,1,0:T(8,128)(2,1)}, bf16[2,256,800]{2,1,0:T(8,128)(2,1)}, bf16[256,2560]{1,0:T(8,128)(...) custom-call(bf16[256,2560]{1,0:T(8,128)(2,1)} %copy-done.5, ...), custom_call_target="tpu_custom_call" | custom-call | flops 1258291200 | bytes 2277376 | tf_op jit(solution)/shard_map/pallas_call | solution.py:612
  307.5 24.1 %shard_map.320 = (bf16[2,256,800]{2,1,0:T(8,128)(2,1)}, bf16[2,256,800]{2,1,0:T(8,128)(2,1)}, bf16[2,256,800]{2,1,0:T(8,128)(2,1)}, bf16[256,2560]{1,0:T(8,128)(...) custom-call(bf16[256,2560]{1,0:T(8,128)(2,1)} %copy-done.92, ...), custom_call_target="tpu_custom_call" | custom-call | flops 1258291200 | bytes 2277376 | tf_op jit(solution)/shard_map/pallas_call | solution.py:612
  332.8 8.6 %shard_map.339 = bf16[2560,800]{1,0:T(8,128)(2,1)} custom-call(bf16[256,2560]{1,0:T(8,128)(2,1)S(1)} %copy-done.8, bf16[256,2560]{1,0:T(8,128)(2,1)} %collective-permute-done.26.gm_oth.refs_1_, bf16[256,2560]{1,0:T(8,128)(2,1)} %pad_maximum_fusion.3.gm_own.refs_2_, bf16[256,2560]{1,0:T(8,128)(2,1)} %collective-permute-done.36.gm_oth.refs_3_, ...), custom_call_target="tpu_custom_call" | custom-call | flops 419430400 | bytes 933888 | tf_op jit(solution)/shard_map/pallas_call | solution.py:649
  341.6 3.1 collective-permute-done.37
  348.2 3.8 collective-permute-start.38
  352.0 13.5 %collective-permute-done.40 = bf16[128,2560]{1,0:T(8,128)(2,1)S(1)} collective-permute-done((bf16[128,2560]{1,0:T(8,128)(2,1)S(1)}, bf16[128,2560]{1,0:T(8,128)(2,1)S(1)}, u32[]{:S(2)}, u32[]{:S(2)}) %collective-permute-start.40) | collective-permute-done | bytes 655392 | tf_op jit(solution)/shard_map/ppermute | solution.py:915
  368.1 14.5 %shard_map.321 = bf16[5120,800]{1,0:T(8,128)(2,1)} custom-call(bf16[256,2560]{1,0:T(8,128)(2,1)S(1)} %copy-done.6, bf16[256,2560]{1,0:T(8,128)(2,1)} %collective-permute-done.25.nm_oth.refs_1_, bf16[256,2560]{1,0:T(8,128)(2,1)} %copy-done.92, bf16[256,2560]{1,0:T(8,128)(2,1)} %collective-permute-done.32.nm_oth.refs_3_, bf16[512,800]{1,0:T(8,128)(2,1)S(1)} %bitcast.184, ...), custom_call_target="tpu_custom_call" | custom-call | flops 838860800 | bytes 1343488 | tf_op jit(solution)/shard_map/pallas_call | solution.py:649
  382.6 12.4 %collective-permute-done.41.refs_2_ = bf16[128,2560]{1,0:T(8,128)(2,1)} collective-permute-done((bf16[128,2560]{1,0:T(8,128)(2,1)}, bf16[128,2560]{1,0:T(8,128)(2,1)}, u32[]{:S(2)}, u32[]{:S(2)}) %collective-permute-start.41) | collective-permute-done | bytes 655392 | tf_op jit(solution)/shard_map/ppermute | solution.py:44
  396.2 3.2 shard_map.322
  401.5 12.9 %collective-permute-done.42 = bf16[128,2560]{1,0:T(8,128)(2,1)S(1)} collective-permute-done((bf16[128,2560]{1,0:T(8,128)(2,1)S(1)}, bf16[128,2560]{1,0:T(8,128)(2,1)S(1)}, u32[]{:S(2)}, u32[]{:S(2)}) %collective-permute-start.42) | collective-permute-done | bytes 655392 | tf_op jit(solution)/shard_map/ppermute | solution.py:44
  417.3 4.5 collective-permute-done.45
  423.4 2.8 collective-permute-done.27
  434.1 6.8 shard_map.323
  440.9 15.9 %shard_map.324 = (bf16[1024,1280]{1,0:T(8,128)(2,1)}, bf16[1024,1280]{1,0:T(8,128)(2,1)}) custom-call(s32[3]{0:T(128)S(1)} %pad_add_fusion.ids, bf16[1024,640]{1,0:T(8,128)(2,1)S(1)} %copy-done.34, bf16[1024,640]{1,0:T(8,128)(2,1)} %get-tuple-element.163.k_ref, bf16[1024,640]{1,0:T(8,128)(2,1)} %get-tuple-element.164.v_ref, ...), custom_call_target="tpu_custom_call" | custom-call | flops 536870912 | bytes 1572864 | tf_op jit(solution)/shard_map/pallas_call | solution.py:410
  456.8 7.7 %shard_map.327 = (f32[4,128,1152]{2,1,0:T(8,128)}, bf16[4,128,1152]{2,1,0:T(8,128)(2,1)S(1)}) custom-call(s32[3]{0:T(128)S(1)} %pad_add_fusion.ids, bf16[1024,1280]{1,0:T(8,128)(2,1)} %get-tuple-element.169.gq, bf16[1024,1280]{1,0:T(8,128)(2,1)} %get-tuple-element.176.gkv, bf16[768,1280]{1,0:T(8,128)(2,1)S(1)} %copy-done.11, bf16[384,1280]{1,0:T(8,128)(2,1)S(1)} %copy-done.4), custom_call_target="tpu_custom_call" | custom-call | flops 301989888 | bytes 1114112 | tf_op jit(solution)/shard_map/pallas_call | solution.py:725
  465.7 4.7 collective-permute-start.51
  475.9 6.8 shard_map.328
  488.4 4.6 collective-permute-done.55.refs_1_
  494.4 7.3 shard_map.329
  508.6 4.3 collective-permute-done.50.refs_2_
  520.7 4.3 shard_map.331
  527.3 4.5 collective-permute-done.71
  536.5 10.1 %collective-permute-done.78 = bf16[256,640]{1,0:T(8,128)(2,1)S(1)} collective-permute-done((bf16[256,640]{1,0:T(8,128)(2,1)S(1)}, bf16[256,640]{1,0:T(8,128)(2,1)S(1)}, u32[]{:S(2)}, u32[]{:S(2)}) %collective-permute-start.78) | collective-permute-done | bytes 327712 | tf_op jit(solution)/shard_map/ppermute | solution.py:44
  549.4 2.9 collective-permute-start.83
  565.7 4.5 collective-permute-start.84
  586.2 2.9 shard_map.333
  589.1 5.5 collective-permute-done.82
  600.6 3.9 collective-permute-done.63
  607.2 14.1 %collective-permute-done.74 = bf16[160,640]{1,0:T(8,128)(2,1)} collective-permute-done((bf16[160,640]{1,0:T(8,128)(2,1)S(1)}, bf16[160,640]{1,0:T(8,128)(2,1)}, u32[]{:S(2)}, u32[]{:S(2)}) %collective-permute-start.74) | collective-permute-done | bytes 204832 | tf_op jit(solution)/shard_map/ppermute | solution.py:915
  624.7 3.3 collective-permute-start.76
  642.7 12.0 %collective-permute-start.94 = (bf16[1,160,320]{2,1,0:T(8,128)(2,1)S(1)}, bf16[1,160,320]{2,1,0:T(8,128)(2,1)S(1)}, u32[]{:S(2)}, u32[]{:S(2)}) collective-permute-start(bf16[1,160,320]{2,1,0:T(8,128)(2,1)S(1)} %get-tuple-element.250), channel_id=1, source_target_pairs={{0,1},{1,0},{2,3},{3,2},{4,5},{5,4},{6,7},{7,6},{8,9},{9,8},{10,11... | collective-permute-start | bytes 307208 | tf_op jit(solution)/shard_map/ppermute | solution.py:44
  654.8 4.6 collective-permute-done.101.refs_2_
  660.6 6.0 collective-permute-done.102.refs_3_
  683.3 2.9 pad_maximum_fusion.source
  686.2 5.0 shard_map.336
  691.2 12.1 %collective-permute-done.97.refs_1_ = bf16[2,160,800]{2,1,0:T(8,128)(2,1)S(1)} collective-permute-done((bf16[2,160,800]{2,1,0:T(8,128)(2,1)S(1)}, bf16[2,160,800]{2,1,0:T(8,128)(2,1)S(1)}, u32[]{:S(2)}, u32[]{:S(2)}) %collective-permute-start.97) | collective-permute-done | bytes 512032 | tf_op jit(solution)/shard_map/ppermute | solution.py:44
  703.3 15.7 %collective-permute-done.98.refs_2_ = bf16[2,160,800]{2,1,0:T(8,128)(2,1)S(1)} collective-permute-done((bf16[2,160,800]{2,1,0:T(8,128)(2,1)S(1)}, bf16[2,160,800]{2,1,0:T(8,128)(2,1)S(1)}, u32[]{:S(2)}, u32[]{:S(2)}) %collective-permute-start.98) | collective-permute-done | bytes 512032 | tf_op jit(solution)/shard_map/ppermute | solution.py:44
  719.0 12.9 %collective-permute-done.99.refs_3_ = bf16[2,160,800]{2,1,0:T(8,128)(2,1)S(1)} collective-permute-done((bf16[2,160,800]{2,1,0:T(8,128)(2,1)S(1)}, bf16[2,160,800]{2,1,0:T(8,128)(2,1)S(1)}, u32[]{:S(2)}, u32[]{:S(2)}) %collective-permute-start.99) | collective-permute-done | bytes 512032 | tf_op jit(solution)/shard_map/ppermute | solution.py:44
  731.9 3.3 shard_map.338
  (499 shorter events, 202.5 us)
Async XLA Ops:
  7.2 259.1 %all-gather.5.cloned.1.call-start = ((), (), s32[]{:S(2)}) async-start(), calls=%async_computation.3 | async-start | bytes 5734400 | tf_op jit(solution)/shard_map/all_gather | solution.py:957
  12.2 23.2 %collective-permute-start.1 = (bf16[1,160,320]{2,1,0:T(8,128)(2,1)}, bf16[1,160,320]{2,1,0:T(8,128)(2,1)}, u32[]{:S(2)}, u32[]{:S(2)}) collective-permute-start(bf16[1,160,320]{2,1,0:T(8,128)(2,1)} %get-tuple-element.118), channel_id=1, source_target_pairs={{0,2},{1,3},{2,0},{3,1},{4,6},{5,7},{6,4},{7,5},{8,10},{9,11},{10,... | collective-permute-start | bytes 307208 | tf_op jit(solution)/shard_map/ppermute | solution.py:44
  12.7 22.7 %collective-permute-start.2 = (bf16[1,160,320]{2,1,0:T(8,128)(2,1)}, bf16[1,160,320]{2,1,0:T(8,128)(2,1)}, u32[]{:S(2)}, u32[]{:S(2)}) collective-permute-start(bf16[1,160,320]{2,1,0:T(8,128)(2,1)} %get-tuple-element.119), channel_id=1, source_target_pairs={{0,3},{1,2},{2,1},{3,0},{4,7},{5,6},{6,5},{7,4},{8,11},{9,10},{10,... | collective-permute-start | bytes 307208 | tf_op jit(solution)/shard_map/ppermute | solution.py:44
  18.1 18.7 %collective-permute-start.3 = (bf16[1,160,800]{2,1,0:T(8,128)(2,1)}, bf16[1,160,800]{2,1,0:T(8,128)(2,1)}, u32[]{:S(2)}, u32[]{:S(2)}) collective-permute-start(bf16[1,160,800]{2,1,0:T(8,128)(2,1)} %get-tuple-element.120), channel_id=1, source_target_pairs={{0,4},{4,0},{8,12},{12,8},{1,5},{5,1},{9,13},{13,9},{2,6},{6,2},{1... | collective-permute-start | bytes 768008 | tf_op jit(solution)/shard_map/ppermute | solution.py:44
  18.5 22.5 %collective-permute-start.4 = (bf16[1,160,800]{2,1,0:T(8,128)(2,1)}, bf16[1,160,800]{2,1,0:T(8,128)(2,1)}, u32[]{:S(2)}, u32[]{:S(2)}) collective-permute-start(bf16[1,160,800]{2,1,0:T(8,128)(2,1)} %get-tuple-element.121), channel_id=1, source_target_pairs={{0,8},{4,12},{8,0},{12,4},{1,9},{5,13},{9,1},{13,5},{2,10},{6,14},... | collective-permute-start | bytes 768008 | tf_op jit(solution)/shard_map/ppermute | solution.py:44
  24.7 21.0 %collective-permute-start.5 = (bf16[1,160,800]{2,1,0:T(8,128)(2,1)}, bf16[1,160,800]{2,1,0:T(8,128)(2,1)S(1)}, u32[]{:S(2)}, u32[]{:S(2)}) collective-permute-start(bf16[1,160,800]{2,1,0:T(8,128)(2,1)} %copy-done.87), channel_id=1, source_target_pairs={{0,12},{4,8},{8,4},{12,0},{1,13},{5,9},{9,5},{13,1},{2,14},{6,10},... | collective-permute-start | bytes 768008 | tf_op jit(solution)/shard_map/ppermute | solution.py:44
  47.9 228.3 %all-gather.3.cloned.1.call-start = ((), (), s32[]{:S(2)}) async-start(), calls=%async_computation.2 | async-start | bytes 11468800 | tf_op jit(solution)/shard_map/all_gather | solution.py:957
  66.2 51.3 %collective-permute-start.11 = (bf16[4,128,1152]{2,1,0:T(8,128)(2,1)S(1)}, bf16[4,128,1152]{2,1,0:T(8,128)(2,1)}, u32[]{:S(2)}, u32[]{:S(2)}) collective-permute-start(bf16[4,128,1152]{2,1,0:T(8,128)(2,1)S(1)} %pad_maximum_fusion.4.own_ref), channel_id=1, source_target_pairs={{0,16},{16,0},{1,17},{17,1},{2,18},{18,2},{3,19},{19,3},{4,20},{20... | collective-permute-start | bytes 3538952 | tf_op jit(solution)/shard_map/ppermute | solution.py:44
  66.3 22.2 %collective-permute-start.12 = (bf16[4,160,320]{2,1,0:T(8,128)(2,1)S(1)}, bf16[4,160,320]{2,1,0:T(8,128)(2,1)S(1)}, u32[]{:S(2)}, u32[]{:S(2)}) collective-permute-start(bf16[4,160,320]{2,1,0:T(8,128)(2,1)S(1)} %bitcast.177), channel_id=1, source_target_pairs={{0,8},{4,12},{8,0},{12,4},{1,9},{5,13},{9,1},{13,5},{2,10},{6,14},... | collective-permute-start | bytes 1228808 | tf_op jit(solution)/shard_map/ppermute | solution.py:44
  66.4 34.7 %collective-permute-start.14 = (bf16[4,160,320]{2,1,0:T(8,128)(2,1)S(1)}, bf16[4,160,320]{2,1,0:T(8,128)(2,1)S(1)}, u32[]{:S(2)}, u32[]{:S(2)}) collective-permute-start(bf16[4,160,320]{2,1,0:T(8,128)(2,1)S(1)} %bitcast.178), channel_id=1, source_target_pairs={{4,8},{8,4},{5,9},{9,5},{6,10},{10,6},{7,11},{11,7},{20,24},{24,20... | collective-permute-start | bytes 1228808 | tf_op jit(solution)/shard_map/ppermute | solution.py:908
  88.5 27.9 %collective-permute-start.13 = (bf16[4,160,320]{2,1,0:T(8,128)(2,1)S(1)}, bf16[4,160,320]{2,1,0:T(8,128)(2,1)}, u32[]{:S(2)}, u32[]{:S(2)}) collective-permute-start(bf16[4,160,320]{2,1,0:T(8,128)(2,1)S(1)} %collective-permute-done.12.refs_2_), channel_id=1, source_target_pairs={{4,0},{8,12},{5,1},{9,13},{6,2},{10,14},{7,3},{11,15},{20,16},{24,... | collective-permute-start | bytes 1228808 | tf_op jit(solution)/shard_map/ppermute | solution.py:909
  98.6 59.0 %collective-permute-start.20 = (bf16[2,160,800]{2,1,0:T(8,128)(2,1)}, bf16[2,160,800]{2,1,0:T(8,128)(2,1)}, u32[]{:S(2)}, u32[]{:S(2)}) collective-permute-start(bf16[2,160,800]{2,1,0:T(8,128)(2,1)} %get-tuple-element.135), channel_id=1, source_target_pairs={{0,4},{4,0},{8,12},{12,8},{1,5},{5,1},{9,13},{13,9},{2,6},{6,2},{1... | collective-permute-start | bytes 1536008 | tf_op jit(solution)/shard_map/ppermute | solution.py:44
  98.6 59.0 %collective-permute-start.21 = (bf16[2,160,800]{2,1,0:T(8,128)(2,1)}, bf16[2,160,800]{2,1,0:T(8,128)(2,1)}, u32[]{:S(2)}, u32[]{:S(2)}) collective-permute-start(bf16[2,160,800]{2,1,0:T(8,128)(2,1)} %get-tuple-element.136), channel_id=1, source_target_pairs={{0,8},{4,12},{8,0},{12,4},{1,9},{5,13},{9,1},{13,5},{2,10},{6,14},... | collective-permute-start | bytes 1536008 | tf_op jit(solution)/shard_map/ppermute | solution.py:44
  101.9 55.7 %collective-permute-start.22 = (bf16[2,160,800]{2,1,0:T(8,128)(2,1)}, bf16[2,160,800]{2,1,0:T(8,128)(2,1)}, u32[]{:S(2)}, u32[]{:S(2)}) collective-permute-start(bf16[2,160,800]{2,1,0:T(8,128)(2,1)} %get-tuple-element.137), channel_id=1, source_target_pairs={{0,12},{4,8},{8,4},{12,0},{1,13},{5,9},{9,5},{13,1},{2,14},{6,10},... | collective-permute-start | bytes 1536008 | tf_op jit(solution)/shard_map/ppermute | solution.py:44
  160.8 446.3 %reduce-scatter.5.cloned.1.call-start = ((), (), s32[]{:S(2)}) async-start(), calls=%async_computation.5 | async-start | bytes 5734400 | tf_op jit(solution)/shard_map/reduce_scatter | solution.py:960
  163.0 58.3 %collective-permute-start.23 = (bf16[128,2560]{1,0:T(8,128)(2,1)}, bf16[128,2560]{1,0:T(8,128)(2,1)S(1)}, u32[]{:S(2)}, u32[]{:S(2)}) collective-permute-start(bf16[128,2560]{1,0:T(8,128)(2,1)} %get-tuple-element.138), channel_id=1, source_target_pairs={{0,4},{4,0},{8,12},{12,8},{1,5},{5,1},{9,13},{13,9},{2,6},{6,2},{1... | collective-permute-start | bytes 1966088 | tf_op jit(solution)/shard_map/ppermute | solution.py:44
  165.7 56.3 %collective-permute-start.33 = (bf16[128,2560]{1,0:T(8,128)(2,1)}, bf16[128,2560]{1,0:T(8,128)(2,1)S(1)}, u32[]{:S(2)}, u32[]{:S(2)}) collective-permute-start(bf16[128,2560]{1,0:T(8,128)(2,1)} %get-tuple-element.138), channel_id=1, source_target_pairs={{0,8},{4,12},{8,0},{12,4},{1,9},{5,13},{9,1},{13,5},{2,10},{6,14},... | collective-permute-start | bytes 1966088 | tf_op jit(solution)/shard_map/ppermute | solution.py:44
  166.2 81.6 %collective-permute-start.35 = (bf16[128,2560]{1,0:T(8,128)(2,1)}, bf16[128,2560]{1,0:T(8,128)(2,1)S(1)}, u32[]{:S(2)}, u32[]{:S(2)}) collective-permute-start(bf16[128,2560]{1,0:T(8,128)(2,1)} %get-tuple-element.138), channel_id=1, source_target_pairs={{4,8},{8,4},{5,9},{9,5},{6,10},{10,6},{7,11},{11,7},{20,24},{24,20... | collective-permute-start | bytes 1966088 | tf_op jit(solution)/shard_map/ppermute | solution.py:908
  174.4 17.2 %collective-permute-start.18 = (bf16[64,2560]{1,0:T(8,128)(2,1)S(1)}, bf16[64,2560]{1,0:T(8,128)(2,1)S(1)}, u32[]{:S(2)}, u32[]{:S(2)}) collective-permute-start(bf16[64,2560]{1,0:T(8,128)(2,1)S(1)} %get-tuple-element.216), channel_id=1, source_target_pairs={{0,1},{1,0},{2,3},{3,2},{4,5},{5,4},{6,7},{7,6},{8,9},{9,8},{10,11... | collective-permute-start | bytes 983048 | tf_op jit(solution)/shard_map/ppermute | solution.py:44
  174.7 17.0 %collective-permute-start.16 = (bf16[64,2560]{1,0:T(8,128)(2,1)S(1)}, bf16[64,2560]{1,0:T(8,128)(2,1)S(1)}, u32[]{:S(2)}, u32[]{:S(2)}) collective-permute-start(bf16[64,2560]{1,0:T(8,128)(2,1)S(1)} %get-tuple-element.218), channel_id=1, source_target_pairs={{0,2},{1,3},{2,0},{3,1},{4,6},{5,7},{6,4},{7,5},{8,10},{9,11},{10,... | collective-permute-start | bytes 983048 | tf_op jit(solution)/shard_map/ppermute | solution.py:44
  192.0 27.2 %collective-permute-start.17 = (bf16[128,2560]{1,0:T(8,128)(2,1)S(1)}, bf16[128,2560]{1,0:T(8,128)(2,1)S(1)}, u32[]{:S(2)}, u32[]{:S(2)}) collective-permute-start(bf16[128,2560]{1,0:T(8,128)(2,1)S(1)} %pad_maximum_fusion.6), channel_id=1, source_target_pairs={{0,1},{1,0},{2,3},{3,2},{4,5},{5,4},{6,7},{7,6},{8,9},{9,8},{10,11... | collective-permute-start | bytes 1966088 | tf_op jit(solution)/shard_map/ppermute | solution.py:44
  193.8 25.4 %collective-permute-start.19 = (bf16[128,2560]{1,0:T(8,128)(2,1)S(1)}, bf16[128,2560]{1,0:T(8,128)(2,1)S(1)}, u32[]{:S(2)}, u32[]{:S(2)}) collective-permute-start(bf16[128,2560]{1,0:T(8,128)(2,1)S(1)} %pad_maximum_fusion.7), channel_id=1, source_target_pairs={{0,2},{1,3},{2,0},{3,1},{4,6},{5,7},{6,4},{7,5},{8,10},{9,11},{10,... | collective-permute-start | bytes 1966088 | tf_op jit(solution)/shard_map/ppermute | solution.py:44
  221.3 26.3 %collective-permute-start.24 = (bf16[128,2560]{1,0:T(8,128)(2,1)}, bf16[128,2560]{1,0:T(8,128)(2,1)S(1)}, u32[]{:S(2)}, u32[]{:S(2)}) collective-permute-start(bf16[128,2560]{1,0:T(8,128)(2,1)} %get-tuple-element.139), channel_id=1, source_target_pairs={{0,4},{4,0},{8,12},{12,8},{1,5},{5,1},{9,13},{13,9},{2,6},{6,2},{1... | collective-permute-start | bytes 1966088 | tf_op jit(solution)/shard_map/ppermute | solution.py:44
  221.9 44.4 %collective-permute-start.26 = (bf16[256,2560]{1,0:T(8,128)(2,1)S(1)}, bf16[256,2560]{1,0:T(8,128)(2,1)}, u32[]{:S(2)}, u32[]{:S(2)}) collective-permute-start(bf16[256,2560]{1,0:T(8,128)(2,1)S(1)} %constant_dynamic-update-slice_fusion.2.gm_own.refs_0_), channel_id=1, source_target_pairs={{0,16},{16,0},{1,17},{17,1},{2,18},{18,2},{3,19},{19,3},{4,20},{20... | collective-permute-start | bytes 3932168 | tf_op jit(solution)/shard_map/ppermute | solution.py:44
  222.0 43.3 %collective-permute-start.34 = (bf16[128,2560]{1,0:T(8,128)(2,1)S(1)}, bf16[128,2560]{1,0:T(8,128)(2,1)S(1)}, u32[]{:S(2)}, u32[]{:S(2)}) collective-permute-start(bf16[128,2560]{1,0:T(8,128)(2,1)S(1)} %collective-permute-done.33), channel_id=1, source_target_pairs={{4,0},{8,12},{5,1},{9,13},{6,2},{10,14},{7,3},{11,15},{20,16},{24,... | collective-permute-start | bytes 1966088 | tf_op jit(solution)/shard_map/ppermute | solution.py:909
  225.5 29.8 %collective-permute-start.29 = (bf16[128,2560]{1,0:T(8,128)(2,1)}, bf16[128,2560]{1,0:T(8,128)(2,1)}, u32[]{:S(2)}, u32[]{:S(2)}) collective-permute-start(bf16[128,2560]{1,0:T(8,128)(2,1)} %get-tuple-element.139), channel_id=1, source_target_pairs={{0,8},{4,12},{8,0},{12,4},{1,9},{5,13},{9,1},{13,5},{2,10},{6,14},... | collective-permute-start | bytes 1966088 | tf_op jit(solution)/shard_map/ppermute | solution.py:44
  247.7 18.6 %collective-permute-start.25 = (bf16[256,2560]{1,0:T(8,128)(2,1)S(1)}, bf16[256,2560]{1,0:T(8,128)(2,1)}, u32[]{:S(2)}, u32[]{:S(2)}) collective-permute-start(bf16[256,2560]{1,0:T(8,128)(2,1)S(1)} %constant_dynamic-update-slice_fusion.nm_own.refs_0_), channel_id=1, source_target_pairs={{0,16},{16,0},{1,17},{17,1},{2,18},{18,2},{3,19},{19,3},{4,20},{20... | collective-permute-start | bytes 3932168 | tf_op jit(solution)/shard_map/ppermute | solution.py:44
  247.8 54.0 %collective-permute-start.31 = (bf16[128,2560]{1,0:T(8,128)(2,1)}, bf16[128,2560]{1,0:T(8,128)(2,1)}, u32[]{:S(2)}, u32[]{:S(2)}) collective-permute-start(bf16[128,2560]{1,0:T(8,128)(2,1)} %get-tuple-element.139), channel_id=1, source_target_pairs={{4,8},{8,4},{5,9},{9,5},{6,10},{10,6},{7,11},{11,7},{20,24},{24,20... | collective-permute-start | bytes 1966088 | tf_op jit(solution)/shard_map/ppermute | solution.py:908
  255.3 46.5 %collective-permute-start.30 = (bf16[128,2560]{1,0:T(8,128)(2,1)}, bf16[128,2560]{1,0:T(8,128)(2,1)}, u32[]{:S(2)}, u32[]{:S(2)}) collective-permute-start(bf16[128,2560]{1,0:T(8,128)(2,1)} %collective-permute-done.29), channel_id=1, source_target_pairs={{4,0},{8,12},{5,1},{9,13},{6,2},{10,14},{7,3},{11,15},{20,16},{24,... | collective-permute-start | bytes 1966088 | tf_op jit(solution)/shard_map/ppermute | solution.py:909
  306.3 25.3 %collective-permute-start.39 = (bf16[128,2560]{1,0:T(8,128)(2,1)}, bf16[128,2560]{1,0:T(8,128)(2,1)}, u32[]{:S(2)}, u32[]{:S(2)}) collective-permute-start(bf16[128,2560]{1,0:T(8,128)(2,1)} %get-tuple-element.234), channel_id=1, source_target_pairs={{0,4},{4,0},{8,12},{12,8},{1,5},{5,1},{9,13},{13,9},{2,6},{6,2},{1... | collective-permute-start | bytes 1966088 | tf_op jit(solution)/shard_map/ppermute | solution.py:44
  341.4 335.2 %reduce-scatter.3.cloned.1.call-start = ((), (), s32[]{:S(2)}) async-start(), calls=%async_computation.4 | async-start | bytes 11468800 | tf_op jit(solution)/shard_map/reduce_scatter | solution.py:960
  346.6 18.9 %collective-permute-start.40 = (bf16[128,2560]{1,0:T(8,128)(2,1)S(1)}, bf16[128,2560]{1,0:T(8,128)(2,1)S(1)}, u32[]{:S(2)}, u32[]{:S(2)}) collective-permute-start(bf16[128,2560]{1,0:T(8,128)(2,1)S(1)} %slice.257), channel_id=1, source_target_pairs={{0,4},{12,8},{1,5},{13,9},{2,6},{14,10},{3,7},{15,11},{16,20},{28,... | collective-permute-start | bytes 1966088 | tf_op jit(solution)/shard_map/ppermute | solution.py:915
  348.2 19.1 %collective-permute-start.38 = (bf16[128,2560]{1,0:T(8,128)(2,1)S(1)}, bf16[128,2560]{1,0:T(8,128)(2,1)S(1)}, u32[]{:S(2)}, u32[]{:S(2)}) collective-permute-start(bf16[128,2560]{1,0:T(8,128)(2,1)S(1)} %slice.257), channel_id=1, source_target_pairs={{4,8},{8,4},{5,9},{9,5},{6,10},{10,6},{7,11},{11,7},{20,24},{24,20... | collective-permute-start | bytes 1966088 | tf_op jit(solution)/shard_map/ppermute | solution.py:917
  366.5 28.5 %collective-permute-start.41 = (bf16[128,2560]{1,0:T(8,128)(2,1)}, bf16[128,2560]{1,0:T(8,128)(2,1)}, u32[]{:S(2)}, u32[]{:S(2)}) collective-permute-start(bf16[128,2560]{1,0:T(8,128)(2,1)} %add_convert_fusion.7), channel_id=1, source_target_pairs={{0,8},{4,12},{8,0},{12,4},{1,9},{5,13},{9,1},{13,5},{2,10},{6,14},... | collective-permute-start | bytes 1966088 | tf_op jit(solution)/shard_map/ppermute | solution.py:44
  432.5 39.5 %collective-permute-start.49 = (bf16[128,2560]{1,0:T(8,128)(2,1)}, bf16[128,2560]{1,0:T(8,128)(2,1)S(1)}, u32[]{:S(2)}, u32[]{:S(2)}) collective-permute-start(bf16[128,2560]{1,0:T(8,128)(2,1)} %get-tuple-element.175), channel_id=1, source_target_pairs={{0,4},{12,8},{1,5},{13,9},{2,6},{14,10},{3,7},{15,11},{16,20},{28,... | collective-permute-start | bytes 1966088 | tf_op jit(solution)/shard_map/ppermute | solution.py:915
  465.7 41.5 %collective-permute-start.51 = (bf16[128,2560]{1,0:T(8,128)(2,1)}, bf16[128,2560]{1,0:T(8,128)(2,1)}, u32[]{:S(2)}, u32[]{:S(2)}) collective-permute-start(bf16[128,2560]{1,0:T(8,128)(2,1)} %get-tuple-element.175), channel_id=1, source_target_pairs={{4,8},{8,4},{5,9},{9,5},{6,10},{10,6},{7,11},{11,7},{20,24},{24,20... | collective-permute-start | bytes 1966088 | tf_op jit(solution)/shard_map/ppermute | solution.py:917
  470.4 34.1 %collective-permute-start.47 = (bf16[128,2560]{1,0:T(8,128)(2,1)}, bf16[128,2560]{1,0:T(8,128)(2,1)S(1)}, u32[]{:S(2)}, u32[]{:S(2)}) collective-permute-start(bf16[128,2560]{1,0:T(8,128)(2,1)} %get-tuple-element.171), channel_id=1, source_target_pairs={{0,4},{4,0},{8,12},{12,8},{1,5},{5,1},{9,13},{13,9},{2,6},{6,2},{1... | collective-permute-start | bytes 1966088 | tf_op jit(solution)/shard_map/ppermute | solution.py:44
  473.1 39.8 %collective-permute-start.50 = (bf16[128,2560]{1,0:T(8,128)(2,1)}, bf16[128,2560]{1,0:T(8,128)(2,1)}, u32[]{:S(2)}, u32[]{:S(2)}) collective-permute-start(bf16[128,2560]{1,0:T(8,128)(2,1)} %add_convert_fusion.6), channel_id=1, source_target_pairs={{0,8},{4,12},{8,0},{12,4},{1,9},{5,13},{9,1},{13,5},{2,10},{6,14},... | collective-permute-start | bytes 1966088 | tf_op jit(solution)/shard_map/ppermute | solution.py:44
  485.5 17.5 %collective-permute-start.57 = (bf16[128,1152]{1,0:T(8,128)(2,1)S(1)}, bf16[128,1152]{1,0:T(8,128)(2,1)S(1)}, u32[]{:S(2)}, u32[]{:S(2)}) collective-permute-start(bf16[128,1152]{1,0:T(8,128)(2,1)S(1)} %pad_maximum_fusion.10), channel_id=1, source_target_pairs={{0,2},{1,3},{2,0},{3,1},{4,6},{5,7},{6,4},{7,5},{8,10},{9,11},{10,... | collective-permute-start | bytes 884744 | tf_op jit(solution)/shard_map/ppermute | solution.py:44
  493.1 24.1 %collective-permute-start.79 = (bf16[256,640]{1,0:T(8,128)(2,1)}, bf16[256,640]{1,0:T(8,128)(2,1)}, u32[]{:S(2)}, u32[]{:S(2)}) collective-permute-start(bf16[256,640]{1,0:T(8,128)(2,1)} %get-tuple-element.228), channel_id=1, source_target_pairs={{0,4},{12,8},{1,5},{13,9},{2,6},{14,10},{3,7},{15,11},{16,20},{28,... | collective-permute-start | bytes 983048 | tf_op jit(solution)/shard_map/ppermute | solution.py:915
  503.9 21.2 %collective-permute-start.68 = (bf16[128,1152]{1,0:T(8,128)(2,1)S(1)}, bf16[128,1152]{1,0:T(8,128)(2,1)S(1)}, u32[]{:S(2)}, u32[]{:S(2)}) collective-permute-start(bf16[128,1152]{1,0:T(8,128)(2,1)S(1)} %get-tuple-element.199.lat), channel_id=1, source_target_pairs={{0,1},{1,0},{2,3},{3,2},{4,5},{5,4},{6,7},{7,6},{8,9},{9,8},{10,11... | collective-permute-start | bytes 884744 | tf_op jit(solution)/shard_map/ppermute | solution.py:44
  505.3 21.8 %collective-permute-start.69 = (bf16[128,1152]{1,0:T(8,128)(2,1)S(1)}, bf16[128,1152]{1,0:T(8,128)(2,1)S(1)}, u32[]{:S(2)}, u32[]{:S(2)}) collective-permute-start(bf16[128,1152]{1,0:T(8,128)(2,1)S(1)} %get-tuple-element.199.lat), channel_id=1, source_target_pairs={{0,2},{1,3},{2,0},{3,1},{4,6},{5,7},{6,4},{7,5},{8,10},{9,11},{10,... | collective-permute-start | bytes 884744 | tf_op jit(solution)/shard_map/ppermute | solution.py:44
  507.2 46.4 %collective-permute-start.66 = (bf16[128,640]{1,0:T(8,128)(2,1)}, bf16[128,640]{1,0:T(8,128)(2,1)S(1)}, u32[]{:S(2)}, u32[]{:S(2)}) collective-permute-start(bf16[128,640]{1,0:T(8,128)(2,1)} %get-tuple-element.198), channel_id=1, source_target_pairs={{0,3},{1,2},{2,1},{3,0},{4,7},{5,6},{6,5},{7,4},{8,11},{9,10},{10,... | collective-permute-start | bytes 491528 | tf_op jit(solution)/shard_map/ppermute | solution.py:44
  517.1 45.9 %collective-permute-start.52 = (bf16[128,2560]{1,0:T(8,128)(2,1)S(1)}, bf16[128,2560]{1,0:T(8,128)(2,1)S(1)}, u32[]{:S(2)}, u32[]{:S(2)}) collective-permute-start(bf16[128,2560]{1,0:T(8,128)(2,1)S(1)} %shard_map.325.own), channel_id=1, source_target_pairs={{0,16},{16,0},{1,17},{17,1},{2,18},{18,2},{3,19},{19,3},{4,20},{20... | collective-permute-start | bytes 1966088 | tf_op jit(solution)/shard_map/ppermute | solution.py:44
  517.2 19.2 %collective-permute-start.81 = (bf16[256,640]{1,0:T(8,128)(2,1)}, bf16[256,640]{1,0:T(8,128)(2,1)S(1)}, u32[]{:S(2)}, u32[]{:S(2)}) collective-permute-start(bf16[256,640]{1,0:T(8,128)(2,1)} %get-tuple-element.228), channel_id=1, source_target_pairs={{4,8},{8,4},{5,9},{9,5},{6,10},{10,6},{7,11},{11,7},{20,24},{24,20... | collective-permute-start | bytes 983048 | tf_op jit(solution)/shard_map/ppermute | solution.py:917
  532.8 16.4 %collective-permute-start.80 = (bf16[256,640]{1,0:T(8,128)(2,1)S(1)}, bf16[256,640]{1,0:T(8,128)(2,1)S(1)}, u32[]{:S(2)}, u32[]{:S(2)}) collective-permute-start(bf16[256,640]{1,0:T(8,128)(2,1)S(1)} %fusion.2), channel_id=1, source_target_pairs={{0,8},{4,12},{8,0},{12,4},{1,9},{5,13},{9,1},{13,5},{2,10},{6,14},... | collective-permute-start | bytes 983048 | tf_op jit(solution)/shard_map/ppermute | solution.py:44
  546.5 37.5 %collective-permute-start.72 = (bf16[4,128,1152]{2,1,0:T(8,128)(2,1)S(1)}, bf16[4,128,1152]{2,1,0:T(8,128)(2,1)}, u32[]{:S(2)}, u32[]{:S(2)}) collective-permute-start(bf16[4,128,1152]{2,1,0:T(8,128)(2,1)S(1)} %pad_maximum_fusion.5.gown), channel_id=1, source_target_pairs={{0,16},{16,0},{1,17},{17,1},{2,18},{18,2},{3,19},{19,3},{4,20},{20... | collective-permute-start | bytes 3538952 | tf_op jit(solution)/shard_map/ppermute | solution.py:44
  562.7 20.7 %collective-permute-start.67 = (bf16[4,128,640]{2,1,0:T(8,128)(2,1)}, bf16[4,128,640]{2,1,0:T(8,128)(2,1)}, u32[]{:S(2)}, u32[]{:S(2)}) collective-permute-start(bf16[4,128,640]{2,1,0:T(8,128)(2,1)} %pad_maximum_fusion.8.own), channel_id=1, source_target_pairs={{0,16},{16,0},{1,17},{17,1},{2,18},{18,2},{3,19},{19,3},{4,20},{20... | collective-permute-start | bytes 1966088 | tf_op jit(solution)/shard_map/ppermute | solution.py:44
  571.3 25.7 %collective-permute-start.91 = (bf16[4,160,320]{2,1,0:T(8,128)(2,1)}, bf16[4,160,320]{2,1,0:T(8,128)(2,1)}, u32[]{:S(2)}, u32[]{:S(2)}) collective-permute-start(bf16[4,160,320]{2,1,0:T(8,128)(2,1)} %get-tuple-element.225), channel_id=1, source_target_pairs={{0,4},{12,8},{1,5},{13,9},{2,6},{14,10},{3,7},{15,11},{16,20},{28,... | collective-permute-start | bytes 1228808 | tf_op jit(solution)/shard_map/ppermute | solution.py:915
  575.6 19.1 %collective-permute-start.82 = (bf16[256,640]{1,0:T(8,128)(2,1)S(1)}, bf16[256,640]{1,0:T(8,128)(2,1)}, u32[]{:S(2)}, u32[]{:S(2)}) collective-permute-start(bf16[256,640]{1,0:T(8,128)(2,1)S(1)} %add_convert_fusion.9), channel_id=1, source_target_pairs={{0,4},{4,0},{8,12},{12,8},{1,5},{5,1},{9,13},{13,9},{2,6},{6,2},{1... | collective-permute-start | bytes 983048 | tf_op jit(solution)/shard_map/ppermute | solution.py:44
  580.7 24.5 %collective-permute-start.93 = (bf16[4,160,320]{2,1,0:T(8,128)(2,1)}, bf16[4,160,320]{2,1,0:T(8,128)(2,1)}, u32[]{:S(2)}, u32[]{:S(2)}) collective-permute-start(bf16[4,160,320]{2,1,0:T(8,128)(2,1)} %get-tuple-element.225), channel_id=1, source_target_pairs={{4,8},{8,4},{5,9},{9,5},{6,10},{10,6},{7,11},{11,7},{20,24},{24,20... | collective-permute-start | bytes 1228808 | tf_op jit(solution)/shard_map/ppermute | solution.py:917
  583.4 40.3 %collective-permute-start.90 = (bf16[4,160,320]{2,1,0:T(8,128)(2,1)}, bf16[4,160,320]{2,1,0:T(8,128)(2,1)}, u32[]{:S(2)}, u32[]{:S(2)}) collective-permute-start(bf16[4,160,320]{2,1,0:T(8,128)(2,1)} %get-tuple-element.226), channel_id=1, source_target_pairs={{0,4},{4,0},{8,12},{12,8},{1,5},{5,1},{9,13},{13,9},{2,6},{6,2},{1... | collective-permute-start | bytes 1228808 | tf_op jit(solution)/shard_map/ppermute | solution.py:44
  584.1 20.4 %collective-permute-start.63 = (f32[48,128]{1,0:T(8,128)S(1)}, f32[48,128]{1,0:T(8,128)S(1)}, u32[]{:S(2)}, u32[]{:S(2)}) collective-permute-start(f32[48,128]{1,0:T(8,128)S(1)} %add.151), channel_id=1, source_target_pairs={{0,8},{4,12},{8,0},{12,4},{1,9},{5,13},{9,1},{13,5},{2,10},{6,14},... | collective-permute-start | bytes 73736 | tf_op jit(solution)/shard_map/ppermute | solution.py:44
  595.9 32.1 %collective-permute-start.86 = (bf16[1024,640]{1,0:T(8,128)(2,1)S(1)}, bf16[1024,640]{1,0:T(8,128)(2,1)}, u32[]{:S(2)}, u32[]{:S(2)}) collective-permute-start(bf16[1024,640]{1,0:T(8,128)(2,1)S(1)} %bitcast.173), channel_id=1, source_target_pairs={{0,1},{1,0},{2,3},{3,2},{4,5},{5,4},{6,7},{7,6},{8,9},{9,8},{10,11... | collective-permute-start | bytes 3932168 | tf_op jit(solution)/shard_map/ppermute | solution.py:44
  597.1 31.7 %collective-permute-start.87 = (bf16[1024,640]{1,0:T(8,128)(2,1)S(1)}, bf16[1024,640]{1,0:T(8,128)(2,1)}, u32[]{:S(2)}, u32[]{:S(2)}) collective-permute-start(bf16[1024,640]{1,0:T(8,128)(2,1)S(1)} %bitcast.174), channel_id=1, source_target_pairs={{0,2},{1,3},{2,0},{3,1},{4,6},{5,7},{6,4},{7,5},{8,10},{9,11},{10,... | collective-permute-start | bytes 3932168 | tf_op jit(solution)/shard_map/ppermute | solution.py:44
  604.4 20.2 %collective-permute-start.92 = (bf16[4,160,320]{2,1,0:T(8,128)(2,1)}, bf16[4,160,320]{2,1,0:T(8,128)(2,1)}, u32[]{:S(2)}, u32[]{:S(2)}) collective-permute-start(bf16[4,160,320]{2,1,0:T(8,128)(2,1)} %fusion), channel_id=1, source_target_pairs={{0,8},{4,12},{8,0},{12,4},{1,9},{5,13},{9,1},{13,5},{2,10},{6,14},... | collective-permute-start | bytes 1228808 | tf_op jit(solution)/shard_map/ppermute | solution.py:44
  635.9 23.4 %collective-permute-start.101 = (bf16[1,160,800]{2,1,0:T(8,128)(2,1)S(1)}, bf16[1,160,800]{2,1,0:T(8,128)(2,1)S(1)}, u32[]{:S(2)}, u32[]{:S(2)}) collective-permute-start(bf16[1,160,800]{2,1,0:T(8,128)(2,1)S(1)} %get-tuple-element.243), channel_id=1, source_target_pairs={{0,8},{4,12},{8,0},{12,4},{1,9},{5,13},{9,1},{13,5},{2,10},{6,14},... | collective-permute-start | bytes 768008 | tf_op jit(solution)/shard_map/ppermute | solution.py:44
  637.2 29.4 %collective-permute-start.102 = (bf16[1,160,800]{2,1,0:T(8,128)(2,1)S(1)}, bf16[1,160,800]{2,1,0:T(8,128)(2,1)S(1)}, u32[]{:S(2)}, u32[]{:S(2)}) collective-permute-start(bf16[1,160,800]{2,1,0:T(8,128)(2,1)S(1)} %get-tuple-element.242), channel_id=1, source_target_pairs={{0,12},{4,8},{8,4},{12,0},{1,13},{5,9},{9,5},{13,1},{2,14},{6,10},... | collective-permute-start | bytes 768008 | tf_op jit(solution)/shard_map/ppermute | solution.py:44
  638.1 43.8 %collective-permute-start.89 = (bf16[512,640]{1,0:T(8,128)(2,1)}, bf16[512,640]{1,0:T(8,128)(2,1)}, u32[]{:S(2)}, u32[]{:S(2)}) collective-permute-start(bf16[512,640]{1,0:T(8,128)(2,1)} %slice.279), channel_id=1, source_target_pairs={{0,2},{1,3},{2,0},{3,1},{4,6},{5,7},{6,4},{7,5},{8,10},{9,11},{10,... | collective-permute-start | bytes 1966088 | tf_op jit(solution)/shard_map/ppermute | solution.py:44
  640.3 41.7 %collective-permute-start.88 = (bf16[512,640]{1,0:T(8,128)(2,1)}, bf16[512,640]{1,0:T(8,128)(2,1)}, u32[]{:S(2)}, u32[]{:S(2)}) collective-permute-start(bf16[512,640]{1,0:T(8,128)(2,1)} %slice.278), channel_id=1, source_target_pairs={{0,1},{1,0},{2,3},{3,2},{4,5},{5,4},{6,7},{7,6},{8,9},{9,8},{10,11... | collective-permute-start | bytes 1966088 | tf_op jit(solution)/shard_map/ppermute | solution.py:44
  642.7 26.0 %collective-permute-start.94 = (bf16[1,160,320]{2,1,0:T(8,128)(2,1)S(1)}, bf16[1,160,320]{2,1,0:T(8,128)(2,1)S(1)}, u32[]{:S(2)}, u32[]{:S(2)}) collective-permute-start(bf16[1,160,320]{2,1,0:T(8,128)(2,1)S(1)} %get-tuple-element.250), channel_id=1, source_target_pairs={{0,1},{1,0},{2,3},{3,2},{4,5},{5,4},{6,7},{7,6},{8,9},{9,8},{10,11... | collective-permute-start | bytes 307208 | tf_op jit(solution)/shard_map/ppermute | solution.py:44
  678.4 24.9 %collective-permute-start.97 = (bf16[2,160,800]{2,1,0:T(8,128)(2,1)S(1)}, bf16[2,160,800]{2,1,0:T(8,128)(2,1)S(1)}, u32[]{:S(2)}, u32[]{:S(2)}) collective-permute-start(bf16[2,160,800]{2,1,0:T(8,128)(2,1)S(1)} %get-tuple-element.222), channel_id=1, source_target_pairs={{0,4},{4,0},{8,12},{12,8},{1,5},{5,1},{9,13},{13,9},{2,6},{6,2},{1... | collective-permute-start | bytes 1536008 | tf_op jit(solution)/shard_map/ppermute | solution.py:44
  678.5 40.6 %collective-permute-start.98 = (bf16[2,160,800]{2,1,0:T(8,128)(2,1)S(1)}, bf16[2,160,800]{2,1,0:T(8,128)(2,1)S(1)}, u32[]{:S(2)}, u32[]{:S(2)}) collective-permute-start(bf16[2,160,800]{2,1,0:T(8,128)(2,1)S(1)} %get-tuple-element.221), channel_id=1, source_target_pairs={{0,8},{4,12},{8,0},{12,4},{1,9},{5,13},{9,1},{13,5},{2,10},{6,14},... | collective-permute-start | bytes 1536008 | tf_op jit(solution)/shard_map/ppermute | solution.py:44
  681.1 50.9 %collective-permute-start.99 = (bf16[2,160,800]{2,1,0:T(8,128)(2,1)S(1)}, bf16[2,160,800]{2,1,0:T(8,128)(2,1)S(1)}, u32[]{:S(2)}, u32[]{:S(2)}) collective-permute-start(bf16[2,160,800]{2,1,0:T(8,128)(2,1)S(1)} %get-tuple-element.220), channel_id=1, source_target_pairs={{0,12},{4,8},{8,4},{12,0},{1,13},{5,9},{9,5},{13,1},{2,14},{6,10},... | collective-permute-start | bytes 1536008 | tf_op jit(solution)/shard_map/ppermute | solution.py:44
  (156 other events, 1892.5 us)
Sparse Core Ops, SparseCore 0:
  48.1 56.6 all-gather.4
  160.9 115.2 all-gather.2
  341.5 55.8 reduce-scatter.4
  422.9 108.1 reduce-scatter.2

commit v5 on v4

--- a/solution.py
+++ b/solution.py
@@ -626,16 +626,11 @@
 
 
 def product_kernel(count, targets, *refs):
-    left = refs[:count]
+    left = jnp.concatenate([ref[...] for ref in refs[:count]], axis=0)
     per = count // 2
     for i in range(targets):
-        right = refs[count + i * per : count + (i + 1) * per]
-        total = None
-        for j in range(count):
-            rows = left[j].shape[0]
-            value = right[j // 2][(j % 2) * rows : (j % 2 + 1) * rows, :]
-            term = dot(left[j][...], value, TN)
-            total = term if total is None else total + term
+        right = [ref[...] for ref in refs[count + i * per : count + (i + 1) * per]]
+        total = dot(left, jnp.concatenate(right, axis=0), TN)
         span = total.shape[0]
         refs[-1][i * span : (i + 1) * span, :] = total.astype(bf16)
 

time: 751 us -> 751 us (level)
  no operation moved by 1% of the time
where the time goes in v5:
time: 751 us; the launch traced here: 742 us
  waiting for transfers between devices  299 us (40%)
  Pallas kernels  201 us (27%)
  starting transfers between devices  143 us (19%)
  local copies, waits for them, and re-layouts  43.5 us (6%)
  other arithmetic  33.6 us (4%)
  between operations  16 us (2%)
    ppermute x85, waiting for transfers between devices, exchange(): return lax.ppermute(value, axis, [(i, i ^ step) for i in range(size)])  241 us
    ppermute x85, starting transfers between devices, exchange(): return lax.ppermute(value, axis, [(i, i ^ step) for i in range(size)])  84.5 us
    pallas_call x22, Pallas kernels, plain(): pl.pallas_call(kernel, in_specs=[SCALARS] + [LOCAL] * len(operands), out_...  54 us
    pallas_call x2, Pallas kernels, feed_forward(): pl.pallas_call(mlp_kernel, grid=(rows // block,), in_specs=[part_of] * 4...  47.8 us
    ppermute x5, waiting for transfers between devices, scatter_dp(): far = lax.ppermute(parts[3], 'dp', [(0, 1), (3, 2)])  27.8 us
    unnamed x228, local copies, waits for them, and re-layouts  27.2 us
    pallas_call x1, Pallas kernels, attend(): pl.pallas_call(functools.partial(forward_kernel, nt), grid_spec=pltpu.Pre...  23.7 us
    pallas_call x2, Pallas kernels, products(): pl.pallas_call(functools.partial(product_kernel, len(lefts), count), grid...  23 us
  transfers between devices with their start and end apart: 107, of which 49 were waited for; matrix products, arithmetic and copies ran while one was open for 8% of the time, Pallas kernels for 25%

profile of v5, /device:TPU:12, one launch (start us, length us, event | category | flops | bytes accessed | tf_op | source)
XLA Modules:
  0.0 742.2 jit_solution(9552224712479079299)
XLA Ops:
  25.2 3.8 convolution_convert_fusion.wq_ref.wq
  29.2 5.6 shard_map.308
  36.8 4.2 collective-permute-done.4.refs_2_
  41.0 4.7 collective-permute-done.5.refs_3_
  50.1 5.3 collective-permute-done.7
  57.7 5.7 collective-permute-done.10
  66.4 4.0 collective-permute-start.14
  70.4 18.1 %collective-permute-done.12.refs_2_ = bf16[4,160,320]{2,1,0:T(8,128)(2,1)S(1)} collective-permute-done((bf16[4,160,320]{2,1,0:T(8,128)(2,1)S(1)}, bf16[4,160,320]{2,1,0:T(8,128)(2,1)S(1)}, u32[]{:S(2)}, u32[]{:S(2)}) %collective-permute-start.12) | collective-permute-done | bytes 409632 | tf_op jit(solution)/shard_map/ppermute | solution.py:44
  88.5 6.5 collective-permute-start.13
  95.0 2.8 shard_map.316
  102.9 13.5 %collective-permute-done.13 = bf16[4,160,320]{2,1,0:T(8,128)(2,1)} collective-permute-done((bf16[4,160,320]{2,1,0:T(8,128)(2,1)S(1)}, bf16[4,160,320]{2,1,0:T(8,128)(2,1)}, u32[]{:S(2)}, u32[]{:S(2)}) %collective-permute-start.13) | collective-permute-done | bytes 409632 | tf_op jit(solution)/shard_map/ppermute | solution.py:904
  118.8 23.7 %shard_map.312 = (bf16[4,128,640]{2,1,0:T(8,128)(2,1)S(1)}, bf16[4,128,640]{2,1,0:T(8,128)(2,1)S(1)}, bf16[1024,640]{1,0:T(8,128)(2,1)}, bf16[1024,640]{1,0:T(8,...) custom-call(s32[3]{0:T(128)S(1)} %pad_add_fusion.ids, ...), custom_call_target="tpu_custom_call" | custom-call | flops 671088640 | bytes 1048576 | tf_op jit(solution)/shard_map/pallas_call | solution.py:376
  148.2 7.9 %shard_map.314 = (f32[4,128,2560]{2,1,0:T(8,128)}, bf16[4,128,2560]{2,1,0:T(8,128)(2,1)S(1)}) custom-call(bf16[4,128,640]{2,1,0:T(8,128)(2,1)S(1)} %get-tuple-element.126.own.oown_ref.oown, bf16[4,128,640]{2,1,0:T(8,128)(2,1)S(1)} %get-tuple-element.127.oth.ooth_ref.ooth, bf16[2560,640]{1,0:T(8,128)(2,1)} %bitcast.165), custom_call_target="tpu_custom_call" | custom-call | flops 335544320 | bytes 2424832 | tf_op jit(solution)/shard_map/pallas_call | solution.py:493
  157.6 3.2 shard_map.317
  166.2 2.9 collective-permute-start.35
  169.1 5.2 add_convert_fusion
  176.8 14.8 %collective-permute-done.18 = bf16[64,2560]{1,0:T(8,128)(2,1)S(1)} collective-permute-done((bf16[64,2560]{1,0:T(8,128)(2,1)S(1)}, bf16[64,2560]{1,0:T(8,128)(2,1)S(1)}, u32[]{:S(2)}, u32[]{:S(2)}) %collective-permute-start.18) | collective-permute-done | bytes 327712 | tf_op jit(solution)/shard_map/ppermute | solution.py:44
  194.4 24.8 %collective-permute-done.17.refs_1_ = bf16[128,2560]{1,0:T(8,128)(2,1)S(1)} collective-permute-done((bf16[128,2560]{1,0:T(8,128)(2,1)S(1)}, bf16[128,2560]{1,0:T(8,128)(2,1)S(1)}, u32[]{:S(2)}, u32[]{:S(2)}) %collective-permute-start.17) | collective-permute-done | bytes 655392 | tf_op jit(solution)/shard_map/ppermute | solution.py:44
  222.0 3.4 collective-permute-start.34
  227.1 20.5 %collective-permute-done.24 = bf16[128,2560]{1,0:T(8,128)(2,1)S(1)} collective-permute-done((bf16[128,2560]{1,0:T(8,128)(2,1)}, bf16[128,2560]{1,0:T(8,128)(2,1)S(1)}, u32[]{:S(2)}, u32[]{:S(2)}) %collective-permute-start.24) | collective-permute-done | bytes 655392 | tf_op jit(solution)/shard_map/ppermute | solution.py:44
  247.8 4.0 collective-permute-start.31
  251.8 3.5 collective-permute-done.29
  255.3 6.1 collective-permute-start.30
  261.4 3.9 collective-permute-done.34
  266.3 10.0 %all-gather.3.cloned.1.call-done.pair_hbm = bf16[5120,800]{1,0:T(8,128)(2,1)} async-done(((bf16[1280,800]{1,0:T(8,128)(2,1)}), bf16[5120,800]{1,0:T(8,128)(2,1)}) %all-gather.3.cloned.1.call-update) | async-done | bytes 8192016 | tf_op jit(solution)/shard_map/all_gather | solution.py:952
  276.3 23.8 %shard_map.319 = (bf16[2,256,800]{2,1,0:T(8,128)(2,1)}, bf16[2,256,800]{2,1,0:T(8,128)(2,1)}, bf16[2,256,800]{2,1,0:T(8,128)(2,1)}, bf16[256,2560]{1,0:T(8,128)(...) custom-call(bf16[256,2560]{1,0:T(8,128)(2,1)} %copy-done.5, ...), custom_call_target="tpu_custom_call" | custom-call | flops 1258291200 | bytes 2277376 | tf_op jit(solution)/shard_map/pallas_call | solution.py:612
  307.5 24.1 %shard_map.320 = (bf16[2,256,800]{2,1,0:T(8,128)(2,1)}, bf16[2,256,800]{2,1,0:T(8,128)(2,1)}, bf16[2,256,800]{2,1,0:T(8,128)(2,1)}, bf16[256,2560]{1,0:T(8,128)(...) custom-call(bf16[256,2560]{1,0:T(8,128)(2,1)} %copy-done.92, ...), custom_call_target="tpu_custom_call" | custom-call | flops 1258291200 | bytes 2277376 | tf_op jit(solution)/shard_map/pallas_call | solution.py:612
  332.8 8.5 %shard_map.339 = bf16[2560,800]{1,0:T(8,128)(2,1)} custom-call(bf16[256,2560]{1,0:T(8,128)(2,1)S(1)} %copy-done.8, bf16[256,2560]{1,0:T(8,128)(2,1)} %collective-permute-done.26.gm_oth.refs_1_, bf16[256,2560]{1,0:T(8,128)(2,1)} %pad_maximum_fusion.3.gm_own.refs_2_, bf16[256,2560]{1,0:T(8,128)(2,1)} %collective-permute-done.36.gm_oth.refs_3_, ...), custom_call_target="tpu_custom_call" | custom-call | flops 419430400 | bytes 933888 | tf_op jit(solution)/shard_map/pallas_call | solution.py:644
  341.6 3.1 collective-permute-done.37
  348.1 3.8 collective-permute-start.38
  352.0 13.5 %collective-permute-done.40 = bf16[128,2560]{1,0:T(8,128)(2,1)S(1)} collective-permute-done((bf16[128,2560]{1,0:T(8,128)(2,1)S(1)}, bf16[128,2560]{1,0:T(8,128)(2,1)S(1)}, u32[]{:S(2)}, u32[]{:S(2)}) %collective-permute-start.40) | collective-permute-done | bytes 655392 | tf_op jit(solution)/shard_map/ppermute | solution.py:910
  368.1 14.5 %shard_map.321 = bf16[5120,800]{1,0:T(8,128)(2,1)} custom-call(bf16[256,2560]{1,0:T(8,128)(2,1)S(1)} %copy-done.6, bf16[256,2560]{1,0:T(8,128)(2,1)} %collective-permute-done.25.nm_oth.refs_1_, bf16[256,2560]{1,0:T(8,128)(2,1)} %copy-done.92, bf16[256,2560]{1,0:T(8,128)(2,1)} %collective-permute-done.32.nm_oth.refs_3_, bf16[512,800]{1,0:T(8,128)(2,1)S(1)} %bitcast.184, ...), custom_call_target="tpu_custom_call" | custom-call | flops 838860800 | bytes 1343488 | tf_op jit(solution)/shard_map/pallas_call | solution.py:644
  382.6 12.5 %collective-permute-done.41.refs_2_ = bf16[128,2560]{1,0:T(8,128)(2,1)} collective-permute-done((bf16[128,2560]{1,0:T(8,128)(2,1)}, bf16[128,2560]{1,0:T(8,128)(2,1)}, u32[]{:S(2)}, u32[]{:S(2)}) %collective-permute-start.41) | collective-permute-done | bytes 655392 | tf_op jit(solution)/shard_map/ppermute | solution.py:44
  396.1 3.2 shard_map.322
  401.5 12.9 %collective-permute-done.42 = bf16[128,2560]{1,0:T(8,128)(2,1)S(1)} collective-permute-done((bf16[128,2560]{1,0:T(8,128)(2,1)S(1)}, bf16[128,2560]{1,0:T(8,128)(2,1)S(1)}, u32[]{:S(2)}, u32[]{:S(2)}) %collective-permute-start.42) | collective-permute-done | bytes 655392 | tf_op jit(solution)/shard_map/ppermute | solution.py:44
  417.3 4.5 collective-permute-done.45
  423.4 2.8 collective-permute-done.27
  434.1 6.8 shard_map.323
  440.9 15.9 %shard_map.324 = (bf16[1024,1280]{1,0:T(8,128)(2,1)}, bf16[1024,1280]{1,0:T(8,128)(2,1)}) custom-call(s32[3]{0:T(128)S(1)} %pad_add_fusion.ids, bf16[1024,640]{1,0:T(8,128)(2,1)S(1)} %copy-done.34, bf16[1024,640]{1,0:T(8,128)(2,1)} %get-tuple-element.163.k_ref, bf16[1024,640]{1,0:T(8,128)(2,1)} %get-tuple-element.164.v_ref, ...), custom_call_target="tpu_custom_call" | custom-call | flops 536870912 | bytes 1572864 | tf_op jit(solution)/shard_map/pallas_call | solution.py:410
  456.8 7.7 %shard_map.327 = (f32[4,128,1152]{2,1,0:T(8,128)}, bf16[4,128,1152]{2,1,0:T(8,128)(2,1)S(1)}) custom-call(s32[3]{0:T(128)S(1)} %pad_add_fusion.ids, bf16[1024,1280]{1,0:T(8,128)(2,1)} %get-tuple-element.169.gq, bf16[1024,1280]{1,0:T(8,128)(2,1)} %get-tuple-element.176.gkv, bf16[768,1280]{1,0:T(8,128)(2,1)S(1)} %copy-done.11, bf16[384,1280]{1,0:T(8,128)(2,1)S(1)} %copy-done.4), custom_call_target="tpu_custom_call" | custom-call | flops 301989888 | bytes 1114112 | tf_op jit(solution)/shard_map/pallas_call | solution.py:720
  465.7 4.7 collective-permute-start.51
  475.8 6.8 shard_map.328
  488.4 4.7 collective-permute-done.55.refs_1_
  494.4 7.3 shard_map.329
  508.6 4.3 collective-permute-done.50.refs_2_
  520.6 4.3 shard_map.331
  527.3 4.5 collective-permute-done.71
  536.4 10.1 %collective-permute-done.78 = bf16[256,640]{1,0:T(8,128)(2,1)S(1)} collective-permute-done((bf16[256,640]{1,0:T(8,128)(2,1)S(1)}, bf16[256,640]{1,0:T(8,128)(2,1)S(1)}, u32[]{:S(2)}, u32[]{:S(2)}) %collective-permute-start.78) | collective-permute-done | bytes 327712 | tf_op jit(solution)/shard_map/ppermute | solution.py:44
  549.4 2.9 collective-permute-start.83
  565.6 4.5 collective-permute-start.84
  586.2 2.9 shard_map.333
  589.1 5.5 collective-permute-done.82
  600.5 3.9 collective-permute-done.63
  607.2 14.2 %collective-permute-done.74 = bf16[160,640]{1,0:T(8,128)(2,1)} collective-permute-done((bf16[160,640]{1,0:T(8,128)(2,1)S(1)}, bf16[160,640]{1,0:T(8,128)(2,1)}, u32[]{:S(2)}, u32[]{:S(2)}) %collective-permute-start.74) | collective-permute-done | bytes 204832 | tf_op jit(solution)/shard_map/ppermute | solution.py:910
  624.7 3.3 collective-permute-start.76
  642.7 11.9 %collective-permute-start.94 = (bf16[1,160,320]{2,1,0:T(8,128)(2,1)S(1)}, bf16[1,160,320]{2,1,0:T(8,128)(2,1)S(1)}, u32[]{:S(2)}, u32[]{:S(2)}) collective-permute-start(bf16[1,160,320]{2,1,0:T(8,128)(2,1)S(1)} %get-tuple-element.250), channel_id=1, source_target_pairs={{0,1},{1,0},{2,3},{3,2},{4,5},{5,4},{6,7},{7,6},{8,9},{9,8},{10,11... | collective-permute-start | bytes 307208 | tf_op jit(solution)/shard_map/ppermute | solution.py:44
  654.7 4.8 collective-permute-done.101.refs_2_
  660.6 6.1 collective-permute-done.102.refs_3_
  683.3 2.9 pad_maximum_fusion.source
  686.2 5.0 shard_map.336
  691.2 12.1 %collective-permute-done.97.refs_1_ = bf16[2,160,800]{2,1,0:T(8,128)(2,1)S(1)} collective-permute-done((bf16[2,160,800]{2,1,0:T(8,128)(2,1)S(1)}, bf16[2,160,800]{2,1,0:T(8,128)(2,1)S(1)}, u32[]{:S(2)}, u32[]{:S(2)}) %collective-permute-start.97) | collective-permute-done | bytes 512032 | tf_op jit(solution)/shard_map/ppermute | solution.py:44
  703.3 15.7 %collective-permute-done.98.refs_2_ = bf16[2,160,800]{2,1,0:T(8,128)(2,1)S(1)} collective-permute-done((bf16[2,160,800]{2,1,0:T(8,128)(2,1)S(1)}, bf16[2,160,800]{2,1,0:T(8,128)(2,1)S(1)}, u32[]{:S(2)}, u32[]{:S(2)}) %collective-permute-start.98) | collective-permute-done | bytes 512032 | tf_op jit(solution)/shard_map/ppermute | solution.py:44
  719.0 12.9 %collective-permute-done.99.refs_3_ = bf16[2,160,800]{2,1,0:T(8,128)(2,1)S(1)} collective-permute-done((bf16[2,160,800]{2,1,0:T(8,128)(2,1)S(1)}, bf16[2,160,800]{2,1,0:T(8,128)(2,1)S(1)}, u32[]{:S(2)}, u32[]{:S(2)}) %collective-permute-start.99) | collective-permute-done | bytes 512032 | tf_op jit(solution)/shard_map/ppermute | solution.py:44
  731.9 3.3 shard_map.338
  (499 shorter events, 202.0 us)
Async XLA Ops:
  7.2 259.1 %all-gather.5.cloned.1.call-start = ((), (), s32[]{:S(2)}) async-start(), calls=%async_computation.3 | async-start | bytes 5734400 | tf_op jit(solution)/shard_map/all_gather | solution.py:952
  12.2 23.2 %collective-permute-start.1 = (bf16[1,160,320]{2,1,0:T(8,128)(2,1)}, bf16[1,160,320]{2,1,0:T(8,128)(2,1)}, u32[]{:S(2)}, u32[]{:S(2)}) collective-permute-start(bf16[1,160,320]{2,1,0:T(8,128)(2,1)} %get-tuple-element.118), channel_id=1, source_target_pairs={{0,2},{1,3},{2,0},{3,1},{4,6},{5,7},{6,4},{7,5},{8,10},{9,11},{10,... | collective-permute-start | bytes 307208 | tf_op jit(solution)/shard_map/ppermute | solution.py:44
  12.7 22.7 %collective-permute-start.2 = (bf16[1,160,320]{2,1,0:T(8,128)(2,1)}, bf16[1,160,320]{2,1,0:T(8,128)(2,1)}, u32[]{:S(2)}, u32[]{:S(2)}) collective-permute-start(bf16[1,160,320]{2,1,0:T(8,128)(2,1)} %get-tuple-element.119), channel_id=1, source_target_pairs={{0,3},{1,2},{2,1},{3,0},{4,7},{5,6},{6,5},{7,4},{8,11},{9,10},{10,... | collective-permute-start | bytes 307208 | tf_op jit(solution)/shard_map/ppermute | solution.py:44
  18.1 18.7 %collective-permute-start.3 = (bf16[1,160,800]{2,1,0:T(8,128)(2,1)}, bf16[1,160,800]{2,1,0:T(8,128)(2,1)}, u32[]{:S(2)}, u32[]{:S(2)}) collective-permute-start(bf16[1,160,800]{2,1,0:T(8,128)(2,1)} %get-tuple-element.120), channel_id=1, source_target_pairs={{0,4},{4,0},{8,12},{12,8},{1,5},{5,1},{9,13},{13,9},{2,6},{6,2},{1... | collective-permute-start | bytes 768008 | tf_op jit(solution)/shard_map/ppermute | solution.py:44
  18.5 22.5 %collective-permute-start.4 = (bf16[1,160,800]{2,1,0:T(8,128)(2,1)}, bf16[1,160,800]{2,1,0:T(8,128)(2,1)}, u32[]{:S(2)}, u32[]{:S(2)}) collective-permute-start(bf16[1,160,800]{2,1,0:T(8,128)(2,1)} %get-tuple-element.121), channel_id=1, source_target_pairs={{0,8},{4,12},{8,0},{12,4},{1,9},{5,13},{9,1},{13,5},{2,10},{6,14},... | collective-permute-start | bytes 768008 | tf_op jit(solution)/shard_map/ppermute | solution.py:44
  24.7 21.0 %collective-permute-start.5 = (bf16[1,160,800]{2,1,0:T(8,128)(2,1)}, bf16[1,160,800]{2,1,0:T(8,128)(2,1)S(1)}, u32[]{:S(2)}, u32[]{:S(2)}) collective-permute-start(bf16[1,160,800]{2,1,0:T(8,128)(2,1)} %copy-done.87), channel_id=1, source_target_pairs={{0,12},{4,8},{8,4},{12,0},{1,13},{5,9},{9,5},{13,1},{2,14},{6,10},... | collective-permute-start | bytes 768008 | tf_op jit(solution)/shard_map/ppermute | solution.py:44
  47.9 228.3 %all-gather.3.cloned.1.call-start = ((), (), s32[]{:S(2)}) async-start(), calls=%async_computation.2 | async-start | bytes 11468800 | tf_op jit(solution)/shard_map/all_gather | solution.py:952
  66.2 51.3 %collective-permute-start.11 = (bf16[4,128,1152]{2,1,0:T(8,128)(2,1)S(1)}, bf16[4,128,1152]{2,1,0:T(8,128)(2,1)}, u32[]{:S(2)}, u32[]{:S(2)}) collective-permute-start(bf16[4,128,1152]{2,1,0:T(8,128)(2,1)S(1)} %pad_maximum_fusion.4.own_ref), channel_id=1, source_target_pairs={{0,16},{16,0},{1,17},{17,1},{2,18},{18,2},{3,19},{19,3},{4,20},{20... | collective-permute-start | bytes 3538952 | tf_op jit(solution)/shard_map/ppermute | solution.py:44
  66.3 22.2 %collective-permute-start.12 = (bf16[4,160,320]{2,1,0:T(8,128)(2,1)S(1)}, bf16[4,160,320]{2,1,0:T(8,128)(2,1)S(1)}, u32[]{:S(2)}, u32[]{:S(2)}) collective-permute-start(bf16[4,160,320]{2,1,0:T(8,128)(2,1)S(1)} %bitcast.177), channel_id=1, source_target_pairs={{0,8},{4,12},{8,0},{12,4},{1,9},{5,13},{9,1},{13,5},{2,10},{6,14},... | collective-permute-start | bytes 1228808 | tf_op jit(solution)/shard_map/ppermute | solution.py:44
  66.4 34.7 %collective-permute-start.14 = (bf16[4,160,320]{2,1,0:T(8,128)(2,1)S(1)}, bf16[4,160,320]{2,1,0:T(8,128)(2,1)S(1)}, u32[]{:S(2)}, u32[]{:S(2)}) collective-permute-start(bf16[4,160,320]{2,1,0:T(8,128)(2,1)S(1)} %bitcast.178), channel_id=1, source_target_pairs={{4,8},{8,4},{5,9},{9,5},{6,10},{10,6},{7,11},{11,7},{20,24},{24,20... | collective-permute-start | bytes 1228808 | tf_op jit(solution)/shard_map/ppermute | solution.py:903
  88.5 27.9 %collective-permute-start.13 = (bf16[4,160,320]{2,1,0:T(8,128)(2,1)S(1)}, bf16[4,160,320]{2,1,0:T(8,128)(2,1)}, u32[]{:S(2)}, u32[]{:S(2)}) collective-permute-start(bf16[4,160,320]{2,1,0:T(8,128)(2,1)S(1)} %collective-permute-done.12.refs_2_), channel_id=1, source_target_pairs={{4,0},{8,12},{5,1},{9,13},{6,2},{10,14},{7,3},{11,15},{20,16},{24,... | collective-permute-start | bytes 1228808 | tf_op jit(solution)/shard_map/ppermute | solution.py:904
  98.6 59.0 %collective-permute-start.20 = (bf16[2,160,800]{2,1,0:T(8,128)(2,1)}, bf16[2,160,800]{2,1,0:T(8,128)(2,1)}, u32[]{:S(2)}, u32[]{:S(2)}) collective-permute-start(bf16[2,160,800]{2,1,0:T(8,128)(2,1)} %get-tuple-element.135), channel_id=1, source_target_pairs={{0,4},{4,0},{8,12},{12,8},{1,5},{5,1},{9,13},{13,9},{2,6},{6,2},{1... | collective-permute-start | bytes 1536008 | tf_op jit(solution)/shard_map/ppermute | solution.py:44
  98.6 59.0 %collective-permute-start.21 = (bf16[2,160,800]{2,1,0:T(8,128)(2,1)}, bf16[2,160,800]{2,1,0:T(8,128)(2,1)}, u32[]{:S(2)}, u32[]{:S(2)}) collective-permute-start(bf16[2,160,800]{2,1,0:T(8,128)(2,1)} %get-tuple-element.136), channel_id=1, source_target_pairs={{0,8},{4,12},{8,0},{12,4},{1,9},{5,13},{9,1},{13,5},{2,10},{6,14},... | collective-permute-start | bytes 1536008 | tf_op jit(solution)/shard_map/ppermute | solution.py:44
  101.9 55.7 %collective-permute-start.22 = (bf16[2,160,800]{2,1,0:T(8,128)(2,1)}, bf16[2,160,800]{2,1,0:T(8,128)(2,1)}, u32[]{:S(2)}, u32[]{:S(2)}) collective-permute-start(bf16[2,160,800]{2,1,0:T(8,128)(2,1)} %get-tuple-element.137), channel_id=1, source_target_pairs={{0,12},{4,8},{8,4},{12,0},{1,13},{5,9},{9,5},{13,1},{2,14},{6,10},... | collective-permute-start | bytes 1536008 | tf_op jit(solution)/shard_map/ppermute | solution.py:44
  160.8 446.3 %reduce-scatter.5.cloned.1.call-start = ((), (), s32[]{:S(2)}) async-start(), calls=%async_computation.5 | async-start | bytes 5734400 | tf_op jit(solution)/shard_map/reduce_scatter | solution.py:955
  163.0 58.3 %collective-permute-start.23 = (bf16[128,2560]{1,0:T(8,128)(2,1)}, bf16[128,2560]{1,0:T(8,128)(2,1)S(1)}, u32[]{:S(2)}, u32[]{:S(2)}) collective-permute-start(bf16[128,2560]{1,0:T(8,128)(2,1)} %get-tuple-element.138), channel_id=1, source_target_pairs={{0,4},{4,0},{8,12},{12,8},{1,5},{5,1},{9,13},{13,9},{2,6},{6,2},{1... | collective-permute-start | bytes 1966088 | tf_op jit(solution)/shard_map/ppermute | solution.py:44
  165.7 56.3 %collective-permute-start.33 = (bf16[128,2560]{1,0:T(8,128)(2,1)}, bf16[128,2560]{1,0:T(8,128)(2,1)S(1)}, u32[]{:S(2)}, u32[]{:S(2)}) collective-permute-start(bf16[128,2560]{1,0:T(8,128)(2,1)} %get-tuple-element.138), channel_id=1, source_target_pairs={{0,8},{4,12},{8,0},{12,4},{1,9},{5,13},{9,1},{13,5},{2,10},{6,14},... | collective-permute-start | bytes 1966088 | tf_op jit(solution)/shard_map/ppermute | solution.py:44
  166.2 81.6 %collective-permute-start.35 = (bf16[128,2560]{1,0:T(8,128)(2,1)}, bf16[128,2560]{1,0:T(8,128)(2,1)S(1)}, u32[]{:S(2)}, u32[]{:S(2)}) collective-permute-start(bf16[128,2560]{1,0:T(8,128)(2,1)} %get-tuple-element.138), channel_id=1, source_target_pairs={{4,8},{8,4},{5,9},{9,5},{6,10},{10,6},{7,11},{11,7},{20,24},{24,20... | collective-permute-start | bytes 1966088 | tf_op jit(solution)/shard_map/ppermute | solution.py:903
  174.4 17.2 %collective-permute-start.18 = (bf16[64,2560]{1,0:T(8,128)(2,1)S(1)}, bf16[64,2560]{1,0:T(8,128)(2,1)S(1)}, u32[]{:S(2)}, u32[]{:S(2)}) collective-permute-start(bf16[64,2560]{1,0:T(8,128)(2,1)S(1)} %get-tuple-element.216), channel_id=1, source_target_pairs={{0,1},{1,0},{2,3},{3,2},{4,5},{5,4},{6,7},{7,6},{8,9},{9,8},{10,11... | collective-permute-start | bytes 983048 | tf_op jit(solution)/shard_map/ppermute | solution.py:44
  174.7 17.0 %collective-permute-start.16 = (bf16[64,2560]{1,0:T(8,128)(2,1)S(1)}, bf16[64,2560]{1,0:T(8,128)(2,1)S(1)}, u32[]{:S(2)}, u32[]{:S(2)}) collective-permute-start(bf16[64,2560]{1,0:T(8,128)(2,1)S(1)} %get-tuple-element.218), channel_id=1, source_target_pairs={{0,2},{1,3},{2,0},{3,1},{4,6},{5,7},{6,4},{7,5},{8,10},{9,11},{10,... | collective-permute-start | bytes 983048 | tf_op jit(solution)/shard_map/ppermute | solution.py:44
  192.0 27.2 %collective-permute-start.17 = (bf16[128,2560]{1,0:T(8,128)(2,1)S(1)}, bf16[128,2560]{1,0:T(8,128)(2,1)S(1)}, u32[]{:S(2)}, u32[]{:S(2)}) collective-permute-start(bf16[128,2560]{1,0:T(8,128)(2,1)S(1)} %pad_maximum_fusion.6), channel_id=1, source_target_pairs={{0,1},{1,0},{2,3},{3,2},{4,5},{5,4},{6,7},{7,6},{8,9},{9,8},{10,11... | collective-permute-start | bytes 1966088 | tf_op jit(solution)/shard_map/ppermute | solution.py:44
  193.8 25.4 %collective-permute-start.19 = (bf16[128,2560]{1,0:T(8,128)(2,1)S(1)}, bf16[128,2560]{1,0:T(8,128)(2,1)S(1)}, u32[]{:S(2)}, u32[]{:S(2)}) collective-permute-start(bf16[128,2560]{1,0:T(8,128)(2,1)S(1)} %pad_maximum_fusion.7), channel_id=1, source_target_pairs={{0,2},{1,3},{2,0},{3,1},{4,6},{5,7},{6,4},{7,5},{8,10},{9,11},{10,... | collective-permute-start | bytes 1966088 | tf_op jit(solution)/shard_map/ppermute | solution.py:44
  221.3 26.3 %collective-permute-start.24 = (bf16[128,2560]{1,0:T(8,128)(2,1)}, bf16[128,2560]{1,0:T(8,128)(2,1)S(1)}, u32[]{:S(2)}, u32[]{:S(2)}) collective-permute-start(bf16[128,2560]{1,0:T(8,128)(2,1)} %get-tuple-element.139), channel_id=1, source_target_pairs={{0,4},{4,0},{8,12},{12,8},{1,5},{5,1},{9,13},{13,9},{2,6},{6,2},{1... | collective-permute-start | bytes 1966088 | tf_op jit(solution)/shard_map/ppermute | solution.py:44
  221.9 44.4 %collective-permute-start.26 = (bf16[256,2560]{1,0:T(8,128)(2,1)S(1)}, bf16[256,2560]{1,0:T(8,128)(2,1)}, u32[]{:S(2)}, u32[]{:S(2)}) collective-permute-start(bf16[256,2560]{1,0:T(8,128)(2,1)S(1)} %constant_dynamic-update-slice_fusion.2.gm_own.refs_0_), channel_id=1, source_target_pairs={{0,16},{16,0},{1,17},{17,1},{2,18},{18,2},{3,19},{19,3},{4,20},{20... | collective-permute-start | bytes 3932168 | tf_op jit(solution)/shard_map/ppermute | solution.py:44
  222.0 43.3 %collective-permute-start.34 = (bf16[128,2560]{1,0:T(8,128)(2,1)S(1)}, bf16[128,2560]{1,0:T(8,128)(2,1)S(1)}, u32[]{:S(2)}, u32[]{:S(2)}) collective-permute-start(bf16[128,2560]{1,0:T(8,128)(2,1)S(1)} %collective-permute-done.33), channel_id=1, source_target_pairs={{4,0},{8,12},{5,1},{9,13},{6,2},{10,14},{7,3},{11,15},{20,16},{24,... | collective-permute-start | bytes 1966088 | tf_op jit(solution)/shard_map/ppermute | solution.py:904
  225.5 29.8 %collective-permute-start.29 = (bf16[128,2560]{1,0:T(8,128)(2,1)}, bf16[128,2560]{1,0:T(8,128)(2,1)}, u32[]{:S(2)}, u32[]{:S(2)}) collective-permute-start(bf16[128,2560]{1,0:T(8,128)(2,1)} %get-tuple-element.139), channel_id=1, source_target_pairs={{0,8},{4,12},{8,0},{12,4},{1,9},{5,13},{9,1},{13,5},{2,10},{6,14},... | collective-permute-start | bytes 1966088 | tf_op jit(solution)/shard_map/ppermute | solution.py:44
  247.7 18.6 %collective-permute-start.25 = (bf16[256,2560]{1,0:T(8,128)(2,1)S(1)}, bf16[256,2560]{1,0:T(8,128)(2,1)}, u32[]{:S(2)}, u32[]{:S(2)}) collective-permute-start(bf16[256,2560]{1,0:T(8,128)(2,1)S(1)} %constant_dynamic-update-slice_fusion.nm_own.refs_0_), channel_id=1, source_target_pairs={{0,16},{16,0},{1,17},{17,1},{2,18},{18,2},{3,19},{19,3},{4,20},{20... | collective-permute-start | bytes 3932168 | tf_op jit(solution)/shard_map/ppermute | solution.py:44
  247.8 54.0 %collective-permute-start.31 = (bf16[128,2560]{1,0:T(8,128)(2,1)}, bf16[128,2560]{1,0:T(8,128)(2,1)}, u32[]{:S(2)}, u32[]{:S(2)}) collective-permute-start(bf16[128,2560]{1,0:T(8,128)(2,1)} %get-tuple-element.139), channel_id=1, source_target_pairs={{4,8},{8,4},{5,9},{9,5},{6,10},{10,6},{7,11},{11,7},{20,24},{24,20... | collective-permute-start | bytes 1966088 | tf_op jit(solution)/shard_map/ppermute | solution.py:903
  255.3 46.5 %collective-permute-start.30 = (bf16[128,2560]{1,0:T(8,128)(2,1)}, bf16[128,2560]{1,0:T(8,128)(2,1)}, u32[]{:S(2)}, u32[]{:S(2)}) collective-permute-start(bf16[128,2560]{1,0:T(8,128)(2,1)} %collective-permute-done.29), channel_id=1, source_target_pairs={{4,0},{8,12},{5,1},{9,13},{6,2},{10,14},{7,3},{11,15},{20,16},{24,... | collective-permute-start | bytes 1966088 | tf_op jit(solution)/shard_map/ppermute | solution.py:904
  306.3 25.3 %collective-permute-start.39 = (bf16[128,2560]{1,0:T(8,128)(2,1)}, bf16[128,2560]{1,0:T(8,128)(2,1)}, u32[]{:S(2)}, u32[]{:S(2)}) collective-permute-start(bf16[128,2560]{1,0:T(8,128)(2,1)} %get-tuple-element.234), channel_id=1, source_target_pairs={{0,4},{4,0},{8,12},{12,8},{1,5},{5,1},{9,13},{13,9},{2,6},{6,2},{1... | collective-permute-start | bytes 1966088 | tf_op jit(solution)/shard_map/ppermute | solution.py:44
  341.4 335.2 %reduce-scatter.3.cloned.1.call-start = ((), (), s32[]{:S(2)}) async-start(), calls=%async_computation.4 | async-start | bytes 11468800 | tf_op jit(solution)/shard_map/reduce_scatter | solution.py:955
  346.6 18.9 %collective-permute-start.40 = (bf16[128,2560]{1,0:T(8,128)(2,1)S(1)}, bf16[128,2560]{1,0:T(8,128)(2,1)S(1)}, u32[]{:S(2)}, u32[]{:S(2)}) collective-permute-start(bf16[128,2560]{1,0:T(8,128)(2,1)S(1)} %slice.257), channel_id=1, source_target_pairs={{0,4},{12,8},{1,5},{13,9},{2,6},{14,10},{3,7},{15,11},{16,20},{28,... | collective-permute-start | bytes 1966088 | tf_op jit(solution)/shard_map/ppermute | solution.py:910
  348.1 19.1 %collective-permute-start.38 = (bf16[128,2560]{1,0:T(8,128)(2,1)S(1)}, bf16[128,2560]{1,0:T(8,128)(2,1)S(1)}, u32[]{:S(2)}, u32[]{:S(2)}) collective-permute-start(bf16[128,2560]{1,0:T(8,128)(2,1)S(1)} %slice.257), channel_id=1, source_target_pairs={{4,8},{8,4},{5,9},{9,5},{6,10},{10,6},{7,11},{11,7},{20,24},{24,20... | collective-permute-start | bytes 1966088 | tf_op jit(solution)/shard_map/ppermute | solution.py:912
  366.5 28.5 %collective-permute-start.41 = (bf16[128,2560]{1,0:T(8,128)(2,1)}, bf16[128,2560]{1,0:T(8,128)(2,1)}, u32[]{:S(2)}, u32[]{:S(2)}) collective-permute-start(bf16[128,2560]{1,0:T(8,128)(2,1)} %add_convert_fusion.7), channel_id=1, source_target_pairs={{0,8},{4,12},{8,0},{12,4},{1,9},{5,13},{9,1},{13,5},{2,10},{6,14},... | collective-permute-start | bytes 1966088 | tf_op jit(solution)/shard_map/ppermute | solution.py:44
  432.5 39.5 %collective-permute-start.49 = (bf16[128,2560]{1,0:T(8,128)(2,1)}, bf16[128,2560]{1,0:T(8,128)(2,1)S(1)}, u32[]{:S(2)}, u32[]{:S(2)}) collective-permute-start(bf16[128,2560]{1,0:T(8,128)(2,1)} %get-tuple-element.175), channel_id=1, source_target_pairs={{0,4},{12,8},{1,5},{13,9},{2,6},{14,10},{3,7},{15,11},{16,20},{28,... | collective-permute-start | bytes 1966088 | tf_op jit(solution)/shard_map/ppermute | solution.py:910
  465.7 41.5 %collective-permute-start.51 = (bf16[128,2560]{1,0:T(8,128)(2,1)}, bf16[128,2560]{1,0:T(8,128)(2,1)}, u32[]{:S(2)}, u32[]{:S(2)}) collective-permute-start(bf16[128,2560]{1,0:T(8,128)(2,1)} %get-tuple-element.175), channel_id=1, source_target_pairs={{4,8},{8,4},{5,9},{9,5},{6,10},{10,6},{7,11},{11,7},{20,24},{24,20... | collective-permute-start | bytes 1966088 | tf_op jit(solution)/shard_map/ppermute | solution.py:912
  470.3 34.1 %collective-permute-start.47 = (bf16[128,2560]{1,0:T(8,128)(2,1)}, bf16[128,2560]{1,0:T(8,128)(2,1)S(1)}, u32[]{:S(2)}, u32[]{:S(2)}) collective-permute-start(bf16[128,2560]{1,0:T(8,128)(2,1)} %get-tuple-element.171), channel_id=1, source_target_pairs={{0,4},{4,0},{8,12},{12,8},{1,5},{5,1},{9,13},{13,9},{2,6},{6,2},{1... | collective-permute-start | bytes 1966088 | tf_op jit(solution)/shard_map/ppermute | solution.py:44
  473.1 39.8 %collective-permute-start.50 = (bf16[128,2560]{1,0:T(8,128)(2,1)}, bf16[128,2560]{1,0:T(8,128)(2,1)}, u32[]{:S(2)}, u32[]{:S(2)}) collective-permute-start(bf16[128,2560]{1,0:T(8,128)(2,1)} %add_convert_fusion.6), channel_id=1, source_target_pairs={{0,8},{4,12},{8,0},{12,4},{1,9},{5,13},{9,1},{13,5},{2,10},{6,14},... | collective-permute-start | bytes 1966088 | tf_op jit(solution)/shard_map/ppermute | solution.py:44
  485.4 17.5 %collective-permute-start.57 = (bf16[128,1152]{1,0:T(8,128)(2,1)S(1)}, bf16[128,1152]{1,0:T(8,128)(2,1)S(1)}, u32[]{:S(2)}, u32[]{:S(2)}) collective-permute-start(bf16[128,1152]{1,0:T(8,128)(2,1)S(1)} %pad_maximum_fusion.10), channel_id=1, source_target_pairs={{0,2},{1,3},{2,0},{3,1},{4,6},{5,7},{6,4},{7,5},{8,10},{9,11},{10,... | collective-permute-start | bytes 884744 | tf_op jit(solution)/shard_map/ppermute | solution.py:44
  493.1 24.0 %collective-permute-start.79 = (bf16[256,640]{1,0:T(8,128)(2,1)}, bf16[256,640]{1,0:T(8,128)(2,1)}, u32[]{:S(2)}, u32[]{:S(2)}) collective-permute-start(bf16[256,640]{1,0:T(8,128)(2,1)} %get-tuple-element.228), channel_id=1, source_target_pairs={{0,4},{12,8},{1,5},{13,9},{2,6},{14,10},{3,7},{15,11},{16,20},{28,... | collective-permute-start | bytes 983048 | tf_op jit(solution)/shard_map/ppermute | solution.py:910
  503.9 21.1 %collective-permute-start.68 = (bf16[128,1152]{1,0:T(8,128)(2,1)S(1)}, bf16[128,1152]{1,0:T(8,128)(2,1)S(1)}, u32[]{:S(2)}, u32[]{:S(2)}) collective-permute-start(bf16[128,1152]{1,0:T(8,128)(2,1)S(1)} %get-tuple-element.199.lat), channel_id=1, source_target_pairs={{0,1},{1,0},{2,3},{3,2},{4,5},{5,4},{6,7},{7,6},{8,9},{9,8},{10,11... | collective-permute-start | bytes 884744 | tf_op jit(solution)/shard_map/ppermute | solution.py:44
  505.3 21.8 %collective-permute-start.69 = (bf16[128,1152]{1,0:T(8,128)(2,1)S(1)}, bf16[128,1152]{1,0:T(8,128)(2,1)S(1)}, u32[]{:S(2)}, u32[]{:S(2)}) collective-permute-start(bf16[128,1152]{1,0:T(8,128)(2,1)S(1)} %get-tuple-element.199.lat), channel_id=1, source_target_pairs={{0,2},{1,3},{2,0},{3,1},{4,6},{5,7},{6,4},{7,5},{8,10},{9,11},{10,... | collective-permute-start | bytes 884744 | tf_op jit(solution)/shard_map/ppermute | solution.py:44
  507.2 46.3 %collective-permute-start.66 = (bf16[128,640]{1,0:T(8,128)(2,1)}, bf16[128,640]{1,0:T(8,128)(2,1)S(1)}, u32[]{:S(2)}, u32[]{:S(2)}) collective-permute-start(bf16[128,640]{1,0:T(8,128)(2,1)} %get-tuple-element.198), channel_id=1, source_target_pairs={{0,3},{1,2},{2,1},{3,0},{4,7},{5,6},{6,5},{7,4},{8,11},{9,10},{10,... | collective-permute-start | bytes 491528 | tf_op jit(solution)/shard_map/ppermute | solution.py:44
  517.0 45.9 %collective-permute-start.52 = (bf16[128,2560]{1,0:T(8,128)(2,1)S(1)}, bf16[128,2560]{1,0:T(8,128)(2,1)S(1)}, u32[]{:S(2)}, u32[]{:S(2)}) collective-permute-start(bf16[128,2560]{1,0:T(8,128)(2,1)S(1)} %shard_map.325.own), channel_id=1, source_target_pairs={{0,16},{16,0},{1,17},{17,1},{2,18},{18,2},{3,19},{19,3},{4,20},{20... | collective-permute-start | bytes 1966088 | tf_op jit(solution)/shard_map/ppermute | solution.py:44
  517.1 19.2 %collective-permute-start.81 = (bf16[256,640]{1,0:T(8,128)(2,1)}, bf16[256,640]{1,0:T(8,128)(2,1)S(1)}, u32[]{:S(2)}, u32[]{:S(2)}) collective-permute-start(bf16[256,640]{1,0:T(8,128)(2,1)} %get-tuple-element.228), channel_id=1, source_target_pairs={{4,8},{8,4},{5,9},{9,5},{6,10},{10,6},{7,11},{11,7},{20,24},{24,20... | collective-permute-start | bytes 983048 | tf_op jit(solution)/shard_map/ppermute | solution.py:912
  532.8 16.4 %collective-permute-start.80 = (bf16[256,640]{1,0:T(8,128)(2,1)S(1)}, bf16[256,640]{1,0:T(8,128)(2,1)S(1)}, u32[]{:S(2)}, u32[]{:S(2)}) collective-permute-start(bf16[256,640]{1,0:T(8,128)(2,1)S(1)} %fusion.2), channel_id=1, source_target_pairs={{0,8},{4,12},{8,0},{12,4},{1,9},{5,13},{9,1},{13,5},{2,10},{6,14},... | collective-permute-start | bytes 983048 | tf_op jit(solution)/shard_map/ppermute | solution.py:44
  546.5 37.5 %collective-permute-start.72 = (bf16[4,128,1152]{2,1,0:T(8,128)(2,1)S(1)}, bf16[4,128,1152]{2,1,0:T(8,128)(2,1)}, u32[]{:S(2)}, u32[]{:S(2)}) collective-permute-start(bf16[4,128,1152]{2,1,0:T(8,128)(2,1)S(1)} %pad_maximum_fusion.5.gown), channel_id=1, source_target_pairs={{0,16},{16,0},{1,17},{17,1},{2,18},{18,2},{3,19},{19,3},{4,20},{20... | collective-permute-start | bytes 3538952 | tf_op jit(solution)/shard_map/ppermute | solution.py:44
  562.7 20.7 %collective-permute-start.67 = (bf16[4,128,640]{2,1,0:T(8,128)(2,1)}, bf16[4,128,640]{2,1,0:T(8,128)(2,1)}, u32[]{:S(2)}, u32[]{:S(2)}) collective-permute-start(bf16[4,128,640]{2,1,0:T(8,128)(2,1)} %pad_maximum_fusion.8.own), channel_id=1, source_target_pairs={{0,16},{16,0},{1,17},{17,1},{2,18},{18,2},{3,19},{19,3},{4,20},{20... | collective-permute-start | bytes 1966088 | tf_op jit(solution)/shard_map/ppermute | solution.py:44
  571.3 25.7 %collective-permute-start.91 = (bf16[4,160,320]{2,1,0:T(8,128)(2,1)}, bf16[4,160,320]{2,1,0:T(8,128)(2,1)}, u32[]{:S(2)}, u32[]{:S(2)}) collective-permute-start(bf16[4,160,320]{2,1,0:T(8,128)(2,1)} %get-tuple-element.225), channel_id=1, source_target_pairs={{0,4},{12,8},{1,5},{13,9},{2,6},{14,10},{3,7},{15,11},{16,20},{28,... | collective-permute-start | bytes 1228808 | tf_op jit(solution)/shard_map/ppermute | solution.py:910
  575.6 19.1 %collective-permute-start.82 = (bf16[256,640]{1,0:T(8,128)(2,1)S(1)}, bf16[256,640]{1,0:T(8,128)(2,1)}, u32[]{:S(2)}, u32[]{:S(2)}) collective-permute-start(bf16[256,640]{1,0:T(8,128)(2,1)S(1)} %add_convert_fusion.9), channel_id=1, source_target_pairs={{0,4},{4,0},{8,12},{12,8},{1,5},{5,1},{9,13},{13,9},{2,6},{6,2},{1... | collective-permute-start | bytes 983048 | tf_op jit(solution)/shard_map/ppermute | solution.py:44
  580.7 24.5 %collective-permute-start.93 = (bf16[4,160,320]{2,1,0:T(8,128)(2,1)}, bf16[4,160,320]{2,1,0:T(8,128)(2,1)}, u32[]{:S(2)}, u32[]{:S(2)}) collective-permute-start(bf16[4,160,320]{2,1,0:T(8,128)(2,1)} %get-tuple-element.225), channel_id=1, source_target_pairs={{4,8},{8,4},{5,9},{9,5},{6,10},{10,6},{7,11},{11,7},{20,24},{24,20... | collective-permute-start | bytes 1228808 | tf_op jit(solution)/shard_map/ppermute | solution.py:912
  583.4 40.4 %collective-permute-start.90 = (bf16[4,160,320]{2,1,0:T(8,128)(2,1)}, bf16[4,160,320]{2,1,0:T(8,128)(2,1)}, u32[]{:S(2)}, u32[]{:S(2)}) collective-permute-start(bf16[4,160,320]{2,1,0:T(8,128)(2,1)} %get-tuple-element.226), channel_id=1, source_target_pairs={{0,4},{4,0},{8,12},{12,8},{1,5},{5,1},{9,13},{13,9},{2,6},{6,2},{1... | collective-permute-start | bytes 1228808 | tf_op jit(solution)/shard_map/ppermute | solution.py:44
  584.0 20.4 %collective-permute-start.63 = (f32[48,128]{1,0:T(8,128)S(1)}, f32[48,128]{1,0:T(8,128)S(1)}, u32[]{:S(2)}, u32[]{:S(2)}) collective-permute-start(f32[48,128]{1,0:T(8,128)S(1)} %add.151), channel_id=1, source_target_pairs={{0,8},{4,12},{8,0},{12,4},{1,9},{5,13},{9,1},{13,5},{2,10},{6,14},... | collective-permute-start | bytes 73736 | tf_op jit(solution)/shard_map/ppermute | solution.py:44
  595.9 32.1 %collective-permute-start.86 = (bf16[1024,640]{1,0:T(8,128)(2,1)S(1)}, bf16[1024,640]{1,0:T(8,128)(2,1)}, u32[]{:S(2)}, u32[]{:S(2)}) collective-permute-start(bf16[1024,640]{1,0:T(8,128)(2,1)S(1)} %bitcast.173), channel_id=1, source_target_pairs={{0,1},{1,0},{2,3},{3,2},{4,5},{5,4},{6,7},{7,6},{8,9},{9,8},{10,11... | collective-permute-start | bytes 3932168 | tf_op jit(solution)/shard_map/ppermute | solution.py:44
  597.0 31.8 %collective-permute-start.87 = (bf16[1024,640]{1,0:T(8,128)(2,1)S(1)}, bf16[1024,640]{1,0:T(8,128)(2,1)}, u32[]{:S(2)}, u32[]{:S(2)}) collective-permute-start(bf16[1024,640]{1,0:T(8,128)(2,1)S(1)} %bitcast.174), channel_id=1, source_target_pairs={{0,2},{1,3},{2,0},{3,1},{4,6},{5,7},{6,4},{7,5},{8,10},{9,11},{10,... | collective-permute-start | bytes 3932168 | tf_op jit(solution)/shard_map/ppermute | solution.py:44
  604.5 20.2 %collective-permute-start.92 = (bf16[4,160,320]{2,1,0:T(8,128)(2,1)}, bf16[4,160,320]{2,1,0:T(8,128)(2,1)}, u32[]{:S(2)}, u32[]{:S(2)}) collective-permute-start(bf16[4,160,320]{2,1,0:T(8,128)(2,1)} %fusion), channel_id=1, source_target_pairs={{0,8},{4,12},{8,0},{12,4},{1,9},{5,13},{9,1},{13,5},{2,10},{6,14},... | collective-permute-start | bytes 1228808 | tf_op jit(solution)/shard_map/ppermute | solution.py:44
  635.9 23.5 %collective-permute-start.101 = (bf16[1,160,800]{2,1,0:T(8,128)(2,1)S(1)}, bf16[1,160,800]{2,1,0:T(8,128)(2,1)S(1)}, u32[]{:S(2)}, u32[]{:S(2)}) collective-permute-start(bf16[1,160,800]{2,1,0:T(8,128)(2,1)S(1)} %get-tuple-element.243), channel_id=1, source_target_pairs={{0,8},{4,12},{8,0},{12,4},{1,9},{5,13},{9,1},{13,5},{2,10},{6,14},... | collective-permute-start | bytes 768008 | tf_op jit(solution)/shard_map/ppermute | solution.py:44
  637.3 29.4 %collective-permute-start.102 = (bf16[1,160,800]{2,1,0:T(8,128)(2,1)S(1)}, bf16[1,160,800]{2,1,0:T(8,128)(2,1)S(1)}, u32[]{:S(2)}, u32[]{:S(2)}) collective-permute-start(bf16[1,160,800]{2,1,0:T(8,128)(2,1)S(1)} %get-tuple-element.242), channel_id=1, source_target_pairs={{0,12},{4,8},{8,4},{12,0},{1,13},{5,9},{9,5},{13,1},{2,14},{6,10},... | collective-permute-start | bytes 768008 | tf_op jit(solution)/shard_map/ppermute | solution.py:44
  638.1 43.8 %collective-permute-start.89 = (bf16[512,640]{1,0:T(8,128)(2,1)}, bf16[512,640]{1,0:T(8,128)(2,1)}, u32[]{:S(2)}, u32[]{:S(2)}) collective-permute-start(bf16[512,640]{1,0:T(8,128)(2,1)} %slice.279), channel_id=1, source_target_pairs={{0,2},{1,3},{2,0},{3,1},{4,6},{5,7},{6,4},{7,5},{8,10},{9,11},{10,... | collective-permute-start | bytes 1966088 | tf_op jit(solution)/shard_map/ppermute | solution.py:44
  640.3 41.6 %collective-permute-start.88 = (bf16[512,640]{1,0:T(8,128)(2,1)}, bf16[512,640]{1,0:T(8,128)(2,1)}, u32[]{:S(2)}, u32[]{:S(2)}) collective-permute-start(bf16[512,640]{1,0:T(8,128)(2,1)} %slice.278), channel_id=1, source_target_pairs={{0,1},{1,0},{2,3},{3,2},{4,5},{5,4},{6,7},{7,6},{8,9},{9,8},{10,11... | collective-permute-start | bytes 1966088 | tf_op jit(solution)/shard_map/ppermute | solution.py:44
  642.7 26.0 %collective-permute-start.94 = (bf16[1,160,320]{2,1,0:T(8,128)(2,1)S(1)}, bf16[1,160,320]{2,1,0:T(8,128)(2,1)S(1)}, u32[]{:S(2)}, u32[]{:S(2)}) collective-permute-start(bf16[1,160,320]{2,1,0:T(8,128)(2,1)S(1)} %get-tuple-element.250), channel_id=1, source_target_pairs={{0,1},{1,0},{2,3},{3,2},{4,5},{5,4},{6,7},{7,6},{8,9},{9,8},{10,11... | collective-permute-start | bytes 307208 | tf_op jit(solution)/shard_map/ppermute | solution.py:44
  678.4 24.9 %collective-permute-start.97 = (bf16[2,160,800]{2,1,0:T(8,128)(2,1)S(1)}, bf16[2,160,800]{2,1,0:T(8,128)(2,1)S(1)}, u32[]{:S(2)}, u32[]{:S(2)}) collective-permute-start(bf16[2,160,800]{2,1,0:T(8,128)(2,1)S(1)} %get-tuple-element.222), channel_id=1, source_target_pairs={{0,4},{4,0},{8,12},{12,8},{1,5},{5,1},{9,13},{13,9},{2,6},{6,2},{1... | collective-permute-start | bytes 1536008 | tf_op jit(solution)/shard_map/ppermute | solution.py:44
  678.4 40.6 %collective-permute-start.98 = (bf16[2,160,800]{2,1,0:T(8,128)(2,1)S(1)}, bf16[2,160,800]{2,1,0:T(8,128)(2,1)S(1)}, u32[]{:S(2)}, u32[]{:S(2)}) collective-permute-start(bf16[2,160,800]{2,1,0:T(8,128)(2,1)S(1)} %get-tuple-element.221), channel_id=1, source_target_pairs={{0,8},{4,12},{8,0},{12,4},{1,9},{5,13},{9,1},{13,5},{2,10},{6,14},... | collective-permute-start | bytes 1536008 | tf_op jit(solution)/shard_map/ppermute | solution.py:44
  681.0 50.9 %collective-permute-start.99 = (bf16[2,160,800]{2,1,0:T(8,128)(2,1)S(1)}, bf16[2,160,800]{2,1,0:T(8,128)(2,1)S(1)}, u32[]{:S(2)}, u32[]{:S(2)}) collective-permute-start(bf16[2,160,800]{2,1,0:T(8,128)(2,1)S(1)} %get-tuple-element.220), channel_id=1, source_target_pairs={{0,12},{4,8},{8,4},{12,0},{1,13},{5,9},{9,5},{13,1},{2,14},{6,10},... | collective-permute-start | bytes 1536008 | tf_op jit(solution)/shard_map/ppermute | solution.py:44
  (156 other events, 1892.2 us)
Sparse Core Ops, SparseCore 0:
  48.1 56.6 all-gather.4
  160.9 115.2 all-gather.2
  341.5 55.8 reduce-scatter.4
  422.8 108.1 reduce-scatter.2
